TPU v7x, 32 devices: a whole 2x2x4 slice. The times are simulated.
32 devices in a mesh: lead: 4 (over y, x), dp: 2 (over core), lat: 4 (over z).
Axes of the slice: x: 2, y: 2, z: 4, core: 2. Of those that a mesh axis runs over, the one named last changes fastest.
Arguments:
- field: bfloat16 [4, 16, 32, 64, 128], P('lead', 'dp', 'lat'), may hold values from -6 to 6
- cotangent: bfloat16 [4, 16, 32, 64, 128], P('lead', 'dp', 'lat'), may hold values from -6 to 6
- land_sea: int32 [4, 16, 32, 64], P('lead', 'dp', 'lat'), may hold values from 0 to 1, as said below
- conv1_weight: bfloat16 [3, 3, 128, 128], replicated, may hold values from -0.1875 to 0.1875
- conv1_bias: float32 [128], replicated, may hold values from -3 to 3
- first_norm_scale: float32 [128], replicated, may hold values from 0.5 to 1.5
- norm1_shift: float32 [128], replicated, may hold values from -3 to 3
- conv2_weight: bfloat16 [3, 3, 128, 128], replicated, may hold values from -0.1875 to 0.1875
- conv2_bias: float32 [128], replicated, may hold values from -3 to 3
- second_norm_scale: float32 [128], replicated, may hold values from 0.5 to 1.5
- norm2_shift: float32 [128], replicated, may hold values from -3 to 3
Outputs:
- output: bfloat16 [4, 16, 32, 64, 128], P('lead', 'dp', 'lat')
- field_grad: bfloat16 [4, 16, 32, 64, 128], P('lead', 'dp', 'lat')
- conv1_weight_grad: float32 [3, 3, 128, 128], replicated
- conv1_bias_grad: float32 [128], replicated
- norm1_gain_grad: float32 [128], replicated
- norm1_shift_grad: float32 [128], replicated
- conv2_weight_grad: float32 [3, 3, 128, 128], replicated
- conv2_bias_grad: float32 [128], replicated
- norm2_gain_grad: float32 [128], replicated
- norm2_shift_grad: float32 [128], replicated
Inputs may be any that keep to these rules, and one draw needn't show every extreme that they name: `land_sea`: 1 marks a pixel that counts in the norms, 0 one that is left out.
All inputs are finite; a program needn't handle non-finite values.
Results may differ from a plain program's by a relative error of at most 0.024.
Values may be sent and summed in bfloat16 or wider, within the bound.
No kernel may reach another device: no remote copies, remote signals or barrier semaphores. Data moves between devices by JAX's collectives and lax.ppermute only.
A program may use at most 64 MiB of HBM per device.

v0:
```python
import functools

import jax
import jax.numpy as jnp
from jax import lax
from jax.experimental import pallas as pl
from jax.experimental.pallas import tpu as pltpu
from jax.sharding import PartitionSpec as P

EPSILON = 1e-05
BF16 = jnp.bfloat16
F32 = jnp.float32
VMEM = pl.BlockSpec(memory_space=pltpu.VMEM)
SMALL = 16


def fill_toeplitz(taps_ref, out_ref):
    c = taps_ref.shape[-1]
    zero = jnp.zeros((c, c), BF16)
    for b in range(3):
        for i in range(4):
            for j in range(2):
                block = taps_ref[i - j, b] if 0 <= i - j < 3 else zero
                out_ref[b, i * c : (i + 1) * c, j * c : (j + 1) * c] = block


def fill_toeplitz_transposed(taps_ref, out_ref):
    c = taps_ref.shape[-1]
    zero = jnp.zeros((c, c), BF16)
    for b in range(3):
        for i in range(4):
            for j in range(2):
                block = taps_ref[2 - (i - j), 2 - b] if 0 <= i - j < 3 else zero
                out_ref[b, j * c : (j + 1) * c, i * c : (i + 1) * c] = block


def convolve_rows(row, starts, weights_ref, across, transposed):
    left = jnp.concatenate(
        [jnp.concatenate([row(r - 1 + i) for r in starts], 0) for i in range(4)], 1
    )
    c = left.shape[1] // 4
    dims = (((1,), (1 if transposed else 0,)), ((), ()))
    taps = [
        lax.dot_general(left, weights_ref[b], dims, preferred_element_type=F32)
        for b in range(3)
    ]

    def piece(pair, j):
        part = [t[pair * across : (pair + 1) * across, j * c : (j + 1) * c] for t in taps]
        return pltpu.roll(part[0], 1, 0) + part[1] + pltpu.roll(part[2], across - 1, 0)

    return piece


def silu_and_slope(hidden):
    gate = 0.5 + 0.5 * jnp.tanh(0.5 * hidden)
    active = hidden * gate
    return active, gate + active * (1.0 - gate)


def silu(value):
    return value * (0.5 + 0.5 * jnp.tanh(0.5 * value))


def fold(value):
    return value.reshape(-1, 8, value.shape[-1]).sum(0)


def join(stats, count, at, sums):
    centres = stats[:, at + 2 : at + 3]
    mean = (stats[:, at : at + 1] + sums * centres).sum(0) / count
    away = centres - mean
    squares = stats[:, at + 1 : at + 2] + away * (2.0 * stats[:, at : at + 1] + sums * away)
    variance = jnp.maximum(squares.sum(0) / count, 0.0)
    return mean, lax.rsqrt(variance + EPSILON)


def pick(even, when_even, when_odd):
    return jnp.where(even, when_even, when_odd)


def column_mask(bits, k, c):
    tile = bits[k // 128]
    return jnp.broadcast_to(tile[:, k % 128 : k % 128 + 1].astype(F32), (tile.shape[0], c))


def near_rows_kernel(x_ref, gx_ref, gp_ref, sems):
    height = x_ref.shape[1]
    even = lax.axis_index("lat") % 2 == 0
    last = jnp.where(even, height - 1, 0)
    copies = [
        pltpu.make_async_copy(x_ref.at[:, pl.ds(at, 1)], out, sems.at[i])
        for i, (at, out) in enumerate(((last, gx_ref), (height - 1 - last, gp_ref)))
    ]
    for copy in copies:
        copy.start()
    for copy in copies:
        copy.wait()


def far_rows_kernel(x_ref, u_ref, bits_ref, gx_ref, gp_ref, hx_ref, hp_ref):
    samples, height, across, c = x_ref.shape
    even = lax.axis_index("lat") % 2 == 0
    for out, down in ((hx_ref, even), (hp_ref, jnp.logical_not(even))):
        first = jnp.where(down, height - 3, 1)
        edge = jnp.where(down, height - 1, 0)
        for s in range(samples):
            out[2 * s] = x_ref[s, first]
            out[2 * s + 1] = x_ref[s, first + 1]
            out[2 * samples + s] = u_ref[s, edge]
        for k in range(bits_ref.shape[0]):
            out[3 * samples + k] = bits_ref[k].astype(BF16)


def stats_block(rows, c):
    return jnp.concatenate(rows + [jnp.zeros((8 - len(rows), c), F32)], 0)


def gather(refs):
    return jnp.concatenate([r[...] for r in refs], 0)


def own_row(inner_ref, outer_ref, s, r, height):
    if 2 <= r < height - 2:
        return inner_ref[s, r - 2]
    return outer_ref[s, r if r < 2 else r - height + 4]


def middle(value):
    return value.mean(0, keepdims=True)


def add_moments(sums, active, mask):
    masked = active * mask
    sums[0] += fold(masked)
    sums[1] += fold(masked * active)
    return masked


def conv1_inner_kernel(x_ref, mask_ref, w_ref, b_ref, a_ref, s_ref, m_ref, bits_ref, t_ref, st_ref):
    samples, height, across, c = x_ref.shape
    for k in range(bits_ref.shape[0]):
        bits = mask_ref[k * 128 : (k + 1) * 128].astype(F32)
        bits = jnp.concatenate([bits, jnp.zeros((bits.shape[0], 128 - across), F32)], 1)
        if bits.shape[0] < 128:
            bits = jnp.concatenate([bits, jnp.zeros((128 - bits.shape[0], 128), F32)], 0)
        bits_ref[k] = bits.T[:across]
    fill_toeplitz(w_ref, t_ref)
    bias = b_ref[...]
    sums = [jnp.zeros((8, c), F32) for _ in range(3)]
    centre = None
    for s in range(samples):
        piece = convolve_rows(lambda r: x_ref[s, r], range(2, height - 2, 2), t_ref, across, False)
        for r in range(height):
            mask = column_mask(bits_ref, s * height + r, c)
            m_ref[s, r] = mask
            sums[2] += fold(mask)
            if not 2 <= r < height - 2:
                continue
            active, slope = silu_and_slope(piece((r - 2) // 2, r % 2) + bias)
            if centre is None:
                centre = middle(active)
            active = active - centre
            a_ref[s, r - 2] = active
            s_ref[s, r - 2] = slope * mask
            add_moments(sums, active, mask)
    rows = [v.sum(0, keepdims=True) for v in sums]
    st_ref[...] = stats_block([rows[0], rows[1], centre, rows[2]], c)


def conv1_outer_kernel(x_ref, gx_ref, gp_ref, m_ref, t_ref, b_ref, part_ref, a_ref, s_ref, st_ref):
    samples, height, across, c = x_ref.shape
    even = lax.axis_index("lat") % 2 == 0
    bias = b_ref[...]
    centre = part_ref[2:3]

    def row(r):
        if r < 0:
            parts = [pick(even, gp_ref[s, 0], gx_ref[s, 0]) for s in range(samples)]
        elif r >= height:
            parts = [pick(even, gx_ref[s, 0], gp_ref[s, 0]) for s in range(samples)]
        else:
            parts = [x_ref[s, r] for s in range(samples)]
        return jnp.concatenate(parts, 0)

    sums = [jnp.zeros((8, c), F32) for _ in range(2)]
    for slot, start in ((0, 0), (2, height - 2)):
        piece = convolve_rows(row, (start,), t_ref, across, False)
        for s in range(samples):
            for j in range(2):
                active, slope = silu_and_slope(piece(s, j) + bias)
                active = active - centre
                mask = m_ref[s, start + j]
                a_ref[s, slot + j] = active
                s_ref[s, slot + j] = slope * mask
                add_moments(sums, active, mask)
    rows = [part_ref[i : i + 1] + v.sum(0, keepdims=True) for i, v in enumerate(sums)]
    st_ref[...] = stats_block([rows[0], rows[1], centre, part_ref[3:4]], c)


def conv1_edge_kernel(
    x_ref, gx_ref, gp_ref, hx_ref, hp_ref, u_ref, m_ref, st_ref, t_ref, b_ref, w2_ref,
    a_ref, mh_ref, mu_ref, su_ref, t2_ref, tt2_ref,
):
    samples, height, across, c = x_ref.shape
    even = lax.axis_index("lat") % 2 == 0
    fill_toeplitz(w2_ref, t2_ref)
    fill_toeplitz_transposed(w2_ref, tt2_ref)
    bias = b_ref[...]
    centre = st_ref[2:3]

    def row(r):
        parts = []
        for s in range(samples):
            if r < -1:
                parts.append(pick(even, hp_ref[2 * s + r + 3], hx_ref[2 * s + r + 3]))
            elif r == -1:
                parts.append(pick(even, gp_ref[s, 0], gx_ref[s, 0]))
            elif r < height:
                parts.append(x_ref[s, r])
            elif r == height:
                parts.append(pick(even, gx_ref[s, 0], gp_ref[s, 0]))
            else:
                j = r - height - 1
                parts.append(pick(even, hx_ref[2 * s + j], hp_ref[2 * s + j]))
        return jnp.concatenate(parts, 0)

    slabs = slice(3 * samples, hx_ref.shape[0])
    above = pick(even, hp_ref[slabs], hx_ref[slabs])
    below = pick(even, hx_ref[slabs], hp_ref[slabs])
    total = jnp.zeros((8, c), F32)
    for slot, start in ((0, -2), (2, height)):
        piece = convolve_rows(row, (start,), t_ref, across, False)
        for s in range(samples):
            for j in range(2):
                a_ref[s, slot + j] = silu(piece(s, j) + bias) - centre
                if start < 0:
                    mask = column_mask(above, s * height + height - 2 + j, c)
                else:
                    mask = column_mask(below, s * height + j, c)
                mh_ref[s, slot + j] = mask
    for s in range(samples):
        up = pick(even, hp_ref[2 * samples + s], hx_ref[2 * samples + s])
        mu_ref[s, 0] = up.astype(F32) * mh_ref[s, 1]
        for r in range(height):
            value = u_ref[s, r].astype(F32) * m_ref[s, r]
            mu_ref[s, r + 1] = value
            total += fold(value)
        down = pick(even, hx_ref[2 * samples + s], hp_ref[2 * samples + s])
        mu_ref[s, height + 1] = down.astype(F32) * mh_ref[s, 2]
    su_ref[...] = stats_block([total.sum(0, keepdims=True)], c)


def conv2_kernel(
    pieces,
    own_ref, a_ref, ao_ref, ah_ref, m_ref, mh_ref, mu_ref, su_ref, k_ref, b_ref, g_ref, t_ref, *refs,
):
    stats, (n_ref, a2_ref, s2_ref, c1_ref, st2_ref, ext_ref) = gather(refs[:pieces]), refs[pieces:]
    samples, height, across, c = m_ref.shape
    counts = stats[:, 3:4]
    count = counts.sum(0)
    mean, inverse = join(stats, count, 0, counts)
    offset = mean - own_ref[2:3]
    scale = inverse * g_ref[...]
    shift = t_ref[...] - offset * scale
    c1_ref[...] = stats_block([offset, inverse, count, mean], c)
    bias = b_ref[...]
    sums = [jnp.zeros((8, c), F32) for _ in range(3)]
    centre = None
    for s in range(samples):
        ext = ext_ref.at[s % 2]
        for i in range(height + 4):
            r = i - 2
            if 0 <= r < height:
                value, mask = own_row(a_ref, ao_ref, s, r, height), m_ref[s, r]
            else:
                j = i if r < 0 else r - height + 2
                value, mask = ah_ref[s, j], mh_ref[s, j]
            ext[i] = ((value * scale + shift) * mask).astype(BF16)
            if 1 <= i < height + 3:
                n_ref[s, i - 1] = ext[i]

        piece = convolve_rows(
            lambda r: ext[r + 2], range(-1, height + 1, 2), k_ref, across, False
        )
        for i in range(height + 2):
            r = i - 1
            active, slope = silu_and_slope(piece(i // 2, i % 2) + bias)
            if centre is None:
                centre = middle(active)
            active = active - centre
            if 0 <= r < height:
                mask = m_ref[s, r]
                add_moments(sums, active, mask)
                sums[2] += fold(active * mu_ref[s, i])
            else:
                mask = mh_ref[s, 1 if r < 0 else 2]
            a2_ref[s, i] = active
            s2_ref[s, i] = slope * mask
    rows = [v.sum(0, keepdims=True) for v in sums]
    st2_ref[...] = stats_block(
        [rows[0], rows[1], centre, rows[2], su_ref[0:1], own_ref[3:4]], c
    )


def back_terms(scale, inverse, offset, gain_sum, shift_sum, count):
    by_active = -scale * gain_sum * inverse / count
    constant = -scale * (shift_sum - offset * inverse * gain_sum) / count
    return by_active, constant


def back2_kernel(
    pieces,
    own_ref, st1_ref, c1_ref, a2_ref, s2_ref, mu_ref, m_ref, a_ref, ao_ref, k_ref, g_ref, t_ref, *refs,
):
    stats, (d_ref, dn_ref, c2_ref, st3_ref, ext_ref) = gather(refs[:pieces]), refs[pieces:]
    samples, height, across, c = m_ref.shape
    count = c1_ref[2:3]
    mean, inverse = join(stats, count, 0, stats[:, 5:6])
    offset = mean - own_ref[2:3]
    shift_sum = stats[:, 4:5].sum(0)
    away = stats[:, 2:3] - mean
    gain_sum = inverse * (stats[:, 3:4] + away * stats[:, 4:5]).sum(0)
    scale = inverse * g_ref[...]
    by_active, constant = back_terms(scale, inverse, offset, gain_sum, shift_sum, count)
    c2_ref[...] = stats_block([scale, t_ref[...] - offset * scale, gain_sum, shift_sum], c)
    sums = [jnp.zeros((8, c), F32) for _ in range(2)]
    for s in range(samples):
        ext = ext_ref.at[s % 2]
        for i in range(height + 2):
            grad = mu_ref[s, i] * scale + (a2_ref[s, i] * by_active + constant)
            ext[i] = (grad * s2_ref[s, i]).astype(BF16)
            if 0 < i <= height:
                d_ref[s, i - 1] = ext[i]
        piece = convolve_rows(
            lambda r: ext[r + 1], range(0, height, 2), k_ref, across, True
        )
        for r in range(height):
            part = piece(r // 2, r % 2)
            dn_ref[s, r] = part
            masked = part * m_ref[s, r]
            sums[0] += fold(masked)
            sums[1] += fold(masked * own_row(a_ref, ao_ref, s, r, height))
    rows = [v.sum(0, keepdims=True) for v in sums]
    st3_ref[...] = stats_block([rows[0], rows[1], st1_ref[2:3]], c)


def weight_products(rows, centre, turned, total_ref, first):
    windows = jnp.concatenate(rows, 1)
    product = lax.dot_general(
        windows,
        jnp.concatenate([turned[0], centre, turned[1]], 1),
        (((0,), (0,)), ((), ())),
        preferred_element_type=F32,
    )
    if first:
        total_ref[...] = product
    else:
        total_ref[...] += product


def turn(value, across):
    c = value.shape[-1]
    return [
        pltpu.roll(value, k, 1).astype(BF16).reshape(-1, c) for k in (across - 1, 1)
    ]


def weight2_kernel(n_ref, d_ref, after_ref, w_ref, b_ref, acc_ref):
    samples, height, across, c = d_ref.shape
    bias = jnp.zeros((8, c), F32)
    for s in range(samples):
        grad = d_ref[s]
        wide = grad.astype(F32)
        bias += fold(wide)
        rows = [n_ref[s, a : a + height].reshape(-1, c) for a in range(3)]
        weight_products(rows, grad.reshape(-1, c), turn(wide, across), acc_ref, s == 0)
    b_ref[...] = jnp.broadcast_to(bias.sum(0, keepdims=True), b_ref.shape)
    for a in range(3):
        for b in range(3):
            at = (a * 3 + b) * c
            w_ref[at : at + c] = acc_ref[a * c : (a + 1) * c, b * c : (b + 1) * c].astype(BF16)


def output_kernel(x_ref, a2_ref, m_ref, c2_ref, after_ref, o_ref, done_ref):
    samples, height, across, c = x_ref.shape
    scale, shift = c2_ref[0:1], c2_ref[1:2]
    for s in range(samples):
        for r in range(height):
            normed = (a2_ref[s, r + 1] * scale + shift) * m_ref[s, r]
            o_ref[s, r] = (x_ref[s, r].astype(F32) + normed).astype(BF16)
    done_ref[...] = jnp.zeros(done_ref.shape, F32)


def small_rows(rows, c):
    high = jnp.concatenate(rows + [jnp.zeros((8 - len(rows), c), F32)], 0)
    first = high.astype(BF16)
    return jnp.concatenate([first, (high - first.astype(F32)).astype(BF16)], 0)


def weight1_kernel(
    group, leads, pieces,
    c1_ref, c2_ref, dn_ref, a_ref, ao_ref, s_ref, so_ref, x_ref, gx_ref, gp_ref, g_ref, w2_ref, b2_ref, *refs,
):
    stats = gather(refs[:pieces])
    d_ref, dx_ref, dp_ref, send_ref, keep_ref, acc_ref = refs[pieces:]
    samples, height, across, c = x_ref.shape
    even = lax.axis_index("lat") % 2 == 0
    lead = lax.axis_index("lead")
    core = lax.axis_index("dp") % 2
    offset, inverse, count, mean = (c1_ref[i : i + 1] for i in range(4))
    shift_sum = stats[:, 0:1].sum(0)
    away = stats[:, 2:3] - mean
    gain_sum = inverse * (stats[:, 1:2] + away * stats[:, 0:1]).sum(0)
    scale = inverse * g_ref[...]
    by_active, constant = back_terms(scale, inverse, offset, gain_sum, shift_sum, count)
    bias = jnp.zeros((8, c), F32)
    for s in range(samples):
        for r in range(height):
            active = own_row(a_ref, ao_ref, s, r, height)
            grad = dn_ref[s, r] * scale + (active * by_active + constant)
            d_ref[s, r] = (grad * own_row(s_ref, so_ref, s, r, height)).astype(BF16)
        grad = d_ref[s]
        dx_ref[s] = pick(even, grad[height - 1], grad[0])
        dp_ref[s] = pick(even, grad[0], grad[height - 1])
        wide = grad.astype(F32)
        bias += fold(wide)
        above = pick(even, gp_ref[s, 0], gx_ref[s, 0])
        below = pick(even, gx_ref[s, 0], gp_ref[s, 0])
        body = x_ref[s].reshape(-1, c)
        rows = [
            jnp.concatenate([above, body[: (height - 1) * across]], 0),
            body,
            jnp.concatenate([body[across:], below], 0),
        ]
        weight_products(rows, grad.reshape(-1, c), turn(wide, across), acc_ref, s == 0)

    share = 1.0 / group
    small = [
        small_rows([bias.sum(0, keepdims=True), gain_sum * share, shift_sum * share], c),
        small_rows([b2_ref[0:1], c2_ref[2:3] * share, c2_ref[3:4] * share], c),
    ]

    def put(target, which):
        size = 9 * c // leads
        for j in range(leads):
            slot = j ^ lead
            if which == 1:
                target[slot, :size] = w2_ref[j * size : (j + 1) * size]
            else:
                at = j * size
                while at < (j + 1) * size:
                    tap, low = at // c, at % c
                    step = min(c - low, (j + 1) * size - at)
                    a, b = tap // 3, tap % 3
                    target[slot, at - j * size : at - j * size + step] = acc_ref[
                        a * c + low : a * c + low + step, b * c : (b + 1) * c
                    ].astype(BF16)
                    at += step
            target[slot, size:] = small[which]

    @pl.when(core == 0)
    def _():
        put(keep_ref, 0)
        put(send_ref, 1)

    @pl.when(core != 0)
    def _():
        put(keep_ref, 1)
        put(send_ref, 0)


def input_grad_kernel(d_ref, ex_ref, ep_ref, u_ref, w_ref, after_ref, o_ref, done_ref, k_ref):
    samples, height, across, c = u_ref.shape
    even = lax.axis_index("lat") % 2 == 0
    fill_toeplitz_transposed(w_ref, k_ref)
    for s in range(samples):

        def row(r):
            if r < 0:
                return pick(even, ep_ref[s], ex_ref[s])
            if r >= height:
                return pick(even, ex_ref[s], ep_ref[s])
            return d_ref[s, r]

        piece = convolve_rows(row, range(0, height, 2), k_ref, across, True)
        for r in range(height):
            o_ref[s, r] = (u_ref[s, r].astype(F32) + piece(r // 2, r % 2)).astype(BF16)
    done_ref[...] = jnp.zeros(done_ref.shape, F32)


def finish_kernel(leads, mine_ref, *refs):
    got_refs, other_ref = refs[: leads - 1], refs[leads - 1]
    first, second = refs[leads + 1 : leads + 5], refs[leads + 5 :]
    core = lax.axis_index("dp") % 2
    lead = lax.axis_index("lead")
    size = mine_ref.shape[0] - SMALL

    def put(outs, chunk, small):
        for k in range(leads):
            at = pl.multiple_of((k ^ lead) * size, 16)
            outs[0][pl.ds(at, size)] = chunk(k).astype(F32)
        total = small[:8].astype(F32) + small[8:].astype(F32)
        for i in range(3):
            outs[i + 1][...] = total[i : i + 1]

    def own(outs):
        put(outs, lambda k: got_refs[k - 1][...] if k else mine_ref[:size], mine_ref[size:])

    def other(outs):
        put(
            outs,
            lambda k: other_ref[k * size : (k + 1) * size],
            other_ref[leads * size :],
        )

    @pl.when(core == 0)
    def _():
        own(first)
        other(second)

    @pl.when(core != 0)
    def _():
        other(first)
        own(second)


def add_kernel(parts, waits, *refs):
    outs = refs[parts + waits :]
    size = outs[0].shape[0] - SMALL
    for k, out in enumerate(outs):
        chunk = [r.at[k] if len(r.shape) == 3 else r for r in refs[:parts]]
        total = functools.reduce(lambda a, b: a + b, [r[...].astype(F32) for r in chunk])
        out[:size] = total[:size].astype(BF16)
        small = total[size : size + 8] + total[size + 8 :]
        high = small.astype(BF16)
        out[size:] = jnp.concatenate([high, (small - high.astype(F32)).astype(BF16)], 0)


def call(kernel, outs, scratch, operands, name, flops=0, waits=(), space=VMEM):
    size = sum(o.size * o.dtype.itemsize for o in operands)
    return pl.pallas_call(
        kernel,
        out_shape=outs,
        in_specs=[space] * len(operands) + [pl.BlockSpec(memory_space=pl.ANY)] * len(waits),
        out_specs=jax.tree.map(lambda _: space, outs),
        scratch_shapes=scratch,
        compiler_params=pltpu.CompilerParams(vmem_limit_bytes=16 * 2**20),
        cost_estimate=pl.CostEstimate(flops=flops, bytes_accessed=size, transcendentals=0),
        name=name,
    )(*operands, *waits)


def swap(value, axis, k):
    return lax.ppermute(value, axis, [(i, i ^ k) for i in range(lax.axis_size(axis))])


def neighbours(value_x, value_p, axis):
    n = lax.axis_size(axis)
    first = [(i, i ^ 1) for i in range(n) if i ^ 1 < n]
    second = [(i, i + 1) for i in range(1, n - 1, 2)]
    second += [(j, i) for i, j in second]
    return lax.ppermute(value_x, axis, first), lax.ppermute(value_p, axis, second)


def spread(stats):
    blocks, k = stats[None], 1
    while k < lax.axis_size("dp"):
        blocks = jnp.concatenate([blocks, swap(blocks, "dp", k)], 0)
        k *= 2
    return [blocks] + [swap(blocks, "lat", k) for k in range(1, lax.axis_size("lat"))]


def add_chunks(parts, name, outs=1, waits=()):
    shape = jax.ShapeDtypeStruct(parts[0].shape[-2:], BF16)
    return call(
        functools.partial(add_kernel, len(parts), len(waits)),
        [shape] * outs,
        [],
        parts,
        name,
        waits=waits,
    )


def sum_everywhere(send, keep, beside_lat, beside_last):
    leads, lats = lax.axis_size("lead"), lax.axis_size("lat")
    chunks = add_chunks([keep, swap(send, "dp", 1)], "add_dp", leads)
    got = [swap(chunks[k], "lead", k) for k in range(1, leads)]
    (mine,) = add_chunks([chunks[0]] + got, "add_lead")
    got = [swap(mine, "lat", k) for k in range(1, lats)]
    first = beside_lat(chunks[0])
    (mine,) = add_chunks([mine] + got, "add_lat", waits=(first[1],))
    k = 2
    while k < lax.axis_size("dp"):
        (mine,) = add_chunks([mine, swap(mine, "dp", k)], "add_far_dp")
        k *= 2
    size, c = mine.shape[0] - SMALL, mine.shape[1]
    got = [swap(mine[:size], "lead", k) for k in range(1, leads)]
    other = swap(jnp.concatenate([mine[:size]] + got + [mine[size:]], 0), "dp", 1)
    last = beside_last(mine)
    one = [jax.ShapeDtypeStruct((leads * size, c), F32)] + [jax.ShapeDtypeStruct((1, c), F32)] * 3
    sums = call(
        functools.partial(finish_kernel, leads),
        one + one,
        [],
        (mine, *got, other),
        "finish",
        waits=(last[1],),
    )
    return sums[:4], sums[4:], first[0], last[0]


def shards(
    field,
    cotangent,
    land_sea,
    conv1_weight,
    conv1_bias,
    first_norm_scale,
    norm1_shift,
    conv2_weight,
    conv2_bias,
    second_norm_scale,
    norm2_shift,
):
    x, u, mask = field[0], cotangent[0], land_sea[0]
    samples, height, across, c = x.shape
    group = lax.axis_size("dp") * lax.axis_size("lat")
    leads = lax.axis_size("lead")
    slabs = -(-samples * height // 128)
    vec = lambda v: v.reshape(1, c)
    b1, g1, t1 = vec(conv1_bias), vec(first_norm_scale), vec(norm1_shift)
    b2, g2, t2 = vec(conv2_bias), vec(second_norm_scale), vec(norm2_shift)

    array = jax.ShapeDtypeStruct
    shape = lambda rows, dtype=F32: array((samples, rows, across, c), dtype)
    edge = array((samples, across, c), BF16)
    vector = array((8, c), F32)
    weights = array((3, 4 * c, 2 * c), BF16)
    turned = array((3, 2 * c, 4 * c), BF16)
    ext = lambda rows: pltpu.VMEM((2, rows, across, c), BF16)
    acc = pltpu.VMEM((3 * c, 3 * c), F32)
    conv_flops = 2 * 9 * c * c * samples * height * across

    near = call(
        near_rows_kernel,
        (shape(1, BF16), shape(1, BF16)),
        [pltpu.SemaphoreType.DMA((2,))],
        (x,),
        "near_rows",
        space=pl.BlockSpec(memory_space=pl.ANY),
    )
    gx, gp = neighbours(*near, "lat")
    a1, s1, wide_mask, bits, w1t, part = call(
        conv1_inner_kernel,
        (
            shape(height - 4),
            shape(height - 4),
            shape(height),
            array((slabs, across, 128), F32),
            weights,
            vector,
        ),
        [],
        (x, mask.reshape(samples * height, across), conv1_weight, b1),
        "conv1_inner",
        conv_flops,
    )
    packed = array((3 * samples + slabs, across, c), BF16)
    hx, hp = neighbours(
        *call(far_rows_kernel, (packed, packed), [], (x, u, bits), "far_rows", waits=(gx, gp)), "lat"
    )
    a1o, s1o, own1 = call(
        conv1_outer_kernel,
        (shape(4), shape(4), vector),
        [],
        (x, gx, gp, wide_mask, w1t, b1, part),
        "conv1_outer",
        conv_flops // 2,
    )
    a1h, halo_mask, mu, mu_sum, w2t, w2tt = call(
        conv1_edge_kernel,
        (shape(4), shape(4), shape(height + 2), vector, weights, turned),
        [],
        (x, gx, gp, hx, hp, u, wide_mask, own1, w1t, b1, conv2_weight),
        "conv1_edges",
        conv_flops // 2,
    )
    st1 = spread(own1)
    n1, a2, s2, c1, own2 = call(
        functools.partial(conv2_kernel, len(st1)),
        (shape(height + 2, BF16), shape(height + 2), shape(height + 2), vector, vector),
        [ext(height + 4)],
        (own1, a1, a1o, a1h, wide_mask, halo_mask, mu, mu_sum, w2t, b2, g1, t1, *st1),
        "conv2",
        conv_flops,
    )
    st2 = spread(own2)
    d2, dn1, c2, own3 = call(
        functools.partial(back2_kernel, len(st2)),
        (shape(height, BF16), shape(height), vector, vector),
        [ext(height + 2)],
        (own2, own1, c1, a2, s2, mu, wide_mask, a1, a1o, w2tt, g2, t2, *st2),
        "conv2_back",
        conv_flops,
    )
    st3 = spread(own3)
    w2, bias2 = call(
        weight2_kernel,
        (array((9 * c, c), BF16), vector),
        [acc],
        (n1, d2),
        "conv2_weight_grad",
        conv_flops,
        waits=(st3[0],),
    )
    chunks = array((leads, 9 * c // leads + SMALL, c), BF16)
    d1, dx, dp, send, keep = call(
        functools.partial(weight1_kernel, group, leads, len(st3)),
        (shape(height, BF16), edge, edge, chunks, chunks),
        [acc],
        (c1, c2, dn1, a1, a1o, s1, s1o, x, gx, gp, g1, w2, bias2, *st3),
        "conv1_weight_grad",
        conv_flops,
    )
    dx, dp = neighbours(dx, dp, "lat")
    first, second, grad_input, output = sum_everywhere(
        send,
        keep,
        lambda after: call(
            input_grad_kernel,
            (shape(height, BF16), vector),
            [pltpu.VMEM(turned.shape, BF16)],
            (d1, dx, dp, u, conv1_weight),
            "conv1_back",
            conv_flops,
            waits=(after,),
        ),
        lambda after: call(
            output_kernel,
            (shape(height, BF16), vector),
            [],
            (x, a2, wide_mask, c2),
            "output",
            conv_flops // 2,
            waits=(after,),
        ),
    )
    sums = []
    for part in (first, second):
        sums += [part[0].reshape(3, 3, c, c)] + [v.reshape(c) for v in part[1:]]
    return (output[None], grad_input[None], *sums)


def solution(mesh):
    tiles = P("lead", "dp", "lat", None, None)
    in_specs = (tiles, tiles, P("lead", "dp", "lat", None)) + (P(),) * 8
    out_specs = (tiles, tiles) + (P(),) * 8
    return jax.shard_map(shards, mesh=mesh, in_specs=in_specs, out_specs=out_specs, check_vma=False)
```

profile of v0, /device:TPU:0, one launch (start us, length us, event | category | flops | bytes accessed | tf_op | source)
XLA Modules:
  0.0 81.9 jit_solution(16052228731611021312)
XLA Ops:
  0.7 1.2 %copy-done = bf16[1,8,8,64,128]{4,3,2,1,0:T(8,128)(2,1)S(1)} copy-done((bf16[1,8,8,64,128]{4,3,2,1,0:T(8,128)(2,1)S(1)}, bf16[1,8,8,64,128]{4,3,2,1,0:T(8,128)(2,1)}, u32[]{:S(2)}) %copy-start) | copy-done | bytes 1048600
  1.9 3.1 %collective-permute-start = (bf16[8,1,64,128]{3,2,1,0:T(8,128)(2,1)S(1)}, bf16[8,1,64,128]{3,2,1,0:T(8,128)(2,1)S(1)}, u32[]{:S(2)}, u32[]{:S(2)}) collective-permute-start(bf16[8,1,64,128]{3,2,1,0:T(8,128)(2,1)S(1)} %get-tuple-element.61), channel_id=1, source_target_pairs={{0,1},{1,0},{2,3},{3,2},{4,5},{5,4},{6,7},{7,6},{8,9},{9,8},{10,11... | collective-permute-start | bytes 393224 | tf_op jit(solution)/shard_map/ppermute | solution.py:563
  8.1 1.6 %conv1_inner.1 = (f32[8,4,64,128]{3,2,1,0:T(8,128)S(1)}, f32[8,4,64,128]{3,2,1,0:T(8,128)S(1)}, f32[8,8,64,128]{3,2,1,0:T(8,128)S(1)}, f32[1,64,128]{2,1,0:T(8,1...) custom-call(bf16[8,8,64,128]{3,2,1,0:T(8,128)(2,1)S(1)} %bitcast.23, s32[64,64]{1,0:T(8,128)S(1)} %bitcast.47, ...), custom_call_target="tpu_custom_call" | custom-call | flops 1207959552 | bytes 1360384 | tf_op jit(solution)/shard_map/conv1_inner/pallas_call | solution.py:542
  9.8 4.5 %collective-permute-start.2 = (bf16[25,64,128]{2,1,0:T(8,128)(2,1)S(1)}, bf16[25,64,128]{2,1,0:T(8,128)(2,1)S(1)}, u32[]{:S(2)}, u32[]{:S(2)}) collective-permute-start(bf16[25,64,128]{2,1,0:T(8,128)(2,1)S(1)} %get-tuple-element.70), channel_id=1, source_target_pairs={{0,1},{1,0},{2,3},{3,2},{4,5},{5,4},{6,7},{7,6},{8,9},{9,8},{10,11... | collective-permute-start | bytes 1228808 | tf_op jit(solution)/shard_map/ppermute | solution.py:563
  14.9 1.4 %conv1_outer.1 = (f32[8,4,64,128]{3,2,1,0:T(8,128)S(1)}, f32[8,4,64,128]{3,2,1,0:T(8,128)S(1)}, f32[8,128]{1,0:T(8,128)S(1)}) custom-call(bf16[8,8,64,128]{3,2,1,0:T(8,128)(2,1)S(1)} %bitcast.25, bf16[8,1,64,128]{3,2,1,0:T(8,128)(2,1)S(1)} %collective-permute-done.gx_ref, bf16[8,1,64,128]{3,2,1,0:T(8,128)(2,1)S(1)} %collective-permute-done.1.gp_ref, ...), custom_call_target="tpu_custom_call" | custom-call | flops 603979776 | bytes 4198912 | tf_op jit(solution)/shard_map/conv1_outer/pallas_call | solution.py:542
  17.6 1.9 %collective-permute-start.7 = (f32[2,8,128]{2,1,0:T(8,128)S(1)}, f32[2,8,128]{2,1,0:T(8,128)S(1)}, u32[]{:S(2)}, u32[]{:S(2)}) collective-permute-start(f32[2,8,128]{2,1,0:T(8,128)S(1)} %pad_maximum_fusion.refs_0_), channel_id=1, source_target_pairs={{0,3},{1,2},{2,1},{3,0},{4,7},{5,6},{6,5},{7,4},{8,11},{9,10},{10,... | collective-permute-start | bytes 24584 | tf_op jit(solution)/shard_map/ppermute | solution.py:555
  19.5 1.8 %collective-permute-start.6 = (f32[2,8,128]{2,1,0:T(8,128)S(1)}, f32[2,8,128]{2,1,0:T(8,128)S(1)}, u32[]{:S(2)}, u32[]{:S(2)}) collective-permute-start(f32[2,8,128]{2,1,0:T(8,128)S(1)} %pad_maximum_fusion.refs_0_), channel_id=1, source_target_pairs={{0,2},{1,3},{2,0},{3,1},{4,6},{5,7},{6,4},{7,5},{8,10},{9,11},{10,... | collective-permute-start | bytes 24584 | tf_op jit(solution)/shard_map/ppermute | solution.py:555
  22.1 1.2 %collective-permute-done.2.hx_ref = bf16[25,64,128]{2,1,0:T(8,128)(2,1)S(1)} collective-permute-done((bf16[25,64,128]{2,1,0:T(8,128)(2,1)S(1)}, bf16[25,64,128]{2,1,0:T(8,128)(2,1)S(1)}, u32[]{:S(2)}, u32[]{:S(2)}) %collective-permute-start.2) | collective-permute-done | bytes 409632 | tf_op jit(solution)/shard_map/ppermute | solution.py:563
  23.3 1.6 %conv1_edges.1 = (f32[8,4,64,128]{3,2,1,0:T(8,128)S(1)}, f32[8,4,64,128]{3,2,1,0:T(8,128)S(1)}, f32[8,10,64,128]{3,2,1,0:T(8,128)S(1)}, f32[8,128]{1,0:T(8,128)S...) custom-call(bf16[8,8,64,128]{3,2,1,0:T(8,128)(2,1)S(1)} %bitcast.26, ...), custom_call_target="tpu_custom_call" | custom-call | flops 603979776 | bytes 6361600 | tf_op jit(solution)/shard_map/conv1_edges/pallas_call | solution.py:542
  24.9 2.0 %collective-permute-done.6.refs_2_ = f32[2,8,128]{2,1,0:T(8,128)S(1)} collective-permute-done((f32[2,8,128]{2,1,0:T(8,128)S(1)}, f32[2,8,128]{2,1,0:T(8,128)S(1)}, u32[]{:S(2)}, u32[]{:S(2)}) %collective-permute-start.6) | collective-permute-done | bytes 8224 | tf_op jit(solution)/shard_map/ppermute | solution.py:555
  27.0 3.7 %conv2.1 = (bf16[8,10,64,128]{3,2,1,0:T(8,128)(2,1)S(1)}, f32[8,10,64,128]{3,2,1,0:T(8,128)S(1)}, f32[8,10,64,128]{3,2,1,0:T(8,128)S(1)}, f32[8,128]{1,0:T(8,128)S(1)}, f32[8,128]{1,0:T(8,128)S(1)}) custom-call(f32[8,128]{1,0:T(8,128)S(1)} %get-tuple-element.66.st_ref.own_ref.st1_ref, f32[8,4,64,128]{3,2,1,0:T(8,128)S(1)} %get-tuple-element.67.a_ref, ...), custom_call_target="tpu_custom_call" | custom-call | flops 1207959552 | bytes 9741824 | tf_op jit(solution)/shard_map/conv2/pallas_call | solution.py:542
  31.9 1.2 %collective-permute-start.11 = (f32[2,8,128]{2,1,0:T(8,128)S(1)}, f32[2,8,128]{2,1,0:T(8,128)S(1)}, u32[]{:S(2)}, u32[]{:S(2)}) collective-permute-start(f32[2,8,128]{2,1,0:T(8,128)S(1)} %pad_maximum_fusion.1.refs_0_), channel_id=1, source_target_pairs={{0,3},{1,2},{2,1},{3,0},{4,7},{5,6},{6,5},{7,4},{8,11},{9,10},{10,... | collective-permute-start | bytes 24584 | tf_op jit(solution)/shard_map/ppermute | solution.py:555
  33.1 2.3 %collective-permute-start.10 = (f32[2,8,128]{2,1,0:T(8,128)S(1)}, f32[2,8,128]{2,1,0:T(8,128)S(1)}, u32[]{:S(2)}, u32[]{:S(2)}) collective-permute-start(f32[2,8,128]{2,1,0:T(8,128)S(1)} %pad_maximum_fusion.1.refs_0_), channel_id=1, source_target_pairs={{0,2},{1,3},{2,0},{3,1},{4,6},{5,7},{6,4},{7,5},{8,10},{9,11},{10,... | collective-permute-start | bytes 24584 | tf_op jit(solution)/shard_map/ppermute | solution.py:555
  37.7 1.4 %collective-permute-done.9.refs_1_ = f32[2,8,128]{2,1,0:T(8,128)S(1)} collective-permute-done((f32[2,8,128]{2,1,0:T(8,128)S(1)}, f32[2,8,128]{2,1,0:T(8,128)S(1)}, u32[]{:S(2)}, u32[]{:S(2)}) %collective-permute-start.9) | collective-permute-done | bytes 8224 | tf_op jit(solution)/shard_map/ppermute | solution.py:555
  39.1 2.5 %conv2_back.1 = (bf16[8,8,64,128]{3,2,1,0:T(8,128)(2,1)S(1)}, f32[8,8,64,128]{3,2,1,0:T(8,128)S(1)}, f32[8,128]{1,0:T(8,128)S(1)}, f32[8,128]{1,0:T(8,128)S(1)}) custom-call(f32[8,128]{1,0:T(8,128)S(1)} %get-tuple-element.78.own_ref, f32[8,128]{1,0:T(8,128)S(1)} %get-tuple-element.66.st_ref.own_ref.st1_ref, f32[8,128]{1,0:T(8,128)S(1)} %get-tuple-element.79.c1_ref, ...), custom_call_target="tpu_custom_call" | custom-call | flops 1207959552 | bytes 12891136 | tf_op jit(solution)/shard_map/conv2_back/pallas_call | solution.py:542
  42.8 1.3 %collective-permute-start.15 = (f32[2,8,128]{2,1,0:T(8,128)S(1)}, f32[2,8,128]{2,1,0:T(8,128)S(1)}, u32[]{:S(2)}, u32[]{:S(2)}) collective-permute-start(f32[2,8,128]{2,1,0:T(8,128)S(1)} %pad_maximum_fusion.2.after_ref.refs_0_), channel_id=1, source_target_pairs={{0,3},{1,2},{2,1},{3,0},{4,7},{5,6},{6,5},{7,4},{8,11},{9,10},{10,... | collective-permute-start | bytes 24584 | tf_op jit(solution)/shard_map/ppermute | solution.py:555
  45.2 2.1 %collective-permute-start.13 = (f32[2,8,128]{2,1,0:T(8,128)S(1)}, f32[2,8,128]{2,1,0:T(8,128)S(1)}, u32[]{:S(2)}, u32[]{:S(2)}) collective-permute-start(f32[2,8,128]{2,1,0:T(8,128)S(1)} %pad_maximum_fusion.2.after_ref.refs_0_), channel_id=1, source_target_pairs={{0,1},{1,0},{2,3},{3,2},{4,5},{5,4},{6,7},{7,6},{8,9},{9,8},{10,11... | collective-permute-start | bytes 24584 | tf_op jit(solution)/shard_map/ppermute | solution.py:555
  47.2 1.8 %conv2_weight_grad.1 = (bf16[1152,128]{1,0:T(8,128)(2,1)S(1)}, f32[8,128]{1,0:T(8,128)S(1)}) custom-call(bf16[8,10,64,128]{3,2,1,0:T(8,128)(2,1)S(1)} %get-tuple-element.86.n_ref, bf16[8,8,64,128]{3,2,1,0:T(8,128)(2,1)S(1)} %get-tuple-element.87.d_ref, f32[2,8,128]{2,1,0:T(8,128)S(1)} %pad_maximum_fusion.2.after_ref.refs_0_), custom_call_target="tpu_custom_call" | custom-call | flops 1207959552 | bytes 2359296 | tf_op jit(solution)/shard_map/conv2_weight_grad/pallas_call | solution.py:542
  49.1 2.4 %conv1_weight_grad.1 = (bf16[8,8,64,128]{3,2,1,0:T(8,128)(2,1)S(1)}, bf16[8,64,128]{2,1,0:T(8,128)(2,1)S(1)}, bf16[8,64,128]{2,1,0:T(8,128)(2,1)S(1)}, bf16[4,30...) custom-call(f32[8,128]{1,0:T(8,128)S(1)} %get-tuple-element.79.c1_ref, f32[8,128]{1,0:T(8,128)S(1)} %get-tuple-element.82.c2_ref, ...), custom_call_target="tpu_custom_call" | custom-call | flops 1207959552 | bytes 7942656 | tf_op jit(solution)/shard_map/conv1_weight_grad/pallas_call | solution.py:542
  51.6 1.8 %collective-permute-start.23 = (bf16[8,64,128]{2,1,0:T(8,128)(2,1)S(1)}, bf16[8,64,128]{2,1,0:T(8,128)(2,1)S(1)}, u32[]{:S(2)}, u32[]{:S(2)}) collective-permute-start(bf16[8,64,128]{2,1,0:T(8,128)(2,1)S(1)} %get-tuple-element.98), channel_id=1, source_target_pairs={{0,1},{1,0},{2,3},{3,2},{4,5},{5,4},{6,7},{7,6},{8,9},{9,8},{10,11... | collective-permute-start | bytes 393224 | tf_op jit(solution)/shard_map/ppermute | solution.py:563
  54.2 1.6 %collective-permute-start.17 = (bf16[304,128]{1,0:T(8,128)(2,1)S(1)}, bf16[304,128]{1,0:T(8,128)(2,1)S(1)}, u32[]{:S(2)}, u32[]{:S(2)}) collective-permute-start(bf16[304,128]{1,0:T(8,128)(2,1)S(1)} %get-tuple-element.94), channel_id=1, source_target_pairs={{0,8},{8,0},{16,24},{24,16},{1,9},{9,1},{17,25},{25,17},{2,10},{10... | collective-permute-start | bytes 233480 | tf_op jit(solution)/shard_map/ppermute | solution.py:555
  55.7 1.5 %collective-permute-start.18 = (bf16[304,128]{1,0:T(8,128)(2,1)S(1)}, bf16[304,128]{1,0:T(8,128)(2,1)S(1)}, u32[]{:S(2)}, u32[]{:S(2)}) collective-permute-start(bf16[304,128]{1,0:T(8,128)(2,1)S(1)} %get-tuple-element.95), channel_id=1, source_target_pairs={{0,16},{8,24},{16,0},{24,8},{1,17},{9,25},{17,1},{25,9},{2,18},{10... | collective-permute-start | bytes 233480 | tf_op jit(solution)/shard_map/ppermute | solution.py:555
  58.7 2.2 %collective-permute-done.18.refs_2_ = bf16[304,128]{1,0:T(8,128)(2,1)S(1)} collective-permute-done((bf16[304,128]{1,0:T(8,128)(2,1)S(1)}, bf16[304,128]{1,0:T(8,128)(2,1)S(1)}, u32[]{:S(2)}, u32[]{:S(2)}) %collective-permute-start.18) | collective-permute-done | bytes 77856 | tf_op jit(solution)/shard_map/ppermute | solution.py:555
  60.9 1.7 %collective-permute-done.19.refs_3_ = bf16[304,128]{1,0:T(8,128)(2,1)S(1)} collective-permute-done((bf16[304,128]{1,0:T(8,128)(2,1)S(1)}, bf16[304,128]{1,0:T(8,128)(2,1)S(1)}, u32[]{:S(2)}, u32[]{:S(2)}) %collective-permute-start.19) | collective-permute-done | bytes 77856 | tf_op jit(solution)/shard_map/ppermute | solution.py:555
  62.6 1.3 %collective-permute-start.22 = (bf16[304,128]{1,0:T(8,128)(2,1)S(1)}, bf16[304,128]{1,0:T(8,128)(2,1)S(1)}, u32[]{:S(2)}, u32[]{:S(2)}) collective-permute-start(bf16[304,128]{1,0:T(8,128)(2,1)S(1)} %add_lead.1.refs_0_), channel_id=1, source_target_pairs={{0,3},{1,2},{2,1},{3,0},{4,7},{5,6},{6,5},{7,4},{8,11},{9,10},{10,... | collective-permute-start | bytes 233480 | tf_op jit(solution)/shard_map/ppermute | solution.py:555
  63.9 2.9 %collective-permute-start.21 = (bf16[304,128]{1,0:T(8,128)(2,1)S(1)}, bf16[304,128]{1,0:T(8,128)(2,1)S(1)}, u32[]{:S(2)}, u32[]{:S(2)}) collective-permute-start(bf16[304,128]{1,0:T(8,128)(2,1)S(1)} %add_lead.1.refs_0_), channel_id=1, source_target_pairs={{0,2},{1,3},{2,0},{3,1},{4,6},{5,7},{6,4},{7,5},{8,10},{9,11},{10,... | collective-permute-start | bytes 233480 | tf_op jit(solution)/shard_map/ppermute | solution.py:555
  67.1 2.9 %conv1_back.1 = (bf16[8,8,64,128]{3,2,1,0:T(8,128)(2,1)}, f32[8,128]{1,0:T(8,128)S(1)}) custom-call(bf16[8,8,64,128]{3,2,1,0:T(8,128)(2,1)S(1)} %get-tuple-element.97.d_ref, bf16[8,64,128]{2,1,0:T(8,128)(2,1)S(1)} %collective-permute-done.23.ex_ref, bf16[8,64,128]{2,1,0:T(8,128)(2,1)S(1)} %collective-permute-done.24.ep_ref, ...), custom_call_target="tpu_custom_call" | custom-call | flops 1207959552 | bytes 2654208 | tf_op jit(solution)/shard_map/conv1_back/pallas_call | solution.py:542
  70.0 2.2 %collective-permute-done.21.refs_2_ = bf16[304,128]{1,0:T(8,128)(2,1)S(1)} collective-permute-done((bf16[304,128]{1,0:T(8,128)(2,1)S(1)}, bf16[304,128]{1,0:T(8,128)(2,1)S(1)}, u32[]{:S(2)}, u32[]{:S(2)}) %collective-permute-start.21) | collective-permute-done | bytes 77856 | tf_op jit(solution)/shard_map/ppermute | solution.py:555
  73.1 1.3 %collective-permute-start.27 = (bf16[288,128]{1,0:T(8,128)(2,1)S(1)}, bf16[288,128]{1,0:T(8,128)(2,1)S(1)}, u32[]{:S(2)}, u32[]{:S(2)}) collective-permute-start(bf16[288,128]{1,0:T(8,128)(2,1)S(1)} %get-tuple-element.113), channel_id=1, source_target_pairs={{0,24},{8,16},{16,8},{24,0},{1,25},{9,17},{17,9},{25,1},{2,26},{10... | collective-permute-start | bytes 221192 | tf_op jit(solution)/shard_map/ppermute | solution.py:555
  74.4 1.4 %collective-permute-start.26 = (bf16[288,128]{1,0:T(8,128)(2,1)S(1)}, bf16[288,128]{1,0:T(8,128)(2,1)S(1)}, u32[]{:S(2)}, u32[]{:S(2)}) collective-permute-start(bf16[288,128]{1,0:T(8,128)(2,1)S(1)} %get-tuple-element.113), channel_id=1, source_target_pairs={{0,16},{8,24},{16,0},{24,8},{1,17},{9,25},{17,1},{25,9},{2,18},{10... | collective-permute-start | bytes 221192 | tf_op jit(solution)/shard_map/ppermute | solution.py:555
  76.7 2.4 %collective-permute-done.26.refs_1_ = bf16[288,128]{1,0:T(8,128)(2,1)S(1)} collective-permute-done((bf16[288,128]{1,0:T(8,128)(2,1)S(1)}, bf16[288,128]{1,0:T(8,128)(2,1)S(1)}, u32[]{:S(2)}, u32[]{:S(2)}) %collective-permute-start.26) | collective-permute-done | bytes 73760 | tf_op jit(solution)/shard_map/ppermute | solution.py:555
  79.3 1.5 %output.1 = (bf16[8,8,64,128]{3,2,1,0:T(8,128)(2,1)}, f32[8,128]{1,0:T(8,128)S(1)}) custom-call(bf16[8,8,64,128]{3,2,1,0:T(8,128)(2,1)S(1)} %bitcast.28, f32[8,10,64,128]{3,2,1,0:T(8,128)S(1)} %get-tuple-element.77.a2_ref, f32[8,8,64,128]{3,2,1,0:T(8,128)S(1)} %get-tuple-element.63.m_ref, f32[8,128]{1,0:T(8,128)S(1)} %get-tuple-element.82.c2_ref, ...), custom_call_target="tpu_custom_call" | custom-call | flops 603979776 | bytes 5771264 | tf_op jit(solution)/shard_map/output/pallas_call | solution.py:542
  (75 shorter events, 17.2 us)
Async XLA Ops:
  1.9 7.7 %collective-permute-start = (bf16[8,1,64,128]{3,2,1,0:T(8,128)(2,1)S(1)}, bf16[8,1,64,128]{3,2,1,0:T(8,128)(2,1)S(1)}, u32[]{:S(2)}, u32[]{:S(2)}) collective-permute-start(bf16[8,1,64,128]{3,2,1,0:T(8,128)(2,1)S(1)} %get-tuple-element.61), channel_id=1, source_target_pairs={{0,1},{1,0},{2,3},{3,2},{4,5},{5,4},{6,7},{7,6},{8,9},{9,8},{10,11... | collective-permute-start | bytes 393224 | tf_op jit(solution)/shard_map/ppermute | solution.py:563
  5.0 4.7 %collective-permute-start.1 = (bf16[8,1,64,128]{3,2,1,0:T(8,128)(2,1)S(1)}, bf16[8,1,64,128]{3,2,1,0:T(8,128)(2,1)S(1)}, u32[]{:S(2)}, u32[]{:S(2)}) collective-permute-start(bf16[8,1,64,128]{3,2,1,0:T(8,128)(2,1)S(1)} %get-tuple-element.62), channel_id=1, source_target_pairs={{1,2},{2,1},{5,6},{6,5},{9,10},{10,9},{13,14},{14,13},{17,18},{18,... | collective-permute-start | bytes 393224 | tf_op jit(solution)/shard_map/ppermute | solution.py:563
  9.8 13.5 %copy-start.3 = (bf16[3,3,128,128]{3,2,1,0:T(8,128)(2,1)S(1)}, bf16[3,3,128,128]{3,2,1,0:T(8,128)(2,1)}, u32[]{:S(2)}) copy-start(bf16[3,3,128,128]{3,2,1,0:T(8,128)(2,1)} %w2_ref.1) | copy-start | bytes 884740
  9.8 13.4 %collective-permute-start.2 = (bf16[25,64,128]{2,1,0:T(8,128)(2,1)S(1)}, bf16[25,64,128]{2,1,0:T(8,128)(2,1)S(1)}, u32[]{:S(2)}, u32[]{:S(2)}) collective-permute-start(bf16[25,64,128]{2,1,0:T(8,128)(2,1)S(1)} %get-tuple-element.70), channel_id=1, source_target_pairs={{0,1},{1,0},{2,3},{3,2},{4,5},{5,4},{6,7},{7,6},{8,9},{9,8},{10,11... | collective-permute-start | bytes 1228808 | tf_op jit(solution)/shard_map/ppermute | solution.py:563
  14.3 9.0 %collective-permute-start.3 = (bf16[25,64,128]{2,1,0:T(8,128)(2,1)S(1)}, bf16[25,64,128]{2,1,0:T(8,128)(2,1)S(1)}, u32[]{:S(2)}, u32[]{:S(2)}) collective-permute-start(bf16[25,64,128]{2,1,0:T(8,128)(2,1)S(1)} %get-tuple-element.71), channel_id=1, source_target_pairs={{1,2},{2,1},{5,6},{6,5},{9,10},{10,9},{13,14},{14,13},{17,18},{18,... | collective-permute-start | bytes 1228808 | tf_op jit(solution)/shard_map/ppermute | solution.py:563
  16.4 1.2 %collective-permute-start.4 = (f32[1,8,128]{2,1,0:T(8,128)S(1)}, f32[1,8,128]{2,1,0:T(8,128)S(1)}, u32[]{:S(2)}, u32[]{:S(2)}) collective-permute-start(f32[1,8,128]{2,1,0:T(8,128)S(1)} %bitcast.32), channel_id=1, source_target_pairs={{0,4},{4,0},{1,5},{5,1},{2,6},{6,2},{3,7},{7,3},{8,12},{12,8},{9,1... | collective-permute-start | bytes 12296 | tf_op jit(solution)/shard_map/ppermute | solution.py:555
  17.6 7.3 %collective-permute-start.7 = (f32[2,8,128]{2,1,0:T(8,128)S(1)}, f32[2,8,128]{2,1,0:T(8,128)S(1)}, u32[]{:S(2)}, u32[]{:S(2)}) collective-permute-start(f32[2,8,128]{2,1,0:T(8,128)S(1)} %pad_maximum_fusion.refs_0_), channel_id=1, source_target_pairs={{0,3},{1,2},{2,1},{3,0},{4,7},{5,6},{6,5},{7,4},{8,11},{9,10},{10,... | collective-permute-start | bytes 24584 | tf_op jit(solution)/shard_map/ppermute | solution.py:555
  19.5 7.5 %collective-permute-start.6 = (f32[2,8,128]{2,1,0:T(8,128)S(1)}, f32[2,8,128]{2,1,0:T(8,128)S(1)}, u32[]{:S(2)}, u32[]{:S(2)}) collective-permute-start(f32[2,8,128]{2,1,0:T(8,128)S(1)} %pad_maximum_fusion.refs_0_), channel_id=1, source_target_pairs={{0,2},{1,3},{2,0},{3,1},{4,6},{5,7},{6,4},{7,5},{8,10},{9,11},{10,... | collective-permute-start | bytes 24584 | tf_op jit(solution)/shard_map/ppermute | solution.py:555
  21.3 5.6 %collective-permute-start.5 = (f32[2,8,128]{2,1,0:T(8,128)S(1)}, f32[2,8,128]{2,1,0:T(8,128)S(1)}, u32[]{:S(2)}, u32[]{:S(2)}) collective-permute-start(f32[2,8,128]{2,1,0:T(8,128)S(1)} %pad_maximum_fusion.refs_0_), channel_id=1, source_target_pairs={{0,1},{1,0},{2,3},{3,2},{4,5},{5,4},{6,7},{7,6},{8,9},{9,8},{10,11... | collective-permute-start | bytes 24584 | tf_op jit(solution)/shard_map/ppermute | solution.py:555
  27.0 12.1 %copy-start.8 = (f32[128]{0:T(128)S(1)}, f32[128]{0:T(128)}, u32[]{:S(2)}) copy-start(f32[128]{0:T(128)} %param.20) | copy-start | bytes 1540
  30.7 1.2 %collective-permute-start.8 = (f32[1,8,128]{2,1,0:T(8,128)S(1)}, f32[1,8,128]{2,1,0:T(8,128)S(1)}, u32[]{:S(2)}, u32[]{:S(2)}) collective-permute-start(f32[1,8,128]{2,1,0:T(8,128)S(1)} %bitcast.34), channel_id=1, source_target_pairs={{0,4},{4,0},{1,5},{5,1},{2,6},{6,2},{3,7},{7,3},{8,12},{12,8},{9,1... | collective-permute-start | bytes 12296 | tf_op jit(solution)/shard_map/ppermute | solution.py:555
  31.9 5.4 %collective-permute-start.11 = (f32[2,8,128]{2,1,0:T(8,128)S(1)}, f32[2,8,128]{2,1,0:T(8,128)S(1)}, u32[]{:S(2)}, u32[]{:S(2)}) collective-permute-start(f32[2,8,128]{2,1,0:T(8,128)S(1)} %pad_maximum_fusion.1.refs_0_), channel_id=1, source_target_pairs={{0,3},{1,2},{2,1},{3,0},{4,7},{5,6},{6,5},{7,4},{8,11},{9,10},{10,... | collective-permute-start | bytes 24584 | tf_op jit(solution)/shard_map/ppermute | solution.py:555
  33.1 4.5 %collective-permute-start.10 = (f32[2,8,128]{2,1,0:T(8,128)S(1)}, f32[2,8,128]{2,1,0:T(8,128)S(1)}, u32[]{:S(2)}, u32[]{:S(2)}) collective-permute-start(f32[2,8,128]{2,1,0:T(8,128)S(1)} %pad_maximum_fusion.1.refs_0_), channel_id=1, source_target_pairs={{0,2},{1,3},{2,0},{3,1},{4,6},{5,7},{6,4},{7,5},{8,10},{9,11},{10,... | collective-permute-start | bytes 24584 | tf_op jit(solution)/shard_map/ppermute | solution.py:555
  35.4 3.7 %collective-permute-start.9 = (f32[2,8,128]{2,1,0:T(8,128)S(1)}, f32[2,8,128]{2,1,0:T(8,128)S(1)}, u32[]{:S(2)}, u32[]{:S(2)}) collective-permute-start(f32[2,8,128]{2,1,0:T(8,128)S(1)} %pad_maximum_fusion.1.refs_0_), channel_id=1, source_target_pairs={{0,1},{1,0},{2,3},{3,2},{4,5},{5,4},{6,7},{7,6},{8,9},{9,8},{10,11... | collective-permute-start | bytes 24584 | tf_op jit(solution)/shard_map/ppermute | solution.py:555
  41.6 1.2 %collective-permute-start.12 = (f32[1,8,128]{2,1,0:T(8,128)S(1)}, f32[1,8,128]{2,1,0:T(8,128)S(1)}, u32[]{:S(2)}, u32[]{:S(2)}) collective-permute-start(f32[1,8,128]{2,1,0:T(8,128)S(1)} %bitcast.36), channel_id=1, source_target_pairs={{0,4},{4,0},{1,5},{5,1},{2,6},{6,2},{3,7},{7,3},{8,12},{12,8},{9,1... | collective-permute-start | bytes 12296 | tf_op jit(solution)/shard_map/ppermute | solution.py:555
  42.8 6.2 %collective-permute-start.15 = (f32[2,8,128]{2,1,0:T(8,128)S(1)}, f32[2,8,128]{2,1,0:T(8,128)S(1)}, u32[]{:S(2)}, u32[]{:S(2)}) collective-permute-start(f32[2,8,128]{2,1,0:T(8,128)S(1)} %pad_maximum_fusion.2.after_ref.refs_0_), channel_id=1, source_target_pairs={{0,3},{1,2},{2,1},{3,0},{4,7},{5,6},{6,5},{7,4},{8,11},{9,10},{10,... | collective-permute-start | bytes 24584 | tf_op jit(solution)/shard_map/ppermute | solution.py:555
  44.1 4.9 %collective-permute-start.14 = (f32[2,8,128]{2,1,0:T(8,128)S(1)}, f32[2,8,128]{2,1,0:T(8,128)S(1)}, u32[]{:S(2)}, u32[]{:S(2)}) collective-permute-start(f32[2,8,128]{2,1,0:T(8,128)S(1)} %pad_maximum_fusion.2.after_ref.refs_0_), channel_id=1, source_target_pairs={{0,2},{1,3},{2,0},{3,1},{4,6},{5,7},{6,4},{7,5},{8,10},{9,11},{10,... | collective-permute-start | bytes 24584 | tf_op jit(solution)/shard_map/ppermute | solution.py:555
  45.2 3.9 %collective-permute-start.13 = (f32[2,8,128]{2,1,0:T(8,128)S(1)}, f32[2,8,128]{2,1,0:T(8,128)S(1)}, u32[]{:S(2)}, u32[]{:S(2)}) collective-permute-start(f32[2,8,128]{2,1,0:T(8,128)S(1)} %pad_maximum_fusion.2.after_ref.refs_0_), channel_id=1, source_target_pairs={{0,1},{1,0},{2,3},{3,2},{4,5},{5,4},{6,7},{7,6},{8,9},{9,8},{10,11... | collective-permute-start | bytes 24584 | tf_op jit(solution)/shard_map/ppermute | solution.py:555
  49.1 17.9 %copy-start.11 = (bf16[3,3,128,128]{3,2,1,0:T(8,128)(2,1)S(1)}, bf16[3,3,128,128]{3,2,1,0:T(8,128)(2,1)}, u32[]{:S(2)}) copy-start(bf16[3,3,128,128]{3,2,1,0:T(8,128)(2,1)} %w_ref.3) | copy-start | bytes 884740
  51.5 2.6 %collective-permute-start.16 = (bf16[4,304,128]{2,1,0:T(8,128)(2,1)S(1)}, bf16[4,304,128]{2,1,0:T(8,128)(2,1)S(1)}, u32[]{:S(2)}, u32[]{:S(2)}) collective-permute-start(bf16[4,304,128]{2,1,0:T(8,128)(2,1)S(1)} %get-tuple-element.92), channel_id=1, source_target_pairs={{0,4},{4,0},{1,5},{5,1},{2,6},{6,2},{3,7},{7,3},{8,12},{12,8},{9,1... | collective-permute-start | bytes 933896 | tf_op jit(solution)/shard_map/ppermute | solution.py:555
  51.6 15.5 %collective-permute-start.23 = (bf16[8,64,128]{2,1,0:T(8,128)(2,1)S(1)}, bf16[8,64,128]{2,1,0:T(8,128)(2,1)S(1)}, u32[]{:S(2)}, u32[]{:S(2)}) collective-permute-start(bf16[8,64,128]{2,1,0:T(8,128)(2,1)S(1)} %get-tuple-element.98), channel_id=1, source_target_pairs={{0,1},{1,0},{2,3},{3,2},{4,5},{5,4},{6,7},{7,6},{8,9},{9,8},{10,11... | collective-permute-start | bytes 393224 | tf_op jit(solution)/shard_map/ppermute | solution.py:563
  53.4 13.7 %collective-permute-start.24 = (bf16[8,64,128]{2,1,0:T(8,128)(2,1)S(1)}, bf16[8,64,128]{2,1,0:T(8,128)(2,1)S(1)}, u32[]{:S(2)}, u32[]{:S(2)}) collective-permute-start(bf16[8,64,128]{2,1,0:T(8,128)(2,1)S(1)} %get-tuple-element.99), channel_id=1, source_target_pairs={{1,2},{2,1},{5,6},{6,5},{9,10},{10,9},{13,14},{14,13},{17,18},{18,... | collective-permute-start | bytes 393224 | tf_op jit(solution)/shard_map/ppermute | solution.py:563
  54.2 4.5 %collective-permute-start.17 = (bf16[304,128]{1,0:T(8,128)(2,1)S(1)}, bf16[304,128]{1,0:T(8,128)(2,1)S(1)}, u32[]{:S(2)}, u32[]{:S(2)}) collective-permute-start(bf16[304,128]{1,0:T(8,128)(2,1)S(1)} %get-tuple-element.94), channel_id=1, source_target_pairs={{0,8},{8,0},{16,24},{24,16},{1,9},{9,1},{17,25},{25,17},{2,10},{10... | collective-permute-start | bytes 233480 | tf_op jit(solution)/shard_map/ppermute | solution.py:555
  55.7 5.1 %collective-permute-start.18 = (bf16[304,128]{1,0:T(8,128)(2,1)S(1)}, bf16[304,128]{1,0:T(8,128)(2,1)S(1)}, u32[]{:S(2)}, u32[]{:S(2)}) collective-permute-start(bf16[304,128]{1,0:T(8,128)(2,1)S(1)} %get-tuple-element.95), channel_id=1, source_target_pairs={{0,16},{8,24},{16,0},{24,8},{1,17},{9,25},{17,1},{25,9},{2,18},{10... | collective-permute-start | bytes 233480 | tf_op jit(solution)/shard_map/ppermute | solution.py:555
  57.2 5.3 %collective-permute-start.19 = (bf16[304,128]{1,0:T(8,128)(2,1)S(1)}, bf16[304,128]{1,0:T(8,128)(2,1)S(1)}, u32[]{:S(2)}, u32[]{:S(2)}) collective-permute-start(bf16[304,128]{1,0:T(8,128)(2,1)S(1)} %get-tuple-element.96), channel_id=1, source_target_pairs={{0,24},{8,16},{16,8},{24,0},{1,25},{9,17},{17,9},{25,1},{2,26},{10... | collective-permute-start | bytes 233480 | tf_op jit(solution)/shard_map/ppermute | solution.py:555
  62.6 7.4 %collective-permute-start.22 = (bf16[304,128]{1,0:T(8,128)(2,1)S(1)}, bf16[304,128]{1,0:T(8,128)(2,1)S(1)}, u32[]{:S(2)}, u32[]{:S(2)}) collective-permute-start(bf16[304,128]{1,0:T(8,128)(2,1)S(1)} %add_lead.1.refs_0_), channel_id=1, source_target_pairs={{0,3},{1,2},{2,1},{3,0},{4,7},{5,6},{6,5},{7,4},{8,11},{9,10},{10,... | collective-permute-start | bytes 233480 | tf_op jit(solution)/shard_map/ppermute | solution.py:555
  63.9 8.2 %collective-permute-start.21 = (bf16[304,128]{1,0:T(8,128)(2,1)S(1)}, bf16[304,128]{1,0:T(8,128)(2,1)S(1)}, u32[]{:S(2)}, u32[]{:S(2)}) collective-permute-start(bf16[304,128]{1,0:T(8,128)(2,1)S(1)} %add_lead.1.refs_0_), channel_id=1, source_target_pairs={{0,2},{1,3},{2,0},{3,1},{4,6},{5,7},{6,4},{7,5},{8,10},{9,11},{10,... | collective-permute-start | bytes 233480 | tf_op jit(solution)/shard_map/ppermute | solution.py:555
  66.8 5.3 %collective-permute-start.20 = (bf16[304,128]{1,0:T(8,128)(2,1)S(1)}, bf16[304,128]{1,0:T(8,128)(2,1)S(1)}, u32[]{:S(2)}, u32[]{:S(2)}) collective-permute-start(bf16[304,128]{1,0:T(8,128)(2,1)S(1)} %add_lead.1.refs_0_), channel_id=1, source_target_pairs={{0,1},{1,0},{2,3},{3,2},{4,5},{5,4},{6,7},{7,6},{8,9},{9,8},{10,11... | collective-permute-start | bytes 233480 | tf_op jit(solution)/shard_map/ppermute | solution.py:555
  72.3 4.4 %collective-permute-start.25 = (bf16[288,128]{1,0:T(8,128)(2,1)S(1)}, bf16[288,128]{1,0:T(8,128)(2,1)S(1)}, u32[]{:S(2)}, u32[]{:S(2)}) collective-permute-start(bf16[288,128]{1,0:T(8,128)(2,1)S(1)} %get-tuple-element.113), channel_id=1, source_target_pairs={{0,8},{8,0},{16,24},{24,16},{1,9},{9,1},{17,25},{25,17},{2,10},{10... | collective-permute-start | bytes 221192 | tf_op jit(solution)/shard_map/ppermute | solution.py:555
  73.1 6.1 %collective-permute-start.27 = (bf16[288,128]{1,0:T(8,128)(2,1)S(1)}, bf16[288,128]{1,0:T(8,128)(2,1)S(1)}, u32[]{:S(2)}, u32[]{:S(2)}) collective-permute-start(bf16[288,128]{1,0:T(8,128)(2,1)S(1)} %get-tuple-element.113), channel_id=1, source_target_pairs={{0,24},{8,16},{16,8},{24,0},{1,25},{9,17},{17,9},{25,1},{2,26},{10... | collective-permute-start | bytes 221192 | tf_op jit(solution)/shard_map/ppermute | solution.py:555
  74.4 4.7 %collective-permute-start.26 = (bf16[288,128]{1,0:T(8,128)(2,1)S(1)}, bf16[288,128]{1,0:T(8,128)(2,1)S(1)}, u32[]{:S(2)}, u32[]{:S(2)}) collective-permute-start(bf16[288,128]{1,0:T(8,128)(2,1)S(1)} %get-tuple-element.113), channel_id=1, source_target_pairs={{0,16},{8,24},{16,0},{24,8},{1,17},{9,25},{17,1},{25,9},{2,18},{10... | collective-permute-start | bytes 221192 | tf_op jit(solution)/shard_map/ppermute | solution.py:555
  79.2 1.7 %collective-permute-start.28 = (bf16[1168,128]{1,0:T(8,128)(2,1)S(1)}, bf16[1168,128]{1,0:T(8,128)(2,1)S(1)}, u32[]{:S(2)}, u32[]{:S(2)}) collective-permute-start(bf16[1168,128]{1,0:T(8,128)(2,1)S(1)} %constant_dynamic-update-slice_fusion), channel_id=1, source_target_pairs={{0,4},{4,0},{1,5},{5,1},{2,6},{6,2},{3,7},{7,3},{8,12},{12,8},{9,1... | collective-permute-start | bytes 897032 | tf_op jit(solution)/shard_map/ppermute | solution.py:555
  (10 other events, 59.1 us)
where the time goes:
time: 82.3 us; the launch traced here: 81.9 us
  starting transfers between devices  36.5 us (44%)
  Pallas kernels  20.8 us (25%)
  waiting for transfers between devices  20 us (24%)
  local copies, waits for them, and re-layouts  3.7 us (4%)
  between operations  0.96 us (1%)
    ppermute x23, starting transfers between devices, swap(): lax.ppermute(value, axis, [(i, i ^ k) for i in range(lax.axis_size(axis))])  25.1 us
    pallas_call x15, Pallas kernels, call(): pl.pallas_call(kernel, out_shape=outs, in_specs=[space] * len(operands) +...  20.8 us
    ppermute x23, waiting for transfers between devices, swap(): lax.ppermute(value, axis, [(i, i ^ k) for i in range(lax.axis_size(axis))])  18.8 us
    ppermute x3, starting transfers between devices, neighbours(): lax.ppermute(value_x, axis, first)  9.38 us
    unnamed x30, local copies, waits for them, and re-layouts  3.69 us
    ppermute x3, starting transfers between devices, neighbours(): lax.ppermute(value_p, axis, second)  1.99 us
  transfers between devices with their start and end apart: 29, of which 15 were waited for; matrix products, arithmetic and copies ran while one was open for 0% of the time, Pallas kernels for 13%

commit v1 on v0

--- a/solution.py
+++ b/solution.py
@@ -11,6 +11,7 @@
 BF16 = jnp.bfloat16
 F32 = jnp.float32
 VMEM = pl.BlockSpec(memory_space=pltpu.VMEM)
+HIDE = 10**11
 SMALL = 16
 
 
@@ -98,9 +99,15 @@
         copy.wait()
 
 
-def far_rows_kernel(x_ref, u_ref, bits_ref, gx_ref, gp_ref, hx_ref, hp_ref):
+def far_rows_kernel(x_ref, u_ref, mask_ref, hx_ref, hp_ref, m_ref, count_ref, bits_ref):
     samples, height, across, c = x_ref.shape
     even = lax.axis_index("lat") % 2 == 0
+    for k in range(bits_ref.shape[0]):
+        bits = mask_ref[k * 128 : (k + 1) * 128].astype(F32)
+        bits = jnp.concatenate([bits, jnp.zeros((bits.shape[0], 128 - across), F32)], 1)
+        if bits.shape[0] < 128:
+            bits = jnp.concatenate([bits, jnp.zeros((128 - bits.shape[0], 128), F32)], 0)
+        bits_ref[k] = bits.T[:across]
     for out, down in ((hx_ref, even), (hp_ref, jnp.logical_not(even))):
         first = jnp.where(down, height - 3, 1)
         edge = jnp.where(down, height - 1, 0)
@@ -110,6 +117,13 @@
             out[2 * samples + s] = u_ref[s, edge]
         for k in range(bits_ref.shape[0]):
             out[3 * samples + k] = bits_ref[k].astype(BF16)
+    count = jnp.zeros((8, c), F32)
+    for s in range(samples):
+        for r in range(height):
+            mask = column_mask(bits_ref, s * height + r, c)
+            m_ref[s, r] = mask
+            count += fold(mask)
+    count_ref[...] = stats_block([count.sum(0, keepdims=True)], c)
 
 
 def stats_block(rows, c):
@@ -118,12 +132,6 @@
 
 def gather(refs):
     return jnp.concatenate([r[...] for r in refs], 0)
-
-
-def own_row(inner_ref, outer_ref, s, r, height):
-    if 2 <= r < height - 2:
-        return inner_ref[s, r - 2]
-    return outer_ref[s, r if r < 2 else r - height + 4]
 
 
 def middle(value):
@@ -137,69 +145,38 @@
     return masked
 
 
-def conv1_inner_kernel(x_ref, mask_ref, w_ref, b_ref, a_ref, s_ref, m_ref, bits_ref, t_ref, st_ref):
+def conv1_kernel(gp_ref, gx_ref, x_ref, m_ref, count_ref, w_ref, b_ref, a_ref, s_ref, t_ref, st_ref):
     samples, height, across, c = x_ref.shape
-    for k in range(bits_ref.shape[0]):
-        bits = mask_ref[k * 128 : (k + 1) * 128].astype(F32)
-        bits = jnp.concatenate([bits, jnp.zeros((bits.shape[0], 128 - across), F32)], 1)
-        if bits.shape[0] < 128:
-            bits = jnp.concatenate([bits, jnp.zeros((128 - bits.shape[0], 128), F32)], 0)
-        bits_ref[k] = bits.T[:across]
+    even = lax.axis_index("lat") % 2 == 0
     fill_toeplitz(w_ref, t_ref)
     bias = b_ref[...]
-    sums = [jnp.zeros((8, c), F32) for _ in range(3)]
+    sums = [jnp.zeros((8, c), F32) for _ in range(2)]
     centre = None
     for s in range(samples):
-        piece = convolve_rows(lambda r: x_ref[s, r], range(2, height - 2, 2), t_ref, across, False)
+
+        def row(r):
+            if r < 0:
+                return pick(even, gp_ref[s, 0], gx_ref[s, 0])
+            if r >= height:
+                return pick(even, gx_ref[s, 0], gp_ref[s, 0])
+            return x_ref[s, r]
+
+        piece = convolve_rows(row, range(0, height, 2), t_ref, across, False)
         for r in range(height):
-            mask = column_mask(bits_ref, s * height + r, c)
-            m_ref[s, r] = mask
-            sums[2] += fold(mask)
-            if not 2 <= r < height - 2:
-                continue
-            active, slope = silu_and_slope(piece((r - 2) // 2, r % 2) + bias)
+            active, slope = silu_and_slope(piece(r // 2, r % 2) + bias)
             if centre is None:
                 centre = middle(active)
             active = active - centre
-            a_ref[s, r - 2] = active
-            s_ref[s, r - 2] = slope * mask
+            mask = m_ref[s, r]
+            a_ref[s, r] = active
+            s_ref[s, r] = slope * mask
             add_moments(sums, active, mask)
     rows = [v.sum(0, keepdims=True) for v in sums]
-    st_ref[...] = stats_block([rows[0], rows[1], centre, rows[2]], c)
-
-
-def conv1_outer_kernel(x_ref, gx_ref, gp_ref, m_ref, t_ref, b_ref, part_ref, a_ref, s_ref, st_ref):
-    samples, height, across, c = x_ref.shape
-    even = lax.axis_index("lat") % 2 == 0
-    bias = b_ref[...]
-    centre = part_ref[2:3]
-
-    def row(r):
-        if r < 0:
-            parts = [pick(even, gp_ref[s, 0], gx_ref[s, 0]) for s in range(samples)]
-        elif r >= height:
-            parts = [pick(even, gx_ref[s, 0], gp_ref[s, 0]) for s in range(samples)]
-        else:
-            parts = [x_ref[s, r] for s in range(samples)]
-        return jnp.concatenate(parts, 0)
-
-    sums = [jnp.zeros((8, c), F32) for _ in range(2)]
-    for slot, start in ((0, 0), (2, height - 2)):
-        piece = convolve_rows(row, (start,), t_ref, across, False)
-        for s in range(samples):
-            for j in range(2):
-                active, slope = silu_and_slope(piece(s, j) + bias)
-                active = active - centre
-                mask = m_ref[s, start + j]
-                a_ref[s, slot + j] = active
-                s_ref[s, slot + j] = slope * mask
-                add_moments(sums, active, mask)
-    rows = [part_ref[i : i + 1] + v.sum(0, keepdims=True) for i, v in enumerate(sums)]
-    st_ref[...] = stats_block([rows[0], rows[1], centre, part_ref[3:4]], c)
+    st_ref[...] = stats_block([rows[0], rows[1], centre, count_ref[0:1]], c)
 
 
 def conv1_edge_kernel(
-    x_ref, gx_ref, gp_ref, hx_ref, hp_ref, u_ref, m_ref, st_ref, t_ref, b_ref, w2_ref,
+    hp_ref, hx_ref, gp_ref, gx_ref, x_ref, u_ref, m_ref, st_ref, t_ref, b_ref, w2_ref,
     a_ref, mh_ref, mu_ref, su_ref, t2_ref, tt2_ref,
 ):
     samples, height, across, c = x_ref.shape
@@ -253,7 +230,7 @@
 
 def conv2_kernel(
     pieces,
-    own_ref, a_ref, ao_ref, ah_ref, m_ref, mh_ref, mu_ref, su_ref, k_ref, b_ref, g_ref, t_ref, *refs,
+    own_ref, a_ref, ah_ref, m_ref, mh_ref, mu_ref, su_ref, k_ref, b_ref, g_ref, t_ref, *refs,
 ):
     stats, (n_ref, a2_ref, s2_ref, c1_ref, st2_ref, ext_ref) = gather(refs[:pieces]), refs[pieces:]
     samples, height, across, c = m_ref.shape
@@ -272,7 +249,7 @@
         for i in range(height + 4):
             r = i - 2
             if 0 <= r < height:
-                value, mask = own_row(a_ref, ao_ref, s, r, height), m_ref[s, r]
+                value, mask = a_ref[s, r], m_ref[s, r]
             else:
                 j = i if r < 0 else r - height + 2
                 value, mask = ah_ref[s, j], mh_ref[s, j]
@@ -311,7 +288,7 @@
 
 def back2_kernel(
     pieces,
-    own_ref, st1_ref, c1_ref, a2_ref, s2_ref, mu_ref, m_ref, a_ref, ao_ref, k_ref, g_ref, t_ref, *refs,
+    own_ref, st1_ref, c1_ref, a2_ref, s2_ref, mu_ref, m_ref, a_ref, k_ref, g_ref, t_ref, *refs,
 ):
     stats, (d_ref, dn_ref, c2_ref, st3_ref, ext_ref) = gather(refs[:pieces]), refs[pieces:]
     samples, height, across, c = m_ref.shape
@@ -340,7 +317,7 @@
             dn_ref[s, r] = part
             masked = part * m_ref[s, r]
             sums[0] += fold(masked)
-            sums[1] += fold(masked * own_row(a_ref, ao_ref, s, r, height))
+            sums[1] += fold(masked * a_ref[s, r])
     rows = [v.sum(0, keepdims=True) for v in sums]
     st3_ref[...] = stats_block([rows[0], rows[1], st1_ref[2:3]], c)
 
@@ -400,10 +377,10 @@
 
 def weight1_kernel(
     group, leads, pieces,
-    c1_ref, c2_ref, dn_ref, a_ref, ao_ref, s_ref, so_ref, x_ref, gx_ref, gp_ref, g_ref, w2_ref, b2_ref, *refs,
+    c1_ref, c2_ref, dn_ref, a_ref, s_ref, x_ref, gx_ref, gp_ref, g_ref, w2_ref, b2_ref, *refs,
 ):
     stats = gather(refs[:pieces])
-    d_ref, dx_ref, dp_ref, send_ref, keep_ref, acc_ref = refs[pieces:]
+    d_ref, send_ref, keep_ref, acc_ref = refs[pieces:]
     samples, height, across, c = x_ref.shape
     even = lax.axis_index("lat") % 2 == 0
     lead = lax.axis_index("lead")
@@ -417,12 +394,10 @@
     bias = jnp.zeros((8, c), F32)
     for s in range(samples):
         for r in range(height):
-            active = own_row(a_ref, ao_ref, s, r, height)
+            active = a_ref[s, r]
             grad = dn_ref[s, r] * scale + (active * by_active + constant)
-            d_ref[s, r] = (grad * own_row(s_ref, so_ref, s, r, height)).astype(BF16)
+            d_ref[s, r] = (grad * s_ref[s, r]).astype(BF16)
         grad = d_ref[s]
-        dx_ref[s] = pick(even, grad[height - 1], grad[0])
-        dp_ref[s] = pick(even, grad[0], grad[height - 1])
         wide = grad.astype(F32)
         bias += fold(wide)
         above = pick(even, gp_ref[s, 0], gx_ref[s, 0])
@@ -470,7 +445,15 @@
         put(send_ref, 0)
 
 
-def input_grad_kernel(d_ref, ex_ref, ep_ref, u_ref, w_ref, after_ref, o_ref, done_ref, k_ref):
+def edge_rows_kernel(d_ref, after_ref, dx_ref, dp_ref):
+    samples, height = d_ref.shape[:2]
+    even = lax.axis_index("lat") % 2 == 0
+    for s in range(samples):
+        dx_ref[s] = pick(even, d_ref[s, height - 1], d_ref[s, 0])
+        dp_ref[s] = pick(even, d_ref[s, 0], d_ref[s, height - 1])
+
+
+def input_grad_kernel(ep_ref, ex_ref, d_ref, u_ref, w_ref, o_ref, done_ref, k_ref):
     samples, height, across, c = u_ref.shape
     even = lax.axis_index("lat") % 2 == 0
     fill_toeplitz_transposed(w_ref, k_ref)
@@ -489,40 +472,38 @@
     done_ref[...] = jnp.zeros(done_ref.shape, F32)
 
 
-def finish_kernel(leads, mine_ref, *refs):
-    got_refs, other_ref = refs[: leads - 1], refs[leads - 1]
-    first, second = refs[leads + 1 : leads + 5], refs[leads + 5 :]
+def join_kernel(leads, *refs):
+    out_ref = refs[-1]
+    size = refs[0].shape[0] - SMALL
+    for k in range(leads):
+        out_ref[k * size : (k + 1) * size] = refs[k][:size]
+    out_ref[leads * size :] = refs[0][size:]
+
+
+def finish_kernel(leads, own_ref, other_ref, *refs):
+    first, second = refs[:4], refs[4:]
     core = lax.axis_index("dp") % 2
     lead = lax.axis_index("lead")
-    size = mine_ref.shape[0] - SMALL
-
-    def put(outs, chunk, small):
+    size = (own_ref.shape[0] - SMALL) // leads
+
+    def put(outs, ref):
         for k in range(leads):
             at = pl.multiple_of((k ^ lead) * size, 16)
-            outs[0][pl.ds(at, size)] = chunk(k).astype(F32)
-        total = small[:8].astype(F32) + small[8:].astype(F32)
+            outs[0][pl.ds(at, size)] = ref[k * size : (k + 1) * size].astype(F32)
+        small = ref[leads * size :].astype(F32)
+        total = small[:8] + small[8:]
         for i in range(3):
             outs[i + 1][...] = total[i : i + 1]
 
-    def own(outs):
-        put(outs, lambda k: got_refs[k - 1][...] if k else mine_ref[:size], mine_ref[size:])
-
-    def other(outs):
-        put(
-            outs,
-            lambda k: other_ref[k * size : (k + 1) * size],
-            other_ref[leads * size :],
-        )
-
     @pl.when(core == 0)
     def _():
-        own(first)
-        other(second)
+        put(first, own_ref)
+        put(second, other_ref)
 
     @pl.when(core != 0)
     def _():
-        other(first)
-        own(second)
+        put(first, other_ref)
+        put(second, own_ref)
 
 
 def add_kernel(parts, waits, *refs):
@@ -537,13 +518,13 @@
         out[size:] = jnp.concatenate([high, (small - high.astype(F32)).astype(BF16)], 0)
 
 
-def call(kernel, outs, scratch, operands, name, flops=0, waits=(), space=VMEM):
+def call(kernel, outs, scratch, operands, name, flops=0, waits=(), spaces=(VMEM, VMEM)):
     size = sum(o.size * o.dtype.itemsize for o in operands)
     return pl.pallas_call(
         kernel,
         out_shape=outs,
-        in_specs=[space] * len(operands) + [pl.BlockSpec(memory_space=pl.ANY)] * len(waits),
-        out_specs=jax.tree.map(lambda _: space, outs),
+        in_specs=[spaces[0]] * len(operands) + [pl.BlockSpec(memory_space=pl.ANY)] * len(waits),
+        out_specs=jax.tree.map(lambda _: spaces[1], outs),
         scratch_shapes=scratch,
         compiler_params=pltpu.CompilerParams(vmem_limit_bytes=16 * 2**20),
         cost_estimate=pl.CostEstimate(flops=flops, bytes_accessed=size, transcendentals=0),
@@ -560,7 +541,8 @@
     first = [(i, i ^ 1) for i in range(n) if i ^ 1 < n]
     second = [(i, i + 1) for i in range(1, n - 1, 2)]
     second += [(j, i) for i, j in second]
-    return lax.ppermute(value_x, axis, first), lax.ppermute(value_p, axis, second)
+    got_p = lax.ppermute(value_p, axis, second)
+    return lax.ppermute(value_x, axis, first), got_p
 
 
 def spread(stats):
@@ -571,7 +553,7 @@
     return [blocks] + [swap(blocks, "lat", k) for k in range(1, lax.axis_size("lat"))]
 
 
-def add_chunks(parts, name, outs=1, waits=()):
+def add_chunks(parts, name, outs=1, waits=(), flops=0):
     shape = jax.ShapeDtypeStruct(parts[0].shape[-2:], BF16)
     return call(
         functools.partial(add_kernel, len(parts), len(waits)),
@@ -579,36 +561,39 @@
         [],
         parts,
         name,
-        waits=waits,
-    )
-
-
-def sum_everywhere(send, keep, beside_lat, beside_last):
+        flops,
+        waits,
+    )
+
+
+def sum_everywhere(send, keep, block_output, input_grad):
     leads, lats = lax.axis_size("lead"), lax.axis_size("lat")
     chunks = add_chunks([keep, swap(send, "dp", 1)], "add_dp", leads)
-    got = [swap(chunks[k], "lead", k) for k in range(1, leads)]
-    (mine,) = add_chunks([chunks[0]] + got, "add_lead")
+    got = [swap(chunks[k], "lead", k) for k in reversed(range(1, leads))]
+    (mine,) = add_chunks([chunks[0]] + got, "add_lead", flops=HIDE)
     got = [swap(mine, "lat", k) for k in range(1, lats)]
-    first = beside_lat(chunks[0])
-    (mine,) = add_chunks([mine] + got, "add_lat", waits=(first[1],))
+    grad_input = input_grad(chunks[0])
+    (mine,) = add_chunks([mine] + got, "add_lat", waits=(grad_input[1],))
     k = 2
     while k < lax.axis_size("dp"):
         (mine,) = add_chunks([mine, swap(mine, "dp", k)], "add_far_dp")
         k *= 2
     size, c = mine.shape[0] - SMALL, mine.shape[1]
-    got = [swap(mine[:size], "lead", k) for k in range(1, leads)]
-    other = swap(jnp.concatenate([mine[:size]] + got + [mine[size:]], 0), "dp", 1)
-    last = beside_last(mine)
+    got = [swap(mine, "lead", k) for k in range(1, leads)]
+    output = block_output(mine)
+    own = call(
+        functools.partial(join_kernel, leads),
+        jax.ShapeDtypeStruct((leads * size + SMALL, c), BF16),
+        [],
+        (mine, *got),
+        "join",
+        waits=(output[1],),
+    )
     one = [jax.ShapeDtypeStruct((leads * size, c), F32)] + [jax.ShapeDtypeStruct((1, c), F32)] * 3
     sums = call(
-        functools.partial(finish_kernel, leads),
-        one + one,
-        [],
-        (mine, *got, other),
-        "finish",
-        waits=(last[1],),
-    )
-    return sums[:4], sums[4:], first[0], last[0]
+        functools.partial(finish_kernel, leads), one + one, [], (own, swap(own, "dp", 1)), "finish"
+    )
+    return sums[:4], sums[4:], output[0], grad_input[0]
 
 
 def shards(
@@ -649,41 +634,33 @@
         [pltpu.SemaphoreType.DMA((2,))],
         (x,),
         "near_rows",
-        space=pl.BlockSpec(memory_space=pl.ANY),
+        conv_flops,
+        spaces=(pl.BlockSpec(memory_space=pl.ANY),) * 2,
     )
     gx, gp = neighbours(*near, "lat")
-    a1, s1, wide_mask, bits, w1t, part = call(
-        conv1_inner_kernel,
-        (
-            shape(height - 4),
-            shape(height - 4),
-            shape(height),
-            array((slabs, across, 128), F32),
-            weights,
-            vector,
-        ),
+    packed = array((3 * samples + slabs, across, c), BF16)
+    far_x, far_p, wide_mask, count = call(
+        far_rows_kernel,
+        (packed, packed, shape(height), vector),
+        [pltpu.VMEM((slabs, across, 128), F32)],
+        (x, u, mask.reshape(samples * height, across)),
+        "far_rows",
+        conv_flops,
+    )
+    hx, hp = neighbours(far_x, far_p, "lat")
+    a1, s1, w1t, own1 = call(
+        conv1_kernel,
+        (shape(height), shape(height), weights, vector),
         [],
-        (x, mask.reshape(samples * height, across), conv1_weight, b1),
-        "conv1_inner",
-        conv_flops,
-    )
-    packed = array((3 * samples + slabs, across, c), BF16)
-    hx, hp = neighbours(
-        *call(far_rows_kernel, (packed, packed), [], (x, u, bits), "far_rows", waits=(gx, gp)), "lat"
-    )
-    a1o, s1o, own1 = call(
-        conv1_outer_kernel,
-        (shape(4), shape(4), vector),
-        [],
-        (x, gx, gp, wide_mask, w1t, b1, part),
-        "conv1_outer",
-        conv_flops // 2,
+        (gp, gx, x, wide_mask, count, conv1_weight, b1),
+        "conv1",
+        16 * conv_flops,
     )
     a1h, halo_mask, mu, mu_sum, w2t, w2tt = call(
         conv1_edge_kernel,
         (shape(4), shape(4), shape(height + 2), vector, weights, turned),
         [],
-        (x, gx, gp, hx, hp, u, wide_mask, own1, w1t, b1, conv2_weight),
+        (hp, hx, gp, gx, x, u, wide_mask, own1, w1t, b1, conv2_weight),
         "conv1_edges",
         conv_flops // 2,
     )
@@ -692,7 +669,7 @@
         functools.partial(conv2_kernel, len(st1)),
         (shape(height + 2, BF16), shape(height + 2), shape(height + 2), vector, vector),
         [ext(height + 4)],
-        (own1, a1, a1o, a1h, wide_mask, halo_mask, mu, mu_sum, w2t, b2, g1, t1, *st1),
+        (own1, a1, a1h, wide_mask, halo_mask, mu, mu_sum, w2t, b2, g1, t1, *st1),
         "conv2",
         conv_flops,
     )
@@ -701,7 +678,7 @@
         functools.partial(back2_kernel, len(st2)),
         (shape(height, BF16), shape(height), vector, vector),
         [ext(height + 2)],
-        (own2, own1, c1, a2, s2, mu, wide_mask, a1, a1o, w2tt, g2, t2, *st2),
+        (own2, own1, c1, a2, s2, mu, wide_mask, a1, w2tt, g2, t2, *st2),
         "conv2_back",
         conv_flops,
     )
@@ -716,28 +693,29 @@
         waits=(st3[0],),
     )
     chunks = array((leads, 9 * c // leads + SMALL, c), BF16)
-    d1, dx, dp, send, keep = call(
+    d1, send, keep = call(
         functools.partial(weight1_kernel, group, leads, len(st3)),
-        (shape(height, BF16), edge, edge, chunks, chunks),
+        (shape(height, BF16), chunks, chunks),
         [acc],
-        (c1, c2, dn1, a1, a1o, s1, s1o, x, gx, gp, g1, w2, bias2, *st3),
+        (c1, c2, dn1, a1, s1, x, gx, gp, g1, w2, bias2, *st3),
         "conv1_weight_grad",
         conv_flops,
     )
-    dx, dp = neighbours(dx, dp, "lat")
-    first, second, grad_input, output = sum_everywhere(
-        send,
-        keep,
-        lambda after: call(
+
+    def input_grad(after):
+        rows = call(edge_rows_kernel, (edge, edge), [], (d1,), "edge_rows", waits=(after,))
+        rows = neighbours(*rows, "lat")
+        return call(
             input_grad_kernel,
             (shape(height, BF16), vector),
             [pltpu.VMEM(turned.shape, BF16)],
-            (d1, dx, dp, u, conv1_weight),
+            (rows[1], rows[0], d1, u, conv1_weight),
             "conv1_back",
             conv_flops,
-            waits=(after,),
-        ),
-        lambda after: call(
+        )
+
+    def block_output(after):
+        return call(
             output_kernel,
             (shape(height, BF16), vector),
             [],
@@ -745,8 +723,9 @@
             "output",
             conv_flops // 2,
             waits=(after,),
-        ),
-    )
+        )
+
+    first, second, output, grad_input = sum_everywhere(send, keep, block_output, input_grad)
     sums = []
     for part in (first, second):
         sums += [part[0].reshape(3, 3, c, c)] + [v.reshape(c) for v in part[1:]]

time: 82.3 us -> 77.8 us (0.945)
  waiting for transfers between devices: 20 us -> 15.2 us
  local copies, waits for them, and re-layouts: 3.7 us -> 1.27 us
  starting transfers between devices: 36.5 us -> 38.8 us
    ppermute x23, waiting for transfers between devices: 18.8 us -> 14.7 us  [swap(): lax.ppermute(value, axis, [(i, i ^ k) for i in range(lax.axis_size(axis))])]
    unnamed x30 -> x24, local copies, waits for them, and re-layouts: 3.69 us -> 1.27 us
    ppermute x6, starting transfers between devices: 11.4 us -> 13.7 us  [the longest x3 11.6 us: neighbours(): return (lax.ppermute(value_x, axis, first), got_p)]
    pallas_call x15 -> x16, Pallas kernels: 20.8 us -> 21.4 us  [call(): pl.pallas_call(kernel, out_shape=outs, in_specs=[spaces[0]] * len(operand...]
  transfers between devices with their start and end apart: 29 -> 29, of which waited for: 15 -> 14; matrix products, arithmetic and copies ran while one was open for 0% -> 0% of each run, Pallas kernels for 13% -> 15%
where the time goes in v1:
time: 77.8 us; the launch traced here: 77.6 us
  starting transfers between devices  38.8 us (50%)
  Pallas kernels  21.4 us (28%)
  waiting for transfers between devices  15.2 us (20%)
  local copies, waits for them, and re-layouts  1.27 us (2%)
  between operations  0.89 us (1%)
    ppermute x23, starting transfers between devices, swap(): lax.ppermute(value, axis, [(i, i ^ k) for i in range(lax.axis_size(axis))])  25.1 us
    pallas_call x16, Pallas kernels, call(): pl.pallas_call(kernel, out_shape=outs, in_specs=[spaces[0]] * len(operand...  21.4 us
    ppermute x23, waiting for transfers between devices, swap(): lax.ppermute(value, axis, [(i, i ^ k) for i in range(lax.axis_size(axis))])  14.7 us
    ppermute x3, starting transfers between devices, neighbours(): return (lax.ppermute(value_x, axis, first), got_p)  11.6 us
    ppermute x3, starting transfers between devices, neighbours(): got_p = lax.ppermute(value_p, axis, second)  2.16 us
  transfers between devices with their start and end apart: 29, of which 14 were waited for; matrix products, arithmetic and copies ran while one was open for 0% of the time, Pallas kernels for 15%

profile of v1, /device:TPU:0, one launch (start us, length us, event | category | flops | bytes accessed | tf_op | source)
XLA Modules:
  0.0 77.6 jit_solution(14600254584329566115)
XLA Ops:
  0.7 1.2 %copy-done = bf16[1,8,8,64,128]{4,3,2,1,0:T(8,128)(2,1)S(1)} copy-done((bf16[1,8,8,64,128]{4,3,2,1,0:T(8,128)(2,1)S(1)}, bf16[1,8,8,64,128]{4,3,2,1,0:T(8,128)(2,1)}, u32[]{:S(2)}) %copy-start) | copy-done | bytes 1048600
  2.8 5.9 %collective-permute-start.1 = (bf16[8,1,64,128]{3,2,1,0:T(8,128)(2,1)S(1)}, bf16[8,1,64,128]{3,2,1,0:T(8,128)(2,1)S(1)}, u32[]{:S(2)}, u32[]{:S(2)}) collective-permute-start(bf16[8,1,64,128]{3,2,1,0:T(8,128)(2,1)S(1)} %get-tuple-element.59), channel_id=1, source_target_pairs={{0,1},{1,0},{2,3},{3,2},{4,5},{5,4},{6,7},{7,6},{8,9},{9,8},{10,11... | collective-permute-start | bytes 393224 | tf_op jit(solution)/shard_map/ppermute | solution.py:545
  10.2 1.8 %collective-permute-start.3 = (bf16[25,64,128]{2,1,0:T(8,128)(2,1)S(1)}, bf16[25,64,128]{2,1,0:T(8,128)(2,1)S(1)}, u32[]{:S(2)}, u32[]{:S(2)}) collective-permute-start(bf16[25,64,128]{2,1,0:T(8,128)(2,1)S(1)} %get-tuple-element.65), channel_id=1, source_target_pairs={{0,1},{1,0},{2,3},{3,2},{4,5},{5,4},{6,7},{7,6},{8,9},{9,8},{10,11... | collective-permute-start | bytes 1228808 | tf_op jit(solution)/shard_map/ppermute | solution.py:545
  12.0 2.8 %conv1.1 = (f32[8,8,64,128]{3,2,1,0:T(8,128)S(1)}, f32[8,8,64,128]{3,2,1,0:T(8,128)S(1)}, bf16[3,512,256]{2,1,0:T(8,128)(2,1)S(1)}, f32[8,128]{1,0:T(8,128)S(1)}) custom-call(bf16[8,1,64,128]{3,2,1,0:T(8,128)(2,1)S(1)} %collective-permute-done.gp_ref, bf16[8,1,64,128]{3,2,1,0:T(8,128)(2,1)S(1)} %collective-permute-done.1.gx_ref, ...), custom_call_target="tpu_custom_call" | custom-call | flops 19327352832 | bytes 3707392 | tf_op jit(solution)/shard_map/conv1/pallas_call | solution.py:523
  14.9 1.2 %collective-permute-done.4 = f32[1,8,128]{2,1,0:T(8,128)S(1)} collective-permute-done((f32[1,8,128]{2,1,0:T(8,128)S(1)}, f32[1,8,128]{2,1,0:T(8,128)S(1)}, u32[]{:S(2)}, u32[]{:S(2)}) %collective-permute-start.4) | collective-permute-done | bytes 4128 | tf_op jit(solution)/shard_map/ppermute | solution.py:536
  16.0 2.5 %collective-permute-start.7 = (f32[2,8,128]{2,1,0:T(8,128)S(1)}, f32[2,8,128]{2,1,0:T(8,128)S(1)}, u32[]{:S(2)}, u32[]{:S(2)}) collective-permute-start(f32[2,8,128]{2,1,0:T(8,128)S(1)} %pad_maximum_fusion.refs_0_), channel_id=1, source_target_pairs={{0,3},{1,2},{2,1},{3,0},{4,7},{5,6},{6,5},{7,4},{8,11},{9,10},{10,... | collective-permute-start | bytes 24584 | tf_op jit(solution)/shard_map/ppermute | solution.py:536
  19.1 1.3 %collective-permute-start.5 = (f32[2,8,128]{2,1,0:T(8,128)S(1)}, f32[2,8,128]{2,1,0:T(8,128)S(1)}, u32[]{:S(2)}, u32[]{:S(2)}) collective-permute-start(f32[2,8,128]{2,1,0:T(8,128)S(1)} %pad_maximum_fusion.refs_0_), channel_id=1, source_target_pairs={{0,1},{1,0},{2,3},{3,2},{4,5},{5,4},{6,7},{7,6},{8,9},{9,8},{10,11... | collective-permute-start | bytes 24584 | tf_op jit(solution)/shard_map/ppermute | solution.py:536
  20.9 1.7 %conv1_edges.1 = (f32[8,4,64,128]{3,2,1,0:T(8,128)S(1)}, f32[8,4,64,128]{3,2,1,0:T(8,128)S(1)}, f32[8,10,64,128]{3,2,1,0:T(8,128)S(1)}, f32[8,128]{1,0:T(8,128)S...) custom-call(bf16[25,64,128]{2,1,0:T(8,128)(2,1)S(1)} %collective-permute-done.2.hp_ref, ...), custom_call_target="tpu_custom_call" | custom-call | flops 603979776 | bytes 6361600 | tf_op jit(solution)/shard_map/conv1_edges/pallas_call | solution.py:523
  23.5 3.7 %conv2.1 = (bf16[8,10,64,128]{3,2,1,0:T(8,128)(2,1)S(1)}, f32[8,10,64,128]{3,2,1,0:T(8,128)S(1)}, f32[8,10,64,128]{3,2,1,0:T(8,128)S(1)}, f32[8,128]{1,0:T(8,128)S(1)}, f32[8,128]{1,0:T(8,128)S(1)}) custom-call(f32[8,128]{1,0:T(8,128)S(1)} %get-tuple-element.62.st_ref.own_ref.st1_ref, f32[8,8,64,128]{3,2,1,0:T(8,128)S(1)} %get-tuple-element.63.a_ref, ...), custom_call_target="tpu_custom_call" | custom-call | flops 1207959552 | bytes 9741824 | tf_op jit(solution)/shard_map/conv2/pallas_call | solution.py:523
  27.3 1.2 %collective-permute-done.8 = f32[1,8,128]{2,1,0:T(8,128)S(1)} collective-permute-done((f32[1,8,128]{2,1,0:T(8,128)S(1)}, f32[1,8,128]{2,1,0:T(8,128)S(1)}, u32[]{:S(2)}, u32[]{:S(2)}) %collective-permute-start.8) | collective-permute-done | bytes 4128 | tf_op jit(solution)/shard_map/ppermute | solution.py:536
  28.4 1.9 %collective-permute-start.11 = (f32[2,8,128]{2,1,0:T(8,128)S(1)}, f32[2,8,128]{2,1,0:T(8,128)S(1)}, u32[]{:S(2)}, u32[]{:S(2)}) collective-permute-start(f32[2,8,128]{2,1,0:T(8,128)S(1)} %pad_maximum_fusion.1.refs_0_), channel_id=1, source_target_pairs={{0,3},{1,2},{2,1},{3,0},{4,7},{5,6},{6,5},{7,4},{8,11},{9,10},{10,... | collective-permute-start | bytes 24584 | tf_op jit(solution)/shard_map/ppermute | solution.py:536
  31.0 1.8 %collective-permute-start.9 = (f32[2,8,128]{2,1,0:T(8,128)S(1)}, f32[2,8,128]{2,1,0:T(8,128)S(1)}, u32[]{:S(2)}, u32[]{:S(2)}) collective-permute-start(f32[2,8,128]{2,1,0:T(8,128)S(1)} %pad_maximum_fusion.1.refs_0_), channel_id=1, source_target_pairs={{0,1},{1,0},{2,3},{3,2},{4,5},{5,4},{6,7},{7,6},{8,9},{9,8},{10,11... | collective-permute-start | bytes 24584 | tf_op jit(solution)/shard_map/ppermute | solution.py:536
  32.8 1.1 %collective-permute-done.11.refs_3_ = f32[2,8,128]{2,1,0:T(8,128)S(1)} collective-permute-done((f32[2,8,128]{2,1,0:T(8,128)S(1)}, f32[2,8,128]{2,1,0:T(8,128)S(1)}, u32[]{:S(2)}, u32[]{:S(2)}) %collective-permute-start.11) | collective-permute-done | bytes 8224 | tf_op jit(solution)/shard_map/ppermute | solution.py:536
  33.9 1.0 %collective-permute-done.10.refs_2_ = f32[2,8,128]{2,1,0:T(8,128)S(1)} collective-permute-done((f32[2,8,128]{2,1,0:T(8,128)S(1)}, f32[2,8,128]{2,1,0:T(8,128)S(1)}, u32[]{:S(2)}, u32[]{:S(2)}) %collective-permute-start.10) | collective-permute-done | bytes 8224 | tf_op jit(solution)/shard_map/ppermute | solution.py:536
  34.8 2.5 %conv2_back.1 = (bf16[8,8,64,128]{3,2,1,0:T(8,128)(2,1)S(1)}, f32[8,8,64,128]{3,2,1,0:T(8,128)S(1)}, f32[8,128]{1,0:T(8,128)S(1)}, f32[8,128]{1,0:T(8,128)S(1)}) custom-call(f32[8,128]{1,0:T(8,128)S(1)} %get-tuple-element.73.own_ref, f32[8,128]{1,0:T(8,128)S(1)} %get-tuple-element.62.st_ref.own_ref.st1_ref, f32[8,128]{1,0:T(8,128)S(1)} %get-tuple-element.74.c1_ref, ...), custom_call_target="tpu_custom_call" | custom-call | flops 1207959552 | bytes 12891136 | tf_op jit(solution)/shard_map/conv2_back/pallas_call | solution.py:523
  37.4 1.2 %collective-permute-done.12 = f32[1,8,128]{2,1,0:T(8,128)S(1)} collective-permute-done((f32[1,8,128]{2,1,0:T(8,128)S(1)}, f32[1,8,128]{2,1,0:T(8,128)S(1)}, u32[]{:S(2)}, u32[]{:S(2)}) %collective-permute-start.12) | collective-permute-done | bytes 4128 | tf_op jit(solution)/shard_map/ppermute | solution.py:536
  38.6 2.3 %collective-permute-start.15 = (f32[2,8,128]{2,1,0:T(8,128)S(1)}, f32[2,8,128]{2,1,0:T(8,128)S(1)}, u32[]{:S(2)}, u32[]{:S(2)}) collective-permute-start(f32[2,8,128]{2,1,0:T(8,128)S(1)} %pad_maximum_fusion.2.after_ref.refs_0_), channel_id=1, source_target_pairs={{0,3},{1,2},{2,1},{3,0},{4,7},{5,6},{6,5},{7,4},{8,11},{9,10},{10,... | collective-permute-start | bytes 24584 | tf_op jit(solution)/shard_map/ppermute | solution.py:536
  41.7 1.3 %collective-permute-start.13 = (f32[2,8,128]{2,1,0:T(8,128)S(1)}, f32[2,8,128]{2,1,0:T(8,128)S(1)}, u32[]{:S(2)}, u32[]{:S(2)}) collective-permute-start(f32[2,8,128]{2,1,0:T(8,128)S(1)} %pad_maximum_fusion.2.after_ref.refs_0_), channel_id=1, source_target_pairs={{0,1},{1,0},{2,3},{3,2},{4,5},{5,4},{6,7},{7,6},{8,9},{9,8},{10,11... | collective-permute-start | bytes 24584 | tf_op jit(solution)/shard_map/ppermute | solution.py:536
  43.0 1.8 %conv2_weight_grad.1 = (bf16[1152,128]{1,0:T(8,128)(2,1)S(1)}, f32[8,128]{1,0:T(8,128)S(1)}) custom-call(bf16[8,10,64,128]{3,2,1,0:T(8,128)(2,1)S(1)} %get-tuple-element.80.n_ref, bf16[8,8,64,128]{3,2,1,0:T(8,128)(2,1)S(1)} %get-tuple-element.81.d_ref, f32[2,8,128]{2,1,0:T(8,128)S(1)} %pad_maximum_fusion.2.after_ref.refs_0_), custom_call_target="tpu_custom_call" | custom-call | flops 1207959552 | bytes 2359296 | tf_op jit(solution)/shard_map/conv2_weight_grad/pallas_call | solution.py:523
  45.4 2.4 %conv1_weight_grad.1 = (bf16[8,8,64,128]{3,2,1,0:T(8,128)(2,1)S(1)}, bf16[4,304,128]{2,1,0:T(8,128)(2,1)S(1)}, bf16[4,304,128]{2,1,0:T(8,128)(2,1)S(1)}) custom-call(f32[8,128]{1,0:T(8,128)S(1)} %get-tuple-element.74.c1_ref, f32[8,128]{1,0:T(8,128)S(1)} %get-tuple-element.77.c2_ref, f32[8,8,64,128]{3,2,1,0:T(8,128)S(1)} %get-tuple-element.78.dn_ref, ...), custom_call_target="tpu_custom_call" | custom-call | flops 1207959552 | bytes 7942656 | tf_op jit(solution)/shard_map/conv1_weight_grad/pallas_call | solution.py:523
  47.9 1.6 %collective-permute-done.16.refs_1_ = bf16[4,304,128]{2,1,0:T(8,128)(2,1)S(1)} collective-permute-done((bf16[4,304,128]{2,1,0:T(8,128)(2,1)S(1)}, bf16[4,304,128]{2,1,0:T(8,128)(2,1)S(1)}, u32[]{:S(2)}, u32[]{:S(2)}) %collective-permute-start.16) | collective-permute-done | bytes 311328 | tf_op jit(solution)/shard_map/ppermute | solution.py:536
  49.6 2.5 %collective-permute-start.17 = (bf16[304,128]{1,0:T(8,128)(2,1)S(1)}, bf16[304,128]{1,0:T(8,128)(2,1)S(1)}, u32[]{:S(2)}, u32[]{:S(2)}) collective-permute-start(bf16[304,128]{1,0:T(8,128)(2,1)S(1)} %get-tuple-element.88), channel_id=1, source_target_pairs={{0,24},{8,16},{16,8},{24,0},{1,25},{9,17},{17,9},{25,1},{2,26},{10... | collective-permute-start | bytes 233480 | tf_op jit(solution)/shard_map/ppermute | solution.py:536
  53.9 3.9 %collective-permute-start.24 = (bf16[8,64,128]{2,1,0:T(8,128)(2,1)S(1)}, bf16[8,64,128]{2,1,0:T(8,128)(2,1)S(1)}, u32[]{:S(2)}, u32[]{:S(2)}) collective-permute-start(bf16[8,64,128]{2,1,0:T(8,128)(2,1)S(1)} %get-tuple-element.93), channel_id=1, source_target_pairs={{0,1},{1,0},{2,3},{3,2},{4,5},{5,4},{6,7},{7,6},{8,9},{9,8},{10,11... | collective-permute-start | bytes 393224 | tf_op jit(solution)/shard_map/ppermute | solution.py:545
  57.8 1.6 %collective-permute-start.22 = (bf16[304,128]{1,0:T(8,128)(2,1)S(1)}, bf16[304,128]{1,0:T(8,128)(2,1)S(1)}, u32[]{:S(2)}, u32[]{:S(2)}) collective-permute-start(bf16[304,128]{1,0:T(8,128)(2,1)S(1)} %add_lead.1.refs_0_), channel_id=1, source_target_pairs={{0,3},{1,2},{2,1},{3,0},{4,7},{5,6},{6,5},{7,4},{8,11},{9,10},{10,... | collective-permute-start | bytes 233480 | tf_op jit(solution)/shard_map/ppermute | solution.py:536
  59.7 2.6 %collective-permute-start.20 = (bf16[304,128]{1,0:T(8,128)(2,1)S(1)}, bf16[304,128]{1,0:T(8,128)(2,1)S(1)}, u32[]{:S(2)}, u32[]{:S(2)}) collective-permute-start(bf16[304,128]{1,0:T(8,128)(2,1)S(1)} %add_lead.1.refs_0_), channel_id=1, source_target_pairs={{0,1},{1,0},{2,3},{3,2},{4,5},{5,4},{6,7},{7,6},{8,9},{9,8},{10,11... | collective-permute-start | bytes 233480 | tf_op jit(solution)/shard_map/ppermute | solution.py:536
  62.3 2.9 %conv1_back.1 = (bf16[8,8,64,128]{3,2,1,0:T(8,128)(2,1)}, f32[8,128]{1,0:T(8,128)S(1)}) custom-call(bf16[8,64,128]{2,1,0:T(8,128)(2,1)S(1)} %collective-permute-done.23.ep_ref, bf16[8,64,128]{2,1,0:T(8,128)(2,1)S(1)} %collective-permute-done.24.ex_ref, bf16[8,8,64,128]{3,2,1,0:T(8,128)(2,1)S(1)} %get-tuple-element.91.d_ref, ...), custom_call_target="tpu_custom_call" | custom-call | flops 1207959552 | bytes 2654208 | tf_op jit(solution)/shard_map/conv1_back/pallas_call | solution.py:523
  65.2 2.1 %collective-permute-done.21.refs_2_ = bf16[304,128]{1,0:T(8,128)(2,1)S(1)} collective-permute-done((bf16[304,128]{1,0:T(8,128)(2,1)S(1)}, bf16[304,128]{1,0:T(8,128)(2,1)S(1)}, u32[]{:S(2)}, u32[]{:S(2)}) %collective-permute-start.21) | collective-permute-done | bytes 77856 | tf_op jit(solution)/shard_map/ppermute | solution.py:536
  67.4 2.2 %collective-permute-start.27 = (bf16[304,128]{1,0:T(8,128)(2,1)S(1)}, bf16[304,128]{1,0:T(8,128)(2,1)S(1)}, u32[]{:S(2)}, u32[]{:S(2)}) collective-permute-start(bf16[304,128]{1,0:T(8,128)(2,1)S(1)} %add_lat.1.after_ref.refs_0_), channel_id=1, source_target_pairs={{0,24},{8,16},{16,8},{24,0},{1,25},{9,17},{17,9},{25,1},{2,26},{10... | collective-permute-start | bytes 233480 | tf_op jit(solution)/shard_map/ppermute | solution.py:536
  70.9 1.4 %output.1 = (bf16[8,8,64,128]{3,2,1,0:T(8,128)(2,1)}, f32[8,128]{1,0:T(8,128)S(1)}) custom-call(bf16[8,8,64,128]{3,2,1,0:T(8,128)(2,1)S(1)} %bitcast.27, f32[8,10,64,128]{3,2,1,0:T(8,128)S(1)} %get-tuple-element.72.a2_ref, f32[8,8,64,128]{3,2,1,0:T(8,128)S(1)} %get-tuple-element.60.m_ref, f32[8,128]{1,0:T(8,128)S(1)} %get-tuple-element.77.c2_ref, ...), custom_call_target="tpu_custom_call" | custom-call | flops 603979776 | bytes 5771264 | tf_op jit(solution)/shard_map/output/pallas_call | solution.py:523
  72.4 1.2 %collective-permute-done.27.refs_3_ = bf16[304,128]{1,0:T(8,128)(2,1)S(1)} collective-permute-done((bf16[304,128]{1,0:T(8,128)(2,1)S(1)}, bf16[304,128]{1,0:T(8,128)(2,1)S(1)}, u32[]{:S(2)}, u32[]{:S(2)}) %collective-permute-start.27) | collective-permute-done | bytes 77856 | tf_op jit(solution)/shard_map/ppermute | solution.py:536
  74.9 1.6 %collective-permute-done.28.other_ref = bf16[1168,128]{1,0:T(8,128)(2,1)S(1)} collective-permute-done((bf16[1168,128]{1,0:T(8,128)(2,1)S(1)}, bf16[1168,128]{1,0:T(8,128)(2,1)S(1)}, u32[]{:S(2)}, u32[]{:S(2)}) %collective-permute-start.28) | collective-permute-done | bytes 299040 | tf_op jit(solution)/shard_map/ppermute | solution.py:536
  76.5 1.1 %finish.1 = (f32[1152,128]{1,0:T(8,128)}, f32[1,128]{1,0:T(1,128)}, f32[1,128]{1,0:T(1,128)}, f32[1,128]{1,0:T(1,128)}, f32[1152,128]{1,0:T(8,128)}, /*index=5*/...) custom-call(bf16[1168,128]{1,0:T(8,128)(2,1)S(1)} %join.1.own_ref, bf16[1168,128]{1,0:T(8,128)(2,1)S(1)} %collective-permute-done.28.other_ref), custom_call_target="tpu_custom_call" | custom-call | bytes 598016 | tf_op jit(solution)/shard_map/finish/pallas_call | solution.py:523
  (69 shorter events, 11.8 us)
Async XLA Ops:
  1.9 10.0 %collective-permute-start = (bf16[8,1,64,128]{3,2,1,0:T(8,128)(2,1)S(1)}, bf16[8,1,64,128]{3,2,1,0:T(8,128)(2,1)S(1)}, u32[]{:S(2)}, u32[]{:S(2)}) collective-permute-start(bf16[8,1,64,128]{3,2,1,0:T(8,128)(2,1)S(1)} %get-tuple-element.58), channel_id=1, source_target_pairs={{1,2},{2,1},{5,6},{6,5},{9,10},{10,9},{13,14},{14,13},{17,18},{18,... | collective-permute-start | bytes 393224 | tf_op jit(solution)/shard_map/ppermute | solution.py:544
  2.8 9.2 %collective-permute-start.1 = (bf16[8,1,64,128]{3,2,1,0:T(8,128)(2,1)S(1)}, bf16[8,1,64,128]{3,2,1,0:T(8,128)(2,1)S(1)}, u32[]{:S(2)}, u32[]{:S(2)}) collective-permute-start(bf16[8,1,64,128]{3,2,1,0:T(8,128)(2,1)S(1)} %get-tuple-element.59), channel_id=1, source_target_pairs={{0,1},{1,0},{2,3},{3,2},{4,5},{5,4},{6,7},{7,6},{8,9},{9,8},{10,11... | collective-permute-start | bytes 393224 | tf_op jit(solution)/shard_map/ppermute | solution.py:545
  9.5 10.9 %collective-permute-start.2 = (bf16[25,64,128]{2,1,0:T(8,128)(2,1)S(1)}, bf16[25,64,128]{2,1,0:T(8,128)(2,1)S(1)}, u32[]{:S(2)}, u32[]{:S(2)}) collective-permute-start(bf16[25,64,128]{2,1,0:T(8,128)(2,1)S(1)} %get-tuple-element.64), channel_id=1, source_target_pairs={{1,2},{2,1},{5,6},{6,5},{9,10},{10,9},{13,14},{14,13},{17,18},{18,... | collective-permute-start | bytes 1228808 | tf_op jit(solution)/shard_map/ppermute | solution.py:544
  10.2 10.7 %collective-permute-start.3 = (bf16[25,64,128]{2,1,0:T(8,128)(2,1)S(1)}, bf16[25,64,128]{2,1,0:T(8,128)(2,1)S(1)}, u32[]{:S(2)}, u32[]{:S(2)}) collective-permute-start(bf16[25,64,128]{2,1,0:T(8,128)(2,1)S(1)} %get-tuple-element.65), channel_id=1, source_target_pairs={{0,1},{1,0},{2,3},{3,2},{4,5},{5,4},{6,7},{7,6},{8,9},{9,8},{10,11... | collective-permute-start | bytes 1228808 | tf_op jit(solution)/shard_map/ppermute | solution.py:545
  12.0 8.9 %copy-start.3 = (bf16[3,3,128,128]{3,2,1,0:T(8,128)(2,1)S(1)}, bf16[3,3,128,128]{3,2,1,0:T(8,128)(2,1)}, u32[]{:S(2)}) copy-start(bf16[3,3,128,128]{3,2,1,0:T(8,128)(2,1)} %w2_ref.1) | copy-start | bytes 884740
  14.8 1.2 %collective-permute-start.4 = (f32[1,8,128]{2,1,0:T(8,128)S(1)}, f32[1,8,128]{2,1,0:T(8,128)S(1)}, u32[]{:S(2)}, u32[]{:S(2)}) collective-permute-start(f32[1,8,128]{2,1,0:T(8,128)S(1)} %bitcast.31), channel_id=1, source_target_pairs={{0,4},{4,0},{1,5},{5,1},{2,6},{6,2},{3,7},{7,3},{8,12},{12,8},{9,1... | collective-permute-start | bytes 12296 | tf_op jit(solution)/shard_map/ppermute | solution.py:536
  16.0 7.4 %collective-permute-start.7 = (f32[2,8,128]{2,1,0:T(8,128)S(1)}, f32[2,8,128]{2,1,0:T(8,128)S(1)}, u32[]{:S(2)}, u32[]{:S(2)}) collective-permute-start(f32[2,8,128]{2,1,0:T(8,128)S(1)} %pad_maximum_fusion.refs_0_), channel_id=1, source_target_pairs={{0,3},{1,2},{2,1},{3,0},{4,7},{5,6},{6,5},{7,4},{8,11},{9,10},{10,... | collective-permute-start | bytes 24584 | tf_op jit(solution)/shard_map/ppermute | solution.py:536
  18.5 4.9 %collective-permute-start.6 = (f32[2,8,128]{2,1,0:T(8,128)S(1)}, f32[2,8,128]{2,1,0:T(8,128)S(1)}, u32[]{:S(2)}, u32[]{:S(2)}) collective-permute-start(f32[2,8,128]{2,1,0:T(8,128)S(1)} %pad_maximum_fusion.refs_0_), channel_id=1, source_target_pairs={{0,2},{1,3},{2,0},{3,1},{4,6},{5,7},{6,4},{7,5},{8,10},{9,11},{10,... | collective-permute-start | bytes 24584 | tf_op jit(solution)/shard_map/ppermute | solution.py:536
  19.1 4.3 %collective-permute-start.5 = (f32[2,8,128]{2,1,0:T(8,128)S(1)}, f32[2,8,128]{2,1,0:T(8,128)S(1)}, u32[]{:S(2)}, u32[]{:S(2)}) collective-permute-start(f32[2,8,128]{2,1,0:T(8,128)S(1)} %pad_maximum_fusion.refs_0_), channel_id=1, source_target_pairs={{0,1},{1,0},{2,3},{3,2},{4,5},{5,4},{6,7},{7,6},{8,9},{9,8},{10,11... | collective-permute-start | bytes 24584 | tf_op jit(solution)/shard_map/ppermute | solution.py:536
  23.5 11.4 %copy-start.8 = (f32[128]{0:T(128)S(1)}, f32[128]{0:T(128)}, u32[]{:S(2)}) copy-start(f32[128]{0:T(128)} %param.20) | copy-start | bytes 1540
  23.5 11.4 %copy-start.9 = (f32[128]{0:T(128)S(1)}, f32[128]{0:T(128)}, u32[]{:S(2)}) copy-start(f32[128]{0:T(128)} %param.21) | copy-start | bytes 1540
  27.2 1.2 %collective-permute-start.8 = (f32[1,8,128]{2,1,0:T(8,128)S(1)}, f32[1,8,128]{2,1,0:T(8,128)S(1)}, u32[]{:S(2)}, u32[]{:S(2)}) collective-permute-start(f32[1,8,128]{2,1,0:T(8,128)S(1)} %bitcast.33), channel_id=1, source_target_pairs={{0,4},{4,0},{1,5},{5,1},{2,6},{6,2},{3,7},{7,3},{8,12},{12,8},{9,1... | collective-permute-start | bytes 12296 | tf_op jit(solution)/shard_map/ppermute | solution.py:536
  28.4 5.4 %collective-permute-start.11 = (f32[2,8,128]{2,1,0:T(8,128)S(1)}, f32[2,8,128]{2,1,0:T(8,128)S(1)}, u32[]{:S(2)}, u32[]{:S(2)}) collective-permute-start(f32[2,8,128]{2,1,0:T(8,128)S(1)} %pad_maximum_fusion.1.refs_0_), channel_id=1, source_target_pairs={{0,3},{1,2},{2,1},{3,0},{4,7},{5,6},{6,5},{7,4},{8,11},{9,10},{10,... | collective-permute-start | bytes 24584 | tf_op jit(solution)/shard_map/ppermute | solution.py:536
  30.3 4.5 %collective-permute-start.10 = (f32[2,8,128]{2,1,0:T(8,128)S(1)}, f32[2,8,128]{2,1,0:T(8,128)S(1)}, u32[]{:S(2)}, u32[]{:S(2)}) collective-permute-start(f32[2,8,128]{2,1,0:T(8,128)S(1)} %pad_maximum_fusion.1.refs_0_), channel_id=1, source_target_pairs={{0,2},{1,3},{2,0},{3,1},{4,6},{5,7},{6,4},{7,5},{8,10},{9,11},{10,... | collective-permute-start | bytes 24584 | tf_op jit(solution)/shard_map/ppermute | solution.py:536
  31.0 3.8 %collective-permute-start.9 = (f32[2,8,128]{2,1,0:T(8,128)S(1)}, f32[2,8,128]{2,1,0:T(8,128)S(1)}, u32[]{:S(2)}, u32[]{:S(2)}) collective-permute-start(f32[2,8,128]{2,1,0:T(8,128)S(1)} %pad_maximum_fusion.1.refs_0_), channel_id=1, source_target_pairs={{0,1},{1,0},{2,3},{3,2},{4,5},{5,4},{6,7},{7,6},{8,9},{9,8},{10,11... | collective-permute-start | bytes 24584 | tf_op jit(solution)/shard_map/ppermute | solution.py:536
  37.3 1.2 %collective-permute-start.12 = (f32[1,8,128]{2,1,0:T(8,128)S(1)}, f32[1,8,128]{2,1,0:T(8,128)S(1)}, u32[]{:S(2)}, u32[]{:S(2)}) collective-permute-start(f32[1,8,128]{2,1,0:T(8,128)S(1)} %bitcast.35), channel_id=1, source_target_pairs={{0,4},{4,0},{1,5},{5,1},{2,6},{6,2},{3,7},{7,3},{8,12},{12,8},{9,1... | collective-permute-start | bytes 12296 | tf_op jit(solution)/shard_map/ppermute | solution.py:536
  38.6 6.2 %collective-permute-start.15 = (f32[2,8,128]{2,1,0:T(8,128)S(1)}, f32[2,8,128]{2,1,0:T(8,128)S(1)}, u32[]{:S(2)}, u32[]{:S(2)}) collective-permute-start(f32[2,8,128]{2,1,0:T(8,128)S(1)} %pad_maximum_fusion.2.after_ref.refs_0_), channel_id=1, source_target_pairs={{0,3},{1,2},{2,1},{3,0},{4,7},{5,6},{6,5},{7,4},{8,11},{9,10},{10,... | collective-permute-start | bytes 24584 | tf_op jit(solution)/shard_map/ppermute | solution.py:536
  40.9 4.5 %collective-permute-start.14 = (f32[2,8,128]{2,1,0:T(8,128)S(1)}, f32[2,8,128]{2,1,0:T(8,128)S(1)}, u32[]{:S(2)}, u32[]{:S(2)}) collective-permute-start(f32[2,8,128]{2,1,0:T(8,128)S(1)} %pad_maximum_fusion.2.after_ref.refs_0_), channel_id=1, source_target_pairs={{0,2},{1,3},{2,0},{3,1},{4,6},{5,7},{6,4},{7,5},{8,10},{9,11},{10,... | collective-permute-start | bytes 24584 | tf_op jit(solution)/shard_map/ppermute | solution.py:536
  41.7 3.8 %collective-permute-start.13 = (f32[2,8,128]{2,1,0:T(8,128)S(1)}, f32[2,8,128]{2,1,0:T(8,128)S(1)}, u32[]{:S(2)}, u32[]{:S(2)}) collective-permute-start(f32[2,8,128]{2,1,0:T(8,128)S(1)} %pad_maximum_fusion.2.after_ref.refs_0_), channel_id=1, source_target_pairs={{0,1},{1,0},{2,3},{3,2},{4,5},{5,4},{6,7},{7,6},{8,9},{9,8},{10,11... | collective-permute-start | bytes 24584 | tf_op jit(solution)/shard_map/ppermute | solution.py:536
  47.8 1.7 %collective-permute-start.16 = (bf16[4,304,128]{2,1,0:T(8,128)(2,1)S(1)}, bf16[4,304,128]{2,1,0:T(8,128)(2,1)S(1)}, u32[]{:S(2)}, u32[]{:S(2)}) collective-permute-start(bf16[4,304,128]{2,1,0:T(8,128)(2,1)S(1)} %get-tuple-element.86), channel_id=1, source_target_pairs={{0,4},{4,0},{1,5},{5,1},{2,6},{6,2},{3,7},{7,3},{8,12},{12,8},{9,1... | collective-permute-start | bytes 933896 | tf_op jit(solution)/shard_map/ppermute | solution.py:536
  49.6 8.2 %collective-permute-start.17 = (bf16[304,128]{1,0:T(8,128)(2,1)S(1)}, bf16[304,128]{1,0:T(8,128)(2,1)S(1)}, u32[]{:S(2)}, u32[]{:S(2)}) collective-permute-start(bf16[304,128]{1,0:T(8,128)(2,1)S(1)} %get-tuple-element.88), channel_id=1, source_target_pairs={{0,24},{8,16},{16,8},{24,0},{1,25},{9,17},{17,9},{25,1},{2,26},{10... | collective-permute-start | bytes 233480 | tf_op jit(solution)/shard_map/ppermute | solution.py:536
  52.1 5.7 %collective-permute-start.18 = (bf16[304,128]{1,0:T(8,128)(2,1)S(1)}, bf16[304,128]{1,0:T(8,128)(2,1)S(1)}, u32[]{:S(2)}, u32[]{:S(2)}) collective-permute-start(bf16[304,128]{1,0:T(8,128)(2,1)S(1)} %get-tuple-element.89), channel_id=1, source_target_pairs={{0,16},{8,24},{16,0},{24,8},{1,17},{9,25},{17,1},{25,9},{2,18},{10... | collective-permute-start | bytes 233480 | tf_op jit(solution)/shard_map/ppermute | solution.py:536
  52.6 5.2 %collective-permute-start.19 = (bf16[304,128]{1,0:T(8,128)(2,1)S(1)}, bf16[304,128]{1,0:T(8,128)(2,1)S(1)}, u32[]{:S(2)}, u32[]{:S(2)}) collective-permute-start(bf16[304,128]{1,0:T(8,128)(2,1)S(1)} %get-tuple-element.90), channel_id=1, source_target_pairs={{0,8},{8,0},{16,24},{24,16},{1,9},{9,1},{17,25},{25,17},{2,10},{10... | collective-permute-start | bytes 233480 | tf_op jit(solution)/shard_map/ppermute | solution.py:536
  53.2 9.1 %collective-permute-start.23 = (bf16[8,64,128]{2,1,0:T(8,128)(2,1)S(1)}, bf16[8,64,128]{2,1,0:T(8,128)(2,1)S(1)}, u32[]{:S(2)}, u32[]{:S(2)}) collective-permute-start(bf16[8,64,128]{2,1,0:T(8,128)(2,1)S(1)} %get-tuple-element.92), channel_id=1, source_target_pairs={{1,2},{2,1},{5,6},{6,5},{9,10},{10,9},{13,14},{14,13},{17,18},{18,... | collective-permute-start | bytes 393224 | tf_op jit(solution)/shard_map/ppermute | solution.py:544
  53.9 8.4 %collective-permute-start.24 = (bf16[8,64,128]{2,1,0:T(8,128)(2,1)S(1)}, bf16[8,64,128]{2,1,0:T(8,128)(2,1)S(1)}, u32[]{:S(2)}, u32[]{:S(2)}) collective-permute-start(bf16[8,64,128]{2,1,0:T(8,128)(2,1)S(1)} %get-tuple-element.93), channel_id=1, source_target_pairs={{0,1},{1,0},{2,3},{3,2},{4,5},{5,4},{6,7},{7,6},{8,9},{9,8},{10,11... | collective-permute-start | bytes 393224 | tf_op jit(solution)/shard_map/ppermute | solution.py:545
  57.8 7.4 %collective-permute-start.22 = (bf16[304,128]{1,0:T(8,128)(2,1)S(1)}, bf16[304,128]{1,0:T(8,128)(2,1)S(1)}, u32[]{:S(2)}, u32[]{:S(2)}) collective-permute-start(bf16[304,128]{1,0:T(8,128)(2,1)S(1)} %add_lead.1.refs_0_), channel_id=1, source_target_pairs={{0,3},{1,2},{2,1},{3,0},{4,7},{5,6},{6,5},{7,4},{8,11},{9,10},{10,... | collective-permute-start | bytes 233480 | tf_op jit(solution)/shard_map/ppermute | solution.py:536
  59.4 7.9 %collective-permute-start.21 = (bf16[304,128]{1,0:T(8,128)(2,1)S(1)}, bf16[304,128]{1,0:T(8,128)(2,1)S(1)}, u32[]{:S(2)}, u32[]{:S(2)}) collective-permute-start(bf16[304,128]{1,0:T(8,128)(2,1)S(1)} %add_lead.1.refs_0_), channel_id=1, source_target_pairs={{0,2},{1,3},{2,0},{3,1},{4,6},{5,7},{6,4},{7,5},{8,10},{9,11},{10,... | collective-permute-start | bytes 233480 | tf_op jit(solution)/shard_map/ppermute | solution.py:536
  59.7 7.6 %collective-permute-start.20 = (bf16[304,128]{1,0:T(8,128)(2,1)S(1)}, bf16[304,128]{1,0:T(8,128)(2,1)S(1)}, u32[]{:S(2)}, u32[]{:S(2)}) collective-permute-start(bf16[304,128]{1,0:T(8,128)(2,1)S(1)} %add_lead.1.refs_0_), channel_id=1, source_target_pairs={{0,1},{1,0},{2,3},{3,2},{4,5},{5,4},{6,7},{7,6},{8,9},{9,8},{10,11... | collective-permute-start | bytes 233480 | tf_op jit(solution)/shard_map/ppermute | solution.py:536
  67.4 6.2 %collective-permute-start.27 = (bf16[304,128]{1,0:T(8,128)(2,1)S(1)}, bf16[304,128]{1,0:T(8,128)(2,1)S(1)}, u32[]{:S(2)}, u32[]{:S(2)}) collective-permute-start(bf16[304,128]{1,0:T(8,128)(2,1)S(1)} %add_lat.1.after_ref.refs_0_), channel_id=1, source_target_pairs={{0,24},{8,16},{16,8},{24,0},{1,25},{9,17},{17,9},{25,1},{2,26},{10... | collective-permute-start | bytes 233480 | tf_op jit(solution)/shard_map/ppermute | solution.py:536
  69.6 4.6 %collective-permute-start.26 = (bf16[304,128]{1,0:T(8,128)(2,1)S(1)}, bf16[304,128]{1,0:T(8,128)(2,1)S(1)}, u32[]{:S(2)}, u32[]{:S(2)}) collective-permute-start(bf16[304,128]{1,0:T(8,128)(2,1)S(1)} %add_lat.1.after_ref.refs_0_), channel_id=1, source_target_pairs={{0,16},{8,24},{16,0},{24,8},{1,17},{9,25},{17,1},{25,9},{2,18},{10... | collective-permute-start | bytes 233480 | tf_op jit(solution)/shard_map/ppermute | solution.py:536
  70.4 4.4 %collective-permute-start.25 = (bf16[304,128]{1,0:T(8,128)(2,1)S(1)}, bf16[304,128]{1,0:T(8,128)(2,1)S(1)}, u32[]{:S(2)}, u32[]{:S(2)}) collective-permute-start(bf16[304,128]{1,0:T(8,128)(2,1)S(1)} %add_lat.1.after_ref.refs_0_), channel_id=1, source_target_pairs={{0,8},{8,0},{16,24},{24,16},{1,9},{9,1},{17,25},{25,17},{2,10},{10... | collective-permute-start | bytes 233480 | tf_op jit(solution)/shard_map/ppermute | solution.py:536
  74.8 1.7 %collective-permute-start.28 = (bf16[1168,128]{1,0:T(8,128)(2,1)S(1)}, bf16[1168,128]{1,0:T(8,128)(2,1)S(1)}, u32[]{:S(2)}, u32[]{:S(2)}) collective-permute-start(bf16[1168,128]{1,0:T(8,128)(2,1)S(1)} %join.1.own_ref), channel_id=1, source_target_pairs={{0,4},{4,0},{1,5},{5,1},{2,6},{6,2},{3,7},{7,3},{8,12},{12,8},{9,1... | collective-permute-start | bytes 897032 | tf_op jit(solution)/shard_map/ppermute | solution.py:536
  (9 other events, 31.5 us)

commit v2 on v1

--- a/solution.py
+++ b/solution.py
@@ -18,10 +18,11 @@
 def fill_toeplitz(taps_ref, out_ref):
     c = taps_ref.shape[-1]
     zero = jnp.zeros((c, c), BF16)
+    half = jnp.asarray(0.5, BF16)
     for b in range(3):
         for i in range(4):
             for j in range(2):
-                block = taps_ref[i - j, b] if 0 <= i - j < 3 else zero
+                block = taps_ref[i - j, b] * half if 0 <= i - j < 3 else zero
                 out_ref[b, i * c : (i + 1) * c, j * c : (j + 1) * c] = block
 
 
@@ -53,14 +54,13 @@
     return piece
 
 
-def silu_and_slope(hidden):
-    gate = 0.5 + 0.5 * jnp.tanh(0.5 * hidden)
-    active = hidden * gate
-    return active, gate + active * (1.0 - gate)
-
-
-def silu(value):
-    return value * (0.5 + 0.5 * jnp.tanh(0.5 * value))
+def silu(half):
+    return half + half * jnp.tanh(half)
+
+
+def silu_slope(half):
+    t = jnp.tanh(half)
+    return (0.5 + 0.5 * t) * (1.0 + half * (1.0 - t))
 
 
 def fold(value):
@@ -99,7 +99,7 @@
         copy.wait()
 
 
-def far_rows_kernel(x_ref, u_ref, mask_ref, hx_ref, hp_ref, m_ref, count_ref, bits_ref):
+def far_rows_kernel(x_ref, u_ref, mask_ref, hx_ref, hp_ref, bits_ref):
     samples, height, across, c = x_ref.shape
     even = lax.axis_index("lat") % 2 == 0
     for k in range(bits_ref.shape[0]):
@@ -117,6 +117,10 @@
             out[2 * samples + s] = u_ref[s, edge]
         for k in range(bits_ref.shape[0]):
             out[3 * samples + k] = bits_ref[k].astype(BF16)
+
+
+def masks_kernel(bits_ref, m_ref, count_ref):
+    samples, height, across, c = m_ref.shape
     count = jnp.zeros((8, c), F32)
     for s in range(samples):
         for r in range(height):
@@ -145,11 +149,11 @@
     return masked
 
 
-def conv1_kernel(gp_ref, gx_ref, x_ref, m_ref, count_ref, w_ref, b_ref, a_ref, s_ref, t_ref, st_ref):
+def conv1_kernel(gp_ref, gx_ref, x_ref, m_ref, count_ref, w_ref, b_ref, a_ref, z_ref, t_ref, st_ref):
     samples, height, across, c = x_ref.shape
     even = lax.axis_index("lat") % 2 == 0
     fill_toeplitz(w_ref, t_ref)
-    bias = b_ref[...]
+    bias = 0.5 * b_ref[...]
     sums = [jnp.zeros((8, c), F32) for _ in range(2)]
     centre = None
     for s in range(samples):
@@ -163,27 +167,37 @@
 
         piece = convolve_rows(row, range(0, height, 2), t_ref, across, False)
         for r in range(height):
-            active, slope = silu_and_slope(piece(r // 2, r % 2) + bias)
+            half = piece(r // 2, r % 2) + bias
+            active = silu(half)
             if centre is None:
                 centre = middle(active)
             active = active - centre
-            mask = m_ref[s, r]
             a_ref[s, r] = active
-            s_ref[s, r] = slope * mask
-            add_moments(sums, active, mask)
+            z_ref[s, r] = half
+            add_moments(sums, active, m_ref[s, r])
     rows = [v.sum(0, keepdims=True) for v in sums]
     st_ref[...] = stats_block([rows[0], rows[1], centre, count_ref[0:1]], c)
 
 
+def prepare_kernel(u_ref, m_ref, w2_ref, mu_ref, su_ref, t2_ref, tt2_ref):
+    samples, height, across, c = u_ref.shape
+    fill_toeplitz(w2_ref, t2_ref)
+    fill_toeplitz_transposed(w2_ref, tt2_ref)
+    total = jnp.zeros((8, c), F32)
+    for s in range(samples):
+        for r in range(height):
+            value = u_ref[s, r].astype(F32) * m_ref[s, r]
+            mu_ref[s, r] = value
+            total += fold(value)
+    su_ref[...] = stats_block([total.sum(0, keepdims=True)], c)
+
+
 def conv1_edge_kernel(
-    hp_ref, hx_ref, gp_ref, gx_ref, x_ref, u_ref, m_ref, st_ref, t_ref, b_ref, w2_ref,
-    a_ref, mh_ref, mu_ref, su_ref, t2_ref, tt2_ref,
+    hp_ref, hx_ref, gp_ref, gx_ref, x_ref, st_ref, t_ref, b_ref, a_ref, mh_ref, muh_ref
 ):
     samples, height, across, c = x_ref.shape
     even = lax.axis_index("lat") % 2 == 0
-    fill_toeplitz(w2_ref, t2_ref)
-    fill_toeplitz_transposed(w2_ref, tt2_ref)
-    bias = b_ref[...]
+    bias = 0.5 * b_ref[...]
     centre = st_ref[2:3]
 
     def row(r):
@@ -205,7 +219,6 @@
     slabs = slice(3 * samples, hx_ref.shape[0])
     above = pick(even, hp_ref[slabs], hx_ref[slabs])
     below = pick(even, hx_ref[slabs], hp_ref[slabs])
-    total = jnp.zeros((8, c), F32)
     for slot, start in ((0, -2), (2, height)):
         piece = convolve_rows(row, (start,), t_ref, across, False)
         for s in range(samples):
@@ -218,21 +231,16 @@
                 mh_ref[s, slot + j] = mask
     for s in range(samples):
         up = pick(even, hp_ref[2 * samples + s], hx_ref[2 * samples + s])
-        mu_ref[s, 0] = up.astype(F32) * mh_ref[s, 1]
-        for r in range(height):
-            value = u_ref[s, r].astype(F32) * m_ref[s, r]
-            mu_ref[s, r + 1] = value
-            total += fold(value)
+        muh_ref[s, 0] = up.astype(F32) * mh_ref[s, 1]
         down = pick(even, hx_ref[2 * samples + s], hp_ref[2 * samples + s])
-        mu_ref[s, height + 1] = down.astype(F32) * mh_ref[s, 2]
-    su_ref[...] = stats_block([total.sum(0, keepdims=True)], c)
+        muh_ref[s, 1] = down.astype(F32) * mh_ref[s, 2]
 
 
 def conv2_kernel(
     pieces,
     own_ref, a_ref, ah_ref, m_ref, mh_ref, mu_ref, su_ref, k_ref, b_ref, g_ref, t_ref, *refs,
 ):
-    stats, (n_ref, a2_ref, s2_ref, c1_ref, st2_ref, ext_ref) = gather(refs[:pieces]), refs[pieces:]
+    stats, (n_ref, a2_ref, z2_ref, c1_ref, st2_ref, ext_ref) = gather(refs[:pieces]), refs[pieces:]
     samples, height, across, c = m_ref.shape
     counts = stats[:, 3:4]
     count = counts.sum(0)
@@ -241,7 +249,7 @@
     scale = inverse * g_ref[...]
     shift = t_ref[...] - offset * scale
     c1_ref[...] = stats_block([offset, inverse, count, mean], c)
-    bias = b_ref[...]
+    bias = 0.5 * b_ref[...]
     sums = [jnp.zeros((8, c), F32) for _ in range(3)]
     centre = None
     for s in range(samples):
@@ -262,22 +270,31 @@
         )
         for i in range(height + 2):
             r = i - 1
-            active, slope = silu_and_slope(piece(i // 2, i % 2) + bias)
+            half = piece(i // 2, i % 2) + bias
+            active = silu(half)
             if centre is None:
                 centre = middle(active)
             active = active - centre
             if 0 <= r < height:
-                mask = m_ref[s, r]
-                add_moments(sums, active, mask)
-                sums[2] += fold(active * mu_ref[s, i])
-            else:
-                mask = mh_ref[s, 1 if r < 0 else 2]
+                add_moments(sums, active, m_ref[s, r])
+                sums[2] += fold(active * mu_ref[s, r])
             a2_ref[s, i] = active
-            s2_ref[s, i] = slope * mask
+            z2_ref[s, i] = half
     rows = [v.sum(0, keepdims=True) for v in sums]
     st2_ref[...] = stats_block(
         [rows[0], rows[1], centre, rows[2], su_ref[0:1], own_ref[3:4]], c
     )
+
+
+def slopes_kernel(z_ref, z2_ref, m_ref, mh_ref, after_ref, s_ref, s2_ref):
+    samples, height = m_ref.shape[:2]
+    for s in range(samples):
+        for r in range(-1, height + 1):
+            mask = mh_ref[s, 1 if r < 0 else 2]
+            if 0 <= r < height:
+                mask = m_ref[s, r]
+                s_ref[s, r] = silu_slope(z_ref[s, r]) * mask
+            s2_ref[s, r + 1] = silu_slope(z2_ref[s, r + 1]) * mask
 
 
 def back_terms(scale, inverse, offset, gain_sum, shift_sum, count):
@@ -288,7 +305,7 @@
 
 def back2_kernel(
     pieces,
-    own_ref, st1_ref, c1_ref, a2_ref, s2_ref, mu_ref, m_ref, a_ref, k_ref, g_ref, t_ref, *refs,
+    own_ref, st1_ref, c1_ref, a2_ref, s2_ref, mu_ref, muh_ref, m_ref, a_ref, k_ref, g_ref, t_ref, *refs,
 ):
     stats, (d_ref, dn_ref, c2_ref, st3_ref, ext_ref) = gather(refs[:pieces]), refs[pieces:]
     samples, height, across, c = m_ref.shape
@@ -305,7 +322,8 @@
     for s in range(samples):
         ext = ext_ref.at[s % 2]
         for i in range(height + 2):
-            grad = mu_ref[s, i] * scale + (a2_ref[s, i] * by_active + constant)
+            upstream = mu_ref[s, i - 1] if 0 < i <= height else muh_ref[s, 0 if i == 0 else 1]
+            grad = upstream * scale + (a2_ref[s, i] * by_active + constant)
             ext[i] = (grad * s2_ref[s, i]).astype(BF16)
             if 0 < i <= height:
                 d_ref[s, i - 1] = ext[i]
@@ -566,28 +584,29 @@
     )
 
 
-def sum_everywhere(send, keep, block_output, input_grad):
+def sum_everywhere(send, keep, edges, block_output, input_grad):
     leads, lats = lax.axis_size("lead"), lax.axis_size("lat")
     chunks = add_chunks([keep, swap(send, "dp", 1)], "add_dp", leads)
     got = [swap(chunks[k], "lead", k) for k in reversed(range(1, leads))]
-    (mine,) = add_chunks([chunks[0]] + got, "add_lead", flops=HIDE)
+    output = block_output(chunks[0])
+    (mine,) = add_chunks([chunks[0]] + got, "add_lead", waits=(output[1],))
     got = [swap(mine, "lat", k) for k in range(1, lats)]
-    grad_input = input_grad(chunks[0])
-    (mine,) = add_chunks([mine] + got, "add_lat", waits=(grad_input[1],))
+    rows = edges(mine)
+    (mine,) = add_chunks([mine] + got, "add_lat", flops=HIDE)
     k = 2
     while k < lax.axis_size("dp"):
         (mine,) = add_chunks([mine, swap(mine, "dp", k)], "add_far_dp")
         k *= 2
     size, c = mine.shape[0] - SMALL, mine.shape[1]
     got = [swap(mine, "lead", k) for k in range(1, leads)]
-    output = block_output(mine)
+    grad_input = input_grad(rows)
     own = call(
         functools.partial(join_kernel, leads),
         jax.ShapeDtypeStruct((leads * size + SMALL, c), BF16),
         [],
         (mine, *got),
         "join",
-        waits=(output[1],),
+        waits=(grad_input[1],),
     )
     one = [jax.ShapeDtypeStruct((leads * size, c), F32)] + [jax.ShapeDtypeStruct((1, c), F32)] * 3
     sums = call(
@@ -639,16 +658,17 @@
     )
     gx, gp = neighbours(*near, "lat")
     packed = array((3 * samples + slabs, across, c), BF16)
-    far_x, far_p, wide_mask, count = call(
+    far_x, far_p, bits = call(
         far_rows_kernel,
-        (packed, packed, shape(height), vector),
-        [pltpu.VMEM((slabs, across, 128), F32)],
+        (packed, packed, array((slabs, across, 128), F32)),
+        [],
         (x, u, mask.reshape(samples * height, across)),
         "far_rows",
         conv_flops,
     )
     hx, hp = neighbours(far_x, far_p, "lat")
-    a1, s1, w1t, own1 = call(
+    wide_mask, count = call(masks_kernel, (shape(height), vector), [], (bits,), "masks", conv_flops)
+    a1, z1, w1t, own1 = call(
         conv1_kernel,
         (shape(height), shape(height), weights, vector),
         [],
@@ -656,16 +676,24 @@
         "conv1",
         16 * conv_flops,
     )
-    a1h, halo_mask, mu, mu_sum, w2t, w2tt = call(
+    mu, mu_sum, w2t, w2tt = call(
+        prepare_kernel,
+        (shape(height), vector, weights, turned),
+        [],
+        (u, wide_mask, conv2_weight),
+        "prepare",
+        conv_flops,
+    )
+    a1h, halo_mask, mu_halo = call(
         conv1_edge_kernel,
-        (shape(4), shape(4), shape(height + 2), vector, weights, turned),
+        (shape(4), shape(4), shape(2)),
         [],
-        (hp, hx, gp, gx, x, u, wide_mask, own1, w1t, b1, conv2_weight),
+        (hp, hx, gp, gx, x, own1, w1t, b1),
         "conv1_edges",
         conv_flops // 2,
     )
     st1 = spread(own1)
-    n1, a2, s2, c1, own2 = call(
+    n1, a2, z2, c1, own2 = call(
         functools.partial(conv2_kernel, len(st1)),
         (shape(height + 2, BF16), shape(height + 2), shape(height + 2), vector, vector),
         [ext(height + 4)],
@@ -674,11 +702,20 @@
         conv_flops,
     )
     st2 = spread(own2)
+    s1, s2 = call(
+        slopes_kernel,
+        (shape(height), shape(height + 2)),
+        [],
+        (z1, z2, wide_mask, halo_mask),
+        "slopes",
+        conv_flops,
+        waits=(st2[0],),
+    )
     d2, dn1, c2, own3 = call(
         functools.partial(back2_kernel, len(st2)),
         (shape(height, BF16), shape(height), vector, vector),
         [ext(height + 2)],
-        (own2, own1, c1, a2, s2, mu, wide_mask, a1, w2tt, g2, t2, *st2),
+        (own2, own1, c1, a2, s2, mu, mu_halo, wide_mask, a1, w2tt, g2, t2, *st2),
         "conv2_back",
         conv_flops,
     )
@@ -702,14 +739,16 @@
         conv_flops,
     )
 
-    def input_grad(after):
+    def edges(after):
         rows = call(edge_rows_kernel, (edge, edge), [], (d1,), "edge_rows", waits=(after,))
-        rows = neighbours(*rows, "lat")
+        return neighbours(*rows, "lat")[::-1]
+
+    def input_grad(rows):
         return call(
             input_grad_kernel,
             (shape(height, BF16), vector),
             [pltpu.VMEM(turned.shape, BF16)],
-            (rows[1], rows[0], d1, u, conv1_weight),
+            (*rows, d1, u, conv1_weight),
             "conv1_back",
             conv_flops,
         )
@@ -725,7 +764,9 @@
             waits=(after,),
         )
 
-    first, second, output, grad_input = sum_everywhere(send, keep, block_output, input_grad)
+    first, second, output, grad_input = sum_everywhere(
+        send, keep, edges, block_output, input_grad
+    )
     sums = []
     for part in (first, second):
         sums += [part[0].reshape(3, 3, c, c)] + [v.reshape(c) for v in part[1:]]

time: 77.8 us -> 76.3 us (0.981)
  waiting for transfers between devices: 15.2 us -> 14.1 us
  starting transfers between devices: 38.8 us -> 37.8 us
    ppermute x23, waiting for transfers between devices: 14.7 us -> 13.6 us  [swap(): lax.ppermute(value, axis, [(i, i ^ k) for i in range(lax.axis_size(axis))])]
    ppermute x3, starting transfers between devices: 11.6 us -> 10.6 us  [neighbours(): return (lax.ppermute(value_x, axis, first), got_p)]
    pallas_call x16 -> x19, Pallas kernels: 21.4 us -> 21.9 us  [call(): pl.pallas_call(kernel, out_shape=outs, in_specs=[spaces[0]] * len(operand...]
  transfers between devices with their start and end apart: 29 -> 29, of which waited for: 14 -> 17; matrix products, arithmetic and copies ran while one was open for 0% -> 0% of each run, Pallas kernels for 15% -> 17%
where the time goes in v2:
time: 76.3 us; the launch traced here: 76 us
  starting transfers between devices  37.8 us (50%)
  Pallas kernels  21.9 us (29%)
  waiting for transfers between devices  14.1 us (18%)
  local copies, waits for them, and re-layouts  1.42 us (2%)
  between operations  0.88 us (1%)
    ppermute x23, starting transfers between devices, swap(): lax.ppermute(value, axis, [(i, i ^ k) for i in range(lax.axis_size(axis))])  25.1 us
    pallas_call x19, Pallas kernels, call(): pl.pallas_call(kernel, out_shape=outs, in_specs=[spaces[0]] * len(operand...  21.9 us
    ppermute x23, waiting for transfers between devices, swap(): lax.ppermute(value, axis, [(i, i ^ k) for i in range(lax.axis_size(axis))])  13.6 us
    ppermute x3, starting transfers between devices, neighbours(): return (lax.ppermute(value_x, axis, first), got_p)  10.6 us
    ppermute x3, starting transfers between devices, neighbours(): got_p = lax.ppermute(value_p, axis, second)  2.16 us
  transfers between devices with their start and end apart: 29, of which 17 were waited for; matrix products, arithmetic and copies ran while one was open for 0% of the time, Pallas kernels for 17%

profile of v2, /device:TPU:0, one launch (start us, length us, event | category | flops | bytes accessed | tf_op | source)
XLA Modules:
  0.0 76.0 jit_solution(7700949050212870486)
XLA Ops:
  0.7 1.2 %copy-done = bf16[1,8,8,64,128]{4,3,2,1,0:T(8,128)(2,1)S(1)} copy-done((bf16[1,8,8,64,128]{4,3,2,1,0:T(8,128)(2,1)S(1)}, bf16[1,8,8,64,128]{4,3,2,1,0:T(8,128)(2,1)}, u32[]{:S(2)}) %copy-start) | copy-done | bytes 1048600
  2.8 5.9 %collective-permute-start.1 = (bf16[8,1,64,128]{3,2,1,0:T(8,128)(2,1)S(1)}, bf16[8,1,64,128]{3,2,1,0:T(8,128)(2,1)S(1)}, u32[]{:S(2)}, u32[]{:S(2)}) collective-permute-start(bf16[8,1,64,128]{3,2,1,0:T(8,128)(2,1)S(1)} %get-tuple-element.63), channel_id=1, source_target_pairs={{0,1},{1,0},{2,3},{3,2},{4,5},{5,4},{6,7},{7,6},{8,9},{9,8},{10,11... | collective-permute-start | bytes 393224 | tf_op jit(solution)/shard_map/ppermute | solution.py:563
  9.4 1.8 %collective-permute-start.3 = (bf16[25,64,128]{2,1,0:T(8,128)(2,1)S(1)}, bf16[25,64,128]{2,1,0:T(8,128)(2,1)S(1)}, u32[]{:S(2)}, u32[]{:S(2)}) collective-permute-start(bf16[25,64,128]{2,1,0:T(8,128)(2,1)S(1)} %get-tuple-element.70), channel_id=1, source_target_pairs={{0,1},{1,0},{2,3},{3,2},{4,5},{5,4},{6,7},{7,6},{8,9},{9,8},{10,11... | collective-permute-start | bytes 1228808 | tf_op jit(solution)/shard_map/ppermute | solution.py:563
  12.5 2.4 %conv1.1 = (f32[8,8,64,128]{3,2,1,0:T(8,128)S(1)}, f32[8,8,64,128]{3,2,1,0:T(8,128)S(1)}, bf16[3,512,256]{2,1,0:T(8,128)(2,1)S(1)}, f32[8,128]{1,0:T(8,128)S(1)}) custom-call(bf16[8,1,64,128]{3,2,1,0:T(8,128)(2,1)S(1)} %collective-permute-done.gp_ref, bf16[8,1,64,128]{3,2,1,0:T(8,128)(2,1)S(1)} %collective-permute-done.1.gx_ref, ...), custom_call_target="tpu_custom_call" | custom-call | flops 19327352832 | bytes 3707392 | tf_op jit(solution)/shard_map/conv1/pallas_call | solution.py:541
  16.2 2.5 %collective-permute-start.7 = (f32[2,8,128]{2,1,0:T(8,128)S(1)}, f32[2,8,128]{2,1,0:T(8,128)S(1)}, u32[]{:S(2)}, u32[]{:S(2)}) collective-permute-start(f32[2,8,128]{2,1,0:T(8,128)S(1)} %pad_maximum_fusion.refs_0_), channel_id=1, source_target_pairs={{0,3},{1,2},{2,1},{3,0},{4,7},{5,6},{6,5},{7,4},{8,11},{9,10},{10,... | collective-permute-start | bytes 24584 | tf_op jit(solution)/shard_map/ppermute | solution.py:554
  19.4 1.2 %collective-permute-start.5 = (f32[2,8,128]{2,1,0:T(8,128)S(1)}, f32[2,8,128]{2,1,0:T(8,128)S(1)}, u32[]{:S(2)}, u32[]{:S(2)}) collective-permute-start(f32[2,8,128]{2,1,0:T(8,128)S(1)} %pad_maximum_fusion.refs_0_), channel_id=1, source_target_pairs={{0,1},{1,0},{2,3},{3,2},{4,5},{5,4},{6,7},{7,6},{8,9},{9,8},{10,11... | collective-permute-start | bytes 24584 | tf_op jit(solution)/shard_map/ppermute | solution.py:554
  20.7 1.1 %conv1_edges.1 = (f32[8,4,64,128]{3,2,1,0:T(8,128)S(1)}, f32[8,4,64,128]{3,2,1,0:T(8,128)S(1)}, f32[8,2,64,128]{3,2,1,0:T(8,128)S(1)}) custom-call(bf16[25,64,128]{2,1,0:T(8,128)(2,1)S(1)} %collective-permute-done.2.hp_ref, bf16[25,64,128]{2,1,0:T(8,128)(2,1)S(1)} %collective-permute-done.3.hx_ref, bf16[8,1,64,128]{3,2,1,0:T(8,128)(2,1)S(1)} %collective-permute-done.gp_ref, ...), custom_call_target="tpu_custom_call" | custom-call | flops 603979776 | bytes 2920960 | tf_op jit(solution)/shard_map/conv1_edges/pallas_call | solution.py:541
  23.2 3.2 %conv2.1 = (bf16[8,10,64,128]{3,2,1,0:T(8,128)(2,1)S(1)}, f32[8,10,64,128]{3,2,1,0:T(8,128)S(1)}, f32[8,10,64,128]{3,2,1,0:T(8,128)S(1)}, f32[8,128]{1,0:T(8,128)S(1)}, f32[8,128]{1,0:T(8,128)S(1)}) custom-call(f32[8,128]{1,0:T(8,128)S(1)} %get-tuple-element.67.st_ref.own_ref.st1_ref, f32[8,8,64,128]{3,2,1,0:T(8,128)S(1)} %get-tuple-element.68.a_ref, ...), custom_call_target="tpu_custom_call" | custom-call | flops 1207959552 | bytes 9217536 | tf_op jit(solution)/shard_map/conv2/pallas_call | solution.py:541
  26.5 1.2 %collective-permute-done.8 = f32[1,8,128]{2,1,0:T(8,128)S(1)} collective-permute-done((f32[1,8,128]{2,1,0:T(8,128)S(1)}, f32[1,8,128]{2,1,0:T(8,128)S(1)}, u32[]{:S(2)}, u32[]{:S(2)}) %collective-permute-start.8) | collective-permute-done | bytes 4128 | tf_op jit(solution)/shard_map/ppermute | solution.py:554
  27.7 1.5 %collective-permute-start.11 = (f32[2,8,128]{2,1,0:T(8,128)S(1)}, f32[2,8,128]{2,1,0:T(8,128)S(1)}, u32[]{:S(2)}, u32[]{:S(2)}) collective-permute-start(f32[2,8,128]{2,1,0:T(8,128)S(1)} %pad_maximum_fusion.1.after_ref.refs_0_), channel_id=1, source_target_pairs={{0,3},{1,2},{2,1},{3,0},{4,7},{5,6},{6,5},{7,4},{8,11},{9,10},{10,... | collective-permute-start | bytes 24584 | tf_op jit(solution)/shard_map/ppermute | solution.py:554
  29.1 1.0 %collective-permute-start.10 = (f32[2,8,128]{2,1,0:T(8,128)S(1)}, f32[2,8,128]{2,1,0:T(8,128)S(1)}, u32[]{:S(2)}, u32[]{:S(2)}) collective-permute-start(f32[2,8,128]{2,1,0:T(8,128)S(1)} %pad_maximum_fusion.1.after_ref.refs_0_), channel_id=1, source_target_pairs={{0,2},{1,3},{2,0},{3,1},{4,6},{5,7},{6,4},{7,5},{8,10},{9,11},{10,... | collective-permute-start | bytes 24584 | tf_op jit(solution)/shard_map/ppermute | solution.py:554
  30.1 1.9 %collective-permute-start.9 = (f32[2,8,128]{2,1,0:T(8,128)S(1)}, f32[2,8,128]{2,1,0:T(8,128)S(1)}, u32[]{:S(2)}, u32[]{:S(2)}) collective-permute-start(f32[2,8,128]{2,1,0:T(8,128)S(1)} %pad_maximum_fusion.1.after_ref.refs_0_), channel_id=1, source_target_pairs={{0,1},{1,0},{2,3},{3,2},{4,5},{5,4},{6,7},{7,6},{8,9},{9,8},{10,11... | collective-permute-start | bytes 24584 | tf_op jit(solution)/shard_map/ppermute | solution.py:554
  32.1 1.6 %slopes.1 = (f32[8,8,64,128]{3,2,1,0:T(8,128)S(1)}, f32[8,10,64,128]{3,2,1,0:T(8,128)S(1)}) custom-call(f32[8,8,64,128]{3,2,1,0:T(8,128)S(1)} %get-tuple-element.80.z_ref, f32[8,10,64,128]{3,2,1,0:T(8,128)S(1)} %get-tuple-element.81.z2_ref, f32[8,8,64,128]{3,2,1,0:T(8,128)S(1)} %get-tuple-element.65.m_ref, f32[8,4,64,128]{3,2,1,0:T(8,128)S(1)} %get-tuple-element.73.mh_ref, ...), custom_call_target="tpu_custom_call" | custom-call | flops 1207959552 | bytes 7864320 | tf_op jit(solution)/shard_map/slopes/pallas_call | solution.py:541
  33.8 2.5 %conv2_back.1 = (bf16[8,8,64,128]{3,2,1,0:T(8,128)(2,1)S(1)}, f32[8,8,64,128]{3,2,1,0:T(8,128)S(1)}, f32[8,128]{1,0:T(8,128)S(1)}, f32[8,128]{1,0:T(8,128)S(1)}) custom-call(f32[8,128]{1,0:T(8,128)S(1)} %get-tuple-element.78.own_ref, f32[8,128]{1,0:T(8,128)S(1)} %get-tuple-element.67.st_ref.own_ref.st1_ref, f32[8,128]{1,0:T(8,128)S(1)} %get-tuple-element.79.c1_ref, ...), custom_call_target="tpu_custom_call" | custom-call | flops 1207959552 | bytes 12891136 | tf_op jit(solution)/shard_map/conv2_back/pallas_call | solution.py:541
  36.3 1.2 %collective-permute-done.12 = f32[1,8,128]{2,1,0:T(8,128)S(1)} collective-permute-done((f32[1,8,128]{2,1,0:T(8,128)S(1)}, f32[1,8,128]{2,1,0:T(8,128)S(1)}, u32[]{:S(2)}, u32[]{:S(2)}) %collective-permute-start.12) | collective-permute-done | bytes 4128 | tf_op jit(solution)/shard_map/ppermute | solution.py:554
  37.5 2.5 %collective-permute-start.15 = (f32[2,8,128]{2,1,0:T(8,128)S(1)}, f32[2,8,128]{2,1,0:T(8,128)S(1)}, u32[]{:S(2)}, u32[]{:S(2)}) collective-permute-start(f32[2,8,128]{2,1,0:T(8,128)S(1)} %pad_maximum_fusion.2.after_ref.refs_0_), channel_id=1, source_target_pairs={{0,3},{1,2},{2,1},{3,0},{4,7},{5,6},{6,5},{7,4},{8,11},{9,10},{10,... | collective-permute-start | bytes 24584 | tf_op jit(solution)/shard_map/ppermute | solution.py:554
  40.9 1.0 %collective-permute-start.13 = (f32[2,8,128]{2,1,0:T(8,128)S(1)}, f32[2,8,128]{2,1,0:T(8,128)S(1)}, u32[]{:S(2)}, u32[]{:S(2)}) collective-permute-start(f32[2,8,128]{2,1,0:T(8,128)S(1)} %pad_maximum_fusion.2.after_ref.refs_0_), channel_id=1, source_target_pairs={{0,1},{1,0},{2,3},{3,2},{4,5},{5,4},{6,7},{7,6},{8,9},{9,8},{10,11... | collective-permute-start | bytes 24584 | tf_op jit(solution)/shard_map/ppermute | solution.py:554
  41.9 2.0 %conv2_weight_grad.1 = (bf16[1152,128]{1,0:T(8,128)(2,1)S(1)}, f32[8,128]{1,0:T(8,128)S(1)}) custom-call(bf16[8,10,64,128]{3,2,1,0:T(8,128)(2,1)S(1)} %get-tuple-element.88.n_ref, bf16[8,8,64,128]{3,2,1,0:T(8,128)(2,1)S(1)} %get-tuple-element.89.d_ref, f32[2,8,128]{2,1,0:T(8,128)S(1)} %pad_maximum_fusion.2.after_ref.refs_0_), custom_call_target="tpu_custom_call" | custom-call | flops 1207959552 | bytes 2359296 | tf_op jit(solution)/shard_map/conv2_weight_grad/pallas_call | solution.py:541
  44.6 2.1 %conv1_weight_grad.1 = (bf16[8,8,64,128]{3,2,1,0:T(8,128)(2,1)S(1)}, bf16[4,304,128]{2,1,0:T(8,128)(2,1)S(1)}, bf16[4,304,128]{2,1,0:T(8,128)(2,1)S(1)}) custom-call(f32[8,128]{1,0:T(8,128)S(1)} %get-tuple-element.79.c1_ref, f32[8,128]{1,0:T(8,128)S(1)} %get-tuple-element.85.c2_ref, f32[8,8,64,128]{3,2,1,0:T(8,128)S(1)} %get-tuple-element.86.dn_ref, ...), custom_call_target="tpu_custom_call" | custom-call | flops 1207959552 | bytes 7942656 | tf_op jit(solution)/shard_map/conv1_weight_grad/pallas_call | solution.py:541
  46.8 1.6 %collective-permute-done.16.refs_1_ = bf16[4,304,128]{2,1,0:T(8,128)(2,1)S(1)} collective-permute-done((bf16[4,304,128]{2,1,0:T(8,128)(2,1)S(1)}, bf16[4,304,128]{2,1,0:T(8,128)(2,1)S(1)}, u32[]{:S(2)}, u32[]{:S(2)}) %collective-permute-start.16) | collective-permute-done | bytes 311328 | tf_op jit(solution)/shard_map/ppermute | solution.py:554
  48.5 2.5 %collective-permute-start.17 = (bf16[304,128]{1,0:T(8,128)(2,1)S(1)}, bf16[304,128]{1,0:T(8,128)(2,1)S(1)}, u32[]{:S(2)}, u32[]{:S(2)}) collective-permute-start(bf16[304,128]{1,0:T(8,128)(2,1)S(1)} %get-tuple-element.98), channel_id=1, source_target_pairs={{0,24},{8,16},{16,8},{24,0},{1,25},{9,17},{17,9},{25,1},{2,26},{10... | collective-permute-start | bytes 233480 | tf_op jit(solution)/shard_map/ppermute | solution.py:554
  52.1 1.3 %output.1 = (bf16[8,8,64,128]{3,2,1,0:T(8,128)(2,1)}, f32[8,128]{1,0:T(8,128)S(1)}) custom-call(bf16[8,8,64,128]{3,2,1,0:T(8,128)(2,1)S(1)} %bitcast.27, f32[8,10,64,128]{3,2,1,0:T(8,128)S(1)} %get-tuple-element.77.a2_ref, f32[8,8,64,128]{3,2,1,0:T(8,128)S(1)} %get-tuple-element.65.m_ref, f32[8,128]{1,0:T(8,128)S(1)} %get-tuple-element.85.c2_ref, ...), custom_call_target="tpu_custom_call" | custom-call | flops 603979776 | bytes 5771264 | tf_op jit(solution)/shard_map/output/pallas_call | solution.py:541
  53.9 1.6 %collective-permute-done.18.refs_2_ = bf16[304,128]{1,0:T(8,128)(2,1)S(1)} collective-permute-done((bf16[304,128]{1,0:T(8,128)(2,1)S(1)}, bf16[304,128]{1,0:T(8,128)(2,1)S(1)}, u32[]{:S(2)}, u32[]{:S(2)}) %collective-permute-start.18) | collective-permute-done | bytes 77856 | tf_op jit(solution)/shard_map/ppermute | solution.py:554
  56.0 1.9 %collective-permute-start.24 = (bf16[304,128]{1,0:T(8,128)(2,1)S(1)}, bf16[304,128]{1,0:T(8,128)(2,1)S(1)}, u32[]{:S(2)}, u32[]{:S(2)}) collective-permute-start(bf16[304,128]{1,0:T(8,128)(2,1)S(1)} %add_lead.1.after_ref.refs_0_), channel_id=1, source_target_pairs={{0,3},{1,2},{2,1},{3,0},{4,7},{5,6},{6,5},{7,4},{8,11},{9,10},{10,... | collective-permute-start | bytes 233480 | tf_op jit(solution)/shard_map/ppermute | solution.py:554
  58.4 2.0 %collective-permute-start.22 = (bf16[304,128]{1,0:T(8,128)(2,1)S(1)}, bf16[304,128]{1,0:T(8,128)(2,1)S(1)}, u32[]{:S(2)}, u32[]{:S(2)}) collective-permute-start(bf16[304,128]{1,0:T(8,128)(2,1)S(1)} %add_lead.1.after_ref.refs_0_), channel_id=1, source_target_pairs={{0,1},{1,0},{2,3},{3,2},{4,5},{5,4},{6,7},{7,6},{8,9},{9,8},{10,11... | collective-permute-start | bytes 233480 | tf_op jit(solution)/shard_map/ppermute | solution.py:554
  61.2 2.9 %collective-permute-start.21 = (bf16[8,64,128]{2,1,0:T(8,128)(2,1)S(1)}, bf16[8,64,128]{2,1,0:T(8,128)(2,1)S(1)}, u32[]{:S(2)}, u32[]{:S(2)}) collective-permute-start(bf16[8,64,128]{2,1,0:T(8,128)(2,1)S(1)} %get-tuple-element.103), channel_id=1, source_target_pairs={{0,1},{1,0},{2,3},{3,2},{4,5},{5,4},{6,7},{7,6},{8,9},{9,8},{10,11... | collective-permute-start | bytes 393224 | tf_op jit(solution)/shard_map/ppermute | solution.py:563
  64.1 2.0 %collective-permute-done.23.refs_2_ = bf16[304,128]{1,0:T(8,128)(2,1)S(1)} collective-permute-done((bf16[304,128]{1,0:T(8,128)(2,1)S(1)}, bf16[304,128]{1,0:T(8,128)(2,1)S(1)}, u32[]{:S(2)}, u32[]{:S(2)}) %collective-permute-start.23) | collective-permute-done | bytes 77856 | tf_op jit(solution)/shard_map/ppermute | solution.py:554
  66.2 1.4 %collective-permute-start.27 = (bf16[304,128]{1,0:T(8,128)(2,1)S(1)}, bf16[304,128]{1,0:T(8,128)(2,1)S(1)}, u32[]{:S(2)}, u32[]{:S(2)}) collective-permute-start(bf16[304,128]{1,0:T(8,128)(2,1)S(1)} %add_lat.1.refs_0_), channel_id=1, source_target_pairs={{0,24},{8,16},{16,8},{24,0},{1,25},{9,17},{17,9},{25,1},{2,26},{10... | collective-permute-start | bytes 233480 | tf_op jit(solution)/shard_map/ppermute | solution.py:554
  67.6 1.2 %collective-permute-start.26 = (bf16[304,128]{1,0:T(8,128)(2,1)S(1)}, bf16[304,128]{1,0:T(8,128)(2,1)S(1)}, u32[]{:S(2)}, u32[]{:S(2)}) collective-permute-start(bf16[304,128]{1,0:T(8,128)(2,1)S(1)} %add_lat.1.refs_0_), channel_id=1, source_target_pairs={{0,16},{8,24},{16,0},{24,8},{1,17},{9,25},{17,1},{25,9},{2,18},{10... | collective-permute-start | bytes 233480 | tf_op jit(solution)/shard_map/ppermute | solution.py:554
  69.7 2.9 %conv1_back.1 = (bf16[8,8,64,128]{3,2,1,0:T(8,128)(2,1)}, f32[8,128]{1,0:T(8,128)S(1)}) custom-call(bf16[8,64,128]{2,1,0:T(8,128)(2,1)S(1)} %collective-permute-done.20.ep_ref, bf16[8,64,128]{2,1,0:T(8,128)(2,1)S(1)} %collective-permute-done.21.ex_ref, bf16[8,8,64,128]{3,2,1,0:T(8,128)(2,1)S(1)} %get-tuple-element.97.d_ref, ...), custom_call_target="tpu_custom_call" | custom-call | flops 1207959552 | bytes 2654208 | tf_op jit(solution)/shard_map/conv1_back/pallas_call | solution.py:541
  73.3 1.6 %collective-permute-done.28.other_ref = bf16[1168,128]{1,0:T(8,128)(2,1)S(1)} collective-permute-done((bf16[1168,128]{1,0:T(8,128)(2,1)S(1)}, bf16[1168,128]{1,0:T(8,128)(2,1)S(1)}, u32[]{:S(2)}, u32[]{:S(2)}) %collective-permute-start.28) | collective-permute-done | bytes 299040 | tf_op jit(solution)/shard_map/ppermute | solution.py:554
  74.9 1.1 %finish.1 = (f32[1152,128]{1,0:T(8,128)}, f32[1,128]{1,0:T(1,128)}, f32[1,128]{1,0:T(1,128)}, f32[1,128]{1,0:T(1,128)}, f32[1152,128]{1,0:T(8,128)}, /*index=5*/...) custom-call(bf16[1168,128]{1,0:T(8,128)(2,1)S(1)} %join.1.own_ref, bf16[1168,128]{1,0:T(8,128)(2,1)S(1)} %collective-permute-done.28.other_ref), custom_call_target="tpu_custom_call" | custom-call | bytes 598016 | tf_op jit(solution)/shard_map/finish/pallas_call | solution.py:541
  (72 shorter events, 13.3 us)
Async XLA Ops:
  1.9 10.0 %collective-permute-start = (bf16[8,1,64,128]{3,2,1,0:T(8,128)(2,1)S(1)}, bf16[8,1,64,128]{3,2,1,0:T(8,128)(2,1)S(1)}, u32[]{:S(2)}, u32[]{:S(2)}) collective-permute-start(bf16[8,1,64,128]{3,2,1,0:T(8,128)(2,1)S(1)} %get-tuple-element.62), channel_id=1, source_target_pairs={{1,2},{2,1},{5,6},{6,5},{9,10},{10,9},{13,14},{14,13},{17,18},{18,... | collective-permute-start | bytes 393224 | tf_op jit(solution)/shard_map/ppermute | solution.py:562
  2.8 9.6 %collective-permute-start.1 = (bf16[8,1,64,128]{3,2,1,0:T(8,128)(2,1)S(1)}, bf16[8,1,64,128]{3,2,1,0:T(8,128)(2,1)S(1)}, u32[]{:S(2)}, u32[]{:S(2)}) collective-permute-start(bf16[8,1,64,128]{3,2,1,0:T(8,128)(2,1)S(1)} %get-tuple-element.63), channel_id=1, source_target_pairs={{0,1},{1,0},{2,3},{3,2},{4,5},{5,4},{6,7},{7,6},{8,9},{9,8},{10,11... | collective-permute-start | bytes 393224 | tf_op jit(solution)/shard_map/ppermute | solution.py:563
  8.8 11.8 %collective-permute-start.2 = (bf16[25,64,128]{2,1,0:T(8,128)(2,1)S(1)}, bf16[25,64,128]{2,1,0:T(8,128)(2,1)S(1)}, u32[]{:S(2)}, u32[]{:S(2)}) collective-permute-start(bf16[25,64,128]{2,1,0:T(8,128)(2,1)S(1)} %get-tuple-element.69), channel_id=1, source_target_pairs={{1,2},{2,1},{5,6},{6,5},{9,10},{10,9},{13,14},{14,13},{17,18},{18,... | collective-permute-start | bytes 1228808 | tf_op jit(solution)/shard_map/ppermute | solution.py:562
  9.4 11.2 %collective-permute-start.3 = (bf16[25,64,128]{2,1,0:T(8,128)(2,1)S(1)}, bf16[25,64,128]{2,1,0:T(8,128)(2,1)S(1)}, u32[]{:S(2)}, u32[]{:S(2)}) collective-permute-start(bf16[25,64,128]{2,1,0:T(8,128)(2,1)S(1)} %get-tuple-element.70), channel_id=1, source_target_pairs={{0,1},{1,0},{2,3},{3,2},{4,5},{5,4},{6,7},{7,6},{8,9},{9,8},{10,11... | collective-permute-start | bytes 1228808 | tf_op jit(solution)/shard_map/ppermute | solution.py:563
  14.9 1.2 %collective-permute-start.4 = (f32[1,8,128]{2,1,0:T(8,128)S(1)}, f32[1,8,128]{2,1,0:T(8,128)S(1)}, u32[]{:S(2)}, u32[]{:S(2)}) collective-permute-start(f32[1,8,128]{2,1,0:T(8,128)S(1)} %bitcast.28), channel_id=1, source_target_pairs={{0,4},{4,0},{1,5},{5,1},{2,6},{6,2},{3,7},{7,3},{8,12},{12,8},{9,1... | collective-permute-start | bytes 12296 | tf_op jit(solution)/shard_map/ppermute | solution.py:554
  15.5 7.8 %copy-start.2 = (f32[128]{0:T(128)S(1)}, f32[128]{0:T(128)}, u32[]{:S(2)}) copy-start(f32[128]{0:T(128)} %param.16) | copy-start | bytes 1540
  15.5 7.7 %copy-start.4 = (f32[128]{0:T(128)S(1)}, f32[128]{0:T(128)}, u32[]{:S(2)}) copy-start(f32[128]{0:T(128)} %param.19) | copy-start | bytes 1540
  15.5 7.7 %copy-start.5 = (f32[128]{0:T(128)S(1)}, f32[128]{0:T(128)}, u32[]{:S(2)}) copy-start(f32[128]{0:T(128)} %param.17) | copy-start | bytes 1540
  16.2 6.4 %collective-permute-start.7 = (f32[2,8,128]{2,1,0:T(8,128)S(1)}, f32[2,8,128]{2,1,0:T(8,128)S(1)}, u32[]{:S(2)}, u32[]{:S(2)}) collective-permute-start(f32[2,8,128]{2,1,0:T(8,128)S(1)} %pad_maximum_fusion.refs_0_), channel_id=1, source_target_pairs={{0,3},{1,2},{2,1},{3,0},{4,7},{5,6},{6,5},{7,4},{8,11},{9,10},{10,... | collective-permute-start | bytes 24584 | tf_op jit(solution)/shard_map/ppermute | solution.py:554
  18.7 4.5 %collective-permute-start.6 = (f32[2,8,128]{2,1,0:T(8,128)S(1)}, f32[2,8,128]{2,1,0:T(8,128)S(1)}, u32[]{:S(2)}, u32[]{:S(2)}) collective-permute-start(f32[2,8,128]{2,1,0:T(8,128)S(1)} %pad_maximum_fusion.refs_0_), channel_id=1, source_target_pairs={{0,2},{1,3},{2,0},{3,1},{4,6},{5,7},{6,4},{7,5},{8,10},{9,11},{10,... | collective-permute-start | bytes 24584 | tf_op jit(solution)/shard_map/ppermute | solution.py:554
  19.4 3.9 %collective-permute-start.5 = (f32[2,8,128]{2,1,0:T(8,128)S(1)}, f32[2,8,128]{2,1,0:T(8,128)S(1)}, u32[]{:S(2)}, u32[]{:S(2)}) collective-permute-start(f32[2,8,128]{2,1,0:T(8,128)S(1)} %pad_maximum_fusion.refs_0_), channel_id=1, source_target_pairs={{0,1},{1,0},{2,3},{3,2},{4,5},{5,4},{6,7},{7,6},{8,9},{9,8},{10,11... | collective-permute-start | bytes 24584 | tf_op jit(solution)/shard_map/ppermute | solution.py:554
  26.4 1.2 %collective-permute-start.8 = (f32[1,8,128]{2,1,0:T(8,128)S(1)}, f32[1,8,128]{2,1,0:T(8,128)S(1)}, u32[]{:S(2)}, u32[]{:S(2)}) collective-permute-start(f32[1,8,128]{2,1,0:T(8,128)S(1)} %bitcast.30), channel_id=1, source_target_pairs={{0,4},{4,0},{1,5},{5,1},{2,6},{6,2},{3,7},{7,3},{8,12},{12,8},{9,1... | collective-permute-start | bytes 12296 | tf_op jit(solution)/shard_map/ppermute | solution.py:554
  27.7 6.0 %collective-permute-start.11 = (f32[2,8,128]{2,1,0:T(8,128)S(1)}, f32[2,8,128]{2,1,0:T(8,128)S(1)}, u32[]{:S(2)}, u32[]{:S(2)}) collective-permute-start(f32[2,8,128]{2,1,0:T(8,128)S(1)} %pad_maximum_fusion.1.after_ref.refs_0_), channel_id=1, source_target_pairs={{0,3},{1,2},{2,1},{3,0},{4,7},{5,6},{6,5},{7,4},{8,11},{9,10},{10,... | collective-permute-start | bytes 24584 | tf_op jit(solution)/shard_map/ppermute | solution.py:554
  29.1 4.5 %collective-permute-start.10 = (f32[2,8,128]{2,1,0:T(8,128)S(1)}, f32[2,8,128]{2,1,0:T(8,128)S(1)}, u32[]{:S(2)}, u32[]{:S(2)}) collective-permute-start(f32[2,8,128]{2,1,0:T(8,128)S(1)} %pad_maximum_fusion.1.after_ref.refs_0_), channel_id=1, source_target_pairs={{0,2},{1,3},{2,0},{3,1},{4,6},{5,7},{6,4},{7,5},{8,10},{9,11},{10,... | collective-permute-start | bytes 24584 | tf_op jit(solution)/shard_map/ppermute | solution.py:554
  30.1 3.7 %collective-permute-start.9 = (f32[2,8,128]{2,1,0:T(8,128)S(1)}, f32[2,8,128]{2,1,0:T(8,128)S(1)}, u32[]{:S(2)}, u32[]{:S(2)}) collective-permute-start(f32[2,8,128]{2,1,0:T(8,128)S(1)} %pad_maximum_fusion.1.after_ref.refs_0_), channel_id=1, source_target_pairs={{0,1},{1,0},{2,3},{3,2},{4,5},{5,4},{6,7},{7,6},{8,9},{9,8},{10,11... | collective-permute-start | bytes 24584 | tf_op jit(solution)/shard_map/ppermute | solution.py:554
  36.2 1.2 %collective-permute-start.12 = (f32[1,8,128]{2,1,0:T(8,128)S(1)}, f32[1,8,128]{2,1,0:T(8,128)S(1)}, u32[]{:S(2)}, u32[]{:S(2)}) collective-permute-start(f32[1,8,128]{2,1,0:T(8,128)S(1)} %bitcast.32), channel_id=1, source_target_pairs={{0,4},{4,0},{1,5},{5,1},{2,6},{6,2},{3,7},{7,3},{8,12},{12,8},{9,1... | collective-permute-start | bytes 12296 | tf_op jit(solution)/shard_map/ppermute | solution.py:554
  37.5 6.4 %collective-permute-start.15 = (f32[2,8,128]{2,1,0:T(8,128)S(1)}, f32[2,8,128]{2,1,0:T(8,128)S(1)}, u32[]{:S(2)}, u32[]{:S(2)}) collective-permute-start(f32[2,8,128]{2,1,0:T(8,128)S(1)} %pad_maximum_fusion.2.after_ref.refs_0_), channel_id=1, source_target_pairs={{0,3},{1,2},{2,1},{3,0},{4,7},{5,6},{6,5},{7,4},{8,11},{9,10},{10,... | collective-permute-start | bytes 24584 | tf_op jit(solution)/shard_map/ppermute | solution.py:554
  40.0 4.6 %collective-permute-start.14 = (f32[2,8,128]{2,1,0:T(8,128)S(1)}, f32[2,8,128]{2,1,0:T(8,128)S(1)}, u32[]{:S(2)}, u32[]{:S(2)}) collective-permute-start(f32[2,8,128]{2,1,0:T(8,128)S(1)} %pad_maximum_fusion.2.after_ref.refs_0_), channel_id=1, source_target_pairs={{0,2},{1,3},{2,0},{3,1},{4,6},{5,7},{6,4},{7,5},{8,10},{9,11},{10,... | collective-permute-start | bytes 24584 | tf_op jit(solution)/shard_map/ppermute | solution.py:554
  40.9 3.7 %collective-permute-start.13 = (f32[2,8,128]{2,1,0:T(8,128)S(1)}, f32[2,8,128]{2,1,0:T(8,128)S(1)}, u32[]{:S(2)}, u32[]{:S(2)}) collective-permute-start(f32[2,8,128]{2,1,0:T(8,128)S(1)} %pad_maximum_fusion.2.after_ref.refs_0_), channel_id=1, source_target_pairs={{0,1},{1,0},{2,3},{3,2},{4,5},{5,4},{6,7},{7,6},{8,9},{9,8},{10,11... | collective-permute-start | bytes 24584 | tf_op jit(solution)/shard_map/ppermute | solution.py:554
  46.7 1.7 %collective-permute-start.16 = (bf16[4,304,128]{2,1,0:T(8,128)(2,1)S(1)}, bf16[4,304,128]{2,1,0:T(8,128)(2,1)S(1)}, u32[]{:S(2)}, u32[]{:S(2)}) collective-permute-start(bf16[4,304,128]{2,1,0:T(8,128)(2,1)S(1)} %get-tuple-element.94), channel_id=1, source_target_pairs={{0,4},{4,0},{1,5},{5,1},{2,6},{6,2},{3,7},{7,3},{8,12},{12,8},{9,1... | collective-permute-start | bytes 933896 | tf_op jit(solution)/shard_map/ppermute | solution.py:554
  48.5 5.4 %collective-permute-start.17 = (bf16[304,128]{1,0:T(8,128)(2,1)S(1)}, bf16[304,128]{1,0:T(8,128)(2,1)S(1)}, u32[]{:S(2)}, u32[]{:S(2)}) collective-permute-start(bf16[304,128]{1,0:T(8,128)(2,1)S(1)} %get-tuple-element.98), channel_id=1, source_target_pairs={{0,24},{8,16},{16,8},{24,0},{1,25},{9,17},{17,9},{25,1},{2,26},{10... | collective-permute-start | bytes 233480 | tf_op jit(solution)/shard_map/ppermute | solution.py:554
  51.0 4.5 %collective-permute-start.18 = (bf16[304,128]{1,0:T(8,128)(2,1)S(1)}, bf16[304,128]{1,0:T(8,128)(2,1)S(1)}, u32[]{:S(2)}, u32[]{:S(2)}) collective-permute-start(bf16[304,128]{1,0:T(8,128)(2,1)S(1)} %get-tuple-element.99), channel_id=1, source_target_pairs={{0,16},{8,24},{16,0},{24,8},{1,17},{9,25},{17,1},{25,9},{2,18},{10... | collective-permute-start | bytes 233480 | tf_op jit(solution)/shard_map/ppermute | solution.py:554
  51.5 4.4 %collective-permute-start.19 = (bf16[304,128]{1,0:T(8,128)(2,1)S(1)}, bf16[304,128]{1,0:T(8,128)(2,1)S(1)}, u32[]{:S(2)}, u32[]{:S(2)}) collective-permute-start(bf16[304,128]{1,0:T(8,128)(2,1)S(1)} %get-tuple-element.100), channel_id=1, source_target_pairs={{0,8},{8,0},{16,24},{24,16},{1,9},{9,1},{17,25},{25,17},{2,10},{10... | collective-permute-start | bytes 233480 | tf_op jit(solution)/shard_map/ppermute | solution.py:554
  56.0 8.1 %collective-permute-start.24 = (bf16[304,128]{1,0:T(8,128)(2,1)S(1)}, bf16[304,128]{1,0:T(8,128)(2,1)S(1)}, u32[]{:S(2)}, u32[]{:S(2)}) collective-permute-start(bf16[304,128]{1,0:T(8,128)(2,1)S(1)} %add_lead.1.after_ref.refs_0_), channel_id=1, source_target_pairs={{0,3},{1,2},{2,1},{3,0},{4,7},{5,6},{6,5},{7,4},{8,11},{9,10},{10,... | collective-permute-start | bytes 233480 | tf_op jit(solution)/shard_map/ppermute | solution.py:554
  57.8 8.3 %collective-permute-start.23 = (bf16[304,128]{1,0:T(8,128)(2,1)S(1)}, bf16[304,128]{1,0:T(8,128)(2,1)S(1)}, u32[]{:S(2)}, u32[]{:S(2)}) collective-permute-start(bf16[304,128]{1,0:T(8,128)(2,1)S(1)} %add_lead.1.after_ref.refs_0_), channel_id=1, source_target_pairs={{0,2},{1,3},{2,0},{3,1},{4,6},{5,7},{6,4},{7,5},{8,10},{9,11},{10,... | collective-permute-start | bytes 233480 | tf_op jit(solution)/shard_map/ppermute | solution.py:554
  58.4 7.7 %collective-permute-start.22 = (bf16[304,128]{1,0:T(8,128)(2,1)S(1)}, bf16[304,128]{1,0:T(8,128)(2,1)S(1)}, u32[]{:S(2)}, u32[]{:S(2)}) collective-permute-start(bf16[304,128]{1,0:T(8,128)(2,1)S(1)} %add_lead.1.after_ref.refs_0_), channel_id=1, source_target_pairs={{0,1},{1,0},{2,3},{3,2},{4,5},{5,4},{6,7},{7,6},{8,9},{9,8},{10,11... | collective-permute-start | bytes 233480 | tf_op jit(solution)/shard_map/ppermute | solution.py:554
  60.5 9.2 %collective-permute-start.20 = (bf16[8,64,128]{2,1,0:T(8,128)(2,1)S(1)}, bf16[8,64,128]{2,1,0:T(8,128)(2,1)S(1)}, u32[]{:S(2)}, u32[]{:S(2)}) collective-permute-start(bf16[8,64,128]{2,1,0:T(8,128)(2,1)S(1)} %get-tuple-element.102), channel_id=1, source_target_pairs={{1,2},{2,1},{5,6},{6,5},{9,10},{10,9},{13,14},{14,13},{17,18},{18,... | collective-permute-start | bytes 393224 | tf_op jit(solution)/shard_map/ppermute | solution.py:562
  61.2 8.6 %collective-permute-start.21 = (bf16[8,64,128]{2,1,0:T(8,128)(2,1)S(1)}, bf16[8,64,128]{2,1,0:T(8,128)(2,1)S(1)}, u32[]{:S(2)}, u32[]{:S(2)}) collective-permute-start(bf16[8,64,128]{2,1,0:T(8,128)(2,1)S(1)} %get-tuple-element.103), channel_id=1, source_target_pairs={{0,1},{1,0},{2,3},{3,2},{4,5},{5,4},{6,7},{7,6},{8,9},{9,8},{10,11... | collective-permute-start | bytes 393224 | tf_op jit(solution)/shard_map/ppermute | solution.py:563
  66.2 6.5 %collective-permute-start.27 = (bf16[304,128]{1,0:T(8,128)(2,1)S(1)}, bf16[304,128]{1,0:T(8,128)(2,1)S(1)}, u32[]{:S(2)}, u32[]{:S(2)}) collective-permute-start(bf16[304,128]{1,0:T(8,128)(2,1)S(1)} %add_lat.1.refs_0_), channel_id=1, source_target_pairs={{0,24},{8,16},{16,8},{24,0},{1,25},{9,17},{17,9},{25,1},{2,26},{10... | collective-permute-start | bytes 233480 | tf_op jit(solution)/shard_map/ppermute | solution.py:554
  67.6 5.0 %collective-permute-start.26 = (bf16[304,128]{1,0:T(8,128)(2,1)S(1)}, bf16[304,128]{1,0:T(8,128)(2,1)S(1)}, u32[]{:S(2)}, u32[]{:S(2)}) collective-permute-start(bf16[304,128]{1,0:T(8,128)(2,1)S(1)} %add_lat.1.refs_0_), channel_id=1, source_target_pairs={{0,16},{8,24},{16,0},{24,8},{1,17},{9,25},{17,1},{25,9},{2,18},{10... | collective-permute-start | bytes 233480 | tf_op jit(solution)/shard_map/ppermute | solution.py:554
  68.8 4.4 %collective-permute-start.25 = (bf16[304,128]{1,0:T(8,128)(2,1)S(1)}, bf16[304,128]{1,0:T(8,128)(2,1)S(1)}, u32[]{:S(2)}, u32[]{:S(2)}) collective-permute-start(bf16[304,128]{1,0:T(8,128)(2,1)S(1)} %add_lat.1.refs_0_), channel_id=1, source_target_pairs={{0,8},{8,0},{16,24},{24,16},{1,9},{9,1},{17,25},{25,17},{2,10},{10... | collective-permute-start | bytes 233480 | tf_op jit(solution)/shard_map/ppermute | solution.py:554
  73.3 1.7 %collective-permute-start.28 = (bf16[1168,128]{1,0:T(8,128)(2,1)S(1)}, bf16[1168,128]{1,0:T(8,128)(2,1)S(1)}, u32[]{:S(2)}, u32[]{:S(2)}) collective-permute-start(bf16[1168,128]{1,0:T(8,128)(2,1)S(1)} %join.1.own_ref), channel_id=1, source_target_pairs={{0,4},{4,0},{1,5},{5,1},{2,6},{6,2},{3,7},{7,3},{8,12},{12,8},{9,1... | collective-permute-start | bytes 897032 | tf_op jit(solution)/shard_map/ppermute | solution.py:554
  (9 other events, 24.5 us)

commit v3 on v2

--- a/solution.py
+++ b/solution.py
@@ -11,6 +11,7 @@
 BF16 = jnp.bfloat16
 F32 = jnp.float32
 VMEM = pl.BlockSpec(memory_space=pltpu.VMEM)
+ANY = pl.BlockSpec(memory_space=pl.ANY)
 HIDE = 10**11
 SMALL = 16
 
@@ -377,14 +378,17 @@
             w_ref[at : at + c] = acc_ref[a * c : (a + 1) * c, b * c : (b + 1) * c].astype(BF16)
 
 
-def output_kernel(x_ref, a2_ref, m_ref, c2_ref, after_ref, o_ref, done_ref):
+def output_kernel(x_ref, a2_ref, m_ref, c2_ref, after_ref, o_hbm, done_ref, o_ref, sems):
     samples, height, across, c = x_ref.shape
     scale, shift = c2_ref[0:1], c2_ref[1:2]
     for s in range(samples):
         for r in range(height):
             normed = (a2_ref[s, r + 1] * scale + shift) * m_ref[s, r]
             o_ref[s, r] = (x_ref[s, r].astype(F32) + normed).astype(BF16)
+        pltpu.make_async_copy(o_ref.at[s], o_hbm.at[s], sems.at[s]).start()
     done_ref[...] = jnp.zeros(done_ref.shape, F32)
+    for s in range(samples):
+        pltpu.make_async_copy(o_ref.at[s], o_hbm.at[s], sems.at[s]).wait()
 
 
 def small_rows(rows, c):
@@ -401,7 +405,6 @@
     d_ref, send_ref, keep_ref, acc_ref = refs[pieces:]
     samples, height, across, c = x_ref.shape
     even = lax.axis_index("lat") % 2 == 0
-    lead = lax.axis_index("lead")
     core = lax.axis_index("dp") % 2
     offset, inverse, count, mean = (c1_ref[i : i + 1] for i in range(4))
     shift_sum = stats[:, 0:1].sum(0)
@@ -437,7 +440,7 @@
     def put(target, which):
         size = 9 * c // leads
         for j in range(leads):
-            slot = j ^ lead
+            slot = j ^ place(which, leads)
             if which == 1:
                 target[slot, :size] = w2_ref[j * size : (j + 1) * size]
             else:
@@ -498,30 +501,62 @@
     out_ref[leads * size :] = refs[0][size:]
 
 
-def finish_kernel(leads, own_ref, other_ref, *refs):
-    first, second = refs[:4], refs[4:]
+def write_chunks(leads, which, ref, out_hbm, sum_ref, sems):
+    size = out_hbm.shape[0] // leads
+    copies = []
+    for k in range(leads):
+        at = pl.multiple_of((k ^ place(which, leads)) * size, 16)
+        rows = slice(k * size, (k + 1) * size)
+        sum_ref[rows] = ref[rows].astype(F32)
+        copies.append(
+            pltpu.make_async_copy(sum_ref.at[rows], out_hbm.at[pl.ds(at, size)], sems.at[k])
+        )
+        copies[-1].start()
+    for copy in copies:
+        copy.wait()
+
+
+def leave_kernel(leads, grad_ref, own_ref, grad_hbm, first_hbm, second_hbm, sum_ref, sems):
     core = lax.axis_index("dp") % 2
-    lead = lax.axis_index("lead")
-    size = (own_ref.shape[0] - SMALL) // leads
-
-    def put(outs, ref):
-        for k in range(leads):
-            at = pl.multiple_of((k ^ lead) * size, 16)
-            outs[0][pl.ds(at, size)] = ref[k * size : (k + 1) * size].astype(F32)
-        small = ref[leads * size :].astype(F32)
-        total = small[:8] + small[8:]
-        for i in range(3):
-            outs[i + 1][...] = total[i : i + 1]
+    grad = pltpu.make_async_copy(grad_ref, grad_hbm, sems.at[leads])
+    grad.start()
 
     @pl.when(core == 0)
     def _():
-        put(first, own_ref)
-        put(second, other_ref)
+        write_chunks(leads, 0, own_ref, first_hbm, sum_ref, sems)
 
     @pl.when(core != 0)
     def _():
-        put(first, other_ref)
-        put(second, own_ref)
+        write_chunks(leads, 1, own_ref, second_hbm, sum_ref, sems)
+
+    grad.wait()
+
+
+def finish_kernel(leads, own_ref, other_ref, first_in, second_in, first_hbm, second_hbm, *refs):
+    small_hbm, (sum_ref, small_ref, sems) = refs[:6], refs[6:]
+    core = lax.axis_index("dp") % 2
+    small = [r[sum_ref.shape[0] :].astype(F32) for r in (own_ref, other_ref)]
+    small = [v[:8] + v[8:] for v in small]
+    for which in range(2):
+        total = jnp.where(core == which, small[0], small[1])
+        for i in range(3):
+            small_ref[3 * which + i] = total[i : i + 1]
+    copies = [
+        pltpu.make_async_copy(small_ref.at[i], small_hbm[i], sems.at[leads + i]) for i in range(6)
+    ]
+    for copy in copies:
+        copy.start()
+
+    @pl.when(core != 0)
+    def _():
+        write_chunks(leads, 0, other_ref, first_hbm, sum_ref, sems)
+
+    @pl.when(core == 0)
+    def _():
+        write_chunks(leads, 1, other_ref, second_hbm, sum_ref, sems)
+
+    for copy in copies:
+        copy.wait()
 
 
 def add_kernel(parts, waits, *refs):
@@ -536,14 +571,18 @@
         out[size:] = jnp.concatenate([high, (small - high.astype(F32)).astype(BF16)], 0)
 
 
-def call(kernel, outs, scratch, operands, name, flops=0, waits=(), spaces=(VMEM, VMEM)):
+def call(
+    kernel, outs, scratch, operands, name, flops=0, waits=(), spaces=(VMEM, VMEM), aliases={}
+):
     size = sum(o.size * o.dtype.itemsize for o in operands)
+    ins, to = (s if isinstance(s, list) else None for s in spaces)
     return pl.pallas_call(
         kernel,
         out_shape=outs,
-        in_specs=[spaces[0]] * len(operands) + [pl.BlockSpec(memory_space=pl.ANY)] * len(waits),
-        out_specs=jax.tree.map(lambda _: spaces[1], outs),
+        in_specs=(ins or [spaces[0]] * len(operands)) + [ANY] * len(waits),
+        out_specs=to or jax.tree.map(lambda _: spaces[1], outs),
         scratch_shapes=scratch,
+        input_output_aliases=aliases,
         compiler_params=pltpu.CompilerParams(vmem_limit_bytes=16 * 2**20),
         cost_estimate=pl.CostEstimate(flops=flops, bytes_accessed=size, transcendentals=0),
         name=name,
@@ -552,6 +591,24 @@
 
 def swap(value, axis, k):
     return lax.ppermute(value, axis, [(i, i ^ k) for i in range(lax.axis_size(axis))])
+
+
+def cross(value, k, first):
+    leads, dps, lats = (lax.axis_size(a) for a in ("lead", "dp", "lat"))
+    pairs = []
+    for lead in range(leads):
+        for dp in range(dps):
+            for lat in range(lats):
+                by_lead = first if leads != lats else (dp % 2 == 0) == first
+                to = (lead ^ k, dp, lat) if by_lead else (lead, dp, lat ^ k)
+                pairs.append(tuple((l * dps + d) * lats + t for l, d, t in ((lead, dp, lat), to)))
+    return lax.ppermute(value, ("lead", "dp", "lat"), pairs)
+
+
+def place(which, leads):
+    if which == 1 and leads == lax.axis_size("lat"):
+        return lax.axis_index("lat")
+    return lax.axis_index("lead")
 
 
 def neighbours(value_x, value_p, axis):
@@ -587,18 +644,18 @@
 def sum_everywhere(send, keep, edges, block_output, input_grad):
     leads, lats = lax.axis_size("lead"), lax.axis_size("lat")
     chunks = add_chunks([keep, swap(send, "dp", 1)], "add_dp", leads)
-    got = [swap(chunks[k], "lead", k) for k in reversed(range(1, leads))]
+    got = [cross(chunks[k], k, True) for k in reversed(range(1, leads))]
     output = block_output(chunks[0])
-    (mine,) = add_chunks([chunks[0]] + got, "add_lead", waits=(output[1],))
-    got = [swap(mine, "lat", k) for k in range(1, lats)]
+    (mine,) = add_chunks([chunks[0]] + got, "add_first", waits=(output[1],))
+    got = [cross(mine, k, False) for k in range(1, lats)]
     rows = edges(mine)
-    (mine,) = add_chunks([mine] + got, "add_lat", flops=HIDE)
+    (mine,) = add_chunks([mine] + got, "add_second", flops=HIDE)
     k = 2
     while k < lax.axis_size("dp"):
         (mine,) = add_chunks([mine, swap(mine, "dp", k)], "add_far_dp")
         k *= 2
     size, c = mine.shape[0] - SMALL, mine.shape[1]
-    got = [swap(mine, "lead", k) for k in range(1, leads)]
+    got = [cross(mine, k, True) for k in range(1, leads)]
     grad_input = input_grad(rows)
     own = call(
         functools.partial(join_kernel, leads),
@@ -608,11 +665,29 @@
         "join",
         waits=(grad_input[1],),
     )
-    one = [jax.ShapeDtypeStruct((leads * size, c), F32)] + [jax.ShapeDtypeStruct((1, c), F32)] * 3
-    sums = call(
-        functools.partial(finish_kernel, leads), one + one, [], (own, swap(own, "dp", 1)), "finish"
-    )
-    return sums[:4], sums[4:], output[0], grad_input[0]
+    whole = jax.ShapeDtypeStruct((leads * size, c), F32)
+    row = jax.ShapeDtypeStruct((1, c), F32)
+    dma = pltpu.SemaphoreType.DMA
+    total = pltpu.VMEM(whole.shape, F32)
+    other = swap(own, "dp", 1)
+    grad_input, first, second = call(
+        functools.partial(leave_kernel, leads),
+        [jax.ShapeDtypeStruct(grad_input[0].shape, BF16), whole, whole],
+        [total, dma((leads + 1,))],
+        (grad_input[0], own),
+        "leave",
+        spaces=(VMEM, ANY),
+    )
+    first, second, *rows = call(
+        functools.partial(finish_kernel, leads),
+        [whole, whole] + [row] * 6,
+        [total, pltpu.VMEM((6, 1, c), F32), dma((leads + 6,))],
+        (own, other, first, second),
+        "finish",
+        spaces=([VMEM, VMEM, ANY, ANY], [ANY] * 8),
+        aliases={2: 0, 3: 1},
+    )
+    return (first, *rows[:3]), (second, *rows[3:]), output[0], grad_input
 
 
 def shards(
@@ -654,7 +729,7 @@
         (x,),
         "near_rows",
         conv_flops,
-        spaces=(pl.BlockSpec(memory_space=pl.ANY),) * 2,
+        spaces=(ANY, ANY),
     )
     gx, gp = neighbours(*near, "lat")
     packed = array((3 * samples + slabs, across, c), BF16)
@@ -757,11 +832,12 @@
         return call(
             output_kernel,
             (shape(height, BF16), vector),
-            [],
+            [pltpu.VMEM(x.shape, BF16), pltpu.SemaphoreType.DMA((samples,))],
             (x, a2, wide_mask, c2),
             "output",
             conv_flops // 2,
             waits=(after,),
+            spaces=(VMEM, [ANY, VMEM]),
         )
 
     first, second, output, grad_input = sum_everywhere(

time: 76.3 us -> 74 us (0.970)
  waiting for transfers between devices: 14.1 us -> 11.7 us
    ppermute x23 -> x14, starting transfers between devices: 25.1 us -> 13.5 us  [swap(): lax.ppermute(value, axis, [(i, i ^ k) for i in range(lax.axis_size(axis))])]
    ppermute x0 -> x9, starting transfers between devices: none -> 11.6 us  [cross(): return lax.ppermute(value, ('lead', 'dp', 'lat'), pairs)]
    ppermute x23 -> x14, waiting for transfers between devices: 13.6 us -> 7.21 us  [swap(): lax.ppermute(value, axis, [(i, i ^ k) for i in range(lax.axis_size(axis))])]
    ppermute x0 -> x9, waiting for transfers between devices: none -> 3.61 us  [cross(): return lax.ppermute(value, ('lead', 'dp', 'lat'), pairs)]
    pallas_call x19 -> x20, Pallas kernels: 21.9 us -> 21.7 us  [call(): pl.pallas_call(kernel, out_shape=outs, in_specs=(ins or [spaces[0]] * len...]
  transfers between devices with their start and end apart: 29 -> 29, of which waited for: 17 -> 19; matrix products, arithmetic and copies ran while one was open for 0% -> 0% of each run, Pallas kernels for 17% -> 17%
where the time goes in v3:
time: 74 us; the launch traced here: 73.7 us
  starting transfers between devices  37.8 us (51%)
  Pallas kernels  21.7 us (29%)
  waiting for transfers between devices  11.7 us (16%)
  local copies, waits for them, and re-layouts  1.42 us (2%)
  between operations  1.07 us (1%)
    pallas_call x20, Pallas kernels, call(): pl.pallas_call(kernel, out_shape=outs, in_specs=(ins or [spaces[0]] * len...  21.7 us
    ppermute x14, starting transfers between devices, swap(): lax.ppermute(value, axis, [(i, i ^ k) for i in range(lax.axis_size(axis))])  13.5 us
    ppermute x9, starting transfers between devices, cross(): return lax.ppermute(value, ('lead', 'dp', 'lat'), pairs)  11.6 us
    ppermute x3, starting transfers between devices, neighbours(): return (lax.ppermute(value_x, axis, first), got_p)  10.6 us
    ppermute x14, waiting for transfers between devices, swap(): lax.ppermute(value, axis, [(i, i ^ k) for i in range(lax.axis_size(axis))])  7.21 us
    ppermute x9, waiting for transfers between devices, cross(): return lax.ppermute(value, ('lead', 'dp', 'lat'), pairs)  3.61 us
    ppermute x3, starting transfers between devices, neighbours(): got_p = lax.ppermute(value_p, axis, second)  2.16 us
  transfers between devices with their start and end apart: 29, of which 19 were waited for; matrix products, arithmetic and copies ran while one was open for 0% of the time, Pallas kernels for 17%

profile of v3, /device:TPU:0, one launch (start us, length us, event | category | flops | bytes accessed | tf_op | source)
XLA Modules:
  0.0 73.7 jit_solution(13401127265181310014)
XLA Ops:
  0.7 1.2 %copy-done = bf16[1,8,8,64,128]{4,3,2,1,0:T(8,128)(2,1)S(1)} copy-done((bf16[1,8,8,64,128]{4,3,2,1,0:T(8,128)(2,1)S(1)}, bf16[1,8,8,64,128]{4,3,2,1,0:T(8,128)(2,1)}, u32[]{:S(2)}) %copy-start) | copy-done | bytes 1048600
  2.8 5.9 %collective-permute-start.1 = (bf16[8,1,64,128]{3,2,1,0:T(8,128)(2,1)S(1)}, bf16[8,1,64,128]{3,2,1,0:T(8,128)(2,1)S(1)}, u32[]{:S(2)}, u32[]{:S(2)}) collective-permute-start(bf16[8,1,64,128]{3,2,1,0:T(8,128)(2,1)S(1)} %get-tuple-element.66), channel_id=1, source_target_pairs={{0,1},{1,0},{2,3},{3,2},{4,5},{5,4},{6,7},{7,6},{8,9},{9,8},{10,11... | collective-permute-start | bytes 393224 | tf_op jit(solution)/shard_map/ppermute | solution.py:620
  9.4 1.8 %collective-permute-start.3 = (bf16[25,64,128]{2,1,0:T(8,128)(2,1)S(1)}, bf16[25,64,128]{2,1,0:T(8,128)(2,1)S(1)}, u32[]{:S(2)}, u32[]{:S(2)}) collective-permute-start(bf16[25,64,128]{2,1,0:T(8,128)(2,1)S(1)} %get-tuple-element.73), channel_id=1, source_target_pairs={{0,1},{1,0},{2,3},{3,2},{4,5},{5,4},{6,7},{7,6},{8,9},{9,8},{10,11... | collective-permute-start | bytes 1228808 | tf_op jit(solution)/shard_map/ppermute | solution.py:620
  12.5 2.4 %conv1.1 = (f32[8,8,64,128]{3,2,1,0:T(8,128)S(1)}, f32[8,8,64,128]{3,2,1,0:T(8,128)S(1)}, bf16[3,512,256]{2,1,0:T(8,128)(2,1)S(1)}, f32[8,128]{1,0:T(8,128)S(1)}) custom-call(bf16[8,1,64,128]{3,2,1,0:T(8,128)(2,1)S(1)} %collective-permute-done.gp_ref, bf16[8,1,64,128]{3,2,1,0:T(8,128)(2,1)S(1)} %collective-permute-done.1.gx_ref, ...), custom_call_target="tpu_custom_call" | custom-call | flops 19327352832 | bytes 3707392 | tf_op jit(solution)/shard_map/conv1/pallas_call | solution.py:579
  16.2 2.5 %collective-permute-start.7 = (f32[2,8,128]{2,1,0:T(8,128)S(1)}, f32[2,8,128]{2,1,0:T(8,128)S(1)}, u32[]{:S(2)}, u32[]{:S(2)}) collective-permute-start(f32[2,8,128]{2,1,0:T(8,128)S(1)} %pad_maximum_fusion.refs_0_), channel_id=1, source_target_pairs={{0,3},{1,2},{2,1},{3,0},{4,7},{5,6},{6,5},{7,4},{8,11},{9,10},{10,... | collective-permute-start | bytes 24584 | tf_op jit(solution)/shard_map/ppermute | solution.py:593
  19.4 1.2 %collective-permute-start.5 = (f32[2,8,128]{2,1,0:T(8,128)S(1)}, f32[2,8,128]{2,1,0:T(8,128)S(1)}, u32[]{:S(2)}, u32[]{:S(2)}) collective-permute-start(f32[2,8,128]{2,1,0:T(8,128)S(1)} %pad_maximum_fusion.refs_0_), channel_id=1, source_target_pairs={{0,1},{1,0},{2,3},{3,2},{4,5},{5,4},{6,7},{7,6},{8,9},{9,8},{10,11... | collective-permute-start | bytes 24584 | tf_op jit(solution)/shard_map/ppermute | solution.py:593
  20.7 1.1 %conv1_edges.1 = (f32[8,4,64,128]{3,2,1,0:T(8,128)S(1)}, f32[8,4,64,128]{3,2,1,0:T(8,128)S(1)}, f32[8,2,64,128]{3,2,1,0:T(8,128)S(1)}) custom-call(bf16[25,64,128]{2,1,0:T(8,128)(2,1)S(1)} %collective-permute-done.2.hp_ref, bf16[25,64,128]{2,1,0:T(8,128)(2,1)S(1)} %collective-permute-done.3.hx_ref, bf16[8,1,64,128]{3,2,1,0:T(8,128)(2,1)S(1)} %collective-permute-done.gp_ref, ...), custom_call_target="tpu_custom_call" | custom-call | flops 603979776 | bytes 2920960 | tf_op jit(solution)/shard_map/conv1_edges/pallas_call | solution.py:579
  23.2 3.2 %conv2.1 = (bf16[8,10,64,128]{3,2,1,0:T(8,128)(2,1)S(1)}, f32[8,10,64,128]{3,2,1,0:T(8,128)S(1)}, f32[8,10,64,128]{3,2,1,0:T(8,128)S(1)}, f32[8,128]{1,0:T(8,128)S(1)}, f32[8,128]{1,0:T(8,128)S(1)}) custom-call(f32[8,128]{1,0:T(8,128)S(1)} %get-tuple-element.70.st_ref.own_ref.st1_ref, f32[8,8,64,128]{3,2,1,0:T(8,128)S(1)} %get-tuple-element.71.a_ref, ...), custom_call_target="tpu_custom_call" | custom-call | flops 1207959552 | bytes 9217536 | tf_op jit(solution)/shard_map/conv2/pallas_call | solution.py:579
  26.5 1.2 %collective-permute-done.8 = f32[1,8,128]{2,1,0:T(8,128)S(1)} collective-permute-done((f32[1,8,128]{2,1,0:T(8,128)S(1)}, f32[1,8,128]{2,1,0:T(8,128)S(1)}, u32[]{:S(2)}, u32[]{:S(2)}) %collective-permute-start.8) | collective-permute-done | bytes 4128 | tf_op jit(solution)/shard_map/ppermute | solution.py:593
  27.7 1.5 %collective-permute-start.11 = (f32[2,8,128]{2,1,0:T(8,128)S(1)}, f32[2,8,128]{2,1,0:T(8,128)S(1)}, u32[]{:S(2)}, u32[]{:S(2)}) collective-permute-start(f32[2,8,128]{2,1,0:T(8,128)S(1)} %pad_maximum_fusion.1.after_ref.refs_0_), channel_id=1, source_target_pairs={{0,3},{1,2},{2,1},{3,0},{4,7},{5,6},{6,5},{7,4},{8,11},{9,10},{10,... | collective-permute-start | bytes 24584 | tf_op jit(solution)/shard_map/ppermute | solution.py:593
  29.1 1.0 %collective-permute-start.10 = (f32[2,8,128]{2,1,0:T(8,128)S(1)}, f32[2,8,128]{2,1,0:T(8,128)S(1)}, u32[]{:S(2)}, u32[]{:S(2)}) collective-permute-start(f32[2,8,128]{2,1,0:T(8,128)S(1)} %pad_maximum_fusion.1.after_ref.refs_0_), channel_id=1, source_target_pairs={{0,2},{1,3},{2,0},{3,1},{4,6},{5,7},{6,4},{7,5},{8,10},{9,11},{10,... | collective-permute-start | bytes 24584 | tf_op jit(solution)/shard_map/ppermute | solution.py:593
  30.1 1.9 %collective-permute-start.9 = (f32[2,8,128]{2,1,0:T(8,128)S(1)}, f32[2,8,128]{2,1,0:T(8,128)S(1)}, u32[]{:S(2)}, u32[]{:S(2)}) collective-permute-start(f32[2,8,128]{2,1,0:T(8,128)S(1)} %pad_maximum_fusion.1.after_ref.refs_0_), channel_id=1, source_target_pairs={{0,1},{1,0},{2,3},{3,2},{4,5},{5,4},{6,7},{7,6},{8,9},{9,8},{10,11... | collective-permute-start | bytes 24584 | tf_op jit(solution)/shard_map/ppermute | solution.py:593
  32.1 1.6 %slopes.1 = (f32[8,8,64,128]{3,2,1,0:T(8,128)S(1)}, f32[8,10,64,128]{3,2,1,0:T(8,128)S(1)}) custom-call(f32[8,8,64,128]{3,2,1,0:T(8,128)S(1)} %get-tuple-element.83.z_ref, f32[8,10,64,128]{3,2,1,0:T(8,128)S(1)} %get-tuple-element.84.z2_ref, f32[8,8,64,128]{3,2,1,0:T(8,128)S(1)} %get-tuple-element.68.m_ref, f32[8,4,64,128]{3,2,1,0:T(8,128)S(1)} %get-tuple-element.76.mh_ref, ...), custom_call_target="tpu_custom_call" | custom-call | flops 1207959552 | bytes 7864320 | tf_op jit(solution)/shard_map/slopes/pallas_call | solution.py:579
  33.8 2.5 %conv2_back.1 = (bf16[8,8,64,128]{3,2,1,0:T(8,128)(2,1)S(1)}, f32[8,8,64,128]{3,2,1,0:T(8,128)S(1)}, f32[8,128]{1,0:T(8,128)S(1)}, f32[8,128]{1,0:T(8,128)S(1)}) custom-call(f32[8,128]{1,0:T(8,128)S(1)} %get-tuple-element.81.own_ref, f32[8,128]{1,0:T(8,128)S(1)} %get-tuple-element.70.st_ref.own_ref.st1_ref, f32[8,128]{1,0:T(8,128)S(1)} %get-tuple-element.82.c1_ref, ...), custom_call_target="tpu_custom_call" | custom-call | flops 1207959552 | bytes 12891136 | tf_op jit(solution)/shard_map/conv2_back/pallas_call | solution.py:579
  36.3 1.2 %collective-permute-done.12 = f32[1,8,128]{2,1,0:T(8,128)S(1)} collective-permute-done((f32[1,8,128]{2,1,0:T(8,128)S(1)}, f32[1,8,128]{2,1,0:T(8,128)S(1)}, u32[]{:S(2)}, u32[]{:S(2)}) %collective-permute-start.12) | collective-permute-done | bytes 4128 | tf_op jit(solution)/shard_map/ppermute | solution.py:593
  37.5 2.5 %collective-permute-start.15 = (f32[2,8,128]{2,1,0:T(8,128)S(1)}, f32[2,8,128]{2,1,0:T(8,128)S(1)}, u32[]{:S(2)}, u32[]{:S(2)}) collective-permute-start(f32[2,8,128]{2,1,0:T(8,128)S(1)} %pad_maximum_fusion.2.after_ref.refs_0_), channel_id=1, source_target_pairs={{0,3},{1,2},{2,1},{3,0},{4,7},{5,6},{6,5},{7,4},{8,11},{9,10},{10,... | collective-permute-start | bytes 24584 | tf_op jit(solution)/shard_map/ppermute | solution.py:593
  40.0 0.9 %collective-permute-start.14 = (f32[2,8,128]{2,1,0:T(8,128)S(1)}, f32[2,8,128]{2,1,0:T(8,128)S(1)}, u32[]{:S(2)}, u32[]{:S(2)}) collective-permute-start(f32[2,8,128]{2,1,0:T(8,128)S(1)} %pad_maximum_fusion.2.after_ref.refs_0_), channel_id=1, source_target_pairs={{0,2},{1,3},{2,0},{3,1},{4,6},{5,7},{6,4},{7,5},{8,10},{9,11},{10,... | collective-permute-start | bytes 24584 | tf_op jit(solution)/shard_map/ppermute | solution.py:593
  40.9 1.0 %collective-permute-start.13 = (f32[2,8,128]{2,1,0:T(8,128)S(1)}, f32[2,8,128]{2,1,0:T(8,128)S(1)}, u32[]{:S(2)}, u32[]{:S(2)}) collective-permute-start(f32[2,8,128]{2,1,0:T(8,128)S(1)} %pad_maximum_fusion.2.after_ref.refs_0_), channel_id=1, source_target_pairs={{0,1},{1,0},{2,3},{3,2},{4,5},{5,4},{6,7},{7,6},{8,9},{9,8},{10,11... | collective-permute-start | bytes 24584 | tf_op jit(solution)/shard_map/ppermute | solution.py:593
  41.9 2.0 %conv2_weight_grad.1 = (bf16[1152,128]{1,0:T(8,128)(2,1)S(1)}, f32[8,128]{1,0:T(8,128)S(1)}) custom-call(bf16[8,10,64,128]{3,2,1,0:T(8,128)(2,1)S(1)} %get-tuple-element.91.n_ref, bf16[8,8,64,128]{3,2,1,0:T(8,128)(2,1)S(1)} %get-tuple-element.92.d_ref, f32[2,8,128]{2,1,0:T(8,128)S(1)} %pad_maximum_fusion.2.after_ref.refs_0_), custom_call_target="tpu_custom_call" | custom-call | flops 1207959552 | bytes 2359296 | tf_op jit(solution)/shard_map/conv2_weight_grad/pallas_call | solution.py:579
  44.6 2.2 %conv1_weight_grad.1 = (bf16[8,8,64,128]{3,2,1,0:T(8,128)(2,1)S(1)}, bf16[4,304,128]{2,1,0:T(8,128)(2,1)S(1)}, bf16[4,304,128]{2,1,0:T(8,128)(2,1)S(1)}) custom-call(f32[8,128]{1,0:T(8,128)S(1)} %get-tuple-element.82.c1_ref, f32[8,128]{1,0:T(8,128)S(1)} %get-tuple-element.88.c2_ref, f32[8,8,64,128]{3,2,1,0:T(8,128)S(1)} %get-tuple-element.89.dn_ref, ...), custom_call_target="tpu_custom_call" | custom-call | flops 1207959552 | bytes 7942656 | tf_op jit(solution)/shard_map/conv1_weight_grad/pallas_call | solution.py:579
  46.8 1.6 %collective-permute-done.16.refs_1_ = bf16[4,304,128]{2,1,0:T(8,128)(2,1)S(1)} collective-permute-done((bf16[4,304,128]{2,1,0:T(8,128)(2,1)S(1)}, bf16[4,304,128]{2,1,0:T(8,128)(2,1)S(1)}, u32[]{:S(2)}, u32[]{:S(2)}) %collective-permute-start.16) | collective-permute-done | bytes 311328 | tf_op jit(solution)/shard_map/ppermute | solution.py:593
  48.5 2.5 %collective-permute-start.17 = (bf16[304,128]{1,0:T(8,128)(2,1)S(1)}, bf16[304,128]{1,0:T(8,128)(2,1)S(1)}, u32[]{:S(2)}, u32[]{:S(2)}) collective-permute-start(bf16[304,128]{1,0:T(8,128)(2,1)S(1)} %get-tuple-element.101), channel_id=1, source_target_pairs={{0,24},{1,25},{2,26},{3,27},{4,7},{5,6},{6,5},{7,4},{8,16},{9,17},... | collective-permute-start | bytes 233480 | tf_op jit(solution)/shard_map/ppermute | solution.py:605
  52.1 1.1 %output.1 = (bf16[8,8,64,128]{3,2,1,0:T(8,128)(2,1)}, f32[8,128]{1,0:T(8,128)S(1)}) custom-call(bf16[8,8,64,128]{3,2,1,0:T(8,128)(2,1)S(1)} %bitcast.27, f32[8,10,64,128]{3,2,1,0:T(8,128)S(1)} %get-tuple-element.80.a2_ref, f32[8,8,64,128]{3,2,1,0:T(8,128)S(1)} %get-tuple-element.68.m_ref, f32[8,128]{1,0:T(8,128)S(1)} %get-tuple-element.88.c2_ref, ...), custom_call_target="tpu_custom_call" | custom-call | flops 603979776 | bytes 5771264 | tf_op jit(solution)/shard_map/output/pallas_call | solution.py:579
  53.9 1.5 %collective-permute-done.18.refs_2_ = bf16[304,128]{1,0:T(8,128)(2,1)S(1)} collective-permute-done((bf16[304,128]{1,0:T(8,128)(2,1)S(1)}, bf16[304,128]{1,0:T(8,128)(2,1)S(1)}, u32[]{:S(2)}, u32[]{:S(2)}) %collective-permute-start.18) | collective-permute-done | bytes 77856 | tf_op jit(solution)/shard_map/ppermute | solution.py:605
  56.0 1.9 %collective-permute-start.24 = (bf16[304,128]{1,0:T(8,128)(2,1)S(1)}, bf16[304,128]{1,0:T(8,128)(2,1)S(1)}, u32[]{:S(2)}, u32[]{:S(2)}) collective-permute-start(bf16[304,128]{1,0:T(8,128)(2,1)S(1)} %add_first.1.after_ref.refs_0_), channel_id=1, source_target_pairs={{0,3},{1,2},{2,1},{3,0},{4,28},{5,29},{6,30},{7,31},{8,11},{9,10},... | collective-permute-start | bytes 233480 | tf_op jit(solution)/shard_map/ppermute | solution.py:605
  58.5 2.0 %collective-permute-start.22 = (bf16[304,128]{1,0:T(8,128)(2,1)S(1)}, bf16[304,128]{1,0:T(8,128)(2,1)S(1)}, u32[]{:S(2)}, u32[]{:S(2)}) collective-permute-start(bf16[304,128]{1,0:T(8,128)(2,1)S(1)} %add_first.1.after_ref.refs_0_), channel_id=1, source_target_pairs={{0,1},{1,0},{2,3},{3,2},{4,12},{5,13},{6,14},{7,15},{8,9},{9,8},{1... | collective-permute-start | bytes 233480 | tf_op jit(solution)/shard_map/ppermute | solution.py:605
  61.2 2.9 %collective-permute-start.21 = (bf16[8,64,128]{2,1,0:T(8,128)(2,1)S(1)}, bf16[8,64,128]{2,1,0:T(8,128)(2,1)S(1)}, u32[]{:S(2)}, u32[]{:S(2)}) collective-permute-start(bf16[8,64,128]{2,1,0:T(8,128)(2,1)S(1)} %get-tuple-element.106), channel_id=1, source_target_pairs={{0,1},{1,0},{2,3},{3,2},{4,5},{5,4},{6,7},{7,6},{8,9},{9,8},{10,11... | collective-permute-start | bytes 393224 | tf_op jit(solution)/shard_map/ppermute | solution.py:620
  64.8 1.1 %collective-permute-start.27 = (bf16[304,128]{1,0:T(8,128)(2,1)S(1)}, bf16[304,128]{1,0:T(8,128)(2,1)S(1)}, u32[]{:S(2)}, u32[]{:S(2)}) collective-permute-start(bf16[304,128]{1,0:T(8,128)(2,1)S(1)} %add_second.1.refs_0_), channel_id=1, source_target_pairs={{0,24},{1,25},{2,26},{3,27},{4,7},{5,6},{6,5},{7,4},{8,16},{9,17},... | collective-permute-start | bytes 233480 | tf_op jit(solution)/shard_map/ppermute | solution.py:605
  66.4 2.0 %collective-permute-start.25 = (bf16[304,128]{1,0:T(8,128)(2,1)S(1)}, bf16[304,128]{1,0:T(8,128)(2,1)S(1)}, u32[]{:S(2)}, u32[]{:S(2)}) collective-permute-start(bf16[304,128]{1,0:T(8,128)(2,1)S(1)} %add_second.1.refs_0_), channel_id=1, source_target_pairs={{0,8},{1,9},{2,10},{3,11},{4,5},{5,4},{6,7},{7,6},{8,0},{9,1},{10,... | collective-permute-start | bytes 233480 | tf_op jit(solution)/shard_map/ppermute | solution.py:605
  68.8 2.0 %conv1_back.1 = (bf16[8,8,64,128]{3,2,1,0:T(8,128)(2,1)S(1)}, f32[8,128]{1,0:T(8,128)S(1)}) custom-call(bf16[8,64,128]{2,1,0:T(8,128)(2,1)S(1)} %collective-permute-done.20.ep_ref, bf16[8,64,128]{2,1,0:T(8,128)(2,1)S(1)} %collective-permute-done.21.ex_ref, bf16[8,8,64,128]{3,2,1,0:T(8,128)(2,1)S(1)} %get-tuple-element.100.d_ref, ...), custom_call_target="tpu_custom_call" | custom-call | flops 1207959552 | bytes 2654208 | tf_op jit(solution)/shard_map/conv1_back/pallas_call | solution.py:579
  71.1 1.2 %leave.1 = (bf16[8,8,64,128]{3,2,1,0:T(8,128)(2,1)}, f32[1152,128]{1,0:T(8,128)}, f32[1152,128]{1,0:T(8,128)}) custom-call(bf16[8,8,64,128]{3,2,1,0:T(8,128)(2,1)S(1)} %get-tuple-element.107.grad_ref, bf16[1168,128]{1,0:T(8,128)(2,1)S(1)} %join.1.own_ref), custom_call_target="tpu_custom_call" | custom-call | bytes 1347584 | tf_op jit(solution)/shard_map/leave/pallas_call | solution.py:579
  72.6 0.9 %finish.1 = (f32[1152,128]{1,0:T(8,128)}, f32[1152,128]{1,0:T(8,128)}, f32[1,128]{1,0:T(1,128)}, f32[1,128]{1,0:T(1,128)}, f32[1,128]{1,0:T(1,128)}, /*index=5*/...) custom-call(bf16[1168,128]{1,0:T(8,128)(2,1)S(1)} %join.1.own_ref, ...), custom_call_target="tpu_custom_call", output_to_operand_aliasing={{0}: (2, {}), {1}: (3, {})} | custom-call | bytes 1777664 | tf_op jit(solution)/shard_map/finish/pallas_call | solution.py:579
  (73 shorter events, 13.5 us)
Async XLA Ops:
  1.9 10.0 %collective-permute-start = (bf16[8,1,64,128]{3,2,1,0:T(8,128)(2,1)S(1)}, bf16[8,1,64,128]{3,2,1,0:T(8,128)(2,1)S(1)}, u32[]{:S(2)}, u32[]{:S(2)}) collective-permute-start(bf16[8,1,64,128]{3,2,1,0:T(8,128)(2,1)S(1)} %get-tuple-element.65), channel_id=1, source_target_pairs={{1,2},{2,1},{5,6},{6,5},{9,10},{10,9},{13,14},{14,13},{17,18},{18,... | collective-permute-start | bytes 393224 | tf_op jit(solution)/shard_map/ppermute | solution.py:619
  2.8 9.6 %collective-permute-start.1 = (bf16[8,1,64,128]{3,2,1,0:T(8,128)(2,1)S(1)}, bf16[8,1,64,128]{3,2,1,0:T(8,128)(2,1)S(1)}, u32[]{:S(2)}, u32[]{:S(2)}) collective-permute-start(bf16[8,1,64,128]{3,2,1,0:T(8,128)(2,1)S(1)} %get-tuple-element.66), channel_id=1, source_target_pairs={{0,1},{1,0},{2,3},{3,2},{4,5},{5,4},{6,7},{7,6},{8,9},{9,8},{10,11... | collective-permute-start | bytes 393224 | tf_op jit(solution)/shard_map/ppermute | solution.py:620
  8.8 11.8 %collective-permute-start.2 = (bf16[25,64,128]{2,1,0:T(8,128)(2,1)S(1)}, bf16[25,64,128]{2,1,0:T(8,128)(2,1)S(1)}, u32[]{:S(2)}, u32[]{:S(2)}) collective-permute-start(bf16[25,64,128]{2,1,0:T(8,128)(2,1)S(1)} %get-tuple-element.72), channel_id=1, source_target_pairs={{1,2},{2,1},{5,6},{6,5},{9,10},{10,9},{13,14},{14,13},{17,18},{18,... | collective-permute-start | bytes 1228808 | tf_op jit(solution)/shard_map/ppermute | solution.py:619
  9.4 11.2 %collective-permute-start.3 = (bf16[25,64,128]{2,1,0:T(8,128)(2,1)S(1)}, bf16[25,64,128]{2,1,0:T(8,128)(2,1)S(1)}, u32[]{:S(2)}, u32[]{:S(2)}) collective-permute-start(bf16[25,64,128]{2,1,0:T(8,128)(2,1)S(1)} %get-tuple-element.73), channel_id=1, source_target_pairs={{0,1},{1,0},{2,3},{3,2},{4,5},{5,4},{6,7},{7,6},{8,9},{9,8},{10,11... | collective-permute-start | bytes 1228808 | tf_op jit(solution)/shard_map/ppermute | solution.py:620
  14.9 1.2 %collective-permute-start.4 = (f32[1,8,128]{2,1,0:T(8,128)S(1)}, f32[1,8,128]{2,1,0:T(8,128)S(1)}, u32[]{:S(2)}, u32[]{:S(2)}) collective-permute-start(f32[1,8,128]{2,1,0:T(8,128)S(1)} %bitcast.28), channel_id=1, source_target_pairs={{0,4},{4,0},{1,5},{5,1},{2,6},{6,2},{3,7},{7,3},{8,12},{12,8},{9,1... | collective-permute-start | bytes 12296 | tf_op jit(solution)/shard_map/ppermute | solution.py:593
  15.5 7.8 %copy-start.2 = (f32[128]{0:T(128)S(1)}, f32[128]{0:T(128)}, u32[]{:S(2)}) copy-start(f32[128]{0:T(128)} %param.16) | copy-start | bytes 1540
  15.5 7.7 %copy-start.4 = (f32[128]{0:T(128)S(1)}, f32[128]{0:T(128)}, u32[]{:S(2)}) copy-start(f32[128]{0:T(128)} %param.19) | copy-start | bytes 1540
  15.5 7.7 %copy-start.5 = (f32[128]{0:T(128)S(1)}, f32[128]{0:T(128)}, u32[]{:S(2)}) copy-start(f32[128]{0:T(128)} %param.17) | copy-start | bytes 1540
  16.2 6.4 %collective-permute-start.7 = (f32[2,8,128]{2,1,0:T(8,128)S(1)}, f32[2,8,128]{2,1,0:T(8,128)S(1)}, u32[]{:S(2)}, u32[]{:S(2)}) collective-permute-start(f32[2,8,128]{2,1,0:T(8,128)S(1)} %pad_maximum_fusion.refs_0_), channel_id=1, source_target_pairs={{0,3},{1,2},{2,1},{3,0},{4,7},{5,6},{6,5},{7,4},{8,11},{9,10},{10,... | collective-permute-start | bytes 24584 | tf_op jit(solution)/shard_map/ppermute | solution.py:593
  18.7 4.5 %collective-permute-start.6 = (f32[2,8,128]{2,1,0:T(8,128)S(1)}, f32[2,8,128]{2,1,0:T(8,128)S(1)}, u32[]{:S(2)}, u32[]{:S(2)}) collective-permute-start(f32[2,8,128]{2,1,0:T(8,128)S(1)} %pad_maximum_fusion.refs_0_), channel_id=1, source_target_pairs={{0,2},{1,3},{2,0},{3,1},{4,6},{5,7},{6,4},{7,5},{8,10},{9,11},{10,... | collective-permute-start | bytes 24584 | tf_op jit(solution)/shard_map/ppermute | solution.py:593
  19.4 3.9 %collective-permute-start.5 = (f32[2,8,128]{2,1,0:T(8,128)S(1)}, f32[2,8,128]{2,1,0:T(8,128)S(1)}, u32[]{:S(2)}, u32[]{:S(2)}) collective-permute-start(f32[2,8,128]{2,1,0:T(8,128)S(1)} %pad_maximum_fusion.refs_0_), channel_id=1, source_target_pairs={{0,1},{1,0},{2,3},{3,2},{4,5},{5,4},{6,7},{7,6},{8,9},{9,8},{10,11... | collective-permute-start | bytes 24584 | tf_op jit(solution)/shard_map/ppermute | solution.py:593
  26.4 1.2 %collective-permute-start.8 = (f32[1,8,128]{2,1,0:T(8,128)S(1)}, f32[1,8,128]{2,1,0:T(8,128)S(1)}, u32[]{:S(2)}, u32[]{:S(2)}) collective-permute-start(f32[1,8,128]{2,1,0:T(8,128)S(1)} %bitcast.30), channel_id=1, source_target_pairs={{0,4},{4,0},{1,5},{5,1},{2,6},{6,2},{3,7},{7,3},{8,12},{12,8},{9,1... | collective-permute-start | bytes 12296 | tf_op jit(solution)/shard_map/ppermute | solution.py:593
  27.7 6.0 %collective-permute-start.11 = (f32[2,8,128]{2,1,0:T(8,128)S(1)}, f32[2,8,128]{2,1,0:T(8,128)S(1)}, u32[]{:S(2)}, u32[]{:S(2)}) collective-permute-start(f32[2,8,128]{2,1,0:T(8,128)S(1)} %pad_maximum_fusion.1.after_ref.refs_0_), channel_id=1, source_target_pairs={{0,3},{1,2},{2,1},{3,0},{4,7},{5,6},{6,5},{7,4},{8,11},{9,10},{10,... | collective-permute-start | bytes 24584 | tf_op jit(solution)/shard_map/ppermute | solution.py:593
  29.1 4.5 %collective-permute-start.10 = (f32[2,8,128]{2,1,0:T(8,128)S(1)}, f32[2,8,128]{2,1,0:T(8,128)S(1)}, u32[]{:S(2)}, u32[]{:S(2)}) collective-permute-start(f32[2,8,128]{2,1,0:T(8,128)S(1)} %pad_maximum_fusion.1.after_ref.refs_0_), channel_id=1, source_target_pairs={{0,2},{1,3},{2,0},{3,1},{4,6},{5,7},{6,4},{7,5},{8,10},{9,11},{10,... | collective-permute-start | bytes 24584 | tf_op jit(solution)/shard_map/ppermute | solution.py:593
  30.1 3.7 %collective-permute-start.9 = (f32[2,8,128]{2,1,0:T(8,128)S(1)}, f32[2,8,128]{2,1,0:T(8,128)S(1)}, u32[]{:S(2)}, u32[]{:S(2)}) collective-permute-start(f32[2,8,128]{2,1,0:T(8,128)S(1)} %pad_maximum_fusion.1.after_ref.refs_0_), channel_id=1, source_target_pairs={{0,1},{1,0},{2,3},{3,2},{4,5},{5,4},{6,7},{7,6},{8,9},{9,8},{10,11... | collective-permute-start | bytes 24584 | tf_op jit(solution)/shard_map/ppermute | solution.py:593
  36.2 1.2 %collective-permute-start.12 = (f32[1,8,128]{2,1,0:T(8,128)S(1)}, f32[1,8,128]{2,1,0:T(8,128)S(1)}, u32[]{:S(2)}, u32[]{:S(2)}) collective-permute-start(f32[1,8,128]{2,1,0:T(8,128)S(1)} %bitcast.32), channel_id=1, source_target_pairs={{0,4},{4,0},{1,5},{5,1},{2,6},{6,2},{3,7},{7,3},{8,12},{12,8},{9,1... | collective-permute-start | bytes 12296 | tf_op jit(solution)/shard_map/ppermute | solution.py:593
  37.5 6.4 %collective-permute-start.15 = (f32[2,8,128]{2,1,0:T(8,128)S(1)}, f32[2,8,128]{2,1,0:T(8,128)S(1)}, u32[]{:S(2)}, u32[]{:S(2)}) collective-permute-start(f32[2,8,128]{2,1,0:T(8,128)S(1)} %pad_maximum_fusion.2.after_ref.refs_0_), channel_id=1, source_target_pairs={{0,3},{1,2},{2,1},{3,0},{4,7},{5,6},{6,5},{7,4},{8,11},{9,10},{10,... | collective-permute-start | bytes 24584 | tf_op jit(solution)/shard_map/ppermute | solution.py:593
  40.0 4.6 %collective-permute-start.14 = (f32[2,8,128]{2,1,0:T(8,128)S(1)}, f32[2,8,128]{2,1,0:T(8,128)S(1)}, u32[]{:S(2)}, u32[]{:S(2)}) collective-permute-start(f32[2,8,128]{2,1,0:T(8,128)S(1)} %pad_maximum_fusion.2.after_ref.refs_0_), channel_id=1, source_target_pairs={{0,2},{1,3},{2,0},{3,1},{4,6},{5,7},{6,4},{7,5},{8,10},{9,11},{10,... | collective-permute-start | bytes 24584 | tf_op jit(solution)/shard_map/ppermute | solution.py:593
  40.9 3.7 %collective-permute-start.13 = (f32[2,8,128]{2,1,0:T(8,128)S(1)}, f32[2,8,128]{2,1,0:T(8,128)S(1)}, u32[]{:S(2)}, u32[]{:S(2)}) collective-permute-start(f32[2,8,128]{2,1,0:T(8,128)S(1)} %pad_maximum_fusion.2.after_ref.refs_0_), channel_id=1, source_target_pairs={{0,1},{1,0},{2,3},{3,2},{4,5},{5,4},{6,7},{7,6},{8,9},{9,8},{10,11... | collective-permute-start | bytes 24584 | tf_op jit(solution)/shard_map/ppermute | solution.py:593
  46.8 1.7 %collective-permute-start.16 = (bf16[4,304,128]{2,1,0:T(8,128)(2,1)S(1)}, bf16[4,304,128]{2,1,0:T(8,128)(2,1)S(1)}, u32[]{:S(2)}, u32[]{:S(2)}) collective-permute-start(bf16[4,304,128]{2,1,0:T(8,128)(2,1)S(1)} %get-tuple-element.97), channel_id=1, source_target_pairs={{0,4},{4,0},{1,5},{5,1},{2,6},{6,2},{3,7},{7,3},{8,12},{12,8},{9,1... | collective-permute-start | bytes 933896 | tf_op jit(solution)/shard_map/ppermute | solution.py:593
  48.5 5.4 %collective-permute-start.17 = (bf16[304,128]{1,0:T(8,128)(2,1)S(1)}, bf16[304,128]{1,0:T(8,128)(2,1)S(1)}, u32[]{:S(2)}, u32[]{:S(2)}) collective-permute-start(bf16[304,128]{1,0:T(8,128)(2,1)S(1)} %get-tuple-element.101), channel_id=1, source_target_pairs={{0,24},{1,25},{2,26},{3,27},{4,7},{5,6},{6,5},{7,4},{8,16},{9,17},... | collective-permute-start | bytes 233480 | tf_op jit(solution)/shard_map/ppermute | solution.py:605
  51.0 4.4 %collective-permute-start.18 = (bf16[304,128]{1,0:T(8,128)(2,1)S(1)}, bf16[304,128]{1,0:T(8,128)(2,1)S(1)}, u32[]{:S(2)}, u32[]{:S(2)}) collective-permute-start(bf16[304,128]{1,0:T(8,128)(2,1)S(1)} %get-tuple-element.102), channel_id=1, source_target_pairs={{0,16},{1,17},{2,18},{3,19},{4,6},{5,7},{6,4},{7,5},{8,24},{9,25},... | collective-permute-start | bytes 233480 | tf_op jit(solution)/shard_map/ppermute | solution.py:605
  51.5 4.4 %collective-permute-start.19 = (bf16[304,128]{1,0:T(8,128)(2,1)S(1)}, bf16[304,128]{1,0:T(8,128)(2,1)S(1)}, u32[]{:S(2)}, u32[]{:S(2)}) collective-permute-start(bf16[304,128]{1,0:T(8,128)(2,1)S(1)} %get-tuple-element.103), channel_id=1, source_target_pairs={{0,8},{1,9},{2,10},{3,11},{4,5},{5,4},{6,7},{7,6},{8,0},{9,1},{10,... | collective-permute-start | bytes 233480 | tf_op jit(solution)/shard_map/ppermute | solution.py:605
  56.0 8.1 %collective-permute-start.24 = (bf16[304,128]{1,0:T(8,128)(2,1)S(1)}, bf16[304,128]{1,0:T(8,128)(2,1)S(1)}, u32[]{:S(2)}, u32[]{:S(2)}) collective-permute-start(bf16[304,128]{1,0:T(8,128)(2,1)S(1)} %add_first.1.after_ref.refs_0_), channel_id=1, source_target_pairs={{0,3},{1,2},{2,1},{3,0},{4,28},{5,29},{6,30},{7,31},{8,11},{9,10},... | collective-permute-start | bytes 233480 | tf_op jit(solution)/shard_map/ppermute | solution.py:605
  57.8 6.7 %collective-permute-start.23 = (bf16[304,128]{1,0:T(8,128)(2,1)S(1)}, bf16[304,128]{1,0:T(8,128)(2,1)S(1)}, u32[]{:S(2)}, u32[]{:S(2)}) collective-permute-start(bf16[304,128]{1,0:T(8,128)(2,1)S(1)} %add_first.1.after_ref.refs_0_), channel_id=1, source_target_pairs={{0,2},{1,3},{2,0},{3,1},{4,20},{5,21},{6,22},{7,23},{8,10},{9,11},... | collective-permute-start | bytes 233480 | tf_op jit(solution)/shard_map/ppermute | solution.py:605
  58.5 6.3 %collective-permute-start.22 = (bf16[304,128]{1,0:T(8,128)(2,1)S(1)}, bf16[304,128]{1,0:T(8,128)(2,1)S(1)}, u32[]{:S(2)}, u32[]{:S(2)}) collective-permute-start(bf16[304,128]{1,0:T(8,128)(2,1)S(1)} %add_first.1.after_ref.refs_0_), channel_id=1, source_target_pairs={{0,1},{1,0},{2,3},{3,2},{4,12},{5,13},{6,14},{7,15},{8,9},{9,8},{1... | collective-permute-start | bytes 233480 | tf_op jit(solution)/shard_map/ppermute | solution.py:605
  60.5 7.8 %collective-permute-start.20 = (bf16[8,64,128]{2,1,0:T(8,128)(2,1)S(1)}, bf16[8,64,128]{2,1,0:T(8,128)(2,1)S(1)}, u32[]{:S(2)}, u32[]{:S(2)}) collective-permute-start(bf16[8,64,128]{2,1,0:T(8,128)(2,1)S(1)} %get-tuple-element.105), channel_id=1, source_target_pairs={{1,2},{2,1},{5,6},{6,5},{9,10},{10,9},{13,14},{14,13},{17,18},{18,... | collective-permute-start | bytes 393224 | tf_op jit(solution)/shard_map/ppermute | solution.py:619
  61.2 7.6 %collective-permute-start.21 = (bf16[8,64,128]{2,1,0:T(8,128)(2,1)S(1)}, bf16[8,64,128]{2,1,0:T(8,128)(2,1)S(1)}, u32[]{:S(2)}, u32[]{:S(2)}) collective-permute-start(bf16[8,64,128]{2,1,0:T(8,128)(2,1)S(1)} %get-tuple-element.106), channel_id=1, source_target_pairs={{0,1},{1,0},{2,3},{3,2},{4,5},{5,4},{6,7},{7,6},{8,9},{9,8},{10,11... | collective-permute-start | bytes 393224 | tf_op jit(solution)/shard_map/ppermute | solution.py:620
  64.8 6.0 %collective-permute-start.27 = (bf16[304,128]{1,0:T(8,128)(2,1)S(1)}, bf16[304,128]{1,0:T(8,128)(2,1)S(1)}, u32[]{:S(2)}, u32[]{:S(2)}) collective-permute-start(bf16[304,128]{1,0:T(8,128)(2,1)S(1)} %add_second.1.refs_0_), channel_id=1, source_target_pairs={{0,24},{1,25},{2,26},{3,27},{4,7},{5,6},{6,5},{7,4},{8,16},{9,17},... | collective-permute-start | bytes 233480 | tf_op jit(solution)/shard_map/ppermute | solution.py:605
  65.8 5.1 %collective-permute-start.26 = (bf16[304,128]{1,0:T(8,128)(2,1)S(1)}, bf16[304,128]{1,0:T(8,128)(2,1)S(1)}, u32[]{:S(2)}, u32[]{:S(2)}) collective-permute-start(bf16[304,128]{1,0:T(8,128)(2,1)S(1)} %add_second.1.refs_0_), channel_id=1, source_target_pairs={{0,16},{1,17},{2,18},{3,19},{4,6},{5,7},{6,4},{7,5},{8,24},{9,25},... | collective-permute-start | bytes 233480 | tf_op jit(solution)/shard_map/ppermute | solution.py:605
  66.4 4.6 %collective-permute-start.25 = (bf16[304,128]{1,0:T(8,128)(2,1)S(1)}, bf16[304,128]{1,0:T(8,128)(2,1)S(1)}, u32[]{:S(2)}, u32[]{:S(2)}) collective-permute-start(bf16[304,128]{1,0:T(8,128)(2,1)S(1)} %add_second.1.refs_0_), channel_id=1, source_target_pairs={{0,8},{1,9},{2,10},{3,11},{4,5},{5,4},{6,7},{7,6},{8,0},{9,1},{10,... | collective-permute-start | bytes 233480 | tf_op jit(solution)/shard_map/ppermute | solution.py:605
  71.0 1.7 %collective-permute-start.28 = (bf16[1168,128]{1,0:T(8,128)(2,1)S(1)}, bf16[1168,128]{1,0:T(8,128)(2,1)S(1)}, u32[]{:S(2)}, u32[]{:S(2)}) collective-permute-start(bf16[1168,128]{1,0:T(8,128)(2,1)S(1)} %join.1.own_ref), channel_id=1, source_target_pairs={{0,4},{4,0},{1,5},{5,1},{2,6},{6,2},{3,7},{7,3},{8,12},{12,8},{9,1... | collective-permute-start | bytes 897032 | tf_op jit(solution)/shard_map/ppermute | solution.py:593
  (9 other events, 24.5 us)

commit v4 on v3

--- a/solution.py
+++ b/solution.py
@@ -77,6 +77,12 @@
     return mean, lax.rsqrt(variance + EPSILON)
 
 
+def has_pair():
+    count, me = lax.axis_size("lat"), lax.axis_index("lat")
+    inside = jnp.logical_and(me != 0, me != count - 1)
+    return (me == me, inside) if count % 2 == 0 else (me != count - 1, me != 0)
+
+
 def pick(even, when_even, when_odd):
     return jnp.where(even, when_even, when_odd)
 
@@ -86,18 +92,12 @@
     return jnp.broadcast_to(tile[:, k % 128 : k % 128 + 1].astype(F32), (tile.shape[0], c))
 
 
-def near_rows_kernel(x_ref, gx_ref, gp_ref, sems):
-    height = x_ref.shape[1]
+def near_rows_kernel(top_ref, bottom_ref, gx_ref, gp_ref):
     even = lax.axis_index("lat") % 2 == 0
-    last = jnp.where(even, height - 1, 0)
-    copies = [
-        pltpu.make_async_copy(x_ref.at[:, pl.ds(at, 1)], out, sems.at[i])
-        for i, (at, out) in enumerate(((last, gx_ref), (height - 1 - last, gp_ref)))
-    ]
-    for copy in copies:
-        copy.start()
-    for copy in copies:
-        copy.wait()
+    top, bottom = top_ref[...], bottom_ref[...]
+    paired_x, paired_p = has_pair()
+    gx_ref[...] = pick(paired_x, pick(even, bottom, top), jnp.zeros_like(top))
+    gp_ref[...] = pick(paired_p, pick(even, top, bottom), jnp.zeros_like(top))
 
 
 def far_rows_kernel(x_ref, u_ref, mask_ref, hx_ref, hp_ref, bits_ref):
@@ -109,15 +109,17 @@
         if bits.shape[0] < 128:
             bits = jnp.concatenate([bits, jnp.zeros((128 - bits.shape[0], 128), F32)], 0)
         bits_ref[k] = bits.T[:across]
-    for out, down in ((hx_ref, even), (hp_ref, jnp.logical_not(even))):
+    zero = jnp.zeros((across, c), BF16)
+    for out, down, paired in zip((hx_ref, hp_ref), (even, jnp.logical_not(even)), has_pair()):
         first = jnp.where(down, height - 3, 1)
         edge = jnp.where(down, height - 1, 0)
         for s in range(samples):
-            out[2 * s] = x_ref[s, first]
-            out[2 * s + 1] = x_ref[s, first + 1]
-            out[2 * samples + s] = u_ref[s, edge]
+            out[2 * s] = pick(paired, x_ref[s, first], zero)
+            out[2 * s + 1] = pick(paired, x_ref[s, first + 1], zero)
+            out[2 * samples + s] = pick(paired, u_ref[s, edge], zero)
         for k in range(bits_ref.shape[0]):
-            out[3 * samples + k] = bits_ref[k].astype(BF16)
+            bits = bits_ref[k]
+            out[3 * samples + k] = pick(paired, bits, jnp.zeros_like(bits)).astype(BF16)
 
 
 def masks_kernel(bits_ref, m_ref, count_ref):
@@ -150,33 +152,61 @@
     return masked
 
 
-def conv1_kernel(gp_ref, gx_ref, x_ref, m_ref, count_ref, w_ref, b_ref, a_ref, z_ref, t_ref, st_ref):
+def own_row(inner_ref, outer_ref, s, r, height):
+    if 2 <= r < height - 2:
+        return inner_ref[s, r - 2]
+    return outer_ref[s, r if r < 2 else r - height + 4]
+
+
+def conv1_inner_kernel(x_ref, m_ref, w_ref, b_ref, a_ref, z_ref, t_ref, part_ref):
     samples, height, across, c = x_ref.shape
-    even = lax.axis_index("lat") % 2 == 0
     fill_toeplitz(w_ref, t_ref)
     bias = 0.5 * b_ref[...]
     sums = [jnp.zeros((8, c), F32) for _ in range(2)]
     centre = None
     for s in range(samples):
-
-        def row(r):
-            if r < 0:
-                return pick(even, gp_ref[s, 0], gx_ref[s, 0])
-            if r >= height:
-                return pick(even, gx_ref[s, 0], gp_ref[s, 0])
-            return x_ref[s, r]
-
-        piece = convolve_rows(row, range(0, height, 2), t_ref, across, False)
-        for r in range(height):
-            half = piece(r // 2, r % 2) + bias
+        piece = convolve_rows(lambda r: x_ref[s, r], range(2, height - 2, 2), t_ref, across, False)
+        for i in range(height - 4):
+            half = piece(i // 2, i % 2) + bias
             active = silu(half)
             if centre is None:
                 centre = middle(active)
             active = active - centre
-            a_ref[s, r] = active
-            z_ref[s, r] = half
-            add_moments(sums, active, m_ref[s, r])
+            a_ref[s, i] = active
+            z_ref[s, i] = half
+            add_moments(sums, active, m_ref[s, i + 2])
     rows = [v.sum(0, keepdims=True) for v in sums]
+    part_ref[...] = stats_block([rows[0], rows[1], centre], c)
+
+
+def conv1_outer_kernel(
+    gp_ref, gx_ref, x_ref, m_ref, count_ref, t_ref, b_ref, part_ref, a_ref, z_ref, st_ref
+):
+    samples, height, across, c = x_ref.shape
+    even = lax.axis_index("lat") % 2 == 0
+    bias = 0.5 * b_ref[...]
+    centre = part_ref[2:3]
+
+    def row(r):
+        if r < 0:
+            parts = [pick(even, gp_ref[s, 0], gx_ref[s, 0]) for s in range(samples)]
+        elif r >= height:
+            parts = [pick(even, gx_ref[s, 0], gp_ref[s, 0]) for s in range(samples)]
+        else:
+            parts = [x_ref[s, r] for s in range(samples)]
+        return jnp.concatenate(parts, 0)
+
+    sums = [jnp.zeros((8, c), F32) for _ in range(2)]
+    for slot, start in ((0, 0), (2, height - 2)):
+        piece = convolve_rows(row, (start,), t_ref, across, False)
+        for s in range(samples):
+            for j in range(2):
+                half = piece(s, j) + bias
+                active = silu(half) - centre
+                a_ref[s, slot + j] = active
+                z_ref[s, slot + j] = half
+                add_moments(sums, active, m_ref[s, start + j])
+    rows = [part_ref[i : i + 1] + v.sum(0, keepdims=True) for i, v in enumerate(sums)]
     st_ref[...] = stats_block([rows[0], rows[1], centre, count_ref[0:1]], c)
 
 
@@ -239,7 +269,7 @@
 
 def conv2_kernel(
     pieces,
-    own_ref, a_ref, ah_ref, m_ref, mh_ref, mu_ref, su_ref, k_ref, b_ref, g_ref, t_ref, *refs,
+    own_ref, a_ref, ao_ref, ah_ref, m_ref, mh_ref, mu_ref, su_ref, k_ref, b_ref, g_ref, t_ref, *refs,
 ):
     stats, (n_ref, a2_ref, z2_ref, c1_ref, st2_ref, ext_ref) = gather(refs[:pieces]), refs[pieces:]
     samples, height, across, c = m_ref.shape
@@ -258,7 +288,7 @@
         for i in range(height + 4):
             r = i - 2
             if 0 <= r < height:
-                value, mask = a_ref[s, r], m_ref[s, r]
+                value, mask = own_row(a_ref, ao_ref, s, r, height), m_ref[s, r]
             else:
                 j = i if r < 0 else r - height + 2
                 value, mask = ah_ref[s, j], mh_ref[s, j]
@@ -287,14 +317,14 @@
     )
 
 
-def slopes_kernel(z_ref, z2_ref, m_ref, mh_ref, after_ref, s_ref, s2_ref):
+def slopes_kernel(z_ref, zo_ref, z2_ref, m_ref, mh_ref, after_ref, s_ref, s2_ref):
     samples, height = m_ref.shape[:2]
     for s in range(samples):
         for r in range(-1, height + 1):
             mask = mh_ref[s, 1 if r < 0 else 2]
             if 0 <= r < height:
                 mask = m_ref[s, r]
-                s_ref[s, r] = silu_slope(z_ref[s, r]) * mask
+                s_ref[s, r] = silu_slope(own_row(z_ref, zo_ref, s, r, height)) * mask
             s2_ref[s, r + 1] = silu_slope(z2_ref[s, r + 1]) * mask
 
 
@@ -306,7 +336,7 @@
 
 def back2_kernel(
     pieces,
-    own_ref, st1_ref, c1_ref, a2_ref, s2_ref, mu_ref, muh_ref, m_ref, a_ref, k_ref, g_ref, t_ref, *refs,
+    own_ref, st1_ref, c1_ref, a2_ref, s2_ref, mu_ref, muh_ref, m_ref, a_ref, ao_ref, k_ref, g_ref, t_ref, *refs,
 ):
     stats, (d_ref, dn_ref, c2_ref, st3_ref, ext_ref) = gather(refs[:pieces]), refs[pieces:]
     samples, height, across, c = m_ref.shape
@@ -336,7 +366,7 @@
             dn_ref[s, r] = part
             masked = part * m_ref[s, r]
             sums[0] += fold(masked)
-            sums[1] += fold(masked * a_ref[s, r])
+            sums[1] += fold(masked * own_row(a_ref, ao_ref, s, r, height))
     rows = [v.sum(0, keepdims=True) for v in sums]
     st3_ref[...] = stats_block([rows[0], rows[1], st1_ref[2:3]], c)
 
@@ -399,7 +429,7 @@
 
 def weight1_kernel(
     group, leads, pieces,
-    c1_ref, c2_ref, dn_ref, a_ref, s_ref, x_ref, gx_ref, gp_ref, g_ref, w2_ref, b2_ref, *refs,
+    c1_ref, c2_ref, dn_ref, a_ref, ao_ref, s_ref, x_ref, gx_ref, gp_ref, g_ref, w2_ref, b2_ref, *refs,
 ):
     stats = gather(refs[:pieces])
     d_ref, send_ref, keep_ref, acc_ref = refs[pieces:]
@@ -415,7 +445,7 @@
     bias = jnp.zeros((8, c), F32)
     for s in range(samples):
         for r in range(height):
-            active = a_ref[s, r]
+            active = own_row(a_ref, ao_ref, s, r, height)
             grad = dn_ref[s, r] * scale + (active * by_active + constant)
             d_ref[s, r] = (grad * s_ref[s, r]).astype(BF16)
         grad = d_ref[s]
@@ -469,9 +499,11 @@
 def edge_rows_kernel(d_ref, after_ref, dx_ref, dp_ref):
     samples, height = d_ref.shape[:2]
     even = lax.axis_index("lat") % 2 == 0
-    for s in range(samples):
-        dx_ref[s] = pick(even, d_ref[s, height - 1], d_ref[s, 0])
-        dp_ref[s] = pick(even, d_ref[s, 0], d_ref[s, height - 1])
+    paired_x, paired_p = has_pair()
+    for s in range(samples):
+        top, bottom = d_ref[s, 0], d_ref[s, height - 1]
+        dx_ref[s] = pick(paired_x, pick(even, bottom, top), jnp.zeros_like(top))
+        dp_ref[s] = pick(paired_p, pick(even, top, bottom), jnp.zeros_like(top))
 
 
 def input_grad_kernel(ep_ref, ex_ref, d_ref, u_ref, w_ref, o_ref, done_ref, k_ref):
@@ -611,13 +643,28 @@
     return lax.axis_index("lead")
 
 
-def neighbours(value_x, value_p, axis):
-    n = lax.axis_size(axis)
-    first = [(i, i ^ 1) for i in range(n) if i ^ 1 < n]
-    second = [(i, i + 1) for i in range(1, n - 1, 2)]
-    second += [(j, i) for i, j in second]
-    got_p = lax.ppermute(value_p, axis, second)
-    return lax.ppermute(value_x, axis, first), got_p
+def over_dp_and_lat(value, to):
+    dps, lats = lax.axis_size("dp"), lax.axis_size("lat")
+    pairs = []
+    for dp in range(dps):
+        for lat in range(lats):
+            to_dp, to_lat = to(dp, lat)
+            pairs.append((dp * lats + lat, to_dp * lats + to_lat))
+    return lax.ppermute(value, ("dp", "lat"), pairs)
+
+
+def neighbours(value_x, value_p):
+    lats = lax.axis_size("lat")
+
+    def exchange(value, offset):
+        def to(dp, lat):
+            other = ((lat - offset) ^ 1) + offset if lat >= offset else lats
+            return (dp, other) if other < lats else (dp ^ 1, lat)
+
+        return over_dp_and_lat(value, to)
+
+    got_p = exchange(value_p, 1)
+    return exchange(value_x, 0), got_p
 
 
 def spread(stats):
@@ -625,7 +672,10 @@
     while k < lax.axis_size("dp"):
         blocks = jnp.concatenate([blocks, swap(blocks, "dp", k)], 0)
         k *= 2
-    return [blocks] + [swap(blocks, "lat", k) for k in range(1, lax.axis_size("lat"))]
+    return [blocks] + [
+        over_dp_and_lat(blocks, lambda dp, lat, k=k: (dp ^ 1, lat ^ k))
+        for k in range(1, lax.axis_size("lat"))
+    ]
 
 
 def add_chunks(parts, name, outs=1, waits=(), flops=0):
@@ -725,13 +775,12 @@
     near = call(
         near_rows_kernel,
         (shape(1, BF16), shape(1, BF16)),
-        [pltpu.SemaphoreType.DMA((2,))],
-        (x,),
+        [],
+        (x[:, :1], x[:, height - 1 :]),
         "near_rows",
         conv_flops,
-        spaces=(ANY, ANY),
-    )
-    gx, gp = neighbours(*near, "lat")
+    )
+    gx, gp = neighbours(*near)
     packed = array((3 * samples + slabs, across, c), BF16)
     far_x, far_p, bits = call(
         far_rows_kernel,
@@ -741,14 +790,22 @@
         "far_rows",
         conv_flops,
     )
-    hx, hp = neighbours(far_x, far_p, "lat")
+    hx, hp = neighbours(far_x, far_p)
     wide_mask, count = call(masks_kernel, (shape(height), vector), [], (bits,), "masks", conv_flops)
-    a1, z1, w1t, own1 = call(
-        conv1_kernel,
-        (shape(height), shape(height), weights, vector),
+    a1, z1, w1t, part = call(
+        conv1_inner_kernel,
+        (shape(height - 4), shape(height - 4), weights, vector),
         [],
-        (gp, gx, x, wide_mask, count, conv1_weight, b1),
-        "conv1",
+        (x, wide_mask, conv1_weight, b1),
+        "conv1_inner",
+        4 * conv_flops,
+    )
+    a1o, z1o, own1 = call(
+        conv1_outer_kernel,
+        (shape(4), shape(4), vector),
+        [],
+        (gp, gx, x, wide_mask, count, w1t, b1, part),
+        "conv1_outer",
         16 * conv_flops,
     )
     mu, mu_sum, w2t, w2tt = call(
@@ -772,7 +829,7 @@
         functools.partial(conv2_kernel, len(st1)),
         (shape(height + 2, BF16), shape(height + 2), shape(height + 2), vector, vector),
         [ext(height + 4)],
-        (own1, a1, a1h, wide_mask, halo_mask, mu, mu_sum, w2t, b2, g1, t1, *st1),
+        (own1, a1, a1o, a1h, wide_mask, halo_mask, mu, mu_sum, w2t, b2, g1, t1, *st1),
         "conv2",
         conv_flops,
     )
@@ -781,7 +838,7 @@
         slopes_kernel,
         (shape(height), shape(height + 2)),
         [],
-        (z1, z2, wide_mask, halo_mask),
+        (z1, z1o, z2, wide_mask, halo_mask),
         "slopes",
         conv_flops,
         waits=(st2[0],),
@@ -790,7 +847,7 @@
         functools.partial(back2_kernel, len(st2)),
         (shape(height, BF16), shape(height), vector, vector),
         [ext(height + 2)],
-        (own2, own1, c1, a2, s2, mu, mu_halo, wide_mask, a1, w2tt, g2, t2, *st2),
+        (own2, own1, c1, a2, s2, mu, mu_halo, wide_mask, a1, a1o, w2tt, g2, t2, *st2),
         "conv2_back",
         conv_flops,
     )
@@ -809,14 +866,14 @@
         functools.partial(weight1_kernel, group, leads, len(st3)),
         (shape(height, BF16), chunks, chunks),
         [acc],
-        (c1, c2, dn1, a1, s1, x, gx, gp, g1, w2, bias2, *st3),
+        (c1, c2, dn1, a1, a1o, s1, x, gx, gp, g1, w2, bias2, *st3),
         "conv1_weight_grad",
         conv_flops,
     )
 
     def edges(after):
         rows = call(edge_rows_kernel, (edge, edge), [], (d1,), "edge_rows", waits=(after,))
-        return neighbours(*rows, "lat")[::-1]
+        return neighbours(*rows)[::-1]
 
     def input_grad(rows):
         return call(

time: 74 us -> 70.6 us (0.954)
  starting transfers between devices: 37.8 us -> 32.1 us
  waiting for transfers between devices: 11.7 us -> 14.4 us
    ppermute x14 -> x5, starting transfers between devices: 13.5 us -> 1.07 us  [swap(): lax.ppermute(value, axis, [(i, i ^ k) for i in range(lax.axis_size(axis))])]
    ppermute x6 -> x15, starting transfers between devices: 12.7 us -> 19.5 us  [over_dp_and_lat(): return lax.ppermute(value, ('dp', 'lat'), pairs)]
    ppermute x9, waiting for transfers between devices: 3.61 us -> 6.72 us  [cross(): return lax.ppermute(value, ('lead', 'dp', 'lat'), pairs)]
    ppermute x14 -> x5, waiting for transfers between devices: 7.21 us -> 4.23 us  [swap(): lax.ppermute(value, axis, [(i, i ^ k) for i in range(lax.axis_size(axis))])]
    ppermute x6 -> x15, waiting for transfers between devices: 0.92 us -> 3.43 us  [over_dp_and_lat(): return lax.ppermute(value, ('dp', 'lat'), pairs)]
    unnamed x24 -> x22, local copies, waits for them, and re-layouts: 1.42 us -> 0.29 us
    slice x0 -> x1, local copies, waits for them, and re-layouts: none -> 1 us  [shards(): x[:, height - 1:]]
    pallas_call x20 -> x21, Pallas kernels: 21.7 us -> 21.5 us  [call(): pl.pallas_call(kernel, out_shape=outs, in_specs=(ins or [spaces[0]] * len...]
  transfers between devices with their start and end apart: 29 -> 29, of which waited for: 19 -> 14; matrix products, arithmetic and copies ran while one was open for 0% -> 0% of each run, Pallas kernels for 17% -> 18%
where the time goes in v4:
time: 70.6 us; the launch traced here: 70.4 us
  starting transfers between devices  32.1 us (45%)
  Pallas kernels  21.5 us (30%)
  waiting for transfers between devices  14.4 us (20%)
  local copies, waits for them, and re-layouts  1.29 us (2%)
  between operations  1.13 us (2%)
    pallas_call x21, Pallas kernels, call(): pl.pallas_call(kernel, out_shape=outs, in_specs=(ins or [spaces[0]] * len...  21.5 us
    ppermute x15, starting transfers between devices, over_dp_and_lat(): return lax.ppermute(value, ('dp', 'lat'), pairs)  19.5 us
    ppermute x9, starting transfers between devices, cross(): return lax.ppermute(value, ('lead', 'dp', 'lat'), pairs)  11.6 us
    ppermute x9, waiting for transfers between devices, cross(): return lax.ppermute(value, ('lead', 'dp', 'lat'), pairs)  6.72 us
    ppermute x5, waiting for transfers between devices, swap(): lax.ppermute(value, axis, [(i, i ^ k) for i in range(lax.axis_size(axis))])  4.23 us
    ppermute x15, waiting for transfers between devices, over_dp_and_lat(): return lax.ppermute(value, ('dp', 'lat'), pairs)  3.43 us
  transfers between devices with their start and end apart: 29, of which 14 were waited for; matrix products, arithmetic and copies ran while one was open for 0% of the time, Pallas kernels for 18%

profile of v4, /device:TPU:0, one launch (start us, length us, event | category | flops | bytes accessed | tf_op | source)
XLA Modules:
  0.0 70.4 jit_solution(9516847315292062639)
XLA Ops:
  0.6 1.0 %fusion = (bf16[8,1,64,128]{3,2,1,0:T(8,128)(2,1)S(1)}, bf16[8,1,64,128]{3,2,1,0:T(8,128)(2,1)S(1)}) fusion(bf16[8,8,64,128]{3,2,1,0:T(8,128)(2,1)} %bitcast.22), kind=kLoop, calls=%fused_computation.3 | loop fusion | bytes 524288 | tf_op jit(solution)/shard_map/slice | solution.py:779
  2.3 4.1 %collective-permute-start.1 = (bf16[8,1,64,128]{3,2,1,0:T(8,128)(2,1)S(1)}, bf16[8,1,64,128]{3,2,1,0:T(8,128)(2,1)S(1)}, u32[]{:S(2)}, u32[]{:S(2)}) collective-permute-start(bf16[8,1,64,128]{3,2,1,0:T(8,128)(2,1)S(1)} %get-tuple-element.69), channel_id=1, source_target_pairs={{0,1},{1,0},{2,3},{3,2},{4,5},{5,4},{6,7},{7,6},{8,9},{9,8},{10,11... | collective-permute-start | bytes 393224 | tf_op jit(solution)/shard_map/ppermute | solution.py:653
  6.6 1.6 %collective-permute-start.3 = (bf16[25,64,128]{2,1,0:T(8,128)(2,1)S(1)}, bf16[25,64,128]{2,1,0:T(8,128)(2,1)S(1)}, u32[]{:S(2)}, u32[]{:S(2)}) collective-permute-start(bf16[25,64,128]{2,1,0:T(8,128)(2,1)S(1)} %get-tuple-element.79), channel_id=1, source_target_pairs={{0,1},{1,0},{2,3},{3,2},{4,5},{5,4},{6,7},{7,6},{8,9},{9,8},{10,11... | collective-permute-start | bytes 1228808 | tf_op jit(solution)/shard_map/ppermute | solution.py:653
  9.3 1.2 %conv1_inner.1 = (f32[8,4,64,128]{3,2,1,0:T(8,128)S(1)}, f32[8,4,64,128]{3,2,1,0:T(8,128)S(1)}, bf16[3,512,256]{2,1,0:T(8,128)(2,1)S(1)}, f32[8,128]{1,0:T(8,128)S(1)}) custom-call(bf16[8,8,64,128]{3,2,1,0:T(8,128)(2,1)S(1)} %bitcast.24, f32[8,8,64,128]{3,2,1,0:T(8,128)S(1)} %get-tuple-element.71.m_ref, bf16[3,3,128,128]{3,2,1,0:T(8,128)(2,1)S(1)} %copy-done.9, ...), custom_call_target="tpu_custom_call" | custom-call | flops 4831838208 | bytes 3441152 | tf_op jit(solution)/shard_map/conv1_inner/pallas_call | solution.py:611
  10.5 1.2 %conv1_outer.1 = (f32[8,4,64,128]{3,2,1,0:T(8,128)S(1)}, f32[8,4,64,128]{3,2,1,0:T(8,128)S(1)}, f32[8,128]{1,0:T(8,128)S(1)}) custom-call(bf16[8,1,64,128]{3,2,1,0:T(8,128)(2,1)S(1)} %collective-permute-done.gp_ref, bf16[8,1,64,128]{3,2,1,0:T(8,128)(2,1)S(1)} %collective-permute-done.1.gx_ref, bf16[8,8,64,128]{3,2,1,0:T(8,128)(2,1)S(1)} %bitcast.25, ...), custom_call_target="tpu_custom_call" | custom-call | flops 19327352832 | bytes 4203008 | tf_op jit(solution)/shard_map/conv1_outer/pallas_call | solution.py:611
  12.9 2.5 %collective-permute-start.7 = (f32[2,8,128]{2,1,0:T(8,128)S(1)}, f32[2,8,128]{2,1,0:T(8,128)S(1)}, u32[]{:S(2)}, u32[]{:S(2)}) collective-permute-start(f32[2,8,128]{2,1,0:T(8,128)S(1)} %pad_maximum_fusion.refs_0_), channel_id=1, source_target_pairs={{0,7},{1,6},{2,5},{3,4},{4,3},{5,2},{6,1},{7,0},{8,15},{9,14},{10,... | collective-permute-start | bytes 24584 | tf_op jit(solution)/shard_map/ppermute | solution.py:653
  15.6 1.1 %collective-permute-start.5 = (f32[2,8,128]{2,1,0:T(8,128)S(1)}, f32[2,8,128]{2,1,0:T(8,128)S(1)}, u32[]{:S(2)}, u32[]{:S(2)}) collective-permute-start(f32[2,8,128]{2,1,0:T(8,128)S(1)} %pad_maximum_fusion.refs_0_), channel_id=1, source_target_pairs={{0,5},{1,4},{2,7},{3,6},{4,1},{5,0},{6,3},{7,2},{8,13},{9,12},{10,... | collective-permute-start | bytes 24584 | tf_op jit(solution)/shard_map/ppermute | solution.py:653
  16.8 1.7 %collective-permute-done.3.hx_ref = bf16[25,64,128]{2,1,0:T(8,128)(2,1)S(1)} collective-permute-done((bf16[25,64,128]{2,1,0:T(8,128)(2,1)S(1)}, bf16[25,64,128]{2,1,0:T(8,128)(2,1)S(1)}, u32[]{:S(2)}, u32[]{:S(2)}) %collective-permute-start.3) | collective-permute-done | bytes 409632 | tf_op jit(solution)/shard_map/ppermute | solution.py:653
  18.5 1.1 %conv1_edges.1 = (f32[8,4,64,128]{3,2,1,0:T(8,128)S(1)}, f32[8,4,64,128]{3,2,1,0:T(8,128)S(1)}, f32[8,2,64,128]{3,2,1,0:T(8,128)S(1)}) custom-call(bf16[25,64,128]{2,1,0:T(8,128)(2,1)S(1)} %collective-permute-done.2.hp_ref, bf16[25,64,128]{2,1,0:T(8,128)(2,1)S(1)} %collective-permute-done.3.hx_ref, bf16[8,1,64,128]{3,2,1,0:T(8,128)(2,1)S(1)} %collective-permute-done.gp_ref, ...), custom_call_target="tpu_custom_call" | custom-call | flops 603979776 | bytes 2920960 | tf_op jit(solution)/shard_map/conv1_edges/pallas_call | solution.py:611
  19.7 3.2 %conv2.1 = (bf16[8,10,64,128]{3,2,1,0:T(8,128)(2,1)S(1)}, f32[8,10,64,128]{3,2,1,0:T(8,128)S(1)}, f32[8,10,64,128]{3,2,1,0:T(8,128)S(1)}, f32[8,128]{1,0:T(8,128)S(1)}, f32[8,128]{1,0:T(8,128)S(1)}) custom-call(f32[8,128]{1,0:T(8,128)S(1)} %get-tuple-element.75.st_ref.own_ref.st1_ref, f32[8,4,64,128]{3,2,1,0:T(8,128)S(1)} %get-tuple-element.76.a_ref, ...), custom_call_target="tpu_custom_call" | custom-call | flops 1207959552 | bytes 9217536 | tf_op jit(solution)/shard_map/conv2/pallas_call | solution.py:611
  23.2 1.0 %collective-permute-done.8 = f32[1,8,128]{2,1,0:T(8,128)S(1)} collective-permute-done((f32[1,8,128]{2,1,0:T(8,128)S(1)}, f32[1,8,128]{2,1,0:T(8,128)S(1)}, u32[]{:S(2)}, u32[]{:S(2)}) %collective-permute-start.8) | collective-permute-done | bytes 4128 | tf_op jit(solution)/shard_map/ppermute | solution.py:625
  24.2 3.2 %collective-permute-start.11 = (f32[2,8,128]{2,1,0:T(8,128)S(1)}, f32[2,8,128]{2,1,0:T(8,128)S(1)}, u32[]{:S(2)}, u32[]{:S(2)}) collective-permute-start(f32[2,8,128]{2,1,0:T(8,128)S(1)} %pad_maximum_fusion.1.after_ref.refs_0_), channel_id=1, source_target_pairs={{0,7},{1,6},{2,5},{3,4},{4,3},{5,2},{6,1},{7,0},{8,15},{9,14},{10,... | collective-permute-start | bytes 24584 | tf_op jit(solution)/shard_map/ppermute | solution.py:653
  28.1 1.6 %slopes.1 = (f32[8,8,64,128]{3,2,1,0:T(8,128)S(1)}, f32[8,10,64,128]{3,2,1,0:T(8,128)S(1)}) custom-call(f32[8,4,64,128]{3,2,1,0:T(8,128)S(1)} %get-tuple-element.88.z_ref, f32[8,4,64,128]{3,2,1,0:T(8,128)S(1)} %get-tuple-element.89.zo_ref, f32[8,10,64,128]{3,2,1,0:T(8,128)S(1)} %get-tuple-element.90.z2_ref, f32[8,8,64,128]{3,2,1,0:T(8,128)S(1)} %get-tuple-element.71.m_ref, ...), custom_call_target="tpu_custom_call" | custom-call | flops 1207959552 | bytes 7864320 | tf_op jit(solution)/shard_map/slopes/pallas_call | solution.py:611
  29.7 1.7 %collective-permute-done.10.refs_2_ = f32[2,8,128]{2,1,0:T(8,128)S(1)} collective-permute-done((f32[2,8,128]{2,1,0:T(8,128)S(1)}, f32[2,8,128]{2,1,0:T(8,128)S(1)}, u32[]{:S(2)}, u32[]{:S(2)}) %collective-permute-start.10) | collective-permute-done | bytes 8224 | tf_op jit(solution)/shard_map/ppermute | solution.py:653
  31.3 2.5 %conv2_back.1 = (bf16[8,8,64,128]{3,2,1,0:T(8,128)(2,1)S(1)}, f32[8,8,64,128]{3,2,1,0:T(8,128)S(1)}, f32[8,128]{1,0:T(8,128)S(1)}, f32[8,128]{1,0:T(8,128)S(1)}) custom-call(f32[8,128]{1,0:T(8,128)S(1)} %get-tuple-element.86.own_ref, f32[8,128]{1,0:T(8,128)S(1)} %get-tuple-element.75.st_ref.own_ref.st1_ref, f32[8,128]{1,0:T(8,128)S(1)} %get-tuple-element.87.c1_ref, ...), custom_call_target="tpu_custom_call" | custom-call | flops 1207959552 | bytes 12891136 | tf_op jit(solution)/shard_map/conv2_back/pallas_call | solution.py:611
  35.0 1.7 %collective-permute-start.15 = (f32[2,8,128]{2,1,0:T(8,128)S(1)}, f32[2,8,128]{2,1,0:T(8,128)S(1)}, u32[]{:S(2)}, u32[]{:S(2)}) collective-permute-start(f32[2,8,128]{2,1,0:T(8,128)S(1)} %pad_maximum_fusion.2.after_ref.refs_0_), channel_id=1, source_target_pairs={{0,7},{1,6},{2,5},{3,4},{4,3},{5,2},{6,1},{7,0},{8,15},{9,14},{10,... | collective-permute-start | bytes 24584 | tf_op jit(solution)/shard_map/ppermute | solution.py:653
  36.8 2.3 %collective-permute-start.13 = (f32[2,8,128]{2,1,0:T(8,128)S(1)}, f32[2,8,128]{2,1,0:T(8,128)S(1)}, u32[]{:S(2)}, u32[]{:S(2)}) collective-permute-start(f32[2,8,128]{2,1,0:T(8,128)S(1)} %pad_maximum_fusion.2.after_ref.refs_0_), channel_id=1, source_target_pairs={{0,5},{1,4},{2,7},{3,6},{4,1},{5,0},{6,3},{7,2},{8,13},{9,12},{10,... | collective-permute-start | bytes 24584 | tf_op jit(solution)/shard_map/ppermute | solution.py:653
  39.1 1.8 %conv2_weight_grad.1 = (bf16[1152,128]{1,0:T(8,128)(2,1)S(1)}, f32[8,128]{1,0:T(8,128)S(1)}) custom-call(bf16[8,10,64,128]{3,2,1,0:T(8,128)(2,1)S(1)} %get-tuple-element.97.n_ref, bf16[8,8,64,128]{3,2,1,0:T(8,128)(2,1)S(1)} %get-tuple-element.98.d_ref, f32[2,8,128]{2,1,0:T(8,128)S(1)} %pad_maximum_fusion.2.after_ref.refs_0_), custom_call_target="tpu_custom_call" | custom-call | flops 1207959552 | bytes 2359296 | tf_op jit(solution)/shard_map/conv2_weight_grad/pallas_call | solution.py:611
  40.9 2.2 %conv1_weight_grad.1 = (bf16[8,8,64,128]{3,2,1,0:T(8,128)(2,1)S(1)}, bf16[4,304,128]{2,1,0:T(8,128)(2,1)S(1)}, bf16[4,304,128]{2,1,0:T(8,128)(2,1)S(1)}) custom-call(f32[8,128]{1,0:T(8,128)S(1)} %get-tuple-element.87.c1_ref, f32[8,128]{1,0:T(8,128)S(1)} %get-tuple-element.94.c2_ref, f32[8,8,64,128]{3,2,1,0:T(8,128)S(1)} %get-tuple-element.95.dn_ref, ...), custom_call_target="tpu_custom_call" | custom-call | flops 1207959552 | bytes 7942656 | tf_op jit(solution)/shard_map/conv1_weight_grad/pallas_call | solution.py:611
  43.4 1.4 %collective-permute-done.16.refs_1_ = bf16[4,304,128]{2,1,0:T(8,128)(2,1)S(1)} collective-permute-done((bf16[4,304,128]{2,1,0:T(8,128)(2,1)S(1)}, bf16[4,304,128]{2,1,0:T(8,128)(2,1)S(1)}, u32[]{:S(2)}, u32[]{:S(2)}) %collective-permute-start.16) | collective-permute-done | bytes 311328 | tf_op jit(solution)/shard_map/ppermute | solution.py:625
  44.9 2.5 %collective-permute-start.17 = (bf16[304,128]{1,0:T(8,128)(2,1)S(1)}, bf16[304,128]{1,0:T(8,128)(2,1)S(1)}, u32[]{:S(2)}, u32[]{:S(2)}) collective-permute-start(bf16[304,128]{1,0:T(8,128)(2,1)S(1)} %get-tuple-element.107), channel_id=1, source_target_pairs={{0,24},{1,25},{2,26},{3,27},{4,7},{5,6},{6,5},{7,4},{8,16},{9,17},... | collective-permute-start | bytes 233480 | tf_op jit(solution)/shard_map/ppermute | solution.py:637
  48.4 1.1 %output.1 = (bf16[8,8,64,128]{3,2,1,0:T(8,128)(2,1)}, f32[8,128]{1,0:T(8,128)S(1)}) custom-call(bf16[8,8,64,128]{3,2,1,0:T(8,128)(2,1)S(1)} %bitcast.28, f32[8,10,64,128]{3,2,1,0:T(8,128)S(1)} %get-tuple-element.85.a2_ref, f32[8,8,64,128]{3,2,1,0:T(8,128)S(1)} %get-tuple-element.71.m_ref, f32[8,128]{1,0:T(8,128)S(1)} %get-tuple-element.94.c2_ref, ...), custom_call_target="tpu_custom_call" | custom-call | flops 603979776 | bytes 5771264 | tf_op jit(solution)/shard_map/output/pallas_call | solution.py:611
  50.2 1.6 %collective-permute-done.18.refs_2_ = bf16[304,128]{1,0:T(8,128)(2,1)S(1)} collective-permute-done((bf16[304,128]{1,0:T(8,128)(2,1)S(1)}, bf16[304,128]{1,0:T(8,128)(2,1)S(1)}, u32[]{:S(2)}, u32[]{:S(2)}) %collective-permute-start.18) | collective-permute-done | bytes 77856 | tf_op jit(solution)/shard_map/ppermute | solution.py:637
  52.3 1.9 %collective-permute-start.24 = (bf16[304,128]{1,0:T(8,128)(2,1)S(1)}, bf16[304,128]{1,0:T(8,128)(2,1)S(1)}, u32[]{:S(2)}, u32[]{:S(2)}) collective-permute-start(bf16[304,128]{1,0:T(8,128)(2,1)S(1)} %add_first.1.after_ref.refs_0_), channel_id=1, source_target_pairs={{0,3},{1,2},{2,1},{3,0},{4,28},{5,29},{6,30},{7,31},{8,11},{9,10},... | collective-permute-start | bytes 233480 | tf_op jit(solution)/shard_map/ppermute | solution.py:637
  55.1 1.7 %collective-permute-start.22 = (bf16[304,128]{1,0:T(8,128)(2,1)S(1)}, bf16[304,128]{1,0:T(8,128)(2,1)S(1)}, u32[]{:S(2)}, u32[]{:S(2)}) collective-permute-start(bf16[304,128]{1,0:T(8,128)(2,1)S(1)} %add_first.1.after_ref.refs_0_), channel_id=1, source_target_pairs={{0,1},{1,0},{2,3},{3,2},{4,12},{5,13},{6,14},{7,15},{8,9},{9,8},{1... | collective-permute-start | bytes 233480 | tf_op jit(solution)/shard_map/ppermute | solution.py:637
  56.9 1.2 %collective-permute-start.21 = (bf16[8,64,128]{2,1,0:T(8,128)(2,1)S(1)}, bf16[8,64,128]{2,1,0:T(8,128)(2,1)S(1)}, u32[]{:S(2)}, u32[]{:S(2)}) collective-permute-start(bf16[8,64,128]{2,1,0:T(8,128)(2,1)S(1)} %get-tuple-element.112), channel_id=1, source_target_pairs={{0,1},{1,0},{2,3},{3,2},{4,5},{5,4},{6,7},{7,6},{8,9},{9,8},{10,11... | collective-permute-start | bytes 393224 | tf_op jit(solution)/shard_map/ppermute | solution.py:653
  58.7 2.5 %collective-permute-done.23.refs_2_ = bf16[304,128]{1,0:T(8,128)(2,1)S(1)} collective-permute-done((bf16[304,128]{1,0:T(8,128)(2,1)S(1)}, bf16[304,128]{1,0:T(8,128)(2,1)S(1)}, u32[]{:S(2)}, u32[]{:S(2)}) %collective-permute-start.23) | collective-permute-done | bytes 77856 | tf_op jit(solution)/shard_map/ppermute | solution.py:637
  61.3 1.4 %collective-permute-start.27 = (bf16[304,128]{1,0:T(8,128)(2,1)S(1)}, bf16[304,128]{1,0:T(8,128)(2,1)S(1)}, u32[]{:S(2)}, u32[]{:S(2)}) collective-permute-start(bf16[304,128]{1,0:T(8,128)(2,1)S(1)} %add_second.1.refs_0_), channel_id=1, source_target_pairs={{0,24},{1,25},{2,26},{3,27},{4,7},{5,6},{6,5},{7,4},{8,16},{9,17},... | collective-permute-start | bytes 233480 | tf_op jit(solution)/shard_map/ppermute | solution.py:637
  63.2 1.6 %collective-permute-start.25 = (bf16[304,128]{1,0:T(8,128)(2,1)S(1)}, bf16[304,128]{1,0:T(8,128)(2,1)S(1)}, u32[]{:S(2)}, u32[]{:S(2)}) collective-permute-start(bf16[304,128]{1,0:T(8,128)(2,1)S(1)} %add_second.1.refs_0_), channel_id=1, source_target_pairs={{0,8},{1,9},{2,10},{3,11},{4,5},{5,4},{6,7},{7,6},{8,0},{9,1},{10,... | collective-permute-start | bytes 233480 | tf_op jit(solution)/shard_map/ppermute | solution.py:637
  64.9 1.9 %conv1_back.1 = (bf16[8,8,64,128]{3,2,1,0:T(8,128)(2,1)S(1)}, f32[8,128]{1,0:T(8,128)S(1)}) custom-call(bf16[8,64,128]{2,1,0:T(8,128)(2,1)S(1)} %collective-permute-done.20.ep_ref, bf16[8,64,128]{2,1,0:T(8,128)(2,1)S(1)} %collective-permute-done.21.ex_ref, bf16[8,8,64,128]{3,2,1,0:T(8,128)(2,1)S(1)} %get-tuple-element.106.d_ref, ...), custom_call_target="tpu_custom_call" | custom-call | flops 1207959552 | bytes 2654208 | tf_op jit(solution)/shard_map/conv1_back/pallas_call | solution.py:611
  67.8 1.2 %leave.1 = (bf16[8,8,64,128]{3,2,1,0:T(8,128)(2,1)}, f32[1152,128]{1,0:T(8,128)}, f32[1152,128]{1,0:T(8,128)}) custom-call(bf16[8,8,64,128]{3,2,1,0:T(8,128)(2,1)S(1)} %get-tuple-element.113.grad_ref, bf16[1168,128]{1,0:T(8,128)(2,1)S(1)} %join.1.own_ref), custom_call_target="tpu_custom_call" | custom-call | bytes 1347584 | tf_op jit(solution)/shard_map/leave/pallas_call | solution.py:611
  69.3 0.9 %finish.1 = (f32[1152,128]{1,0:T(8,128)}, f32[1152,128]{1,0:T(8,128)}, f32[1,128]{1,0:T(1,128)}, f32[1,128]{1,0:T(1,128)}, f32[1,128]{1,0:T(1,128)}, /*index=5*/...) custom-call(bf16[1168,128]{1,0:T(8,128)(2,1)S(1)} %join.1.own_ref, ...), custom_call_target="tpu_custom_call", output_to_operand_aliasing={{0}: (2, {}), {1}: (3, {})} | custom-call | bytes 1777664 | tf_op jit(solution)/shard_map/finish/pallas_call | solution.py:611
  (73 shorter events, 11.6 us)
Async XLA Ops:
  1.8 8.7 %collective-permute-start = (bf16[8,1,64,128]{3,2,1,0:T(8,128)(2,1)S(1)}, bf16[8,1,64,128]{3,2,1,0:T(8,128)(2,1)S(1)}, u32[]{:S(2)}, u32[]{:S(2)}) collective-permute-start(bf16[8,1,64,128]{3,2,1,0:T(8,128)(2,1)S(1)} %get-tuple-element.68), channel_id=1, source_target_pairs={{0,4},{1,2},{2,1},{3,7},{4,0},{5,6},{6,5},{7,3},{8,12},{9,10},{10,... | collective-permute-start | bytes 393224 | tf_op jit(solution)/shard_map/ppermute | solution.py:653
  2.3 8.2 %collective-permute-start.1 = (bf16[8,1,64,128]{3,2,1,0:T(8,128)(2,1)S(1)}, bf16[8,1,64,128]{3,2,1,0:T(8,128)(2,1)S(1)}, u32[]{:S(2)}, u32[]{:S(2)}) collective-permute-start(bf16[8,1,64,128]{3,2,1,0:T(8,128)(2,1)S(1)} %get-tuple-element.69), channel_id=1, source_target_pairs={{0,1},{1,0},{2,3},{3,2},{4,5},{5,4},{6,7},{7,6},{8,9},{9,8},{10,11... | collective-permute-start | bytes 393224 | tf_op jit(solution)/shard_map/ppermute | solution.py:653
  6.6 10.2 %collective-permute-start.2 = (bf16[25,64,128]{2,1,0:T(8,128)(2,1)S(1)}, bf16[25,64,128]{2,1,0:T(8,128)(2,1)S(1)}, u32[]{:S(2)}, u32[]{:S(2)}) collective-permute-start(bf16[25,64,128]{2,1,0:T(8,128)(2,1)S(1)} %get-tuple-element.78), channel_id=1, source_target_pairs={{0,4},{1,2},{2,1},{3,7},{4,0},{5,6},{6,5},{7,3},{8,12},{9,10},{10,... | collective-permute-start | bytes 1228808 | tf_op jit(solution)/shard_map/ppermute | solution.py:653
  6.6 11.9 %collective-permute-start.3 = (bf16[25,64,128]{2,1,0:T(8,128)(2,1)S(1)}, bf16[25,64,128]{2,1,0:T(8,128)(2,1)S(1)}, u32[]{:S(2)}, u32[]{:S(2)}) collective-permute-start(bf16[25,64,128]{2,1,0:T(8,128)(2,1)S(1)} %get-tuple-element.79), channel_id=1, source_target_pairs={{0,1},{1,0},{2,3},{3,2},{4,5},{5,4},{6,7},{7,6},{8,9},{9,8},{10,11... | collective-permute-start | bytes 1228808 | tf_op jit(solution)/shard_map/ppermute | solution.py:653
  11.7 1.2 %collective-permute-start.4 = (f32[1,8,128]{2,1,0:T(8,128)S(1)}, f32[1,8,128]{2,1,0:T(8,128)S(1)}, u32[]{:S(2)}, u32[]{:S(2)}) collective-permute-start(f32[1,8,128]{2,1,0:T(8,128)S(1)} %bitcast.29), channel_id=1, source_target_pairs={{0,4},{4,0},{1,5},{5,1},{2,6},{6,2},{3,7},{7,3},{8,12},{12,8},{9,1... | collective-permute-start | bytes 12296 | tf_op jit(solution)/shard_map/ppermute | solution.py:625
  12.2 7.5 %copy-start.1 = (f32[128]{0:T(128)S(1)}, f32[128]{0:T(128)}, u32[]{:S(2)}) copy-start(f32[128]{0:T(128)} %param.16) | copy-start | bytes 1540
  12.2 7.5 %copy-start.3 = (f32[128]{0:T(128)S(1)}, f32[128]{0:T(128)}, u32[]{:S(2)}) copy-start(f32[128]{0:T(128)} %param.19) | copy-start | bytes 1540
  12.2 7.5 %copy-start.4 = (f32[128]{0:T(128)S(1)}, f32[128]{0:T(128)}, u32[]{:S(2)}) copy-start(f32[128]{0:T(128)} %param.17) | copy-start | bytes 1540
  12.9 6.8 %collective-permute-start.7 = (f32[2,8,128]{2,1,0:T(8,128)S(1)}, f32[2,8,128]{2,1,0:T(8,128)S(1)}, u32[]{:S(2)}, u32[]{:S(2)}) collective-permute-start(f32[2,8,128]{2,1,0:T(8,128)S(1)} %pad_maximum_fusion.refs_0_), channel_id=1, source_target_pairs={{0,7},{1,6},{2,5},{3,4},{4,3},{5,2},{6,1},{7,0},{8,15},{9,14},{10,... | collective-permute-start | bytes 24584 | tf_op jit(solution)/shard_map/ppermute | solution.py:653
  15.4 4.2 %collective-permute-start.6 = (f32[2,8,128]{2,1,0:T(8,128)S(1)}, f32[2,8,128]{2,1,0:T(8,128)S(1)}, u32[]{:S(2)}, u32[]{:S(2)}) collective-permute-start(f32[2,8,128]{2,1,0:T(8,128)S(1)} %pad_maximum_fusion.refs_0_), channel_id=1, source_target_pairs={{0,6},{1,7},{2,4},{3,5},{4,2},{5,3},{6,0},{7,1},{8,14},{9,15},{10,... | collective-permute-start | bytes 24584 | tf_op jit(solution)/shard_map/ppermute | solution.py:653
  15.6 4.0 %collective-permute-start.5 = (f32[2,8,128]{2,1,0:T(8,128)S(1)}, f32[2,8,128]{2,1,0:T(8,128)S(1)}, u32[]{:S(2)}, u32[]{:S(2)}) collective-permute-start(f32[2,8,128]{2,1,0:T(8,128)S(1)} %pad_maximum_fusion.refs_0_), channel_id=1, source_target_pairs={{0,5},{1,4},{2,7},{3,6},{4,1},{5,0},{6,3},{7,2},{8,13},{9,12},{10,... | collective-permute-start | bytes 24584 | tf_op jit(solution)/shard_map/ppermute | solution.py:653
  22.9 1.2 %collective-permute-start.8 = (f32[1,8,128]{2,1,0:T(8,128)S(1)}, f32[1,8,128]{2,1,0:T(8,128)S(1)}, u32[]{:S(2)}, u32[]{:S(2)}) collective-permute-start(f32[1,8,128]{2,1,0:T(8,128)S(1)} %bitcast.31), channel_id=1, source_target_pairs={{0,4},{4,0},{1,5},{5,1},{2,6},{6,2},{3,7},{7,3},{8,12},{12,8},{9,1... | collective-permute-start | bytes 12296 | tf_op jit(solution)/shard_map/ppermute | solution.py:625
  24.2 5.5 %collective-permute-start.11 = (f32[2,8,128]{2,1,0:T(8,128)S(1)}, f32[2,8,128]{2,1,0:T(8,128)S(1)}, u32[]{:S(2)}, u32[]{:S(2)}) collective-permute-start(f32[2,8,128]{2,1,0:T(8,128)S(1)} %pad_maximum_fusion.1.after_ref.refs_0_), channel_id=1, source_target_pairs={{0,7},{1,6},{2,5},{3,4},{4,3},{5,2},{6,1},{7,0},{8,15},{9,14},{10,... | collective-permute-start | bytes 24584 | tf_op jit(solution)/shard_map/ppermute | solution.py:653
  27.3 4.0 %collective-permute-start.10 = (f32[2,8,128]{2,1,0:T(8,128)S(1)}, f32[2,8,128]{2,1,0:T(8,128)S(1)}, u32[]{:S(2)}, u32[]{:S(2)}) collective-permute-start(f32[2,8,128]{2,1,0:T(8,128)S(1)} %pad_maximum_fusion.1.after_ref.refs_0_), channel_id=1, source_target_pairs={{0,6},{1,7},{2,4},{3,5},{4,2},{5,3},{6,0},{7,1},{8,14},{9,15},{10,... | collective-permute-start | bytes 24584 | tf_op jit(solution)/shard_map/ppermute | solution.py:653
  27.3 4.0 %collective-permute-start.9 = (f32[2,8,128]{2,1,0:T(8,128)S(1)}, f32[2,8,128]{2,1,0:T(8,128)S(1)}, u32[]{:S(2)}, u32[]{:S(2)}) collective-permute-start(f32[2,8,128]{2,1,0:T(8,128)S(1)} %pad_maximum_fusion.1.after_ref.refs_0_), channel_id=1, source_target_pairs={{0,5},{1,4},{2,7},{3,6},{4,1},{5,0},{6,3},{7,2},{8,13},{9,12},{10,... | collective-permute-start | bytes 24584 | tf_op jit(solution)/shard_map/ppermute | solution.py:653
  33.8 1.2 %collective-permute-start.12 = (f32[1,8,128]{2,1,0:T(8,128)S(1)}, f32[1,8,128]{2,1,0:T(8,128)S(1)}, u32[]{:S(2)}, u32[]{:S(2)}) collective-permute-start(f32[1,8,128]{2,1,0:T(8,128)S(1)} %bitcast.33), channel_id=1, source_target_pairs={{0,4},{4,0},{1,5},{5,1},{2,6},{6,2},{3,7},{7,3},{8,12},{12,8},{9,1... | collective-permute-start | bytes 12296 | tf_op jit(solution)/shard_map/ppermute | solution.py:625
  35.0 5.9 %collective-permute-start.15 = (f32[2,8,128]{2,1,0:T(8,128)S(1)}, f32[2,8,128]{2,1,0:T(8,128)S(1)}, u32[]{:S(2)}, u32[]{:S(2)}) collective-permute-start(f32[2,8,128]{2,1,0:T(8,128)S(1)} %pad_maximum_fusion.2.after_ref.refs_0_), channel_id=1, source_target_pairs={{0,7},{1,6},{2,5},{3,4},{4,3},{5,2},{6,1},{7,0},{8,15},{9,14},{10,... | collective-permute-start | bytes 24584 | tf_op jit(solution)/shard_map/ppermute | solution.py:653
  36.7 4.2 %collective-permute-start.14 = (f32[2,8,128]{2,1,0:T(8,128)S(1)}, f32[2,8,128]{2,1,0:T(8,128)S(1)}, u32[]{:S(2)}, u32[]{:S(2)}) collective-permute-start(f32[2,8,128]{2,1,0:T(8,128)S(1)} %pad_maximum_fusion.2.after_ref.refs_0_), channel_id=1, source_target_pairs={{0,6},{1,7},{2,4},{3,5},{4,2},{5,3},{6,0},{7,1},{8,14},{9,15},{10,... | collective-permute-start | bytes 24584 | tf_op jit(solution)/shard_map/ppermute | solution.py:653
  36.8 4.2 %collective-permute-start.13 = (f32[2,8,128]{2,1,0:T(8,128)S(1)}, f32[2,8,128]{2,1,0:T(8,128)S(1)}, u32[]{:S(2)}, u32[]{:S(2)}) collective-permute-start(f32[2,8,128]{2,1,0:T(8,128)S(1)} %pad_maximum_fusion.2.after_ref.refs_0_), channel_id=1, source_target_pairs={{0,5},{1,4},{2,7},{3,6},{4,1},{5,0},{6,3},{7,2},{8,13},{9,12},{10,... | collective-permute-start | bytes 24584 | tf_op jit(solution)/shard_map/ppermute | solution.py:653
  43.1 1.7 %collective-permute-start.16 = (bf16[4,304,128]{2,1,0:T(8,128)(2,1)S(1)}, bf16[4,304,128]{2,1,0:T(8,128)(2,1)S(1)}, u32[]{:S(2)}, u32[]{:S(2)}) collective-permute-start(bf16[4,304,128]{2,1,0:T(8,128)(2,1)S(1)} %get-tuple-element.103), channel_id=1, source_target_pairs={{0,4},{4,0},{1,5},{5,1},{2,6},{6,2},{3,7},{7,3},{8,12},{12,8},{9,1... | collective-permute-start | bytes 933896 | tf_op jit(solution)/shard_map/ppermute | solution.py:625
  44.9 5.4 %collective-permute-start.17 = (bf16[304,128]{1,0:T(8,128)(2,1)S(1)}, bf16[304,128]{1,0:T(8,128)(2,1)S(1)}, u32[]{:S(2)}, u32[]{:S(2)}) collective-permute-start(bf16[304,128]{1,0:T(8,128)(2,1)S(1)} %get-tuple-element.107), channel_id=1, source_target_pairs={{0,24},{1,25},{2,26},{3,27},{4,7},{5,6},{6,5},{7,4},{8,16},{9,17},... | collective-permute-start | bytes 233480 | tf_op jit(solution)/shard_map/ppermute | solution.py:637
  47.4 4.4 %collective-permute-start.18 = (bf16[304,128]{1,0:T(8,128)(2,1)S(1)}, bf16[304,128]{1,0:T(8,128)(2,1)S(1)}, u32[]{:S(2)}, u32[]{:S(2)}) collective-permute-start(bf16[304,128]{1,0:T(8,128)(2,1)S(1)} %get-tuple-element.108), channel_id=1, source_target_pairs={{0,16},{1,17},{2,18},{3,19},{4,6},{5,7},{6,4},{7,5},{8,24},{9,25},... | collective-permute-start | bytes 233480 | tf_op jit(solution)/shard_map/ppermute | solution.py:637
  47.9 4.4 %collective-permute-start.19 = (bf16[304,128]{1,0:T(8,128)(2,1)S(1)}, bf16[304,128]{1,0:T(8,128)(2,1)S(1)}, u32[]{:S(2)}, u32[]{:S(2)}) collective-permute-start(bf16[304,128]{1,0:T(8,128)(2,1)S(1)} %get-tuple-element.109), channel_id=1, source_target_pairs={{0,8},{1,9},{2,10},{3,11},{4,5},{5,4},{6,7},{7,6},{8,0},{9,1},{10,... | collective-permute-start | bytes 233480 | tf_op jit(solution)/shard_map/ppermute | solution.py:637
  52.3 6.4 %collective-permute-start.24 = (bf16[304,128]{1,0:T(8,128)(2,1)S(1)}, bf16[304,128]{1,0:T(8,128)(2,1)S(1)}, u32[]{:S(2)}, u32[]{:S(2)}) collective-permute-start(bf16[304,128]{1,0:T(8,128)(2,1)S(1)} %add_first.1.after_ref.refs_0_), channel_id=1, source_target_pairs={{0,3},{1,2},{2,1},{3,0},{4,28},{5,29},{6,30},{7,31},{8,11},{9,10},... | collective-permute-start | bytes 233480 | tf_op jit(solution)/shard_map/ppermute | solution.py:637
  54.3 7.0 %collective-permute-start.23 = (bf16[304,128]{1,0:T(8,128)(2,1)S(1)}, bf16[304,128]{1,0:T(8,128)(2,1)S(1)}, u32[]{:S(2)}, u32[]{:S(2)}) collective-permute-start(bf16[304,128]{1,0:T(8,128)(2,1)S(1)} %add_first.1.after_ref.refs_0_), channel_id=1, source_target_pairs={{0,2},{1,3},{2,0},{3,1},{4,20},{5,21},{6,22},{7,23},{8,10},{9,11},... | collective-permute-start | bytes 233480 | tf_op jit(solution)/shard_map/ppermute | solution.py:637
  55.1 6.1 %collective-permute-start.22 = (bf16[304,128]{1,0:T(8,128)(2,1)S(1)}, bf16[304,128]{1,0:T(8,128)(2,1)S(1)}, u32[]{:S(2)}, u32[]{:S(2)}) collective-permute-start(bf16[304,128]{1,0:T(8,128)(2,1)S(1)} %add_first.1.after_ref.refs_0_), channel_id=1, source_target_pairs={{0,1},{1,0},{2,3},{3,2},{4,12},{5,13},{6,14},{7,15},{8,9},{9,8},{1... | collective-permute-start | bytes 233480 | tf_op jit(solution)/shard_map/ppermute | solution.py:637
  56.9 8.0 %collective-permute-start.20 = (bf16[8,64,128]{2,1,0:T(8,128)(2,1)S(1)}, bf16[8,64,128]{2,1,0:T(8,128)(2,1)S(1)}, u32[]{:S(2)}, u32[]{:S(2)}) collective-permute-start(bf16[8,64,128]{2,1,0:T(8,128)(2,1)S(1)} %get-tuple-element.111), channel_id=1, source_target_pairs={{0,4},{1,2},{2,1},{3,7},{4,0},{5,6},{6,5},{7,3},{8,12},{9,10},{10,... | collective-permute-start | bytes 393224 | tf_op jit(solution)/shard_map/ppermute | solution.py:653
  56.9 7.9 %collective-permute-start.21 = (bf16[8,64,128]{2,1,0:T(8,128)(2,1)S(1)}, bf16[8,64,128]{2,1,0:T(8,128)(2,1)S(1)}, u32[]{:S(2)}, u32[]{:S(2)}) collective-permute-start(bf16[8,64,128]{2,1,0:T(8,128)(2,1)S(1)} %get-tuple-element.112), channel_id=1, source_target_pairs={{0,1},{1,0},{2,3},{3,2},{4,5},{5,4},{6,7},{7,6},{8,9},{9,8},{10,11... | collective-permute-start | bytes 393224 | tf_op jit(solution)/shard_map/ppermute | solution.py:653
  61.3 5.5 %collective-permute-start.27 = (bf16[304,128]{1,0:T(8,128)(2,1)S(1)}, bf16[304,128]{1,0:T(8,128)(2,1)S(1)}, u32[]{:S(2)}, u32[]{:S(2)}) collective-permute-start(bf16[304,128]{1,0:T(8,128)(2,1)S(1)} %add_second.1.refs_0_), channel_id=1, source_target_pairs={{0,24},{1,25},{2,26},{3,27},{4,7},{5,6},{6,5},{7,4},{8,16},{9,17},... | collective-permute-start | bytes 233480 | tf_op jit(solution)/shard_map/ppermute | solution.py:637
  62.8 4.7 %collective-permute-start.26 = (bf16[304,128]{1,0:T(8,128)(2,1)S(1)}, bf16[304,128]{1,0:T(8,128)(2,1)S(1)}, u32[]{:S(2)}, u32[]{:S(2)}) collective-permute-start(bf16[304,128]{1,0:T(8,128)(2,1)S(1)} %add_second.1.refs_0_), channel_id=1, source_target_pairs={{0,16},{1,17},{2,18},{3,19},{4,6},{5,7},{6,4},{7,5},{8,24},{9,25},... | collective-permute-start | bytes 233480 | tf_op jit(solution)/shard_map/ppermute | solution.py:637
  63.2 4.4 %collective-permute-start.25 = (bf16[304,128]{1,0:T(8,128)(2,1)S(1)}, bf16[304,128]{1,0:T(8,128)(2,1)S(1)}, u32[]{:S(2)}, u32[]{:S(2)}) collective-permute-start(bf16[304,128]{1,0:T(8,128)(2,1)S(1)} %add_second.1.refs_0_), channel_id=1, source_target_pairs={{0,8},{1,9},{2,10},{3,11},{4,5},{5,4},{6,7},{7,6},{8,0},{9,1},{10,... | collective-permute-start | bytes 233480 | tf_op jit(solution)/shard_map/ppermute | solution.py:637
  67.7 1.7 %collective-permute-start.28 = (bf16[1168,128]{1,0:T(8,128)(2,1)S(1)}, bf16[1168,128]{1,0:T(8,128)(2,1)S(1)}, u32[]{:S(2)}, u32[]{:S(2)}) collective-permute-start(bf16[1168,128]{1,0:T(8,128)(2,1)S(1)} %join.1.own_ref), channel_id=1, source_target_pairs={{0,4},{4,0},{1,5},{5,1},{2,6},{6,2},{3,7},{7,3},{8,12},{12,8},{9,1... | collective-permute-start | bytes 897032 | tf_op jit(solution)/shard_map/ppermute | solution.py:625
  (8 other events, 23.8 us)

commit v5 on v4

--- a/solution.py
+++ b/solution.py
@@ -100,7 +100,7 @@
     gp_ref[...] = pick(paired_p, pick(even, top, bottom), jnp.zeros_like(top))
 
 
-def far_rows_kernel(x_ref, u_ref, mask_ref, hx_ref, hp_ref, bits_ref):
+def far_rows_kernel(x_ref, mask_ref, hx_ref, hp_ref, bits_ref):
     samples, height, across, c = x_ref.shape
     even = lax.axis_index("lat") % 2 == 0
     for k in range(bits_ref.shape[0]):
@@ -112,14 +112,12 @@
     zero = jnp.zeros((across, c), BF16)
     for out, down, paired in zip((hx_ref, hp_ref), (even, jnp.logical_not(even)), has_pair()):
         first = jnp.where(down, height - 3, 1)
-        edge = jnp.where(down, height - 1, 0)
         for s in range(samples):
             out[2 * s] = pick(paired, x_ref[s, first], zero)
             out[2 * s + 1] = pick(paired, x_ref[s, first + 1], zero)
-            out[2 * samples + s] = pick(paired, u_ref[s, edge], zero)
         for k in range(bits_ref.shape[0]):
             bits = bits_ref[k]
-            out[3 * samples + k] = pick(paired, bits, jnp.zeros_like(bits)).astype(BF16)
+            out[2 * samples + k] = pick(paired, bits, jnp.zeros_like(bits)).astype(BF16)
 
 
 def masks_kernel(bits_ref, m_ref, count_ref):
@@ -224,7 +222,7 @@
 
 
 def conv1_edge_kernel(
-    hp_ref, hx_ref, gp_ref, gx_ref, x_ref, st_ref, t_ref, b_ref, a_ref, mh_ref, muh_ref
+    hp_ref, hx_ref, gp_ref, gx_ref, x_ref, st_ref, t_ref, b_ref, a_ref, mh_ref
 ):
     samples, height, across, c = x_ref.shape
     even = lax.axis_index("lat") % 2 == 0
@@ -247,7 +245,7 @@
                 parts.append(pick(even, hx_ref[2 * s + j], hp_ref[2 * s + j]))
         return jnp.concatenate(parts, 0)
 
-    slabs = slice(3 * samples, hx_ref.shape[0])
+    slabs = slice(2 * samples, hx_ref.shape[0])
     above = pick(even, hp_ref[slabs], hx_ref[slabs])
     below = pick(even, hx_ref[slabs], hp_ref[slabs])
     for slot, start in ((0, -2), (2, height)):
@@ -260,11 +258,6 @@
                 else:
                     mask = column_mask(below, s * height + j, c)
                 mh_ref[s, slot + j] = mask
-    for s in range(samples):
-        up = pick(even, hp_ref[2 * samples + s], hx_ref[2 * samples + s])
-        muh_ref[s, 0] = up.astype(F32) * mh_ref[s, 1]
-        down = pick(even, hx_ref[2 * samples + s], hp_ref[2 * samples + s])
-        muh_ref[s, 1] = down.astype(F32) * mh_ref[s, 2]
 
 
 def conv2_kernel(
@@ -336,10 +329,11 @@
 
 def back2_kernel(
     pieces,
-    own_ref, st1_ref, c1_ref, a2_ref, s2_ref, mu_ref, muh_ref, m_ref, a_ref, ao_ref, k_ref, g_ref, t_ref, *refs,
+    own_ref, st1_ref, c1_ref, a2_ref, s2_ref, mu_ref, ux_ref, up_ref, m_ref, a_ref, ao_ref, k_ref, g_ref, t_ref, *refs,
 ):
     stats, (d_ref, dn_ref, c2_ref, st3_ref, ext_ref) = gather(refs[:pieces]), refs[pieces:]
     samples, height, across, c = m_ref.shape
+    even = lax.axis_index("lat") % 2 == 0
     count = c1_ref[2:3]
     mean, inverse = join(stats, count, 0, stats[:, 5:6])
     offset = mean - own_ref[2:3]
@@ -353,7 +347,11 @@
     for s in range(samples):
         ext = ext_ref.at[s % 2]
         for i in range(height + 2):
-            upstream = mu_ref[s, i - 1] if 0 < i <= height else muh_ref[s, 0 if i == 0 else 1]
+            if 0 < i <= height:
+                upstream = mu_ref[s, i - 1]
+            else:
+                edges = (up_ref[s], ux_ref[s]) if i == 0 else (ux_ref[s], up_ref[s])
+                upstream = pick(even, *edges).astype(F32)
             grad = upstream * scale + (a2_ref[s, i] * by_active + constant)
             ext[i] = (grad * s2_ref[s, i]).astype(BF16)
             if 0 < i <= height:
@@ -496,7 +494,8 @@
         put(send_ref, 0)
 
 
-def edge_rows_kernel(d_ref, after_ref, dx_ref, dp_ref):
+def edge_rows_kernel(d_ref, *refs):
+    dx_ref, dp_ref = refs[-2:]
     samples, height = d_ref.shape[:2]
     even = lax.axis_index("lat") % 2 == 0
     paired_x, paired_p = has_pair()
@@ -667,10 +666,16 @@
     return exchange(value_x, 0), got_p
 
 
-def spread(stats):
+def blocks_kernel(parts, *refs):
+    refs[-1][...] = jnp.concatenate([r[...] for r in refs[:parts]], 0)
+
+
+def spread(stats, flops=0):
     blocks, k = stats[None], 1
     while k < lax.axis_size("dp"):
-        blocks = jnp.concatenate([blocks, swap(blocks, "dp", k)], 0)
+        both = (blocks, swap(blocks, "dp", k))
+        shape = jax.ShapeDtypeStruct((2 * k, *stats.shape), F32)
+        blocks = call(functools.partial(blocks_kernel, 2), shape, [], both, "blocks", flops)
         k *= 2
     return [blocks] + [
         over_dp_and_lat(blocks, lambda dp, lat, k=k: (dp ^ 1, lat ^ k))
@@ -781,12 +786,12 @@
         conv_flops,
     )
     gx, gp = neighbours(*near)
-    packed = array((3 * samples + slabs, across, c), BF16)
+    packed = array((2 * samples + slabs, across, c), BF16)
     far_x, far_p, bits = call(
         far_rows_kernel,
         (packed, packed, array((slabs, across, 128), F32)),
         [],
-        (x, u, mask.reshape(samples * height, across)),
+        (x, mask.reshape(samples * height, across)),
         "far_rows",
         conv_flops,
     )
@@ -816,9 +821,9 @@
         "prepare",
         conv_flops,
     )
-    a1h, halo_mask, mu_halo = call(
+    a1h, halo_mask = call(
         conv1_edge_kernel,
-        (shape(4), shape(4), shape(2)),
+        (shape(4), shape(4)),
         [],
         (hp, hx, gp, gx, x, own1, w1t, b1),
         "conv1_edges",
@@ -833,7 +838,8 @@
         "conv2",
         conv_flops,
     )
-    st2 = spread(own2)
+    ux, up = neighbours(*call(edge_rows_kernel, (edge, edge), [], (u,), "u_rows", waits=(own2,)))
+    st2 = spread(own2, HIDE)
     s1, s2 = call(
         slopes_kernel,
         (shape(height), shape(height + 2)),
@@ -847,7 +853,7 @@
         functools.partial(back2_kernel, len(st2)),
         (shape(height, BF16), shape(height), vector, vector),
         [ext(height + 2)],
-        (own2, own1, c1, a2, s2, mu, mu_halo, wide_mask, a1, a1o, w2tt, g2, t2, *st2),
+        (own2, own1, c1, a2, s2, mu, ux, up, wide_mask, a1, a1o, w2tt, g2, t2, *st2),
         "conv2_back",
         conv_flops,
     )

time: 70.6 us -> 69.9 us (0.990)
  waiting for transfers between devices: 14.4 us -> 12.7 us
  starting transfers between devices: 32.1 us -> 33 us
    ppermute x15 -> x17, starting transfers between devices: 19.5 us -> 20.3 us  [over_dp_and_lat(): return lax.ppermute(value, ('dp', 'lat'), pairs)]
    ppermute x15 -> x17, waiting for transfers between devices: 3.43 us -> 2.67 us  [over_dp_and_lat(): return lax.ppermute(value, ('dp', 'lat'), pairs)]
    pallas_call x21 -> x25, Pallas kernels: 21.5 us -> 21.7 us  [call(): pl.pallas_call(kernel, out_shape=outs, in_specs=(ins or [spaces[0]] * len...]
  transfers between devices with their start and end apart: 29 -> 31, of which waited for: 14 -> 15; matrix products, arithmetic and copies ran while one was open for 0% -> 0% of each run, Pallas kernels for 18% -> 18%
where the time goes in v5:
time: 69.9 us; the launch traced here: 69.7 us
  starting transfers between devices  33 us (47%)
  Pallas kernels  21.7 us (31%)
  waiting for transfers between devices  12.7 us (18%)
  local copies, waits for them, and re-layouts  1.3 us (2%)
  between operations  1.15 us (2%)
    pallas_call x25, Pallas kernels, call(): pl.pallas_call(kernel, out_shape=outs, in_specs=(ins or [spaces[0]] * len...  21.7 us
    ppermute x17, starting transfers between devices, over_dp_and_lat(): return lax.ppermute(value, ('dp', 'lat'), pairs)  20.3 us
    ppermute x9, starting transfers between devices, cross(): return lax.ppermute(value, ('lead', 'dp', 'lat'), pairs)  11.6 us
    ppermute x9, waiting for transfers between devices, cross(): return lax.ppermute(value, ('lead', 'dp', 'lat'), pairs)  6.47 us
    ppermute x5, waiting for transfers between devices, swap(): lax.ppermute(value, axis, [(i, i ^ k) for i in range(lax.axis_size(axis))])  3.54 us
    ppermute x17, waiting for transfers between devices, over_dp_and_lat(): return lax.ppermute(value, ('dp', 'lat'), pairs)  2.67 us
  transfers between devices with their start and end apart: 31, of which 15 were waited for; matrix products, arithmetic and copies ran while one was open for 0% of the time, Pallas kernels for 18%

profile of v5, /device:TPU:0, one launch (start us, length us, event | category | flops | bytes accessed | tf_op | source)
XLA Modules:
  0.0 69.7 jit_solution(1472011000268145852)
XLA Ops:
  0.6 1.0 %fusion = (bf16[8,1,64,128]{3,2,1,0:T(8,128)(2,1)S(1)}, bf16[8,1,64,128]{3,2,1,0:T(8,128)(2,1)S(1)}) fusion(bf16[8,8,64,128]{3,2,1,0:T(8,128)(2,1)} %bitcast.22), kind=kLoop, calls=%fused_computation | loop fusion | bytes 524288 | tf_op jit(solution)/shard_map/slice | solution.py:784
  2.3 4.1 %collective-permute-start.1 = (bf16[8,1,64,128]{3,2,1,0:T(8,128)(2,1)S(1)}, bf16[8,1,64,128]{3,2,1,0:T(8,128)(2,1)S(1)}, u32[]{:S(2)}, u32[]{:S(2)}) collective-permute-start(bf16[8,1,64,128]{3,2,1,0:T(8,128)(2,1)S(1)} %get-tuple-element.70), channel_id=1, source_target_pairs={{0,1},{1,0},{2,3},{3,2},{4,5},{5,4},{6,7},{7,6},{8,9},{9,8},{10,11... | collective-permute-start | bytes 393224 | tf_op jit(solution)/shard_map/ppermute | solution.py:652
  6.6 1.6 %collective-permute-start.3 = (bf16[17,64,128]{2,1,0:T(8,128)(2,1)S(1)}, bf16[17,64,128]{2,1,0:T(8,128)(2,1)S(1)}, u32[]{:S(2)}, u32[]{:S(2)}) collective-permute-start(bf16[17,64,128]{2,1,0:T(8,128)(2,1)S(1)} %get-tuple-element.80), channel_id=1, source_target_pairs={{0,1},{1,0},{2,3},{3,2},{4,5},{5,4},{6,7},{7,6},{8,9},{9,8},{10,11... | collective-permute-start | bytes 835592 | tf_op jit(solution)/shard_map/ppermute | solution.py:652
  9.2 1.2 %conv1_inner.1 = (f32[8,4,64,128]{3,2,1,0:T(8,128)S(1)}, f32[8,4,64,128]{3,2,1,0:T(8,128)S(1)}, bf16[3,512,256]{2,1,0:T(8,128)(2,1)S(1)}, f32[8,128]{1,0:T(8,128)S(1)}) custom-call(bf16[8,8,64,128]{3,2,1,0:T(8,128)(2,1)S(1)} %bitcast.24, f32[8,8,64,128]{3,2,1,0:T(8,128)S(1)} %get-tuple-element.72.m_ref, bf16[3,3,128,128]{3,2,1,0:T(8,128)(2,1)S(1)} %copy-done.10, ...), custom_call_target="tpu_custom_call" | custom-call | flops 4831838208 | bytes 3441152 | tf_op jit(solution)/shard_map/conv1_inner/pallas_call | solution.py:610
  10.4 1.2 %conv1_outer.1 = (f32[8,4,64,128]{3,2,1,0:T(8,128)S(1)}, f32[8,4,64,128]{3,2,1,0:T(8,128)S(1)}, f32[8,128]{1,0:T(8,128)S(1)}) custom-call(bf16[8,1,64,128]{3,2,1,0:T(8,128)(2,1)S(1)} %collective-permute-done.gp_ref, bf16[8,1,64,128]{3,2,1,0:T(8,128)(2,1)S(1)} %collective-permute-done.1.gx_ref, bf16[8,8,64,128]{3,2,1,0:T(8,128)(2,1)S(1)} %bitcast.25, ...), custom_call_target="tpu_custom_call" | custom-call | flops 19327352832 | bytes 4203008 | tf_op jit(solution)/shard_map/conv1_outer/pallas_call | solution.py:610
  12.9 2.6 %collective-permute-start.7 = (f32[2,8,128]{2,1,0:T(8,128)S(1)}, f32[2,8,128]{2,1,0:T(8,128)S(1)}, u32[]{:S(2)}, u32[]{:S(2)}) collective-permute-start(f32[2,8,128]{2,1,0:T(8,128)S(1)} %blocks.3.refs_0_), channel_id=1, source_target_pairs={{0,7},{1,6},{2,5},{3,4},{4,3},{5,2},{6,1},{7,0},{8,15},{9,14},{10,... | collective-permute-start | bytes 24584 | tf_op jit(solution)/shard_map/ppermute | solution.py:652
  15.7 1.1 %collective-permute-start.5 = (f32[2,8,128]{2,1,0:T(8,128)S(1)}, f32[2,8,128]{2,1,0:T(8,128)S(1)}, u32[]{:S(2)}, u32[]{:S(2)}) collective-permute-start(f32[2,8,128]{2,1,0:T(8,128)S(1)} %blocks.3.refs_0_), channel_id=1, source_target_pairs={{0,5},{1,4},{2,7},{3,6},{4,1},{5,0},{6,3},{7,2},{8,13},{9,12},{10,... | collective-permute-start | bytes 24584 | tf_op jit(solution)/shard_map/ppermute | solution.py:652
  16.7 1.1 %conv1_edges.1 = (f32[8,4,64,128]{3,2,1,0:T(8,128)S(1)}, f32[8,4,64,128]{3,2,1,0:T(8,128)S(1)}) custom-call(bf16[17,64,128]{2,1,0:T(8,128)(2,1)S(1)} %collective-permute-done.2.hp_ref, bf16[17,64,128]{2,1,0:T(8,128)(2,1)S(1)} %collective-permute-done.3.hx_ref, bf16[8,1,64,128]{3,2,1,0:T(8,128)(2,1)S(1)} %collective-permute-done.gp_ref, ...), custom_call_target="tpu_custom_call" | custom-call | flops 603979776 | bytes 2658816 | tf_op jit(solution)/shard_map/conv1_edges/pallas_call | solution.py:610
  17.8 1.6 %collective-permute-done.6.refs_2_ = f32[2,8,128]{2,1,0:T(8,128)S(1)} collective-permute-done((f32[2,8,128]{2,1,0:T(8,128)S(1)}, f32[2,8,128]{2,1,0:T(8,128)S(1)}, u32[]{:S(2)}, u32[]{:S(2)}) %collective-permute-start.6) | collective-permute-done | bytes 8224 | tf_op jit(solution)/shard_map/ppermute | solution.py:652
  19.5 3.2 %conv2.1 = (bf16[8,10,64,128]{3,2,1,0:T(8,128)(2,1)S(1)}, f32[8,10,64,128]{3,2,1,0:T(8,128)S(1)}, f32[8,10,64,128]{3,2,1,0:T(8,128)S(1)}, f32[8,128]{1,0:T(8,128)S(1)}, f32[8,128]{1,0:T(8,128)S(1)}) custom-call(f32[8,128]{1,0:T(8,128)S(1)} %get-tuple-element.76.st_ref.own_ref.st1_ref, f32[8,4,64,128]{3,2,1,0:T(8,128)S(1)} %get-tuple-element.77.a_ref, ...), custom_call_target="tpu_custom_call" | custom-call | flops 1207959552 | bytes 9217536 | tf_op jit(solution)/shard_map/conv2/pallas_call | solution.py:610
  23.9 2.6 %collective-permute-start.13 = (f32[2,8,128]{2,1,0:T(8,128)S(1)}, f32[2,8,128]{2,1,0:T(8,128)S(1)}, u32[]{:S(2)}, u32[]{:S(2)}) collective-permute-start(f32[2,8,128]{2,1,0:T(8,128)S(1)} %blocks.4.after_ref.refs_0_), channel_id=1, source_target_pairs={{0,7},{1,6},{2,5},{3,4},{4,3},{5,2},{6,1},{7,0},{8,15},{9,14},{10,... | collective-permute-start | bytes 24584 | tf_op jit(solution)/shard_map/ppermute | solution.py:652
  26.9 1.0 %collective-permute-start.11 = (f32[2,8,128]{2,1,0:T(8,128)S(1)}, f32[2,8,128]{2,1,0:T(8,128)S(1)}, u32[]{:S(2)}, u32[]{:S(2)}) collective-permute-start(f32[2,8,128]{2,1,0:T(8,128)S(1)} %blocks.4.after_ref.refs_0_), channel_id=1, source_target_pairs={{0,5},{1,4},{2,7},{3,6},{4,1},{5,0},{6,3},{7,2},{8,13},{9,12},{10,... | collective-permute-start | bytes 24584 | tf_op jit(solution)/shard_map/ppermute | solution.py:652
  27.9 1.6 %slopes.1 = (f32[8,8,64,128]{3,2,1,0:T(8,128)S(1)}, f32[8,10,64,128]{3,2,1,0:T(8,128)S(1)}) custom-call(f32[8,4,64,128]{3,2,1,0:T(8,128)S(1)} %get-tuple-element.89.z_ref, f32[8,4,64,128]{3,2,1,0:T(8,128)S(1)} %get-tuple-element.90.zo_ref, f32[8,10,64,128]{3,2,1,0:T(8,128)S(1)} %get-tuple-element.91.z2_ref, f32[8,8,64,128]{3,2,1,0:T(8,128)S(1)} %get-tuple-element.72.m_ref, ...), custom_call_target="tpu_custom_call" | custom-call | flops 1207959552 | bytes 7864320 | tf_op jit(solution)/shard_map/slopes/pallas_call | solution.py:610
  30.5 2.7 %conv2_back.1 = (bf16[8,8,64,128]{3,2,1,0:T(8,128)(2,1)S(1)}, f32[8,8,64,128]{3,2,1,0:T(8,128)S(1)}, f32[8,128]{1,0:T(8,128)S(1)}, f32[8,128]{1,0:T(8,128)S(1)}) custom-call(f32[8,128]{1,0:T(8,128)S(1)} %get-tuple-element.87.refs_0_.own_ref, f32[8,128]{1,0:T(8,128)S(1)} %get-tuple-element.76.st_ref.own_ref.st1_ref, f32[8,128]{1,0:T(8,128)S(1)} %get-tuple-element.88.c1_ref, ...), custom_call_target="tpu_custom_call" | custom-call | flops 1207959552 | bytes 12628992 | tf_op jit(solution)/shard_map/conv2_back/pallas_call | solution.py:610
  33.4 1.1 %collective-permute-done.14.refs_1_ = f32[1,8,128]{2,1,0:T(8,128)S(1)} collective-permute-done((f32[1,8,128]{2,1,0:T(8,128)S(1)}, f32[1,8,128]{2,1,0:T(8,128)S(1)}, u32[]{:S(2)}, u32[]{:S(2)}) %collective-permute-start.14) | collective-permute-done | bytes 4128 | tf_op jit(solution)/shard_map/ppermute | solution.py:624
  34.4 1.7 %collective-permute-start.17 = (f32[2,8,128]{2,1,0:T(8,128)S(1)}, f32[2,8,128]{2,1,0:T(8,128)S(1)}, u32[]{:S(2)}, u32[]{:S(2)}) collective-permute-start(f32[2,8,128]{2,1,0:T(8,128)S(1)} %blocks.5.after_ref.refs_0_), channel_id=1, source_target_pairs={{0,7},{1,6},{2,5},{3,4},{4,3},{5,2},{6,1},{7,0},{8,15},{9,14},{10,... | collective-permute-start | bytes 24584 | tf_op jit(solution)/shard_map/ppermute | solution.py:652
  36.2 2.1 %collective-permute-start.15 = (f32[2,8,128]{2,1,0:T(8,128)S(1)}, f32[2,8,128]{2,1,0:T(8,128)S(1)}, u32[]{:S(2)}, u32[]{:S(2)}) collective-permute-start(f32[2,8,128]{2,1,0:T(8,128)S(1)} %blocks.5.after_ref.refs_0_), channel_id=1, source_target_pairs={{0,5},{1,4},{2,7},{3,6},{4,1},{5,0},{6,3},{7,2},{8,13},{9,12},{10,... | collective-permute-start | bytes 24584 | tf_op jit(solution)/shard_map/ppermute | solution.py:652
  38.3 1.8 %conv2_weight_grad.1 = (bf16[1152,128]{1,0:T(8,128)(2,1)S(1)}, f32[8,128]{1,0:T(8,128)S(1)}) custom-call(bf16[8,10,64,128]{3,2,1,0:T(8,128)(2,1)S(1)} %get-tuple-element.99.n_ref, bf16[8,8,64,128]{3,2,1,0:T(8,128)(2,1)S(1)} %get-tuple-element.100.d_ref, f32[2,8,128]{2,1,0:T(8,128)S(1)} %blocks.5.after_ref.refs_0_), custom_call_target="tpu_custom_call" | custom-call | flops 1207959552 | bytes 2359296 | tf_op jit(solution)/shard_map/conv2_weight_grad/pallas_call | solution.py:610
  40.2 2.2 %conv1_weight_grad.1 = (bf16[8,8,64,128]{3,2,1,0:T(8,128)(2,1)S(1)}, bf16[4,304,128]{2,1,0:T(8,128)(2,1)S(1)}, bf16[4,304,128]{2,1,0:T(8,128)(2,1)S(1)}) custom-call(f32[8,128]{1,0:T(8,128)S(1)} %get-tuple-element.88.c1_ref, f32[8,128]{1,0:T(8,128)S(1)} %get-tuple-element.96.c2_ref, f32[8,8,64,128]{3,2,1,0:T(8,128)S(1)} %get-tuple-element.97.dn_ref, ...), custom_call_target="tpu_custom_call" | custom-call | flops 1207959552 | bytes 7942656 | tf_op jit(solution)/shard_map/conv1_weight_grad/pallas_call | solution.py:610
  42.8 1.2 %collective-permute-done.18.refs_1_ = bf16[4,304,128]{2,1,0:T(8,128)(2,1)S(1)} collective-permute-done((bf16[4,304,128]{2,1,0:T(8,128)(2,1)S(1)}, bf16[4,304,128]{2,1,0:T(8,128)(2,1)S(1)}, u32[]{:S(2)}, u32[]{:S(2)}) %collective-permute-start.18) | collective-permute-done | bytes 311328 | tf_op jit(solution)/shard_map/ppermute | solution.py:624
  44.1 2.5 %collective-permute-start.19 = (bf16[304,128]{1,0:T(8,128)(2,1)S(1)}, bf16[304,128]{1,0:T(8,128)(2,1)S(1)}, u32[]{:S(2)}, u32[]{:S(2)}) collective-permute-start(bf16[304,128]{1,0:T(8,128)(2,1)S(1)} %get-tuple-element.109), channel_id=1, source_target_pairs={{0,24},{1,25},{2,26},{3,27},{4,7},{5,6},{6,5},{7,4},{8,16},{9,17},... | collective-permute-start | bytes 233480 | tf_op jit(solution)/shard_map/ppermute | solution.py:636
  47.6 1.1 %output.1 = (bf16[8,8,64,128]{3,2,1,0:T(8,128)(2,1)}, f32[8,128]{1,0:T(8,128)S(1)}) custom-call(bf16[8,8,64,128]{3,2,1,0:T(8,128)(2,1)S(1)} %bitcast.28, f32[8,10,64,128]{3,2,1,0:T(8,128)S(1)} %get-tuple-element.86.a2_ref, f32[8,8,64,128]{3,2,1,0:T(8,128)S(1)} %get-tuple-element.72.m_ref, f32[8,128]{1,0:T(8,128)S(1)} %get-tuple-element.96.c2_ref, ...), custom_call_target="tpu_custom_call" | custom-call | flops 603979776 | bytes 5771264 | tf_op jit(solution)/shard_map/output/pallas_call | solution.py:610
  49.5 1.5 %collective-permute-done.20.refs_2_ = bf16[304,128]{1,0:T(8,128)(2,1)S(1)} collective-permute-done((bf16[304,128]{1,0:T(8,128)(2,1)S(1)}, bf16[304,128]{1,0:T(8,128)(2,1)S(1)}, u32[]{:S(2)}, u32[]{:S(2)}) %collective-permute-start.20) | collective-permute-done | bytes 77856 | tf_op jit(solution)/shard_map/ppermute | solution.py:636
  51.6 1.9 %collective-permute-start.26 = (bf16[304,128]{1,0:T(8,128)(2,1)S(1)}, bf16[304,128]{1,0:T(8,128)(2,1)S(1)}, u32[]{:S(2)}, u32[]{:S(2)}) collective-permute-start(bf16[304,128]{1,0:T(8,128)(2,1)S(1)} %add_first.1.refs_0_), channel_id=1, source_target_pairs={{0,3},{1,2},{2,1},{3,0},{4,28},{5,29},{6,30},{7,31},{8,11},{9,10},... | collective-permute-start | bytes 233480 | tf_op jit(solution)/shard_map/ppermute | solution.py:636
  53.5 1.0 %collective-permute-start.25 = (bf16[304,128]{1,0:T(8,128)(2,1)S(1)}, bf16[304,128]{1,0:T(8,128)(2,1)S(1)}, u32[]{:S(2)}, u32[]{:S(2)}) collective-permute-start(bf16[304,128]{1,0:T(8,128)(2,1)S(1)} %add_first.1.refs_0_), channel_id=1, source_target_pairs={{0,2},{1,3},{2,0},{3,1},{4,20},{5,21},{6,22},{7,23},{8,10},{9,11},... | collective-permute-start | bytes 233480 | tf_op jit(solution)/shard_map/ppermute | solution.py:636
  54.5 1.5 %collective-permute-start.24 = (bf16[304,128]{1,0:T(8,128)(2,1)S(1)}, bf16[304,128]{1,0:T(8,128)(2,1)S(1)}, u32[]{:S(2)}, u32[]{:S(2)}) collective-permute-start(bf16[304,128]{1,0:T(8,128)(2,1)S(1)} %add_first.1.refs_0_), channel_id=1, source_target_pairs={{0,1},{1,0},{2,3},{3,2},{4,12},{5,13},{6,14},{7,15},{8,9},{9,8},{1... | collective-permute-start | bytes 233480 | tf_op jit(solution)/shard_map/ppermute | solution.py:636
  56.2 1.5 %collective-permute-start.23 = (bf16[8,64,128]{2,1,0:T(8,128)(2,1)S(1)}, bf16[8,64,128]{2,1,0:T(8,128)(2,1)S(1)}, u32[]{:S(2)}, u32[]{:S(2)}) collective-permute-start(bf16[8,64,128]{2,1,0:T(8,128)(2,1)S(1)} %get-tuple-element.114), channel_id=1, source_target_pairs={{0,1},{1,0},{2,3},{3,2},{4,5},{5,4},{6,7},{7,6},{8,9},{9,8},{10,11... | collective-permute-start | bytes 393224 | tf_op jit(solution)/shard_map/ppermute | solution.py:652
  57.9 2.5 %collective-permute-done.25.refs_2_ = bf16[304,128]{1,0:T(8,128)(2,1)S(1)} collective-permute-done((bf16[304,128]{1,0:T(8,128)(2,1)S(1)}, bf16[304,128]{1,0:T(8,128)(2,1)S(1)}, u32[]{:S(2)}, u32[]{:S(2)}) %collective-permute-start.25) | collective-permute-done | bytes 77856 | tf_op jit(solution)/shard_map/ppermute | solution.py:636
  60.5 1.6 %collective-permute-start.29 = (bf16[304,128]{1,0:T(8,128)(2,1)S(1)}, bf16[304,128]{1,0:T(8,128)(2,1)S(1)}, u32[]{:S(2)}, u32[]{:S(2)}) collective-permute-start(bf16[304,128]{1,0:T(8,128)(2,1)S(1)} %add_second.1.refs_0_), channel_id=1, source_target_pairs={{0,24},{1,25},{2,26},{3,27},{4,7},{5,6},{6,5},{7,4},{8,16},{9,17},... | collective-permute-start | bytes 233480 | tf_op jit(solution)/shard_map/ppermute | solution.py:636
  62.6 1.5 %collective-permute-start.27 = (bf16[304,128]{1,0:T(8,128)(2,1)S(1)}, bf16[304,128]{1,0:T(8,128)(2,1)S(1)}, u32[]{:S(2)}, u32[]{:S(2)}) collective-permute-start(bf16[304,128]{1,0:T(8,128)(2,1)S(1)} %add_second.1.refs_0_), channel_id=1, source_target_pairs={{0,8},{1,9},{2,10},{3,11},{4,5},{5,4},{6,7},{7,6},{8,0},{9,1},{10,... | collective-permute-start | bytes 233480 | tf_op jit(solution)/shard_map/ppermute | solution.py:636
  64.1 1.9 %conv1_back.1 = (bf16[8,8,64,128]{3,2,1,0:T(8,128)(2,1)S(1)}, f32[8,128]{1,0:T(8,128)S(1)}) custom-call(bf16[8,64,128]{2,1,0:T(8,128)(2,1)S(1)} %collective-permute-done.22.ep_ref, bf16[8,64,128]{2,1,0:T(8,128)(2,1)S(1)} %collective-permute-done.23.ex_ref, bf16[8,8,64,128]{3,2,1,0:T(8,128)(2,1)S(1)} %get-tuple-element.108.d_ref, ...), custom_call_target="tpu_custom_call" | custom-call | flops 1207959552 | bytes 2654208 | tf_op jit(solution)/shard_map/conv1_back/pallas_call | solution.py:610
  67.1 1.2 %leave.1 = (bf16[8,8,64,128]{3,2,1,0:T(8,128)(2,1)}, f32[1152,128]{1,0:T(8,128)}, f32[1152,128]{1,0:T(8,128)}) custom-call(bf16[8,8,64,128]{3,2,1,0:T(8,128)(2,1)S(1)} %get-tuple-element.115.grad_ref, bf16[1168,128]{1,0:T(8,128)(2,1)S(1)} %join.1.own_ref), custom_call_target="tpu_custom_call" | custom-call | bytes 1347584 | tf_op jit(solution)/shard_map/leave/pallas_call | solution.py:610
  (82 shorter events, 12.3 us)
Async XLA Ops:
  1.7 8.7 %collective-permute-start = (bf16[8,1,64,128]{3,2,1,0:T(8,128)(2,1)S(1)}, bf16[8,1,64,128]{3,2,1,0:T(8,128)(2,1)S(1)}, u32[]{:S(2)}, u32[]{:S(2)}) collective-permute-start(bf16[8,1,64,128]{3,2,1,0:T(8,128)(2,1)S(1)} %get-tuple-element.69), channel_id=1, source_target_pairs={{0,4},{1,2},{2,1},{3,7},{4,0},{5,6},{6,5},{7,3},{8,12},{9,10},{10,... | collective-permute-start | bytes 393224 | tf_op jit(solution)/shard_map/ppermute | solution.py:652
  2.3 8.2 %collective-permute-start.1 = (bf16[8,1,64,128]{3,2,1,0:T(8,128)(2,1)S(1)}, bf16[8,1,64,128]{3,2,1,0:T(8,128)(2,1)S(1)}, u32[]{:S(2)}, u32[]{:S(2)}) collective-permute-start(bf16[8,1,64,128]{3,2,1,0:T(8,128)(2,1)S(1)} %get-tuple-element.70), channel_id=1, source_target_pairs={{0,1},{1,0},{2,3},{3,2},{4,5},{5,4},{6,7},{7,6},{8,9},{9,8},{10,11... | collective-permute-start | bytes 393224 | tf_op jit(solution)/shard_map/ppermute | solution.py:652
  6.5 10.2 %collective-permute-start.2 = (bf16[17,64,128]{2,1,0:T(8,128)(2,1)S(1)}, bf16[17,64,128]{2,1,0:T(8,128)(2,1)S(1)}, u32[]{:S(2)}, u32[]{:S(2)}) collective-permute-start(bf16[17,64,128]{2,1,0:T(8,128)(2,1)S(1)} %get-tuple-element.79), channel_id=1, source_target_pairs={{0,4},{1,2},{2,1},{3,7},{4,0},{5,6},{6,5},{7,3},{8,12},{9,10},{10,... | collective-permute-start | bytes 835592 | tf_op jit(solution)/shard_map/ppermute | solution.py:652
  6.6 10.2 %collective-permute-start.3 = (bf16[17,64,128]{2,1,0:T(8,128)(2,1)S(1)}, bf16[17,64,128]{2,1,0:T(8,128)(2,1)S(1)}, u32[]{:S(2)}, u32[]{:S(2)}) collective-permute-start(bf16[17,64,128]{2,1,0:T(8,128)(2,1)S(1)} %get-tuple-element.80), channel_id=1, source_target_pairs={{0,1},{1,0},{2,3},{3,2},{4,5},{5,4},{6,7},{7,6},{8,9},{9,8},{10,11... | collective-permute-start | bytes 835592 | tf_op jit(solution)/shard_map/ppermute | solution.py:652
  11.6 1.2 %collective-permute-start.4 = (f32[1,8,128]{2,1,0:T(8,128)S(1)}, f32[1,8,128]{2,1,0:T(8,128)S(1)}, u32[]{:S(2)}, u32[]{:S(2)}) collective-permute-start(f32[1,8,128]{2,1,0:T(8,128)S(1)} %bitcast.32), channel_id=1, source_target_pairs={{0,4},{4,0},{1,5},{5,1},{2,6},{6,2},{3,7},{7,3},{8,12},{12,8},{9,1... | collective-permute-start | bytes 12296 | tf_op jit(solution)/shard_map/ppermute | solution.py:624
  12.9 5.0 %collective-permute-start.7 = (f32[2,8,128]{2,1,0:T(8,128)S(1)}, f32[2,8,128]{2,1,0:T(8,128)S(1)}, u32[]{:S(2)}, u32[]{:S(2)}) collective-permute-start(f32[2,8,128]{2,1,0:T(8,128)S(1)} %blocks.3.refs_0_), channel_id=1, source_target_pairs={{0,7},{1,6},{2,5},{3,4},{4,3},{5,2},{6,1},{7,0},{8,15},{9,14},{10,... | collective-permute-start | bytes 24584 | tf_op jit(solution)/shard_map/ppermute | solution.py:652
  15.4 4.0 %collective-permute-start.6 = (f32[2,8,128]{2,1,0:T(8,128)S(1)}, f32[2,8,128]{2,1,0:T(8,128)S(1)}, u32[]{:S(2)}, u32[]{:S(2)}) collective-permute-start(f32[2,8,128]{2,1,0:T(8,128)S(1)} %blocks.3.refs_0_), channel_id=1, source_target_pairs={{0,6},{1,7},{2,4},{3,5},{4,2},{5,3},{6,0},{7,1},{8,14},{9,15},{10,... | collective-permute-start | bytes 24584 | tf_op jit(solution)/shard_map/ppermute | solution.py:652
  15.7 3.8 %collective-permute-start.5 = (f32[2,8,128]{2,1,0:T(8,128)S(1)}, f32[2,8,128]{2,1,0:T(8,128)S(1)}, u32[]{:S(2)}, u32[]{:S(2)}) collective-permute-start(f32[2,8,128]{2,1,0:T(8,128)S(1)} %blocks.3.refs_0_), channel_id=1, source_target_pairs={{0,5},{1,4},{2,7},{3,6},{4,1},{5,0},{6,3},{7,2},{8,13},{9,12},{10,... | collective-permute-start | bytes 24584 | tf_op jit(solution)/shard_map/ppermute | solution.py:652
  22.7 1.2 %collective-permute-start.8 = (f32[1,8,128]{2,1,0:T(8,128)S(1)}, f32[1,8,128]{2,1,0:T(8,128)S(1)}, u32[]{:S(2)}, u32[]{:S(2)}) collective-permute-start(f32[1,8,128]{2,1,0:T(8,128)S(1)} %bitcast.34), channel_id=1, source_target_pairs={{0,4},{4,0},{1,5},{5,1},{2,6},{6,2},{3,7},{7,3},{8,12},{12,8},{9,1... | collective-permute-start | bytes 12296 | tf_op jit(solution)/shard_map/ppermute | solution.py:624
  23.1 7.4 %collective-permute-start.9 = (bf16[8,64,128]{2,1,0:T(8,128)(2,1)S(1)}, bf16[8,64,128]{2,1,0:T(8,128)(2,1)S(1)}, u32[]{:S(2)}, u32[]{:S(2)}) collective-permute-start(bf16[8,64,128]{2,1,0:T(8,128)(2,1)S(1)} %get-tuple-element.93), channel_id=1, source_target_pairs={{0,1},{1,0},{2,3},{3,2},{4,5},{5,4},{6,7},{7,6},{8,9},{9,8},{10,11... | collective-permute-start | bytes 393224 | tf_op jit(solution)/shard_map/ppermute | solution.py:652
  23.6 6.9 %collective-permute-start.10 = (bf16[8,64,128]{2,1,0:T(8,128)(2,1)S(1)}, bf16[8,64,128]{2,1,0:T(8,128)(2,1)S(1)}, u32[]{:S(2)}, u32[]{:S(2)}) collective-permute-start(bf16[8,64,128]{2,1,0:T(8,128)(2,1)S(1)} %get-tuple-element.94), channel_id=1, source_target_pairs={{0,4},{1,2},{2,1},{3,7},{4,0},{5,6},{6,5},{7,3},{8,12},{9,10},{10,... | collective-permute-start | bytes 393224 | tf_op jit(solution)/shard_map/ppermute | solution.py:652
  23.9 5.8 %collective-permute-start.13 = (f32[2,8,128]{2,1,0:T(8,128)S(1)}, f32[2,8,128]{2,1,0:T(8,128)S(1)}, u32[]{:S(2)}, u32[]{:S(2)}) collective-permute-start(f32[2,8,128]{2,1,0:T(8,128)S(1)} %blocks.4.after_ref.refs_0_), channel_id=1, source_target_pairs={{0,7},{1,6},{2,5},{3,4},{4,3},{5,2},{6,1},{7,0},{8,15},{9,14},{10,... | collective-permute-start | bytes 24584 | tf_op jit(solution)/shard_map/ppermute | solution.py:652
  26.5 4.0 %collective-permute-start.12 = (f32[2,8,128]{2,1,0:T(8,128)S(1)}, f32[2,8,128]{2,1,0:T(8,128)S(1)}, u32[]{:S(2)}, u32[]{:S(2)}) collective-permute-start(f32[2,8,128]{2,1,0:T(8,128)S(1)} %blocks.4.after_ref.refs_0_), channel_id=1, source_target_pairs={{0,6},{1,7},{2,4},{3,5},{4,2},{5,3},{6,0},{7,1},{8,14},{9,15},{10,... | collective-permute-start | bytes 24584 | tf_op jit(solution)/shard_map/ppermute | solution.py:652
  26.9 3.6 %collective-permute-start.11 = (f32[2,8,128]{2,1,0:T(8,128)S(1)}, f32[2,8,128]{2,1,0:T(8,128)S(1)}, u32[]{:S(2)}, u32[]{:S(2)}) collective-permute-start(f32[2,8,128]{2,1,0:T(8,128)S(1)} %blocks.4.after_ref.refs_0_), channel_id=1, source_target_pairs={{0,5},{1,4},{2,7},{3,6},{4,1},{5,0},{6,3},{7,2},{8,13},{9,12},{10,... | collective-permute-start | bytes 24584 | tf_op jit(solution)/shard_map/ppermute | solution.py:652
  33.2 1.2 %collective-permute-start.14 = (f32[1,8,128]{2,1,0:T(8,128)S(1)}, f32[1,8,128]{2,1,0:T(8,128)S(1)}, u32[]{:S(2)}, u32[]{:S(2)}) collective-permute-start(f32[1,8,128]{2,1,0:T(8,128)S(1)} %bitcast.36), channel_id=1, source_target_pairs={{0,4},{4,0},{1,5},{5,1},{2,6},{6,2},{3,7},{7,3},{8,12},{12,8},{9,1... | collective-permute-start | bytes 12296 | tf_op jit(solution)/shard_map/ppermute | solution.py:624
  34.4 5.7 %collective-permute-start.17 = (f32[2,8,128]{2,1,0:T(8,128)S(1)}, f32[2,8,128]{2,1,0:T(8,128)S(1)}, u32[]{:S(2)}, u32[]{:S(2)}) collective-permute-start(f32[2,8,128]{2,1,0:T(8,128)S(1)} %blocks.5.after_ref.refs_0_), channel_id=1, source_target_pairs={{0,7},{1,6},{2,5},{3,4},{4,3},{5,2},{6,1},{7,0},{8,15},{9,14},{10,... | collective-permute-start | bytes 24584 | tf_op jit(solution)/shard_map/ppermute | solution.py:652
  36.1 4.1 %collective-permute-start.16 = (f32[2,8,128]{2,1,0:T(8,128)S(1)}, f32[2,8,128]{2,1,0:T(8,128)S(1)}, u32[]{:S(2)}, u32[]{:S(2)}) collective-permute-start(f32[2,8,128]{2,1,0:T(8,128)S(1)} %blocks.5.after_ref.refs_0_), channel_id=1, source_target_pairs={{0,6},{1,7},{2,4},{3,5},{4,2},{5,3},{6,0},{7,1},{8,14},{9,15},{10,... | collective-permute-start | bytes 24584 | tf_op jit(solution)/shard_map/ppermute | solution.py:652
  36.2 4.0 %collective-permute-start.15 = (f32[2,8,128]{2,1,0:T(8,128)S(1)}, f32[2,8,128]{2,1,0:T(8,128)S(1)}, u32[]{:S(2)}, u32[]{:S(2)}) collective-permute-start(f32[2,8,128]{2,1,0:T(8,128)S(1)} %blocks.5.after_ref.refs_0_), channel_id=1, source_target_pairs={{0,5},{1,4},{2,7},{3,6},{4,1},{5,0},{6,3},{7,2},{8,13},{9,12},{10,... | collective-permute-start | bytes 24584 | tf_op jit(solution)/shard_map/ppermute | solution.py:652
  42.3 1.7 %collective-permute-start.18 = (bf16[4,304,128]{2,1,0:T(8,128)(2,1)S(1)}, bf16[4,304,128]{2,1,0:T(8,128)(2,1)S(1)}, u32[]{:S(2)}, u32[]{:S(2)}) collective-permute-start(bf16[4,304,128]{2,1,0:T(8,128)(2,1)S(1)} %get-tuple-element.105), channel_id=1, source_target_pairs={{0,4},{4,0},{1,5},{5,1},{2,6},{6,2},{3,7},{7,3},{8,12},{12,8},{9,1... | collective-permute-start | bytes 933896 | tf_op jit(solution)/shard_map/ppermute | solution.py:624
  44.1 5.4 %collective-permute-start.19 = (bf16[304,128]{1,0:T(8,128)(2,1)S(1)}, bf16[304,128]{1,0:T(8,128)(2,1)S(1)}, u32[]{:S(2)}, u32[]{:S(2)}) collective-permute-start(bf16[304,128]{1,0:T(8,128)(2,1)S(1)} %get-tuple-element.109), channel_id=1, source_target_pairs={{0,24},{1,25},{2,26},{3,27},{4,7},{5,6},{6,5},{7,4},{8,16},{9,17},... | collective-permute-start | bytes 233480 | tf_op jit(solution)/shard_map/ppermute | solution.py:636
  46.6 4.4 %collective-permute-start.20 = (bf16[304,128]{1,0:T(8,128)(2,1)S(1)}, bf16[304,128]{1,0:T(8,128)(2,1)S(1)}, u32[]{:S(2)}, u32[]{:S(2)}) collective-permute-start(bf16[304,128]{1,0:T(8,128)(2,1)S(1)} %get-tuple-element.110), channel_id=1, source_target_pairs={{0,16},{1,17},{2,18},{3,19},{4,6},{5,7},{6,4},{7,5},{8,24},{9,25},... | collective-permute-start | bytes 233480 | tf_op jit(solution)/shard_map/ppermute | solution.py:636
  47.1 4.4 %collective-permute-start.21 = (bf16[304,128]{1,0:T(8,128)(2,1)S(1)}, bf16[304,128]{1,0:T(8,128)(2,1)S(1)}, u32[]{:S(2)}, u32[]{:S(2)}) collective-permute-start(bf16[304,128]{1,0:T(8,128)(2,1)S(1)} %get-tuple-element.111), channel_id=1, source_target_pairs={{0,8},{1,9},{2,10},{3,11},{4,5},{5,4},{6,7},{7,6},{8,0},{9,1},{10,... | collective-permute-start | bytes 233480 | tf_op jit(solution)/shard_map/ppermute | solution.py:636
  51.6 6.4 %collective-permute-start.26 = (bf16[304,128]{1,0:T(8,128)(2,1)S(1)}, bf16[304,128]{1,0:T(8,128)(2,1)S(1)}, u32[]{:S(2)}, u32[]{:S(2)}) collective-permute-start(bf16[304,128]{1,0:T(8,128)(2,1)S(1)} %add_first.1.refs_0_), channel_id=1, source_target_pairs={{0,3},{1,2},{2,1},{3,0},{4,28},{5,29},{6,30},{7,31},{8,11},{9,10},... | collective-permute-start | bytes 233480 | tf_op jit(solution)/shard_map/ppermute | solution.py:636
  53.5 6.9 %collective-permute-start.25 = (bf16[304,128]{1,0:T(8,128)(2,1)S(1)}, bf16[304,128]{1,0:T(8,128)(2,1)S(1)}, u32[]{:S(2)}, u32[]{:S(2)}) collective-permute-start(bf16[304,128]{1,0:T(8,128)(2,1)S(1)} %add_first.1.refs_0_), channel_id=1, source_target_pairs={{0,2},{1,3},{2,0},{3,1},{4,20},{5,21},{6,22},{7,23},{8,10},{9,11},... | collective-permute-start | bytes 233480 | tf_op jit(solution)/shard_map/ppermute | solution.py:636
  54.5 5.9 %collective-permute-start.24 = (bf16[304,128]{1,0:T(8,128)(2,1)S(1)}, bf16[304,128]{1,0:T(8,128)(2,1)S(1)}, u32[]{:S(2)}, u32[]{:S(2)}) collective-permute-start(bf16[304,128]{1,0:T(8,128)(2,1)S(1)} %add_first.1.refs_0_), channel_id=1, source_target_pairs={{0,1},{1,0},{2,3},{3,2},{4,12},{5,13},{6,14},{7,15},{8,9},{9,8},{1... | collective-permute-start | bytes 233480 | tf_op jit(solution)/shard_map/ppermute | solution.py:636
  56.1 8.0 %collective-permute-start.22 = (bf16[8,64,128]{2,1,0:T(8,128)(2,1)S(1)}, bf16[8,64,128]{2,1,0:T(8,128)(2,1)S(1)}, u32[]{:S(2)}, u32[]{:S(2)}) collective-permute-start(bf16[8,64,128]{2,1,0:T(8,128)(2,1)S(1)} %get-tuple-element.113), channel_id=1, source_target_pairs={{0,4},{1,2},{2,1},{3,7},{4,0},{5,6},{6,5},{7,3},{8,12},{9,10},{10,... | collective-permute-start | bytes 393224 | tf_op jit(solution)/shard_map/ppermute | solution.py:652
  56.2 7.9 %copy-start.2 = (bf16[1,8,8,64,128]{4,3,2,1,0:T(8,128)(2,1)S(1)}, bf16[1,8,8,64,128]{4,3,2,1,0:T(8,128)(2,1)}, u32[]{:S(2)}) copy-start(bf16[1,8,8,64,128]{4,3,2,1,0:T(8,128)(2,1)} %param.12) | copy-start | bytes 3145732
  56.2 7.9 %collective-permute-start.23 = (bf16[8,64,128]{2,1,0:T(8,128)(2,1)S(1)}, bf16[8,64,128]{2,1,0:T(8,128)(2,1)S(1)}, u32[]{:S(2)}, u32[]{:S(2)}) collective-permute-start(bf16[8,64,128]{2,1,0:T(8,128)(2,1)S(1)} %get-tuple-element.114), channel_id=1, source_target_pairs={{0,1},{1,0},{2,3},{3,2},{4,5},{5,4},{6,7},{7,6},{8,9},{9,8},{10,11... | collective-permute-start | bytes 393224 | tf_op jit(solution)/shard_map/ppermute | solution.py:652
  60.5 5.5 %collective-permute-start.29 = (bf16[304,128]{1,0:T(8,128)(2,1)S(1)}, bf16[304,128]{1,0:T(8,128)(2,1)S(1)}, u32[]{:S(2)}, u32[]{:S(2)}) collective-permute-start(bf16[304,128]{1,0:T(8,128)(2,1)S(1)} %add_second.1.refs_0_), channel_id=1, source_target_pairs={{0,24},{1,25},{2,26},{3,27},{4,7},{5,6},{6,5},{7,4},{8,16},{9,17},... | collective-permute-start | bytes 233480 | tf_op jit(solution)/shard_map/ppermute | solution.py:636
  62.1 4.6 %collective-permute-start.28 = (bf16[304,128]{1,0:T(8,128)(2,1)S(1)}, bf16[304,128]{1,0:T(8,128)(2,1)S(1)}, u32[]{:S(2)}, u32[]{:S(2)}) collective-permute-start(bf16[304,128]{1,0:T(8,128)(2,1)S(1)} %add_second.1.refs_0_), channel_id=1, source_target_pairs={{0,16},{1,17},{2,18},{3,19},{4,6},{5,7},{6,4},{7,5},{8,24},{9,25},... | collective-permute-start | bytes 233480 | tf_op jit(solution)/shard_map/ppermute | solution.py:636
  62.6 4.4 %collective-permute-start.27 = (bf16[304,128]{1,0:T(8,128)(2,1)S(1)}, bf16[304,128]{1,0:T(8,128)(2,1)S(1)}, u32[]{:S(2)}, u32[]{:S(2)}) collective-permute-start(bf16[304,128]{1,0:T(8,128)(2,1)S(1)} %add_second.1.refs_0_), channel_id=1, source_target_pairs={{0,8},{1,9},{2,10},{3,11},{4,5},{5,4},{6,7},{7,6},{8,0},{9,1},{10,... | collective-permute-start | bytes 233480 | tf_op jit(solution)/shard_map/ppermute | solution.py:636
  67.0 1.7 %collective-permute-start.30 = (bf16[1168,128]{1,0:T(8,128)(2,1)S(1)}, bf16[1168,128]{1,0:T(8,128)(2,1)S(1)}, u32[]{:S(2)}, u32[]{:S(2)}) collective-permute-start(bf16[1168,128]{1,0:T(8,128)(2,1)S(1)} %join.1.own_ref), channel_id=1, source_target_pairs={{0,4},{4,0},{1,5},{5,1},{2,6},{6,2},{3,7},{7,3},{8,12},{12,8},{9,1... | collective-permute-start | bytes 897032 | tf_op jit(solution)/shard_map/ppermute | solution.py:624
  (12 other events, 48.8 us)

commit v6 on v5

--- a/solution.py
+++ b/solution.py
@@ -100,15 +100,10 @@
     gp_ref[...] = pick(paired_p, pick(even, top, bottom), jnp.zeros_like(top))
 
 
-def far_rows_kernel(x_ref, mask_ref, hx_ref, hp_ref, bits_ref):
+def far_rows_kernel(x_ref, bits_ref, *refs):
     samples, height, across, c = x_ref.shape
     even = lax.axis_index("lat") % 2 == 0
-    for k in range(bits_ref.shape[0]):
-        bits = mask_ref[k * 128 : (k + 1) * 128].astype(F32)
-        bits = jnp.concatenate([bits, jnp.zeros((bits.shape[0], 128 - across), F32)], 1)
-        if bits.shape[0] < 128:
-            bits = jnp.concatenate([bits, jnp.zeros((128 - bits.shape[0], 128), F32)], 0)
-        bits_ref[k] = bits.T[:across]
+    hx_ref, hp_ref = refs[-2:]
     zero = jnp.zeros((across, c), BF16)
     for out, down, paired in zip((hx_ref, hp_ref), (even, jnp.logical_not(even)), has_pair()):
         first = jnp.where(down, height - 3, 1)
@@ -120,8 +115,14 @@
             out[2 * samples + k] = pick(paired, bits, jnp.zeros_like(bits)).astype(BF16)
 
 
-def masks_kernel(bits_ref, m_ref, count_ref):
+def masks_kernel(mask_ref, x_ref, w_ref, b_ref, m_ref, count_ref, bits_ref):
     samples, height, across, c = m_ref.shape
+    for k in range(bits_ref.shape[0]):
+        bits = mask_ref[k * 128 : (k + 1) * 128].astype(F32)
+        bits = jnp.concatenate([bits, jnp.zeros((bits.shape[0], 128 - across), F32)], 1)
+        if bits.shape[0] < 128:
+            bits = jnp.concatenate([bits, jnp.zeros((128 - bits.shape[0], 128), F32)], 0)
+        bits_ref[k] = bits.T[:across]
     count = jnp.zeros((8, c), F32)
     for s in range(samples):
         for r in range(height):
@@ -787,16 +788,14 @@
     )
     gx, gp = neighbours(*near)
     packed = array((2 * samples + slabs, across, c), BF16)
-    far_x, far_p, bits = call(
-        far_rows_kernel,
-        (packed, packed, array((slabs, across, 128), F32)),
+    wide_mask, count, bits = call(
+        masks_kernel,
+        (shape(height), vector, array((slabs, across, 128), F32)),
         [],
-        (x, mask.reshape(samples * height, across)),
-        "far_rows",
+        (mask.reshape(samples * height, across), x, conv1_weight, b1),
+        "masks",
         conv_flops,
     )
-    hx, hp = neighbours(far_x, far_p)
-    wide_mask, count = call(masks_kernel, (shape(height), vector), [], (bits,), "masks", conv_flops)
     a1, z1, w1t, part = call(
         conv1_inner_kernel,
         (shape(height - 4), shape(height - 4), weights, vector),
@@ -804,6 +803,9 @@
         (x, wide_mask, conv1_weight, b1),
         "conv1_inner",
         4 * conv_flops,
+    )
+    hx, hp = neighbours(
+        *call(far_rows_kernel, (packed, packed), [], (x, bits), "far_rows", conv_flops, (part,))
     )
     a1o, z1o, own1 = call(
         conv1_outer_kernel,

time: 69.9 us -> 69.5 us (level)
  waiting for transfers between devices: 12.7 us -> 11.9 us
  transfers between devices with their start and end apart: 31 -> 31, of which waited for: 15 -> 13; matrix products, arithmetic and copies ran while one was open for 0% -> 0% of each run, Pallas kernels for 18% -> 18%
where the time goes in v6:
time: 69.5 us; the launch traced here: 69.3 us
  starting transfers between devices  33.5 us (48%)
  Pallas kernels  21.8 us (31%)
  waiting for transfers between devices  11.9 us (17%)
  between operations  1.14 us (2%)
  local copies, waits for them, and re-layouts  1.07 us (2%)
    pallas_call x25, Pallas kernels, call(): pl.pallas_call(kernel, out_shape=outs, in_specs=(ins or [spaces[0]] * len...  21.8 us
    ppermute x17, starting transfers between devices, over_dp_and_lat(): return lax.ppermute(value, ('dp', 'lat'), pairs)  20.8 us
    ppermute x9, starting transfers between devices, cross(): return lax.ppermute(value, ('lead', 'dp', 'lat'), pairs)  11.6 us
    ppermute x9, waiting for transfers between devices, cross(): return lax.ppermute(value, ('lead', 'dp', 'lat'), pairs)  6.46 us
    ppermute x5, waiting for transfers between devices, swap(): lax.ppermute(value, axis, [(i, i ^ k) for i in range(lax.axis_size(axis))])  3.33 us
    ppermute x17, waiting for transfers between devices, over_dp_and_lat(): return lax.ppermute(value, ('dp', 'lat'), pairs)  2.08 us
  transfers between devices with their start and end apart: 31, of which 13 were waited for; matrix products, arithmetic and copies ran while one was open for 0% of the time, Pallas kernels for 18%

profile of v6, /device:TPU:0, one launch (start us, length us, event | category | flops | bytes accessed | tf_op | source)
XLA Modules:
  0.0 69.3 jit_solution(10333244102966906292)
XLA Ops:
  0.6 1.0 %fusion = (bf16[8,1,64,128]{3,2,1,0:T(8,128)(2,1)S(1)}, bf16[8,1,64,128]{3,2,1,0:T(8,128)(2,1)S(1)}) fusion(bf16[8,8,64,128]{3,2,1,0:T(8,128)(2,1)} %bitcast.22), kind=kLoop, calls=%fused_computation | loop fusion | bytes 524288 | tf_op jit(solution)/shard_map/slice | solution.py:785
  2.3 4.1 %collective-permute-start.1 = (bf16[8,1,64,128]{3,2,1,0:T(8,128)(2,1)S(1)}, bf16[8,1,64,128]{3,2,1,0:T(8,128)(2,1)S(1)}, u32[]{:S(2)}, u32[]{:S(2)}) collective-permute-start(bf16[8,1,64,128]{3,2,1,0:T(8,128)(2,1)S(1)} %get-tuple-element.70), channel_id=1, source_target_pairs={{0,1},{1,0},{2,3},{3,2},{4,5},{5,4},{6,7},{7,6},{8,9},{9,8},{10,11... | collective-permute-start | bytes 393224 | tf_op jit(solution)/shard_map/ppermute | solution.py:653
  7.3 1.2 %conv1_inner.1 = (f32[8,4,64,128]{3,2,1,0:T(8,128)S(1)}, f32[8,4,64,128]{3,2,1,0:T(8,128)S(1)}, bf16[3,512,256]{2,1,0:T(8,128)(2,1)S(1)}, f32[8,128]{1,0:T(8,128)S(1)}) custom-call(bf16[8,8,64,128]{3,2,1,0:T(8,128)(2,1)S(1)} %bitcast.24, f32[8,8,64,128]{3,2,1,0:T(8,128)S(1)} %get-tuple-element.71.m_ref, bf16[3,3,128,128]{3,2,1,0:T(8,128)(2,1)S(1)} %copy-done.10, ...), custom_call_target="tpu_custom_call" | custom-call | flops 4831838208 | bytes 3441152 | tf_op jit(solution)/shard_map/conv1_inner/pallas_call | solution.py:611
  8.7 1.6 %collective-permute-start.3 = (bf16[17,64,128]{2,1,0:T(8,128)(2,1)S(1)}, bf16[17,64,128]{2,1,0:T(8,128)(2,1)S(1)}, u32[]{:S(2)}, u32[]{:S(2)}) collective-permute-start(bf16[17,64,128]{2,1,0:T(8,128)(2,1)S(1)} %get-tuple-element.80), channel_id=1, source_target_pairs={{0,1},{1,0},{2,3},{3,2},{4,5},{5,4},{6,7},{7,6},{8,9},{9,8},{10,11... | collective-permute-start | bytes 835592 | tf_op jit(solution)/shard_map/ppermute | solution.py:653
  10.3 1.2 %conv1_outer.1 = (f32[8,4,64,128]{3,2,1,0:T(8,128)S(1)}, f32[8,4,64,128]{3,2,1,0:T(8,128)S(1)}, f32[8,128]{1,0:T(8,128)S(1)}) custom-call(bf16[8,1,64,128]{3,2,1,0:T(8,128)(2,1)S(1)} %collective-permute-done.gp_ref, bf16[8,1,64,128]{3,2,1,0:T(8,128)(2,1)S(1)} %collective-permute-done.1.gx_ref, bf16[8,8,64,128]{3,2,1,0:T(8,128)(2,1)S(1)} %bitcast.26, ...), custom_call_target="tpu_custom_call" | custom-call | flops 19327352832 | bytes 4203008 | tf_op jit(solution)/shard_map/conv1_outer/pallas_call | solution.py:611
  12.7 2.3 %collective-permute-start.7 = (f32[2,8,128]{2,1,0:T(8,128)S(1)}, f32[2,8,128]{2,1,0:T(8,128)S(1)}, u32[]{:S(2)}, u32[]{:S(2)}) collective-permute-start(f32[2,8,128]{2,1,0:T(8,128)S(1)} %blocks.3.refs_0_), channel_id=1, source_target_pairs={{0,7},{1,6},{2,5},{3,4},{4,3},{5,2},{6,1},{7,0},{8,15},{9,14},{10,... | collective-permute-start | bytes 24584 | tf_op jit(solution)/shard_map/ppermute | solution.py:653
  15.0 1.6 %collective-permute-start.5 = (f32[2,8,128]{2,1,0:T(8,128)S(1)}, f32[2,8,128]{2,1,0:T(8,128)S(1)}, u32[]{:S(2)}, u32[]{:S(2)}) collective-permute-start(f32[2,8,128]{2,1,0:T(8,128)S(1)} %blocks.3.refs_0_), channel_id=1, source_target_pairs={{0,5},{1,4},{2,7},{3,6},{4,1},{5,0},{6,3},{7,2},{8,13},{9,12},{10,... | collective-permute-start | bytes 24584 | tf_op jit(solution)/shard_map/ppermute | solution.py:653
  16.6 1.2 %collective-permute-done.3.hx_ref = bf16[17,64,128]{2,1,0:T(8,128)(2,1)S(1)} collective-permute-done((bf16[17,64,128]{2,1,0:T(8,128)(2,1)S(1)}, bf16[17,64,128]{2,1,0:T(8,128)(2,1)S(1)}, u32[]{:S(2)}, u32[]{:S(2)}) %collective-permute-start.3) | collective-permute-done | bytes 278560 | tf_op jit(solution)/shard_map/ppermute | solution.py:653
  17.8 1.1 %conv1_edges.1 = (f32[8,4,64,128]{3,2,1,0:T(8,128)S(1)}, f32[8,4,64,128]{3,2,1,0:T(8,128)S(1)}) custom-call(bf16[17,64,128]{2,1,0:T(8,128)(2,1)S(1)} %collective-permute-done.2.hp_ref, bf16[17,64,128]{2,1,0:T(8,128)(2,1)S(1)} %collective-permute-done.3.hx_ref, bf16[8,1,64,128]{3,2,1,0:T(8,128)(2,1)S(1)} %collective-permute-done.gp_ref, ...), custom_call_target="tpu_custom_call" | custom-call | flops 603979776 | bytes 2658816 | tf_op jit(solution)/shard_map/conv1_edges/pallas_call | solution.py:611
  19.0 3.2 %conv2.1 = (bf16[8,10,64,128]{3,2,1,0:T(8,128)(2,1)S(1)}, f32[8,10,64,128]{3,2,1,0:T(8,128)S(1)}, f32[8,10,64,128]{3,2,1,0:T(8,128)S(1)}, f32[8,128]{1,0:T(8,128)S(1)}, f32[8,128]{1,0:T(8,128)S(1)}) custom-call(f32[8,128]{1,0:T(8,128)S(1)} %get-tuple-element.75.st_ref.own_ref.st1_ref, f32[8,4,64,128]{3,2,1,0:T(8,128)S(1)} %get-tuple-element.76.a_ref, ...), custom_call_target="tpu_custom_call" | custom-call | flops 1207959552 | bytes 9217536 | tf_op jit(solution)/shard_map/conv2/pallas_call | solution.py:611
  23.7 2.4 %collective-permute-start.13 = (f32[2,8,128]{2,1,0:T(8,128)S(1)}, f32[2,8,128]{2,1,0:T(8,128)S(1)}, u32[]{:S(2)}, u32[]{:S(2)}) collective-permute-start(f32[2,8,128]{2,1,0:T(8,128)S(1)} %blocks.4.after_ref.refs_0_), channel_id=1, source_target_pairs={{0,7},{1,6},{2,5},{3,4},{4,3},{5,2},{6,1},{7,0},{8,15},{9,14},{10,... | collective-permute-start | bytes 24584 | tf_op jit(solution)/shard_map/ppermute | solution.py:653
  26.6 1.1 %collective-permute-start.11 = (f32[2,8,128]{2,1,0:T(8,128)S(1)}, f32[2,8,128]{2,1,0:T(8,128)S(1)}, u32[]{:S(2)}, u32[]{:S(2)}) collective-permute-start(f32[2,8,128]{2,1,0:T(8,128)S(1)} %blocks.4.after_ref.refs_0_), channel_id=1, source_target_pairs={{0,5},{1,4},{2,7},{3,6},{4,1},{5,0},{6,3},{7,2},{8,13},{9,12},{10,... | collective-permute-start | bytes 24584 | tf_op jit(solution)/shard_map/ppermute | solution.py:653
  27.7 1.6 %slopes.1 = (f32[8,8,64,128]{3,2,1,0:T(8,128)S(1)}, f32[8,10,64,128]{3,2,1,0:T(8,128)S(1)}) custom-call(f32[8,4,64,128]{3,2,1,0:T(8,128)S(1)} %get-tuple-element.89.z_ref, f32[8,4,64,128]{3,2,1,0:T(8,128)S(1)} %get-tuple-element.90.zo_ref, f32[8,10,64,128]{3,2,1,0:T(8,128)S(1)} %get-tuple-element.91.z2_ref, f32[8,8,64,128]{3,2,1,0:T(8,128)S(1)} %get-tuple-element.71.m_ref, ...), custom_call_target="tpu_custom_call" | custom-call | flops 1207959552 | bytes 7864320 | tf_op jit(solution)/shard_map/slopes/pallas_call | solution.py:611
  30.1 2.7 %conv2_back.1 = (bf16[8,8,64,128]{3,2,1,0:T(8,128)(2,1)S(1)}, f32[8,8,64,128]{3,2,1,0:T(8,128)S(1)}, f32[8,128]{1,0:T(8,128)S(1)}, f32[8,128]{1,0:T(8,128)S(1)}) custom-call(f32[8,128]{1,0:T(8,128)S(1)} %get-tuple-element.87.refs_0_.own_ref, f32[8,128]{1,0:T(8,128)S(1)} %get-tuple-element.75.st_ref.own_ref.st1_ref, f32[8,128]{1,0:T(8,128)S(1)} %get-tuple-element.88.c1_ref, ...), custom_call_target="tpu_custom_call" | custom-call | flops 1207959552 | bytes 12628992 | tf_op jit(solution)/shard_map/conv2_back/pallas_call | solution.py:611
  33.0 1.1 %collective-permute-done.14.refs_1_ = f32[1,8,128]{2,1,0:T(8,128)S(1)} collective-permute-done((f32[1,8,128]{2,1,0:T(8,128)S(1)}, f32[1,8,128]{2,1,0:T(8,128)S(1)}, u32[]{:S(2)}, u32[]{:S(2)}) %collective-permute-start.14) | collective-permute-done | bytes 4128 | tf_op jit(solution)/shard_map/ppermute | solution.py:625
  34.0 1.7 %collective-permute-start.17 = (f32[2,8,128]{2,1,0:T(8,128)S(1)}, f32[2,8,128]{2,1,0:T(8,128)S(1)}, u32[]{:S(2)}, u32[]{:S(2)}) collective-permute-start(f32[2,8,128]{2,1,0:T(8,128)S(1)} %blocks.5.after_ref.refs_0_), channel_id=1, source_target_pairs={{0,7},{1,6},{2,5},{3,4},{4,3},{5,2},{6,1},{7,0},{8,15},{9,14},{10,... | collective-permute-start | bytes 24584 | tf_op jit(solution)/shard_map/ppermute | solution.py:653
  36.0 1.9 %collective-permute-start.15 = (f32[2,8,128]{2,1,0:T(8,128)S(1)}, f32[2,8,128]{2,1,0:T(8,128)S(1)}, u32[]{:S(2)}, u32[]{:S(2)}) collective-permute-start(f32[2,8,128]{2,1,0:T(8,128)S(1)} %blocks.5.after_ref.refs_0_), channel_id=1, source_target_pairs={{0,5},{1,4},{2,7},{3,6},{4,1},{5,0},{6,3},{7,2},{8,13},{9,12},{10,... | collective-permute-start | bytes 24584 | tf_op jit(solution)/shard_map/ppermute | solution.py:653
  37.9 1.8 %conv2_weight_grad.1 = (bf16[1152,128]{1,0:T(8,128)(2,1)S(1)}, f32[8,128]{1,0:T(8,128)S(1)}) custom-call(bf16[8,10,64,128]{3,2,1,0:T(8,128)(2,1)S(1)} %get-tuple-element.99.n_ref, bf16[8,8,64,128]{3,2,1,0:T(8,128)(2,1)S(1)} %get-tuple-element.100.d_ref, f32[2,8,128]{2,1,0:T(8,128)S(1)} %blocks.5.after_ref.refs_0_), custom_call_target="tpu_custom_call" | custom-call | flops 1207959552 | bytes 2359296 | tf_op jit(solution)/shard_map/conv2_weight_grad/pallas_call | solution.py:611
  39.8 2.2 %conv1_weight_grad.1 = (bf16[8,8,64,128]{3,2,1,0:T(8,128)(2,1)S(1)}, bf16[4,304,128]{2,1,0:T(8,128)(2,1)S(1)}, bf16[4,304,128]{2,1,0:T(8,128)(2,1)S(1)}) custom-call(f32[8,128]{1,0:T(8,128)S(1)} %get-tuple-element.88.c1_ref, f32[8,128]{1,0:T(8,128)S(1)} %get-tuple-element.96.c2_ref, f32[8,8,64,128]{3,2,1,0:T(8,128)S(1)} %get-tuple-element.97.dn_ref, ...), custom_call_target="tpu_custom_call" | custom-call | flops 1207959552 | bytes 7942656 | tf_op jit(solution)/shard_map/conv1_weight_grad/pallas_call | solution.py:611
  42.3 1.3 %collective-permute-done.18.refs_1_ = bf16[4,304,128]{2,1,0:T(8,128)(2,1)S(1)} collective-permute-done((bf16[4,304,128]{2,1,0:T(8,128)(2,1)S(1)}, bf16[4,304,128]{2,1,0:T(8,128)(2,1)S(1)}, u32[]{:S(2)}, u32[]{:S(2)}) %collective-permute-start.18) | collective-permute-done | bytes 311328 | tf_op jit(solution)/shard_map/ppermute | solution.py:625
  43.7 2.5 %collective-permute-start.19 = (bf16[304,128]{1,0:T(8,128)(2,1)S(1)}, bf16[304,128]{1,0:T(8,128)(2,1)S(1)}, u32[]{:S(2)}, u32[]{:S(2)}) collective-permute-start(bf16[304,128]{1,0:T(8,128)(2,1)S(1)} %get-tuple-element.109), channel_id=1, source_target_pairs={{0,24},{1,25},{2,26},{3,27},{4,7},{5,6},{6,5},{7,4},{8,16},{9,17},... | collective-permute-start | bytes 233480 | tf_op jit(solution)/shard_map/ppermute | solution.py:637
  47.2 1.1 %output.1 = (bf16[8,8,64,128]{3,2,1,0:T(8,128)(2,1)}, f32[8,128]{1,0:T(8,128)S(1)}) custom-call(bf16[8,8,64,128]{3,2,1,0:T(8,128)(2,1)S(1)} %bitcast.29, f32[8,10,64,128]{3,2,1,0:T(8,128)S(1)} %get-tuple-element.86.a2_ref, f32[8,8,64,128]{3,2,1,0:T(8,128)S(1)} %get-tuple-element.71.m_ref, f32[8,128]{1,0:T(8,128)S(1)} %get-tuple-element.96.c2_ref, ...), custom_call_target="tpu_custom_call" | custom-call | flops 603979776 | bytes 5771264 | tf_op jit(solution)/shard_map/output/pallas_call | solution.py:611
  49.0 1.5 %collective-permute-done.20.refs_2_ = bf16[304,128]{1,0:T(8,128)(2,1)S(1)} collective-permute-done((bf16[304,128]{1,0:T(8,128)(2,1)S(1)}, bf16[304,128]{1,0:T(8,128)(2,1)S(1)}, u32[]{:S(2)}, u32[]{:S(2)}) %collective-permute-start.20) | collective-permute-done | bytes 77856 | tf_op jit(solution)/shard_map/ppermute | solution.py:637
  51.1 1.9 %collective-permute-start.26 = (bf16[304,128]{1,0:T(8,128)(2,1)S(1)}, bf16[304,128]{1,0:T(8,128)(2,1)S(1)}, u32[]{:S(2)}, u32[]{:S(2)}) collective-permute-start(bf16[304,128]{1,0:T(8,128)(2,1)S(1)} %add_first.1.refs_0_), channel_id=1, source_target_pairs={{0,3},{1,2},{2,1},{3,0},{4,28},{5,29},{6,30},{7,31},{8,11},{9,10},... | collective-permute-start | bytes 233480 | tf_op jit(solution)/shard_map/ppermute | solution.py:637
  53.1 1.0 %collective-permute-start.25 = (bf16[304,128]{1,0:T(8,128)(2,1)S(1)}, bf16[304,128]{1,0:T(8,128)(2,1)S(1)}, u32[]{:S(2)}, u32[]{:S(2)}) collective-permute-start(bf16[304,128]{1,0:T(8,128)(2,1)S(1)} %add_first.1.refs_0_), channel_id=1, source_target_pairs={{0,2},{1,3},{2,0},{3,1},{4,20},{5,21},{6,22},{7,23},{8,10},{9,11},... | collective-permute-start | bytes 233480 | tf_op jit(solution)/shard_map/ppermute | solution.py:637
  54.1 1.5 %collective-permute-start.24 = (bf16[304,128]{1,0:T(8,128)(2,1)S(1)}, bf16[304,128]{1,0:T(8,128)(2,1)S(1)}, u32[]{:S(2)}, u32[]{:S(2)}) collective-permute-start(bf16[304,128]{1,0:T(8,128)(2,1)S(1)} %add_first.1.refs_0_), channel_id=1, source_target_pairs={{0,1},{1,0},{2,3},{3,2},{4,12},{5,13},{6,14},{7,15},{8,9},{9,8},{1... | collective-permute-start | bytes 233480 | tf_op jit(solution)/shard_map/ppermute | solution.py:637
  55.7 1.5 %collective-permute-start.23 = (bf16[8,64,128]{2,1,0:T(8,128)(2,1)S(1)}, bf16[8,64,128]{2,1,0:T(8,128)(2,1)S(1)}, u32[]{:S(2)}, u32[]{:S(2)}) collective-permute-start(bf16[8,64,128]{2,1,0:T(8,128)(2,1)S(1)} %get-tuple-element.114), channel_id=1, source_target_pairs={{0,1},{1,0},{2,3},{3,2},{4,5},{5,4},{6,7},{7,6},{8,9},{9,8},{10,11... | collective-permute-start | bytes 393224 | tf_op jit(solution)/shard_map/ppermute | solution.py:653
  57.5 2.5 %collective-permute-done.25.refs_2_ = bf16[304,128]{1,0:T(8,128)(2,1)S(1)} collective-permute-done((bf16[304,128]{1,0:T(8,128)(2,1)S(1)}, bf16[304,128]{1,0:T(8,128)(2,1)S(1)}, u32[]{:S(2)}, u32[]{:S(2)}) %collective-permute-start.25) | collective-permute-done | bytes 77856 | tf_op jit(solution)/shard_map/ppermute | solution.py:637
  60.1 1.6 %collective-permute-start.29 = (bf16[304,128]{1,0:T(8,128)(2,1)S(1)}, bf16[304,128]{1,0:T(8,128)(2,1)S(1)}, u32[]{:S(2)}, u32[]{:S(2)}) collective-permute-start(bf16[304,128]{1,0:T(8,128)(2,1)S(1)} %add_second.1.refs_0_), channel_id=1, source_target_pairs={{0,24},{1,25},{2,26},{3,27},{4,7},{5,6},{6,5},{7,4},{8,16},{9,17},... | collective-permute-start | bytes 233480 | tf_op jit(solution)/shard_map/ppermute | solution.py:637
  62.1 1.5 %collective-permute-start.27 = (bf16[304,128]{1,0:T(8,128)(2,1)S(1)}, bf16[304,128]{1,0:T(8,128)(2,1)S(1)}, u32[]{:S(2)}, u32[]{:S(2)}) collective-permute-start(bf16[304,128]{1,0:T(8,128)(2,1)S(1)} %add_second.1.refs_0_), channel_id=1, source_target_pairs={{0,8},{1,9},{2,10},{3,11},{4,5},{5,4},{6,7},{7,6},{8,0},{9,1},{10,... | collective-permute-start | bytes 233480 | tf_op jit(solution)/shard_map/ppermute | solution.py:637
  63.7 1.9 %conv1_back.1 = (bf16[8,8,64,128]{3,2,1,0:T(8,128)(2,1)S(1)}, f32[8,128]{1,0:T(8,128)S(1)}) custom-call(bf16[8,64,128]{2,1,0:T(8,128)(2,1)S(1)} %collective-permute-done.22.ep_ref, bf16[8,64,128]{2,1,0:T(8,128)(2,1)S(1)} %collective-permute-done.23.ex_ref, bf16[8,8,64,128]{3,2,1,0:T(8,128)(2,1)S(1)} %get-tuple-element.108.d_ref, ...), custom_call_target="tpu_custom_call" | custom-call | flops 1207959552 | bytes 2654208 | tf_op jit(solution)/shard_map/conv1_back/pallas_call | solution.py:611
  66.7 1.2 %leave.1 = (bf16[8,8,64,128]{3,2,1,0:T(8,128)(2,1)}, f32[1152,128]{1,0:T(8,128)}, f32[1152,128]{1,0:T(8,128)}) custom-call(bf16[8,8,64,128]{3,2,1,0:T(8,128)(2,1)S(1)} %get-tuple-element.115.grad_ref, bf16[1168,128]{1,0:T(8,128)(2,1)S(1)} %join.1.own_ref), custom_call_target="tpu_custom_call" | custom-call | bytes 1347584 | tf_op jit(solution)/shard_map/leave/pallas_call | solution.py:611
  (82 shorter events, 12.3 us)
Async XLA Ops:
  1.8 8.5 %collective-permute-start = (bf16[8,1,64,128]{3,2,1,0:T(8,128)(2,1)S(1)}, bf16[8,1,64,128]{3,2,1,0:T(8,128)(2,1)S(1)}, u32[]{:S(2)}, u32[]{:S(2)}) collective-permute-start(bf16[8,1,64,128]{3,2,1,0:T(8,128)(2,1)S(1)} %get-tuple-element.69), channel_id=1, source_target_pairs={{0,4},{1,2},{2,1},{3,7},{4,0},{5,6},{6,5},{7,3},{8,12},{9,10},{10,... | collective-permute-start | bytes 393224 | tf_op jit(solution)/shard_map/ppermute | solution.py:653
  2.3 8.0 %collective-permute-start.1 = (bf16[8,1,64,128]{3,2,1,0:T(8,128)(2,1)S(1)}, bf16[8,1,64,128]{3,2,1,0:T(8,128)(2,1)S(1)}, u32[]{:S(2)}, u32[]{:S(2)}) collective-permute-start(bf16[8,1,64,128]{3,2,1,0:T(8,128)(2,1)S(1)} %get-tuple-element.70), channel_id=1, source_target_pairs={{0,1},{1,0},{2,3},{3,2},{4,5},{5,4},{6,7},{7,6},{8,9},{9,8},{10,11... | collective-permute-start | bytes 393224 | tf_op jit(solution)/shard_map/ppermute | solution.py:653
  8.6 8.0 %collective-permute-start.2 = (bf16[17,64,128]{2,1,0:T(8,128)(2,1)S(1)}, bf16[17,64,128]{2,1,0:T(8,128)(2,1)S(1)}, u32[]{:S(2)}, u32[]{:S(2)}) collective-permute-start(bf16[17,64,128]{2,1,0:T(8,128)(2,1)S(1)} %get-tuple-element.79), channel_id=1, source_target_pairs={{0,4},{1,2},{2,1},{3,7},{4,0},{5,6},{6,5},{7,3},{8,12},{9,10},{10,... | collective-permute-start | bytes 835592 | tf_op jit(solution)/shard_map/ppermute | solution.py:653
  8.7 9.2 %collective-permute-start.3 = (bf16[17,64,128]{2,1,0:T(8,128)(2,1)S(1)}, bf16[17,64,128]{2,1,0:T(8,128)(2,1)S(1)}, u32[]{:S(2)}, u32[]{:S(2)}) collective-permute-start(bf16[17,64,128]{2,1,0:T(8,128)(2,1)S(1)} %get-tuple-element.80), channel_id=1, source_target_pairs={{0,1},{1,0},{2,3},{3,2},{4,5},{5,4},{6,7},{7,6},{8,9},{9,8},{10,11... | collective-permute-start | bytes 835592 | tf_op jit(solution)/shard_map/ppermute | solution.py:653
  11.5 1.2 %collective-permute-start.4 = (f32[1,8,128]{2,1,0:T(8,128)S(1)}, f32[1,8,128]{2,1,0:T(8,128)S(1)}, u32[]{:S(2)}, u32[]{:S(2)}) collective-permute-start(f32[1,8,128]{2,1,0:T(8,128)S(1)} %bitcast.33), channel_id=1, source_target_pairs={{0,4},{4,0},{1,5},{5,1},{2,6},{6,2},{3,7},{7,3},{8,12},{12,8},{9,1... | collective-permute-start | bytes 12296 | tf_op jit(solution)/shard_map/ppermute | solution.py:625
  12.7 6.2 %collective-permute-start.7 = (f32[2,8,128]{2,1,0:T(8,128)S(1)}, f32[2,8,128]{2,1,0:T(8,128)S(1)}, u32[]{:S(2)}, u32[]{:S(2)}) collective-permute-start(f32[2,8,128]{2,1,0:T(8,128)S(1)} %blocks.3.refs_0_), channel_id=1, source_target_pairs={{0,7},{1,6},{2,5},{3,4},{4,3},{5,2},{6,1},{7,0},{8,15},{9,14},{10,... | collective-permute-start | bytes 24584 | tf_op jit(solution)/shard_map/ppermute | solution.py:653
  15.0 4.0 %collective-permute-start.6 = (f32[2,8,128]{2,1,0:T(8,128)S(1)}, f32[2,8,128]{2,1,0:T(8,128)S(1)}, u32[]{:S(2)}, u32[]{:S(2)}) collective-permute-start(f32[2,8,128]{2,1,0:T(8,128)S(1)} %blocks.3.refs_0_), channel_id=1, source_target_pairs={{0,6},{1,7},{2,4},{3,5},{4,2},{5,3},{6,0},{7,1},{8,14},{9,15},{10,... | collective-permute-start | bytes 24584 | tf_op jit(solution)/shard_map/ppermute | solution.py:653
  15.0 4.0 %collective-permute-start.5 = (f32[2,8,128]{2,1,0:T(8,128)S(1)}, f32[2,8,128]{2,1,0:T(8,128)S(1)}, u32[]{:S(2)}, u32[]{:S(2)}) collective-permute-start(f32[2,8,128]{2,1,0:T(8,128)S(1)} %blocks.3.refs_0_), channel_id=1, source_target_pairs={{0,5},{1,4},{2,7},{3,6},{4,1},{5,0},{6,3},{7,2},{8,13},{9,12},{10,... | collective-permute-start | bytes 24584 | tf_op jit(solution)/shard_map/ppermute | solution.py:653
  22.2 1.5 %collective-permute-start.8 = (f32[1,8,128]{2,1,0:T(8,128)S(1)}, f32[1,8,128]{2,1,0:T(8,128)S(1)}, u32[]{:S(2)}, u32[]{:S(2)}) collective-permute-start(f32[1,8,128]{2,1,0:T(8,128)S(1)} %bitcast.35), channel_id=1, source_target_pairs={{0,4},{4,0},{1,5},{5,1},{2,6},{6,2},{3,7},{7,3},{8,12},{12,8},{9,1... | collective-permute-start | bytes 12296 | tf_op jit(solution)/shard_map/ppermute | solution.py:625
  22.7 7.4 %collective-permute-start.9 = (bf16[8,64,128]{2,1,0:T(8,128)(2,1)S(1)}, bf16[8,64,128]{2,1,0:T(8,128)(2,1)S(1)}, u32[]{:S(2)}, u32[]{:S(2)}) collective-permute-start(bf16[8,64,128]{2,1,0:T(8,128)(2,1)S(1)} %get-tuple-element.93), channel_id=1, source_target_pairs={{0,1},{1,0},{2,3},{3,2},{4,5},{5,4},{6,7},{7,6},{8,9},{9,8},{10,11... | collective-permute-start | bytes 393224 | tf_op jit(solution)/shard_map/ppermute | solution.py:653
  23.5 6.6 %collective-permute-start.10 = (bf16[8,64,128]{2,1,0:T(8,128)(2,1)S(1)}, bf16[8,64,128]{2,1,0:T(8,128)(2,1)S(1)}, u32[]{:S(2)}, u32[]{:S(2)}) collective-permute-start(bf16[8,64,128]{2,1,0:T(8,128)(2,1)S(1)} %get-tuple-element.94), channel_id=1, source_target_pairs={{0,4},{1,2},{2,1},{3,7},{4,0},{5,6},{6,5},{7,3},{8,12},{9,10},{10,... | collective-permute-start | bytes 393224 | tf_op jit(solution)/shard_map/ppermute | solution.py:653
  23.7 5.6 %collective-permute-start.13 = (f32[2,8,128]{2,1,0:T(8,128)S(1)}, f32[2,8,128]{2,1,0:T(8,128)S(1)}, u32[]{:S(2)}, u32[]{:S(2)}) collective-permute-start(f32[2,8,128]{2,1,0:T(8,128)S(1)} %blocks.4.after_ref.refs_0_), channel_id=1, source_target_pairs={{0,7},{1,6},{2,5},{3,4},{4,3},{5,2},{6,1},{7,0},{8,15},{9,14},{10,... | collective-permute-start | bytes 24584 | tf_op jit(solution)/shard_map/ppermute | solution.py:653
  26.1 4.0 %collective-permute-start.12 = (f32[2,8,128]{2,1,0:T(8,128)S(1)}, f32[2,8,128]{2,1,0:T(8,128)S(1)}, u32[]{:S(2)}, u32[]{:S(2)}) collective-permute-start(f32[2,8,128]{2,1,0:T(8,128)S(1)} %blocks.4.after_ref.refs_0_), channel_id=1, source_target_pairs={{0,6},{1,7},{2,4},{3,5},{4,2},{5,3},{6,0},{7,1},{8,14},{9,15},{10,... | collective-permute-start | bytes 24584 | tf_op jit(solution)/shard_map/ppermute | solution.py:653
  26.6 3.5 %collective-permute-start.11 = (f32[2,8,128]{2,1,0:T(8,128)S(1)}, f32[2,8,128]{2,1,0:T(8,128)S(1)}, u32[]{:S(2)}, u32[]{:S(2)}) collective-permute-start(f32[2,8,128]{2,1,0:T(8,128)S(1)} %blocks.4.after_ref.refs_0_), channel_id=1, source_target_pairs={{0,5},{1,4},{2,7},{3,6},{4,1},{5,0},{6,3},{7,2},{8,13},{9,12},{10,... | collective-permute-start | bytes 24584 | tf_op jit(solution)/shard_map/ppermute | solution.py:653
  32.8 1.2 %collective-permute-start.14 = (f32[1,8,128]{2,1,0:T(8,128)S(1)}, f32[1,8,128]{2,1,0:T(8,128)S(1)}, u32[]{:S(2)}, u32[]{:S(2)}) collective-permute-start(f32[1,8,128]{2,1,0:T(8,128)S(1)} %bitcast.37), channel_id=1, source_target_pairs={{0,4},{4,0},{1,5},{5,1},{2,6},{6,2},{3,7},{7,3},{8,12},{12,8},{9,1... | collective-permute-start | bytes 12296 | tf_op jit(solution)/shard_map/ppermute | solution.py:625
  34.0 5.7 %collective-permute-start.17 = (f32[2,8,128]{2,1,0:T(8,128)S(1)}, f32[2,8,128]{2,1,0:T(8,128)S(1)}, u32[]{:S(2)}, u32[]{:S(2)}) collective-permute-start(f32[2,8,128]{2,1,0:T(8,128)S(1)} %blocks.5.after_ref.refs_0_), channel_id=1, source_target_pairs={{0,7},{1,6},{2,5},{3,4},{4,3},{5,2},{6,1},{7,0},{8,15},{9,14},{10,... | collective-permute-start | bytes 24584 | tf_op jit(solution)/shard_map/ppermute | solution.py:653
  35.7 4.1 %collective-permute-start.16 = (f32[2,8,128]{2,1,0:T(8,128)S(1)}, f32[2,8,128]{2,1,0:T(8,128)S(1)}, u32[]{:S(2)}, u32[]{:S(2)}) collective-permute-start(f32[2,8,128]{2,1,0:T(8,128)S(1)} %blocks.5.after_ref.refs_0_), channel_id=1, source_target_pairs={{0,6},{1,7},{2,4},{3,5},{4,2},{5,3},{6,0},{7,1},{8,14},{9,15},{10,... | collective-permute-start | bytes 24584 | tf_op jit(solution)/shard_map/ppermute | solution.py:653
  36.0 3.7 %collective-permute-start.15 = (f32[2,8,128]{2,1,0:T(8,128)S(1)}, f32[2,8,128]{2,1,0:T(8,128)S(1)}, u32[]{:S(2)}, u32[]{:S(2)}) collective-permute-start(f32[2,8,128]{2,1,0:T(8,128)S(1)} %blocks.5.after_ref.refs_0_), channel_id=1, source_target_pairs={{0,5},{1,4},{2,7},{3,6},{4,1},{5,0},{6,3},{7,2},{8,13},{9,12},{10,... | collective-permute-start | bytes 24584 | tf_op jit(solution)/shard_map/ppermute | solution.py:653
  41.9 1.7 %collective-permute-start.18 = (bf16[4,304,128]{2,1,0:T(8,128)(2,1)S(1)}, bf16[4,304,128]{2,1,0:T(8,128)(2,1)S(1)}, u32[]{:S(2)}, u32[]{:S(2)}) collective-permute-start(bf16[4,304,128]{2,1,0:T(8,128)(2,1)S(1)} %get-tuple-element.105), channel_id=1, source_target_pairs={{0,4},{4,0},{1,5},{5,1},{2,6},{6,2},{3,7},{7,3},{8,12},{12,8},{9,1... | collective-permute-start | bytes 933896 | tf_op jit(solution)/shard_map/ppermute | solution.py:625
  43.7 5.4 %collective-permute-start.19 = (bf16[304,128]{1,0:T(8,128)(2,1)S(1)}, bf16[304,128]{1,0:T(8,128)(2,1)S(1)}, u32[]{:S(2)}, u32[]{:S(2)}) collective-permute-start(bf16[304,128]{1,0:T(8,128)(2,1)S(1)} %get-tuple-element.109), channel_id=1, source_target_pairs={{0,24},{1,25},{2,26},{3,27},{4,7},{5,6},{6,5},{7,4},{8,16},{9,17},... | collective-permute-start | bytes 233480 | tf_op jit(solution)/shard_map/ppermute | solution.py:637
  46.2 4.4 %collective-permute-start.20 = (bf16[304,128]{1,0:T(8,128)(2,1)S(1)}, bf16[304,128]{1,0:T(8,128)(2,1)S(1)}, u32[]{:S(2)}, u32[]{:S(2)}) collective-permute-start(bf16[304,128]{1,0:T(8,128)(2,1)S(1)} %get-tuple-element.110), channel_id=1, source_target_pairs={{0,16},{1,17},{2,18},{3,19},{4,6},{5,7},{6,4},{7,5},{8,24},{9,25},... | collective-permute-start | bytes 233480 | tf_op jit(solution)/shard_map/ppermute | solution.py:637
  46.7 4.4 %collective-permute-start.21 = (bf16[304,128]{1,0:T(8,128)(2,1)S(1)}, bf16[304,128]{1,0:T(8,128)(2,1)S(1)}, u32[]{:S(2)}, u32[]{:S(2)}) collective-permute-start(bf16[304,128]{1,0:T(8,128)(2,1)S(1)} %get-tuple-element.111), channel_id=1, source_target_pairs={{0,8},{1,9},{2,10},{3,11},{4,5},{5,4},{6,7},{7,6},{8,0},{9,1},{10,... | collective-permute-start | bytes 233480 | tf_op jit(solution)/shard_map/ppermute | solution.py:637
  51.1 6.4 %collective-permute-start.26 = (bf16[304,128]{1,0:T(8,128)(2,1)S(1)}, bf16[304,128]{1,0:T(8,128)(2,1)S(1)}, u32[]{:S(2)}, u32[]{:S(2)}) collective-permute-start(bf16[304,128]{1,0:T(8,128)(2,1)S(1)} %add_first.1.refs_0_), channel_id=1, source_target_pairs={{0,3},{1,2},{2,1},{3,0},{4,28},{5,29},{6,30},{7,31},{8,11},{9,10},... | collective-permute-start | bytes 233480 | tf_op jit(solution)/shard_map/ppermute | solution.py:637
  53.1 6.9 %collective-permute-start.25 = (bf16[304,128]{1,0:T(8,128)(2,1)S(1)}, bf16[304,128]{1,0:T(8,128)(2,1)S(1)}, u32[]{:S(2)}, u32[]{:S(2)}) collective-permute-start(bf16[304,128]{1,0:T(8,128)(2,1)S(1)} %add_first.1.refs_0_), channel_id=1, source_target_pairs={{0,2},{1,3},{2,0},{3,1},{4,20},{5,21},{6,22},{7,23},{8,10},{9,11},... | collective-permute-start | bytes 233480 | tf_op jit(solution)/shard_map/ppermute | solution.py:637
  54.1 5.9 %collective-permute-start.24 = (bf16[304,128]{1,0:T(8,128)(2,1)S(1)}, bf16[304,128]{1,0:T(8,128)(2,1)S(1)}, u32[]{:S(2)}, u32[]{:S(2)}) collective-permute-start(bf16[304,128]{1,0:T(8,128)(2,1)S(1)} %add_first.1.refs_0_), channel_id=1, source_target_pairs={{0,1},{1,0},{2,3},{3,2},{4,12},{5,13},{6,14},{7,15},{8,9},{9,8},{1... | collective-permute-start | bytes 233480 | tf_op jit(solution)/shard_map/ppermute | solution.py:637
  55.6 8.0 %collective-permute-start.22 = (bf16[8,64,128]{2,1,0:T(8,128)(2,1)S(1)}, bf16[8,64,128]{2,1,0:T(8,128)(2,1)S(1)}, u32[]{:S(2)}, u32[]{:S(2)}) collective-permute-start(bf16[8,64,128]{2,1,0:T(8,128)(2,1)S(1)} %get-tuple-element.113), channel_id=1, source_target_pairs={{0,4},{1,2},{2,1},{3,7},{4,0},{5,6},{6,5},{7,3},{8,12},{9,10},{10,... | collective-permute-start | bytes 393224 | tf_op jit(solution)/shard_map/ppermute | solution.py:653
  55.7 7.9 %copy-start.2 = (bf16[1,8,8,64,128]{4,3,2,1,0:T(8,128)(2,1)S(1)}, bf16[1,8,8,64,128]{4,3,2,1,0:T(8,128)(2,1)}, u32[]{:S(2)}) copy-start(bf16[1,8,8,64,128]{4,3,2,1,0:T(8,128)(2,1)} %param.12) | copy-start | bytes 3145732
  55.7 7.9 %collective-permute-start.23 = (bf16[8,64,128]{2,1,0:T(8,128)(2,1)S(1)}, bf16[8,64,128]{2,1,0:T(8,128)(2,1)S(1)}, u32[]{:S(2)}, u32[]{:S(2)}) collective-permute-start(bf16[8,64,128]{2,1,0:T(8,128)(2,1)S(1)} %get-tuple-element.114), channel_id=1, source_target_pairs={{0,1},{1,0},{2,3},{3,2},{4,5},{5,4},{6,7},{7,6},{8,9},{9,8},{10,11... | collective-permute-start | bytes 393224 | tf_op jit(solution)/shard_map/ppermute | solution.py:653
  60.1 5.5 %collective-permute-start.29 = (bf16[304,128]{1,0:T(8,128)(2,1)S(1)}, bf16[304,128]{1,0:T(8,128)(2,1)S(1)}, u32[]{:S(2)}, u32[]{:S(2)}) collective-permute-start(bf16[304,128]{1,0:T(8,128)(2,1)S(1)} %add_second.1.refs_0_), channel_id=1, source_target_pairs={{0,24},{1,25},{2,26},{3,27},{4,7},{5,6},{6,5},{7,4},{8,16},{9,17},... | collective-permute-start | bytes 233480 | tf_op jit(solution)/shard_map/ppermute | solution.py:637
  61.6 4.6 %collective-permute-start.28 = (bf16[304,128]{1,0:T(8,128)(2,1)S(1)}, bf16[304,128]{1,0:T(8,128)(2,1)S(1)}, u32[]{:S(2)}, u32[]{:S(2)}) collective-permute-start(bf16[304,128]{1,0:T(8,128)(2,1)S(1)} %add_second.1.refs_0_), channel_id=1, source_target_pairs={{0,16},{1,17},{2,18},{3,19},{4,6},{5,7},{6,4},{7,5},{8,24},{9,25},... | collective-permute-start | bytes 233480 | tf_op jit(solution)/shard_map/ppermute | solution.py:637
  62.1 4.4 %collective-permute-start.27 = (bf16[304,128]{1,0:T(8,128)(2,1)S(1)}, bf16[304,128]{1,0:T(8,128)(2,1)S(1)}, u32[]{:S(2)}, u32[]{:S(2)}) collective-permute-start(bf16[304,128]{1,0:T(8,128)(2,1)S(1)} %add_second.1.refs_0_), channel_id=1, source_target_pairs={{0,8},{1,9},{2,10},{3,11},{4,5},{5,4},{6,7},{7,6},{8,0},{9,1},{10,... | collective-permute-start | bytes 233480 | tf_op jit(solution)/shard_map/ppermute | solution.py:637
  66.6 1.7 %collective-permute-start.30 = (bf16[1168,128]{1,0:T(8,128)(2,1)S(1)}, bf16[1168,128]{1,0:T(8,128)(2,1)S(1)}, u32[]{:S(2)}, u32[]{:S(2)}) collective-permute-start(bf16[1168,128]{1,0:T(8,128)(2,1)S(1)} %join.1.own_ref), channel_id=1, source_target_pairs={{0,4},{4,0},{1,5},{5,1},{2,6},{6,2},{3,7},{7,3},{8,12},{12,8},{9,1... | collective-permute-start | bytes 897032 | tf_op jit(solution)/shard_map/ppermute | solution.py:625
  (12 other events, 55.1 us)

commit v7 on v6

--- a/solution.py
+++ b/solution.py
@@ -702,24 +702,23 @@
     chunks = add_chunks([keep, swap(send, "dp", 1)], "add_dp", leads)
     got = [cross(chunks[k], k, True) for k in reversed(range(1, leads))]
     output = block_output(chunks[0])
-    (mine,) = add_chunks([chunks[0]] + got, "add_first", waits=(output[1],))
+    rows = edges(chunks[0])
+    (mine,) = add_chunks([chunks[0]] + got, "add_first", waits=(output[1],), flops=HIDE)
     got = [cross(mine, k, False) for k in range(1, lats)]
-    rows = edges(mine)
-    (mine,) = add_chunks([mine] + got, "add_second", flops=HIDE)
+    grad_input = input_grad(rows)
+    (mine,) = add_chunks([mine] + got, "add_second", waits=(grad_input[1],))
     k = 2
     while k < lax.axis_size("dp"):
         (mine,) = add_chunks([mine, swap(mine, "dp", k)], "add_far_dp")
         k *= 2
     size, c = mine.shape[0] - SMALL, mine.shape[1]
     got = [cross(mine, k, True) for k in range(1, leads)]
-    grad_input = input_grad(rows)
     own = call(
         functools.partial(join_kernel, leads),
         jax.ShapeDtypeStruct((leads * size + SMALL, c), BF16),
         [],
         (mine, *got),
         "join",
-        waits=(grad_input[1],),
     )
     whole = jax.ShapeDtypeStruct((leads * size, c), F32)
     row = jax.ShapeDtypeStruct((1, c), F32)

time: 69.5 us -> 69.4 us (level)
  waiting for transfers between devices: 11.9 us -> 10.9 us
  starting transfers between devices: 33.5 us -> 34.4 us
    ppermute x9, waiting for transfers between devices: 6.46 us -> 5.53 us  [cross(): return lax.ppermute(value, ('lead', 'dp', 'lat'), pairs)]
    ppermute x17, starting transfers between devices: 20.8 us -> 21.7 us  [over_dp_and_lat(): return lax.ppermute(value, ('dp', 'lat'), pairs)]
  transfers between devices with their start and end apart: 31 -> 31, of which waited for: 13 -> 11; matrix products, arithmetic and copies ran while one was open for 0% -> 0% of each run, Pallas kernels for 18% -> 18%
where the time goes in v7:
time: 69.4 us; the launch traced here: 69.3 us
  starting transfers between devices  34.4 us (50%)
  Pallas kernels  21.8 us (31%)
  waiting for transfers between devices  10.9 us (16%)
  between operations  1.14 us (2%)
  local copies, waits for them, and re-layouts  1.06 us (2%)
    pallas_call x25, Pallas kernels, call(): pl.pallas_call(kernel, out_shape=outs, in_specs=(ins or [spaces[0]] * len...  21.8 us
    ppermute x17, starting transfers between devices, over_dp_and_lat(): return lax.ppermute(value, ('dp', 'lat'), pairs)  21.7 us
    ppermute x9, starting transfers between devices, cross(): return lax.ppermute(value, ('lead', 'dp', 'lat'), pairs)  11.6 us
    ppermute x9, waiting for transfers between devices, cross(): return lax.ppermute(value, ('lead', 'dp', 'lat'), pairs)  5.53 us
    ppermute x5, waiting for transfers between devices, swap(): lax.ppermute(value, axis, [(i, i ^ k) for i in range(lax.axis_size(axis))])  3.33 us
    ppermute x17, waiting for transfers between devices, over_dp_and_lat(): return lax.ppermute(value, ('dp', 'lat'), pairs)  2.08 us
  transfers between devices with their start and end apart: 31, of which 11 were waited for; matrix products, arithmetic and copies ran while one was open for 0% of the time, Pallas kernels for 18%

profile of v7, /device:TPU:0, one launch (start us, length us, event | category | flops | bytes accessed | tf_op | source)
XLA Modules:
  0.0 69.3 jit_solution(17845154754524015398)
XLA Ops:
  0.6 1.0 %fusion = (bf16[8,1,64,128]{3,2,1,0:T(8,128)(2,1)S(1)}, bf16[8,1,64,128]{3,2,1,0:T(8,128)(2,1)S(1)}) fusion(bf16[8,8,64,128]{3,2,1,0:T(8,128)(2,1)} %bitcast.22), kind=kLoop, calls=%fused_computation | loop fusion | bytes 524288 | tf_op jit(solution)/shard_map/slice | solution.py:784
  2.3 4.1 %collective-permute-start.1 = (bf16[8,1,64,128]{3,2,1,0:T(8,128)(2,1)S(1)}, bf16[8,1,64,128]{3,2,1,0:T(8,128)(2,1)S(1)}, u32[]{:S(2)}, u32[]{:S(2)}) collective-permute-start(bf16[8,1,64,128]{3,2,1,0:T(8,128)(2,1)S(1)} %get-tuple-element.70), channel_id=1, source_target_pairs={{0,1},{1,0},{2,3},{3,2},{4,5},{5,4},{6,7},{7,6},{8,9},{9,8},{10,11... | collective-permute-start | bytes 393224 | tf_op jit(solution)/shard_map/ppermute | solution.py:653
  7.3 1.2 %conv1_inner.1 = (f32[8,4,64,128]{3,2,1,0:T(8,128)S(1)}, f32[8,4,64,128]{3,2,1,0:T(8,128)S(1)}, bf16[3,512,256]{2,1,0:T(8,128)(2,1)S(1)}, f32[8,128]{1,0:T(8,128)S(1)}) custom-call(bf16[8,8,64,128]{3,2,1,0:T(8,128)(2,1)S(1)} %bitcast.24, f32[8,8,64,128]{3,2,1,0:T(8,128)S(1)} %get-tuple-element.71.m_ref, bf16[3,3,128,128]{3,2,1,0:T(8,128)(2,1)S(1)} %copy-done.10, ...), custom_call_target="tpu_custom_call" | custom-call | flops 4831838208 | bytes 3441152 | tf_op jit(solution)/shard_map/conv1_inner/pallas_call | solution.py:611
  8.7 1.6 %collective-permute-start.3 = (bf16[17,64,128]{2,1,0:T(8,128)(2,1)S(1)}, bf16[17,64,128]{2,1,0:T(8,128)(2,1)S(1)}, u32[]{:S(2)}, u32[]{:S(2)}) collective-permute-start(bf16[17,64,128]{2,1,0:T(8,128)(2,1)S(1)} %get-tuple-element.80), channel_id=1, source_target_pairs={{0,1},{1,0},{2,3},{3,2},{4,5},{5,4},{6,7},{7,6},{8,9},{9,8},{10,11... | collective-permute-start | bytes 835592 | tf_op jit(solution)/shard_map/ppermute | solution.py:653
  10.3 1.2 %conv1_outer.1 = (f32[8,4,64,128]{3,2,1,0:T(8,128)S(1)}, f32[8,4,64,128]{3,2,1,0:T(8,128)S(1)}, f32[8,128]{1,0:T(8,128)S(1)}) custom-call(bf16[8,1,64,128]{3,2,1,0:T(8,128)(2,1)S(1)} %collective-permute-done.gp_ref, bf16[8,1,64,128]{3,2,1,0:T(8,128)(2,1)S(1)} %collective-permute-done.1.gx_ref, bf16[8,8,64,128]{3,2,1,0:T(8,128)(2,1)S(1)} %bitcast.26, ...), custom_call_target="tpu_custom_call" | custom-call | flops 19327352832 | bytes 4203008 | tf_op jit(solution)/shard_map/conv1_outer/pallas_call | solution.py:611
  12.7 2.3 %collective-permute-start.7 = (f32[2,8,128]{2,1,0:T(8,128)S(1)}, f32[2,8,128]{2,1,0:T(8,128)S(1)}, u32[]{:S(2)}, u32[]{:S(2)}) collective-permute-start(f32[2,8,128]{2,1,0:T(8,128)S(1)} %blocks.3.refs_0_), channel_id=1, source_target_pairs={{0,7},{1,6},{2,5},{3,4},{4,3},{5,2},{6,1},{7,0},{8,15},{9,14},{10,... | collective-permute-start | bytes 24584 | tf_op jit(solution)/shard_map/ppermute | solution.py:653
  15.0 1.6 %collective-permute-start.5 = (f32[2,8,128]{2,1,0:T(8,128)S(1)}, f32[2,8,128]{2,1,0:T(8,128)S(1)}, u32[]{:S(2)}, u32[]{:S(2)}) collective-permute-start(f32[2,8,128]{2,1,0:T(8,128)S(1)} %blocks.3.refs_0_), channel_id=1, source_target_pairs={{0,5},{1,4},{2,7},{3,6},{4,1},{5,0},{6,3},{7,2},{8,13},{9,12},{10,... | collective-permute-start | bytes 24584 | tf_op jit(solution)/shard_map/ppermute | solution.py:653
  16.6 1.2 %collective-permute-done.3.hx_ref = bf16[17,64,128]{2,1,0:T(8,128)(2,1)S(1)} collective-permute-done((bf16[17,64,128]{2,1,0:T(8,128)(2,1)S(1)}, bf16[17,64,128]{2,1,0:T(8,128)(2,1)S(1)}, u32[]{:S(2)}, u32[]{:S(2)}) %collective-permute-start.3) | collective-permute-done | bytes 278560 | tf_op jit(solution)/shard_map/ppermute | solution.py:653
  17.8 1.1 %conv1_edges.1 = (f32[8,4,64,128]{3,2,1,0:T(8,128)S(1)}, f32[8,4,64,128]{3,2,1,0:T(8,128)S(1)}) custom-call(bf16[17,64,128]{2,1,0:T(8,128)(2,1)S(1)} %collective-permute-done.2.hp_ref, bf16[17,64,128]{2,1,0:T(8,128)(2,1)S(1)} %collective-permute-done.3.hx_ref, bf16[8,1,64,128]{3,2,1,0:T(8,128)(2,1)S(1)} %collective-permute-done.gp_ref, ...), custom_call_target="tpu_custom_call" | custom-call | flops 603979776 | bytes 2658816 | tf_op jit(solution)/shard_map/conv1_edges/pallas_call | solution.py:611
  19.0 3.2 %conv2.1 = (bf16[8,10,64,128]{3,2,1,0:T(8,128)(2,1)S(1)}, f32[8,10,64,128]{3,2,1,0:T(8,128)S(1)}, f32[8,10,64,128]{3,2,1,0:T(8,128)S(1)}, f32[8,128]{1,0:T(8,128)S(1)}, f32[8,128]{1,0:T(8,128)S(1)}) custom-call(f32[8,128]{1,0:T(8,128)S(1)} %get-tuple-element.75.st_ref.own_ref.st1_ref, f32[8,4,64,128]{3,2,1,0:T(8,128)S(1)} %get-tuple-element.76.a_ref, ...), custom_call_target="tpu_custom_call" | custom-call | flops 1207959552 | bytes 9217536 | tf_op jit(solution)/shard_map/conv2/pallas_call | solution.py:611
  23.7 2.4 %collective-permute-start.13 = (f32[2,8,128]{2,1,0:T(8,128)S(1)}, f32[2,8,128]{2,1,0:T(8,128)S(1)}, u32[]{:S(2)}, u32[]{:S(2)}) collective-permute-start(f32[2,8,128]{2,1,0:T(8,128)S(1)} %blocks.4.after_ref.refs_0_), channel_id=1, source_target_pairs={{0,7},{1,6},{2,5},{3,4},{4,3},{5,2},{6,1},{7,0},{8,15},{9,14},{10,... | collective-permute-start | bytes 24584 | tf_op jit(solution)/shard_map/ppermute | solution.py:653
  26.6 1.1 %collective-permute-start.11 = (f32[2,8,128]{2,1,0:T(8,128)S(1)}, f32[2,8,128]{2,1,0:T(8,128)S(1)}, u32[]{:S(2)}, u32[]{:S(2)}) collective-permute-start(f32[2,8,128]{2,1,0:T(8,128)S(1)} %blocks.4.after_ref.refs_0_), channel_id=1, source_target_pairs={{0,5},{1,4},{2,7},{3,6},{4,1},{5,0},{6,3},{7,2},{8,13},{9,12},{10,... | collective-permute-start | bytes 24584 | tf_op jit(solution)/shard_map/ppermute | solution.py:653
  27.7 1.6 %slopes.1 = (f32[8,8,64,128]{3,2,1,0:T(8,128)S(1)}, f32[8,10,64,128]{3,2,1,0:T(8,128)S(1)}) custom-call(f32[8,4,64,128]{3,2,1,0:T(8,128)S(1)} %get-tuple-element.89.z_ref, f32[8,4,64,128]{3,2,1,0:T(8,128)S(1)} %get-tuple-element.90.zo_ref, f32[8,10,64,128]{3,2,1,0:T(8,128)S(1)} %get-tuple-element.91.z2_ref, f32[8,8,64,128]{3,2,1,0:T(8,128)S(1)} %get-tuple-element.71.m_ref, ...), custom_call_target="tpu_custom_call" | custom-call | flops 1207959552 | bytes 7864320 | tf_op jit(solution)/shard_map/slopes/pallas_call | solution.py:611
  30.1 2.7 %conv2_back.1 = (bf16[8,8,64,128]{3,2,1,0:T(8,128)(2,1)S(1)}, f32[8,8,64,128]{3,2,1,0:T(8,128)S(1)}, f32[8,128]{1,0:T(8,128)S(1)}, f32[8,128]{1,0:T(8,128)S(1)}) custom-call(f32[8,128]{1,0:T(8,128)S(1)} %get-tuple-element.87.refs_0_.own_ref, f32[8,128]{1,0:T(8,128)S(1)} %get-tuple-element.75.st_ref.own_ref.st1_ref, f32[8,128]{1,0:T(8,128)S(1)} %get-tuple-element.88.c1_ref, ...), custom_call_target="tpu_custom_call" | custom-call | flops 1207959552 | bytes 12628992 | tf_op jit(solution)/shard_map/conv2_back/pallas_call | solution.py:611
  33.0 1.1 %collective-permute-done.14.refs_1_ = f32[1,8,128]{2,1,0:T(8,128)S(1)} collective-permute-done((f32[1,8,128]{2,1,0:T(8,128)S(1)}, f32[1,8,128]{2,1,0:T(8,128)S(1)}, u32[]{:S(2)}, u32[]{:S(2)}) %collective-permute-start.14) | collective-permute-done | bytes 4128 | tf_op jit(solution)/shard_map/ppermute | solution.py:625
  34.0 1.7 %collective-permute-start.17 = (f32[2,8,128]{2,1,0:T(8,128)S(1)}, f32[2,8,128]{2,1,0:T(8,128)S(1)}, u32[]{:S(2)}, u32[]{:S(2)}) collective-permute-start(f32[2,8,128]{2,1,0:T(8,128)S(1)} %blocks.5.after_ref.refs_0_), channel_id=1, source_target_pairs={{0,7},{1,6},{2,5},{3,4},{4,3},{5,2},{6,1},{7,0},{8,15},{9,14},{10,... | collective-permute-start | bytes 24584 | tf_op jit(solution)/shard_map/ppermute | solution.py:653
  36.0 1.9 %collective-permute-start.15 = (f32[2,8,128]{2,1,0:T(8,128)S(1)}, f32[2,8,128]{2,1,0:T(8,128)S(1)}, u32[]{:S(2)}, u32[]{:S(2)}) collective-permute-start(f32[2,8,128]{2,1,0:T(8,128)S(1)} %blocks.5.after_ref.refs_0_), channel_id=1, source_target_pairs={{0,5},{1,4},{2,7},{3,6},{4,1},{5,0},{6,3},{7,2},{8,13},{9,12},{10,... | collective-permute-start | bytes 24584 | tf_op jit(solution)/shard_map/ppermute | solution.py:653
  37.9 1.8 %conv2_weight_grad.1 = (bf16[1152,128]{1,0:T(8,128)(2,1)S(1)}, f32[8,128]{1,0:T(8,128)S(1)}) custom-call(bf16[8,10,64,128]{3,2,1,0:T(8,128)(2,1)S(1)} %get-tuple-element.99.n_ref, bf16[8,8,64,128]{3,2,1,0:T(8,128)(2,1)S(1)} %get-tuple-element.100.d_ref, f32[2,8,128]{2,1,0:T(8,128)S(1)} %blocks.5.after_ref.refs_0_), custom_call_target="tpu_custom_call" | custom-call | flops 1207959552 | bytes 2359296 | tf_op jit(solution)/shard_map/conv2_weight_grad/pallas_call | solution.py:611
  39.8 2.2 %conv1_weight_grad.1 = (bf16[8,8,64,128]{3,2,1,0:T(8,128)(2,1)S(1)}, bf16[4,304,128]{2,1,0:T(8,128)(2,1)S(1)}, bf16[4,304,128]{2,1,0:T(8,128)(2,1)S(1)}) custom-call(f32[8,128]{1,0:T(8,128)S(1)} %get-tuple-element.88.c1_ref, f32[8,128]{1,0:T(8,128)S(1)} %get-tuple-element.96.c2_ref, f32[8,8,64,128]{3,2,1,0:T(8,128)S(1)} %get-tuple-element.97.dn_ref, ...), custom_call_target="tpu_custom_call" | custom-call | flops 1207959552 | bytes 7942656 | tf_op jit(solution)/shard_map/conv1_weight_grad/pallas_call | solution.py:611
  42.3 1.3 %collective-permute-done.18.refs_1_ = bf16[4,304,128]{2,1,0:T(8,128)(2,1)S(1)} collective-permute-done((bf16[4,304,128]{2,1,0:T(8,128)(2,1)S(1)}, bf16[4,304,128]{2,1,0:T(8,128)(2,1)S(1)}, u32[]{:S(2)}, u32[]{:S(2)}) %collective-permute-start.18) | collective-permute-done | bytes 311328 | tf_op jit(solution)/shard_map/ppermute | solution.py:625
  43.7 2.5 %collective-permute-start.21 = (bf16[304,128]{1,0:T(8,128)(2,1)S(1)}, bf16[304,128]{1,0:T(8,128)(2,1)S(1)}, u32[]{:S(2)}, u32[]{:S(2)}) collective-permute-start(bf16[304,128]{1,0:T(8,128)(2,1)S(1)} %get-tuple-element.112), channel_id=1, source_target_pairs={{0,24},{1,25},{2,26},{3,27},{4,7},{5,6},{6,5},{7,4},{8,16},{9,17},... | collective-permute-start | bytes 233480 | tf_op jit(solution)/shard_map/ppermute | solution.py:637
  47.8 2.0 %collective-permute-start.20 = (bf16[8,64,128]{2,1,0:T(8,128)(2,1)S(1)}, bf16[8,64,128]{2,1,0:T(8,128)(2,1)S(1)}, u32[]{:S(2)}, u32[]{:S(2)}) collective-permute-start(bf16[8,64,128]{2,1,0:T(8,128)(2,1)S(1)} %get-tuple-element.110), channel_id=1, source_target_pairs={{0,1},{1,0},{2,3},{3,2},{4,5},{5,4},{6,7},{7,6},{8,9},{9,8},{10,11... | collective-permute-start | bytes 393224 | tf_op jit(solution)/shard_map/ppermute | solution.py:653
  49.8 1.1 %output.1 = (bf16[8,8,64,128]{3,2,1,0:T(8,128)(2,1)}, f32[8,128]{1,0:T(8,128)S(1)}) custom-call(bf16[8,8,64,128]{3,2,1,0:T(8,128)(2,1)S(1)} %bitcast.29, f32[8,10,64,128]{3,2,1,0:T(8,128)S(1)} %get-tuple-element.86.a2_ref, f32[8,8,64,128]{3,2,1,0:T(8,128)S(1)} %get-tuple-element.71.m_ref, f32[8,128]{1,0:T(8,128)S(1)} %get-tuple-element.96.c2_ref, ...), custom_call_target="tpu_custom_call" | custom-call | flops 603979776 | bytes 5771264 | tf_op jit(solution)/shard_map/output/pallas_call | solution.py:611
  51.1 1.9 %collective-permute-start.26 = (bf16[304,128]{1,0:T(8,128)(2,1)S(1)}, bf16[304,128]{1,0:T(8,128)(2,1)S(1)}, u32[]{:S(2)}, u32[]{:S(2)}) collective-permute-start(bf16[304,128]{1,0:T(8,128)(2,1)S(1)} %add_first.1.refs_0_), channel_id=1, source_target_pairs={{0,3},{1,2},{2,1},{3,0},{4,28},{5,29},{6,30},{7,31},{8,11},{9,10},... | collective-permute-start | bytes 233480 | tf_op jit(solution)/shard_map/ppermute | solution.py:637
  53.1 1.0 %collective-permute-start.25 = (bf16[304,128]{1,0:T(8,128)(2,1)S(1)}, bf16[304,128]{1,0:T(8,128)(2,1)S(1)}, u32[]{:S(2)}, u32[]{:S(2)}) collective-permute-start(bf16[304,128]{1,0:T(8,128)(2,1)S(1)} %add_first.1.refs_0_), channel_id=1, source_target_pairs={{0,2},{1,3},{2,0},{3,1},{4,20},{5,21},{6,22},{7,23},{8,10},{9,11},... | collective-permute-start | bytes 233480 | tf_op jit(solution)/shard_map/ppermute | solution.py:637
  54.1 1.5 %collective-permute-start.24 = (bf16[304,128]{1,0:T(8,128)(2,1)S(1)}, bf16[304,128]{1,0:T(8,128)(2,1)S(1)}, u32[]{:S(2)}, u32[]{:S(2)}) collective-permute-start(bf16[304,128]{1,0:T(8,128)(2,1)S(1)} %add_first.1.refs_0_), channel_id=1, source_target_pairs={{0,1},{1,0},{2,3},{3,2},{4,12},{5,13},{6,14},{7,15},{8,9},{9,8},{1... | collective-permute-start | bytes 233480 | tf_op jit(solution)/shard_map/ppermute | solution.py:637
  55.6 1.9 %conv1_back.1 = (bf16[8,8,64,128]{3,2,1,0:T(8,128)(2,1)S(1)}, f32[8,128]{1,0:T(8,128)S(1)}) custom-call(bf16[8,64,128]{2,1,0:T(8,128)(2,1)S(1)} %collective-permute-done.19.ep_ref, bf16[8,64,128]{2,1,0:T(8,128)(2,1)S(1)} %collective-permute-done.20.ex_ref, bf16[8,8,64,128]{3,2,1,0:T(8,128)(2,1)S(1)} %get-tuple-element.108.d_ref, ...), custom_call_target="tpu_custom_call" | custom-call | flops 1207959552 | bytes 2654208 | tf_op jit(solution)/shard_map/conv1_back/pallas_call | solution.py:611
  57.6 1.7 %collective-permute-done.25.refs_2_ = bf16[304,128]{1,0:T(8,128)(2,1)S(1)} collective-permute-done((bf16[304,128]{1,0:T(8,128)(2,1)S(1)}, bf16[304,128]{1,0:T(8,128)(2,1)S(1)}, u32[]{:S(2)}, u32[]{:S(2)}) %collective-permute-start.25) | collective-permute-done | bytes 77856 | tf_op jit(solution)/shard_map/ppermute | solution.py:637
  59.4 2.7 %collective-permute-start.29 = (bf16[304,128]{1,0:T(8,128)(2,1)S(1)}, bf16[304,128]{1,0:T(8,128)(2,1)S(1)}, u32[]{:S(2)}, u32[]{:S(2)}) collective-permute-start(bf16[304,128]{1,0:T(8,128)(2,1)S(1)} %add_second.1.refs_0_), channel_id=1, source_target_pairs={{0,24},{1,25},{2,26},{3,27},{4,7},{5,6},{6,5},{7,4},{8,16},{9,17},... | collective-permute-start | bytes 233480 | tf_op jit(solution)/shard_map/ppermute | solution.py:637
  62.9 1.8 %collective-permute-done.29.refs_3_ = bf16[304,128]{1,0:T(8,128)(2,1)S(1)} collective-permute-done((bf16[304,128]{1,0:T(8,128)(2,1)S(1)}, bf16[304,128]{1,0:T(8,128)(2,1)S(1)}, u32[]{:S(2)}, u32[]{:S(2)}) %collective-permute-start.29) | collective-permute-done | bytes 77856 | tf_op jit(solution)/shard_map/ppermute | solution.py:637
  64.7 1.7 %collective-permute-done.28.refs_2_ = bf16[304,128]{1,0:T(8,128)(2,1)S(1)} collective-permute-done((bf16[304,128]{1,0:T(8,128)(2,1)S(1)}, bf16[304,128]{1,0:T(8,128)(2,1)S(1)}, u32[]{:S(2)}, u32[]{:S(2)}) %collective-permute-start.28) | collective-permute-done | bytes 77856 | tf_op jit(solution)/shard_map/ppermute | solution.py:637
  66.6 1.2 %leave.1 = (bf16[8,8,64,128]{3,2,1,0:T(8,128)(2,1)}, f32[1152,128]{1,0:T(8,128)}, f32[1152,128]{1,0:T(8,128)}) custom-call(bf16[8,8,64,128]{3,2,1,0:T(8,128)(2,1)S(1)} %get-tuple-element.111.grad_ref, bf16[1168,128]{1,0:T(8,128)(2,1)S(1)} %join.1.own_ref), custom_call_target="tpu_custom_call" | custom-call | bytes 1347584 | tf_op jit(solution)/shard_map/leave/pallas_call | solution.py:611
  (82 shorter events, 10.9 us)
Async XLA Ops:
  1.8 8.5 %collective-permute-start = (bf16[8,1,64,128]{3,2,1,0:T(8,128)(2,1)S(1)}, bf16[8,1,64,128]{3,2,1,0:T(8,128)(2,1)S(1)}, u32[]{:S(2)}, u32[]{:S(2)}) collective-permute-start(bf16[8,1,64,128]{3,2,1,0:T(8,128)(2,1)S(1)} %get-tuple-element.69), channel_id=1, source_target_pairs={{0,4},{1,2},{2,1},{3,7},{4,0},{5,6},{6,5},{7,3},{8,12},{9,10},{10,... | collective-permute-start | bytes 393224 | tf_op jit(solution)/shard_map/ppermute | solution.py:653
  2.3 8.0 %collective-permute-start.1 = (bf16[8,1,64,128]{3,2,1,0:T(8,128)(2,1)S(1)}, bf16[8,1,64,128]{3,2,1,0:T(8,128)(2,1)S(1)}, u32[]{:S(2)}, u32[]{:S(2)}) collective-permute-start(bf16[8,1,64,128]{3,2,1,0:T(8,128)(2,1)S(1)} %get-tuple-element.70), channel_id=1, source_target_pairs={{0,1},{1,0},{2,3},{3,2},{4,5},{5,4},{6,7},{7,6},{8,9},{9,8},{10,11... | collective-permute-start | bytes 393224 | tf_op jit(solution)/shard_map/ppermute | solution.py:653
  8.6 8.0 %collective-permute-start.2 = (bf16[17,64,128]{2,1,0:T(8,128)(2,1)S(1)}, bf16[17,64,128]{2,1,0:T(8,128)(2,1)S(1)}, u32[]{:S(2)}, u32[]{:S(2)}) collective-permute-start(bf16[17,64,128]{2,1,0:T(8,128)(2,1)S(1)} %get-tuple-element.79), channel_id=1, source_target_pairs={{0,4},{1,2},{2,1},{3,7},{4,0},{5,6},{6,5},{7,3},{8,12},{9,10},{10,... | collective-permute-start | bytes 835592 | tf_op jit(solution)/shard_map/ppermute | solution.py:653
  8.7 9.2 %collective-permute-start.3 = (bf16[17,64,128]{2,1,0:T(8,128)(2,1)S(1)}, bf16[17,64,128]{2,1,0:T(8,128)(2,1)S(1)}, u32[]{:S(2)}, u32[]{:S(2)}) collective-permute-start(bf16[17,64,128]{2,1,0:T(8,128)(2,1)S(1)} %get-tuple-element.80), channel_id=1, source_target_pairs={{0,1},{1,0},{2,3},{3,2},{4,5},{5,4},{6,7},{7,6},{8,9},{9,8},{10,11... | collective-permute-start | bytes 835592 | tf_op jit(solution)/shard_map/ppermute | solution.py:653
  11.5 1.2 %collective-permute-start.4 = (f32[1,8,128]{2,1,0:T(8,128)S(1)}, f32[1,8,128]{2,1,0:T(8,128)S(1)}, u32[]{:S(2)}, u32[]{:S(2)}) collective-permute-start(f32[1,8,128]{2,1,0:T(8,128)S(1)} %bitcast.33), channel_id=1, source_target_pairs={{0,4},{4,0},{1,5},{5,1},{2,6},{6,2},{3,7},{7,3},{8,12},{12,8},{9,1... | collective-permute-start | bytes 12296 | tf_op jit(solution)/shard_map/ppermute | solution.py:625
  12.0 6.9 %copy-start.3 = (f32[128]{0:T(128)S(1)}, f32[128]{0:T(128)}, u32[]{:S(2)}) copy-start(f32[128]{0:T(128)} %param.16) | copy-start | bytes 1540
  12.7 6.2 %collective-permute-start.7 = (f32[2,8,128]{2,1,0:T(8,128)S(1)}, f32[2,8,128]{2,1,0:T(8,128)S(1)}, u32[]{:S(2)}, u32[]{:S(2)}) collective-permute-start(f32[2,8,128]{2,1,0:T(8,128)S(1)} %blocks.3.refs_0_), channel_id=1, source_target_pairs={{0,7},{1,6},{2,5},{3,4},{4,3},{5,2},{6,1},{7,0},{8,15},{9,14},{10,... | collective-permute-start | bytes 24584 | tf_op jit(solution)/shard_map/ppermute | solution.py:653
  15.0 4.0 %collective-permute-start.6 = (f32[2,8,128]{2,1,0:T(8,128)S(1)}, f32[2,8,128]{2,1,0:T(8,128)S(1)}, u32[]{:S(2)}, u32[]{:S(2)}) collective-permute-start(f32[2,8,128]{2,1,0:T(8,128)S(1)} %blocks.3.refs_0_), channel_id=1, source_target_pairs={{0,6},{1,7},{2,4},{3,5},{4,2},{5,3},{6,0},{7,1},{8,14},{9,15},{10,... | collective-permute-start | bytes 24584 | tf_op jit(solution)/shard_map/ppermute | solution.py:653
  15.0 4.0 %collective-permute-start.5 = (f32[2,8,128]{2,1,0:T(8,128)S(1)}, f32[2,8,128]{2,1,0:T(8,128)S(1)}, u32[]{:S(2)}, u32[]{:S(2)}) collective-permute-start(f32[2,8,128]{2,1,0:T(8,128)S(1)} %blocks.3.refs_0_), channel_id=1, source_target_pairs={{0,5},{1,4},{2,7},{3,6},{4,1},{5,0},{6,3},{7,2},{8,13},{9,12},{10,... | collective-permute-start | bytes 24584 | tf_op jit(solution)/shard_map/ppermute | solution.py:653
  22.2 1.5 %collective-permute-start.8 = (f32[1,8,128]{2,1,0:T(8,128)S(1)}, f32[1,8,128]{2,1,0:T(8,128)S(1)}, u32[]{:S(2)}, u32[]{:S(2)}) collective-permute-start(f32[1,8,128]{2,1,0:T(8,128)S(1)} %bitcast.35), channel_id=1, source_target_pairs={{0,4},{4,0},{1,5},{5,1},{2,6},{6,2},{3,7},{7,3},{8,12},{12,8},{9,1... | collective-permute-start | bytes 12296 | tf_op jit(solution)/shard_map/ppermute | solution.py:625
  22.7 7.4 %collective-permute-start.9 = (bf16[8,64,128]{2,1,0:T(8,128)(2,1)S(1)}, bf16[8,64,128]{2,1,0:T(8,128)(2,1)S(1)}, u32[]{:S(2)}, u32[]{:S(2)}) collective-permute-start(bf16[8,64,128]{2,1,0:T(8,128)(2,1)S(1)} %get-tuple-element.93), channel_id=1, source_target_pairs={{0,1},{1,0},{2,3},{3,2},{4,5},{5,4},{6,7},{7,6},{8,9},{9,8},{10,11... | collective-permute-start | bytes 393224 | tf_op jit(solution)/shard_map/ppermute | solution.py:653
  23.5 6.6 %collective-permute-start.10 = (bf16[8,64,128]{2,1,0:T(8,128)(2,1)S(1)}, bf16[8,64,128]{2,1,0:T(8,128)(2,1)S(1)}, u32[]{:S(2)}, u32[]{:S(2)}) collective-permute-start(bf16[8,64,128]{2,1,0:T(8,128)(2,1)S(1)} %get-tuple-element.94), channel_id=1, source_target_pairs={{0,4},{1,2},{2,1},{3,7},{4,0},{5,6},{6,5},{7,3},{8,12},{9,10},{10,... | collective-permute-start | bytes 393224 | tf_op jit(solution)/shard_map/ppermute | solution.py:653
  23.7 5.6 %collective-permute-start.13 = (f32[2,8,128]{2,1,0:T(8,128)S(1)}, f32[2,8,128]{2,1,0:T(8,128)S(1)}, u32[]{:S(2)}, u32[]{:S(2)}) collective-permute-start(f32[2,8,128]{2,1,0:T(8,128)S(1)} %blocks.4.after_ref.refs_0_), channel_id=1, source_target_pairs={{0,7},{1,6},{2,5},{3,4},{4,3},{5,2},{6,1},{7,0},{8,15},{9,14},{10,... | collective-permute-start | bytes 24584 | tf_op jit(solution)/shard_map/ppermute | solution.py:653
  26.1 4.0 %collective-permute-start.12 = (f32[2,8,128]{2,1,0:T(8,128)S(1)}, f32[2,8,128]{2,1,0:T(8,128)S(1)}, u32[]{:S(2)}, u32[]{:S(2)}) collective-permute-start(f32[2,8,128]{2,1,0:T(8,128)S(1)} %blocks.4.after_ref.refs_0_), channel_id=1, source_target_pairs={{0,6},{1,7},{2,4},{3,5},{4,2},{5,3},{6,0},{7,1},{8,14},{9,15},{10,... | collective-permute-start | bytes 24584 | tf_op jit(solution)/shard_map/ppermute | solution.py:653
  26.6 3.5 %collective-permute-start.11 = (f32[2,8,128]{2,1,0:T(8,128)S(1)}, f32[2,8,128]{2,1,0:T(8,128)S(1)}, u32[]{:S(2)}, u32[]{:S(2)}) collective-permute-start(f32[2,8,128]{2,1,0:T(8,128)S(1)} %blocks.4.after_ref.refs_0_), channel_id=1, source_target_pairs={{0,5},{1,4},{2,7},{3,6},{4,1},{5,0},{6,3},{7,2},{8,13},{9,12},{10,... | collective-permute-start | bytes 24584 | tf_op jit(solution)/shard_map/ppermute | solution.py:653
  32.8 1.2 %collective-permute-start.14 = (f32[1,8,128]{2,1,0:T(8,128)S(1)}, f32[1,8,128]{2,1,0:T(8,128)S(1)}, u32[]{:S(2)}, u32[]{:S(2)}) collective-permute-start(f32[1,8,128]{2,1,0:T(8,128)S(1)} %bitcast.37), channel_id=1, source_target_pairs={{0,4},{4,0},{1,5},{5,1},{2,6},{6,2},{3,7},{7,3},{8,12},{12,8},{9,1... | collective-permute-start | bytes 12296 | tf_op jit(solution)/shard_map/ppermute | solution.py:625
  34.0 5.7 %collective-permute-start.17 = (f32[2,8,128]{2,1,0:T(8,128)S(1)}, f32[2,8,128]{2,1,0:T(8,128)S(1)}, u32[]{:S(2)}, u32[]{:S(2)}) collective-permute-start(f32[2,8,128]{2,1,0:T(8,128)S(1)} %blocks.5.after_ref.refs_0_), channel_id=1, source_target_pairs={{0,7},{1,6},{2,5},{3,4},{4,3},{5,2},{6,1},{7,0},{8,15},{9,14},{10,... | collective-permute-start | bytes 24584 | tf_op jit(solution)/shard_map/ppermute | solution.py:653
  35.7 4.1 %collective-permute-start.16 = (f32[2,8,128]{2,1,0:T(8,128)S(1)}, f32[2,8,128]{2,1,0:T(8,128)S(1)}, u32[]{:S(2)}, u32[]{:S(2)}) collective-permute-start(f32[2,8,128]{2,1,0:T(8,128)S(1)} %blocks.5.after_ref.refs_0_), channel_id=1, source_target_pairs={{0,6},{1,7},{2,4},{3,5},{4,2},{5,3},{6,0},{7,1},{8,14},{9,15},{10,... | collective-permute-start | bytes 24584 | tf_op jit(solution)/shard_map/ppermute | solution.py:653
  36.0 3.7 %collective-permute-start.15 = (f32[2,8,128]{2,1,0:T(8,128)S(1)}, f32[2,8,128]{2,1,0:T(8,128)S(1)}, u32[]{:S(2)}, u32[]{:S(2)}) collective-permute-start(f32[2,8,128]{2,1,0:T(8,128)S(1)} %blocks.5.after_ref.refs_0_), channel_id=1, source_target_pairs={{0,5},{1,4},{2,7},{3,6},{4,1},{5,0},{6,3},{7,2},{8,13},{9,12},{10,... | collective-permute-start | bytes 24584 | tf_op jit(solution)/shard_map/ppermute | solution.py:653
  41.9 1.7 %collective-permute-start.18 = (bf16[4,304,128]{2,1,0:T(8,128)(2,1)S(1)}, bf16[4,304,128]{2,1,0:T(8,128)(2,1)S(1)}, u32[]{:S(2)}, u32[]{:S(2)}) collective-permute-start(bf16[4,304,128]{2,1,0:T(8,128)(2,1)S(1)} %get-tuple-element.105), channel_id=1, source_target_pairs={{0,4},{4,0},{1,5},{5,1},{2,6},{6,2},{3,7},{7,3},{8,12},{12,8},{9,1... | collective-permute-start | bytes 933896 | tf_op jit(solution)/shard_map/ppermute | solution.py:625
  43.7 7.2 %collective-permute-start.21 = (bf16[304,128]{1,0:T(8,128)(2,1)S(1)}, bf16[304,128]{1,0:T(8,128)(2,1)S(1)}, u32[]{:S(2)}, u32[]{:S(2)}) collective-permute-start(bf16[304,128]{1,0:T(8,128)(2,1)S(1)} %get-tuple-element.112), channel_id=1, source_target_pairs={{0,24},{1,25},{2,26},{3,27},{4,7},{5,6},{6,5},{7,4},{8,16},{9,17},... | collective-permute-start | bytes 233480 | tf_op jit(solution)/shard_map/ppermute | solution.py:637
  46.2 4.7 %collective-permute-start.22 = (bf16[304,128]{1,0:T(8,128)(2,1)S(1)}, bf16[304,128]{1,0:T(8,128)(2,1)S(1)}, u32[]{:S(2)}, u32[]{:S(2)}) collective-permute-start(bf16[304,128]{1,0:T(8,128)(2,1)S(1)} %get-tuple-element.113), channel_id=1, source_target_pairs={{0,16},{1,17},{2,18},{3,19},{4,6},{5,7},{6,4},{7,5},{8,24},{9,25},... | collective-permute-start | bytes 233480 | tf_op jit(solution)/shard_map/ppermute | solution.py:637
  46.7 4.4 %collective-permute-start.23 = (bf16[304,128]{1,0:T(8,128)(2,1)S(1)}, bf16[304,128]{1,0:T(8,128)(2,1)S(1)}, u32[]{:S(2)}, u32[]{:S(2)}) collective-permute-start(bf16[304,128]{1,0:T(8,128)(2,1)S(1)} %get-tuple-element.114), channel_id=1, source_target_pairs={{0,8},{1,9},{2,10},{3,11},{4,5},{5,4},{6,7},{7,6},{8,0},{9,1},{10,... | collective-permute-start | bytes 233480 | tf_op jit(solution)/shard_map/ppermute | solution.py:637
  47.3 8.3 %collective-permute-start.19 = (bf16[8,64,128]{2,1,0:T(8,128)(2,1)S(1)}, bf16[8,64,128]{2,1,0:T(8,128)(2,1)S(1)}, u32[]{:S(2)}, u32[]{:S(2)}) collective-permute-start(bf16[8,64,128]{2,1,0:T(8,128)(2,1)S(1)} %get-tuple-element.109), channel_id=1, source_target_pairs={{0,4},{1,2},{2,1},{3,7},{4,0},{5,6},{6,5},{7,3},{8,12},{9,10},{10,... | collective-permute-start | bytes 393224 | tf_op jit(solution)/shard_map/ppermute | solution.py:653
  47.8 7.8 %collective-permute-start.20 = (bf16[8,64,128]{2,1,0:T(8,128)(2,1)S(1)}, bf16[8,64,128]{2,1,0:T(8,128)(2,1)S(1)}, u32[]{:S(2)}, u32[]{:S(2)}) collective-permute-start(bf16[8,64,128]{2,1,0:T(8,128)(2,1)S(1)} %get-tuple-element.110), channel_id=1, source_target_pairs={{0,1},{1,0},{2,3},{3,2},{4,5},{5,4},{6,7},{7,6},{8,9},{9,8},{10,11... | collective-permute-start | bytes 393224 | tf_op jit(solution)/shard_map/ppermute | solution.py:653
  51.1 6.4 %collective-permute-start.26 = (bf16[304,128]{1,0:T(8,128)(2,1)S(1)}, bf16[304,128]{1,0:T(8,128)(2,1)S(1)}, u32[]{:S(2)}, u32[]{:S(2)}) collective-permute-start(bf16[304,128]{1,0:T(8,128)(2,1)S(1)} %add_first.1.refs_0_), channel_id=1, source_target_pairs={{0,3},{1,2},{2,1},{3,0},{4,28},{5,29},{6,30},{7,31},{8,11},{9,10},... | collective-permute-start | bytes 233480 | tf_op jit(solution)/shard_map/ppermute | solution.py:637
  53.1 6.2 %collective-permute-start.25 = (bf16[304,128]{1,0:T(8,128)(2,1)S(1)}, bf16[304,128]{1,0:T(8,128)(2,1)S(1)}, u32[]{:S(2)}, u32[]{:S(2)}) collective-permute-start(bf16[304,128]{1,0:T(8,128)(2,1)S(1)} %add_first.1.refs_0_), channel_id=1, source_target_pairs={{0,2},{1,3},{2,0},{3,1},{4,20},{5,21},{6,22},{7,23},{8,10},{9,11},... | collective-permute-start | bytes 233480 | tf_op jit(solution)/shard_map/ppermute | solution.py:637
  54.1 5.2 %collective-permute-start.24 = (bf16[304,128]{1,0:T(8,128)(2,1)S(1)}, bf16[304,128]{1,0:T(8,128)(2,1)S(1)}, u32[]{:S(2)}, u32[]{:S(2)}) collective-permute-start(bf16[304,128]{1,0:T(8,128)(2,1)S(1)} %add_first.1.refs_0_), channel_id=1, source_target_pairs={{0,1},{1,0},{2,3},{3,2},{4,12},{5,13},{6,14},{7,15},{8,9},{9,8},{1... | collective-permute-start | bytes 233480 | tf_op jit(solution)/shard_map/ppermute | solution.py:637
  59.4 5.4 %collective-permute-start.29 = (bf16[304,128]{1,0:T(8,128)(2,1)S(1)}, bf16[304,128]{1,0:T(8,128)(2,1)S(1)}, u32[]{:S(2)}, u32[]{:S(2)}) collective-permute-start(bf16[304,128]{1,0:T(8,128)(2,1)S(1)} %add_second.1.refs_0_), channel_id=1, source_target_pairs={{0,24},{1,25},{2,26},{3,27},{4,7},{5,6},{6,5},{7,4},{8,16},{9,17},... | collective-permute-start | bytes 233480 | tf_op jit(solution)/shard_map/ppermute | solution.py:637
  62.0 4.4 %collective-permute-start.28 = (bf16[304,128]{1,0:T(8,128)(2,1)S(1)}, bf16[304,128]{1,0:T(8,128)(2,1)S(1)}, u32[]{:S(2)}, u32[]{:S(2)}) collective-permute-start(bf16[304,128]{1,0:T(8,128)(2,1)S(1)} %add_second.1.refs_0_), channel_id=1, source_target_pairs={{0,16},{1,17},{2,18},{3,19},{4,6},{5,7},{6,4},{7,5},{8,24},{9,25},... | collective-permute-start | bytes 233480 | tf_op jit(solution)/shard_map/ppermute | solution.py:637
  62.1 4.4 %collective-permute-start.27 = (bf16[304,128]{1,0:T(8,128)(2,1)S(1)}, bf16[304,128]{1,0:T(8,128)(2,1)S(1)}, u32[]{:S(2)}, u32[]{:S(2)}) collective-permute-start(bf16[304,128]{1,0:T(8,128)(2,1)S(1)} %add_second.1.refs_0_), channel_id=1, source_target_pairs={{0,8},{1,9},{2,10},{3,11},{4,5},{5,4},{6,7},{7,6},{8,0},{9,1},{10,... | collective-permute-start | bytes 233480 | tf_op jit(solution)/shard_map/ppermute | solution.py:637
  66.5 1.7 %collective-permute-start.30 = (bf16[1168,128]{1,0:T(8,128)(2,1)S(1)}, bf16[1168,128]{1,0:T(8,128)(2,1)S(1)}, u32[]{:S(2)}, u32[]{:S(2)}) collective-permute-start(bf16[1168,128]{1,0:T(8,128)(2,1)S(1)} %join.1.own_ref), channel_id=1, source_target_pairs={{0,4},{4,0},{1,5},{5,1},{2,6},{6,2},{3,7},{7,3},{8,12},{12,8},{9,1... | collective-permute-start | bytes 897032 | tf_op jit(solution)/shard_map/ppermute | solution.py:625
  (12 other events, 49.3 us)

commit v8 on v7

--- a/solution.py
+++ b/solution.py
@@ -265,7 +265,7 @@
     pieces,
     own_ref, a_ref, ao_ref, ah_ref, m_ref, mh_ref, mu_ref, su_ref, k_ref, b_ref, g_ref, t_ref, *refs,
 ):
-    stats, (n_ref, a2_ref, z2_ref, c1_ref, st2_ref, ext_ref) = gather(refs[:pieces]), refs[pieces:]
+    stats, (n_ref, a2_ref, z2_ref, c1_ref, st2_ref) = gather(refs[:pieces]), refs[pieces:]
     samples, height, across, c = m_ref.shape
     counts = stats[:, 3:4]
     count = counts.sum(0)
@@ -278,7 +278,6 @@
     sums = [jnp.zeros((8, c), F32) for _ in range(3)]
     centre = None
     for s in range(samples):
-        ext = ext_ref.at[s % 2]
         for i in range(height + 4):
             r = i - 2
             if 0 <= r < height:
@@ -286,12 +285,10 @@
             else:
                 j = i if r < 0 else r - height + 2
                 value, mask = ah_ref[s, j], mh_ref[s, j]
-            ext[i] = ((value * scale + shift) * mask).astype(BF16)
-            if 1 <= i < height + 3:
-                n_ref[s, i - 1] = ext[i]
+            n_ref[s, i] = ((value * scale + shift) * mask).astype(BF16)
 
         piece = convolve_rows(
-            lambda r: ext[r + 2], range(-1, height + 1, 2), k_ref, across, False
+            lambda r: n_ref[s, r + 2], range(-1, height + 1, 2), k_ref, across, False
         )
         for i in range(height + 2):
             r = i - 1
@@ -332,7 +329,7 @@
     pieces,
     own_ref, st1_ref, c1_ref, a2_ref, s2_ref, mu_ref, ux_ref, up_ref, m_ref, a_ref, ao_ref, k_ref, g_ref, t_ref, *refs,
 ):
-    stats, (d_ref, dn_ref, c2_ref, st3_ref, ext_ref) = gather(refs[:pieces]), refs[pieces:]
+    stats, (d_ref, dn_ref, c2_ref, st3_ref) = gather(refs[:pieces]), refs[pieces:]
     samples, height, across, c = m_ref.shape
     even = lax.axis_index("lat") % 2 == 0
     count = c1_ref[2:3]
@@ -346,7 +343,6 @@
     c2_ref[...] = stats_block([scale, t_ref[...] - offset * scale, gain_sum, shift_sum], c)
     sums = [jnp.zeros((8, c), F32) for _ in range(2)]
     for s in range(samples):
-        ext = ext_ref.at[s % 2]
         for i in range(height + 2):
             if 0 < i <= height:
                 upstream = mu_ref[s, i - 1]
@@ -354,11 +350,9 @@
                 edges = (up_ref[s], ux_ref[s]) if i == 0 else (ux_ref[s], up_ref[s])
                 upstream = pick(even, *edges).astype(F32)
             grad = upstream * scale + (a2_ref[s, i] * by_active + constant)
-            ext[i] = (grad * s2_ref[s, i]).astype(BF16)
-            if 0 < i <= height:
-                d_ref[s, i - 1] = ext[i]
+            d_ref[s, i] = (grad * s2_ref[s, i]).astype(BF16)
         piece = convolve_rows(
-            lambda r: ext[r + 1], range(0, height, 2), k_ref, across, True
+            lambda r: d_ref[s, r + 1], range(0, height, 2), k_ref, across, True
         )
         for r in range(height):
             part = piece(r // 2, r % 2)
@@ -392,13 +386,14 @@
 
 
 def weight2_kernel(n_ref, d_ref, after_ref, w_ref, b_ref, acc_ref):
-    samples, height, across, c = d_ref.shape
+    samples, rows, across, c = d_ref.shape
+    height = rows - 2
     bias = jnp.zeros((8, c), F32)
     for s in range(samples):
-        grad = d_ref[s]
+        grad = d_ref[s, 1 : 1 + height]
         wide = grad.astype(F32)
         bias += fold(wide)
-        rows = [n_ref[s, a : a + height].reshape(-1, c) for a in range(3)]
+        rows = [n_ref[s, a + 1 : a + 1 + height].reshape(-1, c) for a in range(3)]
         weight_products(rows, grad.reshape(-1, c), turn(wide, across), acc_ref, s == 0)
     b_ref[...] = jnp.broadcast_to(bias.sum(0, keepdims=True), b_ref.shape)
     for a in range(3):
@@ -680,7 +675,7 @@
         k *= 2
     return [blocks] + [
         over_dp_and_lat(blocks, lambda dp, lat, k=k: (dp ^ 1, lat ^ k))
-        for k in range(1, lax.axis_size("lat"))
+        for k in [1, *reversed(range(2, lax.axis_size("lat")))]
     ]
 
 
@@ -773,7 +768,6 @@
     vector = array((8, c), F32)
     weights = array((3, 4 * c, 2 * c), BF16)
     turned = array((3, 2 * c, 4 * c), BF16)
-    ext = lambda rows: pltpu.VMEM((2, rows, across, c), BF16)
     acc = pltpu.VMEM((3 * c, 3 * c), F32)
     conv_flops = 2 * 9 * c * c * samples * height * across
 
@@ -833,8 +827,8 @@
     st1 = spread(own1)
     n1, a2, z2, c1, own2 = call(
         functools.partial(conv2_kernel, len(st1)),
-        (shape(height + 2, BF16), shape(height + 2), shape(height + 2), vector, vector),
-        [ext(height + 4)],
+        (shape(height + 4, BF16), shape(height + 2), shape(height + 2), vector, vector),
+        [],
         (own1, a1, a1o, a1h, wide_mask, halo_mask, mu, mu_sum, w2t, b2, g1, t1, *st1),
         "conv2",
         conv_flops,
@@ -852,8 +846,8 @@
     )
     d2, dn1, c2, own3 = call(
         functools.partial(back2_kernel, len(st2)),
-        (shape(height, BF16), shape(height), vector, vector),
-        [ext(height + 2)],
+        (shape(height + 2, BF16), shape(height), vector, vector),
+        [],
         (own2, own1, c1, a2, s2, mu, ux, up, wide_mask, a1, a1o, w2tt, g2, t2, *st2),
         "conv2_back",
         conv_flops,

time: 69.4 us -> 68.9 us (level)
  starting transfers between devices: 34.4 us -> 32 us
  waiting for transfers between devices: 10.9 us -> 13 us
    ppermute x17, waiting for transfers between devices: 2.08 us -> 4.25 us  [over_dp_and_lat(): return lax.ppermute(value, ('dp', 'lat'), pairs)]
    ppermute x17, starting transfers between devices: 21.7 us -> 19.6 us  [over_dp_and_lat(): return lax.ppermute(value, ('dp', 'lat'), pairs)]
  transfers between devices with their start and end apart: 31 -> 31, of which waited for: 11 -> 15; matrix products, arithmetic and copies ran while one was open for 0% -> 0% of each run, Pallas kernels for 18% -> 18%
where the time goes in v8:
time: 68.9 us; the launch traced here: 68.7 us
  starting transfers between devices  32 us (46%)
  Pallas kernels  21.5 us (31%)
  waiting for transfers between devices  13 us (19%)
  between operations  1.15 us (2%)
  local copies, waits for them, and re-layouts  1.06 us (2%)
    pallas_call x25, Pallas kernels, call(): pl.pallas_call(kernel, out_shape=outs, in_specs=(ins or [spaces[0]] * len...  21.5 us
    ppermute x17, starting transfers between devices, over_dp_and_lat(): return lax.ppermute(value, ('dp', 'lat'), pairs)  19.6 us
    ppermute x9, starting transfers between devices, cross(): return lax.ppermute(value, ('lead', 'dp', 'lat'), pairs)  11.6 us
    ppermute x9, waiting for transfers between devices, cross(): return lax.ppermute(value, ('lead', 'dp', 'lat'), pairs)  5.41 us
    ppermute x17, waiting for transfers between devices, over_dp_and_lat(): return lax.ppermute(value, ('dp', 'lat'), pairs)  4.25 us
    ppermute x5, waiting for transfers between devices, swap(): lax.ppermute(value, axis, [(i, i ^ k) for i in range(lax.axis_size(axis))])  3.35 us
  transfers between devices with their start and end apart: 31, of which 15 were waited for; matrix products, arithmetic and copies ran while one was open for 0% of the time, Pallas kernels for 18%

profile of v8, /device:TPU:0, one launch (start us, length us, event | category | flops | bytes accessed | tf_op | source)
XLA Modules:
  0.0 68.7 jit_solution(10950779330774066698)
XLA Ops:
  0.6 1.0 %fusion = (bf16[8,1,64,128]{3,2,1,0:T(8,128)(2,1)S(1)}, bf16[8,1,64,128]{3,2,1,0:T(8,128)(2,1)S(1)}) fusion(bf16[8,8,64,128]{3,2,1,0:T(8,128)(2,1)} %bitcast.22), kind=kLoop, calls=%fused_computation | loop fusion | bytes 524288 | tf_op jit(solution)/shard_map/slice | solution.py:778
  2.3 4.1 %collective-permute-start.1 = (bf16[8,1,64,128]{3,2,1,0:T(8,128)(2,1)S(1)}, bf16[8,1,64,128]{3,2,1,0:T(8,128)(2,1)S(1)}, u32[]{:S(2)}, u32[]{:S(2)}) collective-permute-start(bf16[8,1,64,128]{3,2,1,0:T(8,128)(2,1)S(1)} %get-tuple-element.70), channel_id=1, source_target_pairs={{0,1},{1,0},{2,3},{3,2},{4,5},{5,4},{6,7},{7,6},{8,9},{9,8},{10,11... | collective-permute-start | bytes 393224 | tf_op jit(solution)/shard_map/ppermute | solution.py:648
  7.3 1.2 %conv1_inner.1 = (f32[8,4,64,128]{3,2,1,0:T(8,128)S(1)}, f32[8,4,64,128]{3,2,1,0:T(8,128)S(1)}, bf16[3,512,256]{2,1,0:T(8,128)(2,1)S(1)}, f32[8,128]{1,0:T(8,128)S(1)}) custom-call(bf16[8,8,64,128]{3,2,1,0:T(8,128)(2,1)S(1)} %bitcast.24, f32[8,8,64,128]{3,2,1,0:T(8,128)S(1)} %get-tuple-element.71.m_ref, bf16[3,3,128,128]{3,2,1,0:T(8,128)(2,1)S(1)} %copy-done.10, ...), custom_call_target="tpu_custom_call" | custom-call | flops 4831838208 | bytes 3441152 | tf_op jit(solution)/shard_map/conv1_inner/pallas_call | solution.py:606
  8.7 1.6 %collective-permute-start.3 = (bf16[17,64,128]{2,1,0:T(8,128)(2,1)S(1)}, bf16[17,64,128]{2,1,0:T(8,128)(2,1)S(1)}, u32[]{:S(2)}, u32[]{:S(2)}) collective-permute-start(bf16[17,64,128]{2,1,0:T(8,128)(2,1)S(1)} %get-tuple-element.80), channel_id=1, source_target_pairs={{0,1},{1,0},{2,3},{3,2},{4,5},{5,4},{6,7},{7,6},{8,9},{9,8},{10,11... | collective-permute-start | bytes 835592 | tf_op jit(solution)/shard_map/ppermute | solution.py:648
  10.3 1.2 %conv1_outer.1 = (f32[8,4,64,128]{3,2,1,0:T(8,128)S(1)}, f32[8,4,64,128]{3,2,1,0:T(8,128)S(1)}, f32[8,128]{1,0:T(8,128)S(1)}) custom-call(bf16[8,1,64,128]{3,2,1,0:T(8,128)(2,1)S(1)} %collective-permute-done.gp_ref, bf16[8,1,64,128]{3,2,1,0:T(8,128)(2,1)S(1)} %collective-permute-done.1.gx_ref, bf16[8,8,64,128]{3,2,1,0:T(8,128)(2,1)S(1)} %bitcast.26, ...), custom_call_target="tpu_custom_call" | custom-call | flops 19327352832 | bytes 4203008 | tf_op jit(solution)/shard_map/conv1_outer/pallas_call | solution.py:606
  12.7 1.1 %collective-permute-start.7 = (f32[2,8,128]{2,1,0:T(8,128)S(1)}, f32[2,8,128]{2,1,0:T(8,128)S(1)}, u32[]{:S(2)}, u32[]{:S(2)}) collective-permute-start(f32[2,8,128]{2,1,0:T(8,128)S(1)} %blocks.3.refs_0_), channel_id=1, source_target_pairs={{0,6},{1,7},{2,4},{3,5},{4,2},{5,3},{6,0},{7,1},{8,14},{9,15},{10,... | collective-permute-start | bytes 24584 | tf_op jit(solution)/shard_map/ppermute | solution.py:648
  13.8 2.1 %collective-permute-start.6 = (f32[2,8,128]{2,1,0:T(8,128)S(1)}, f32[2,8,128]{2,1,0:T(8,128)S(1)}, u32[]{:S(2)}, u32[]{:S(2)}) collective-permute-start(f32[2,8,128]{2,1,0:T(8,128)S(1)} %blocks.3.refs_0_), channel_id=1, source_target_pairs={{0,7},{1,6},{2,5},{3,4},{4,3},{5,2},{6,1},{7,0},{8,15},{9,14},{10,... | collective-permute-start | bytes 24584 | tf_op jit(solution)/shard_map/ppermute | solution.py:648
  15.9 2.0 %collective-permute-done.3.hx_ref = bf16[17,64,128]{2,1,0:T(8,128)(2,1)S(1)} collective-permute-done((bf16[17,64,128]{2,1,0:T(8,128)(2,1)S(1)}, bf16[17,64,128]{2,1,0:T(8,128)(2,1)S(1)}, u32[]{:S(2)}, u32[]{:S(2)}) %collective-permute-start.3) | collective-permute-done | bytes 278560 | tf_op jit(solution)/shard_map/ppermute | solution.py:648
  17.9 1.1 %conv1_edges.1 = (f32[8,4,64,128]{3,2,1,0:T(8,128)S(1)}, f32[8,4,64,128]{3,2,1,0:T(8,128)S(1)}) custom-call(bf16[17,64,128]{2,1,0:T(8,128)(2,1)S(1)} %collective-permute-done.2.hp_ref, bf16[17,64,128]{2,1,0:T(8,128)(2,1)S(1)} %collective-permute-done.3.hx_ref, bf16[8,1,64,128]{3,2,1,0:T(8,128)(2,1)S(1)} %collective-permute-done.gp_ref, ...), custom_call_target="tpu_custom_call" | custom-call | flops 603979776 | bytes 2658816 | tf_op jit(solution)/shard_map/conv1_edges/pallas_call | solution.py:606
  19.1 3.2 %conv2.1 = (bf16[8,12,64,128]{3,2,1,0:T(8,128)(2,1)S(1)}, f32[8,10,64,128]{3,2,1,0:T(8,128)S(1)}, f32[8,10,64,128]{3,2,1,0:T(8,128)S(1)}, f32[8,128]{1,0:T(8,128)S(1)}, f32[8,128]{1,0:T(8,128)S(1)}) custom-call(f32[8,128]{1,0:T(8,128)S(1)} %get-tuple-element.75.st_ref.own_ref.st1_ref, f32[8,4,64,128]{3,2,1,0:T(8,128)S(1)} %get-tuple-element.76.a_ref, ...), custom_call_target="tpu_custom_call" | custom-call | flops 1207959552 | bytes 9217536 | tf_op jit(solution)/shard_map/conv2/pallas_call | solution.py:606
  23.6 1.9 %collective-permute-start.13 = (f32[2,8,128]{2,1,0:T(8,128)S(1)}, f32[2,8,128]{2,1,0:T(8,128)S(1)}, u32[]{:S(2)}, u32[]{:S(2)}) collective-permute-start(f32[2,8,128]{2,1,0:T(8,128)S(1)} %blocks.4.after_ref.refs_0_), channel_id=1, source_target_pairs={{0,6},{1,7},{2,4},{3,5},{4,2},{5,3},{6,0},{7,1},{8,14},{9,15},{10,... | collective-permute-start | bytes 24584 | tf_op jit(solution)/shard_map/ppermute | solution.py:648
  25.5 2.3 %collective-permute-start.12 = (f32[2,8,128]{2,1,0:T(8,128)S(1)}, f32[2,8,128]{2,1,0:T(8,128)S(1)}, u32[]{:S(2)}, u32[]{:S(2)}) collective-permute-start(f32[2,8,128]{2,1,0:T(8,128)S(1)} %blocks.4.after_ref.refs_0_), channel_id=1, source_target_pairs={{0,7},{1,6},{2,5},{3,4},{4,3},{5,2},{6,1},{7,0},{8,15},{9,14},{10,... | collective-permute-start | bytes 24584 | tf_op jit(solution)/shard_map/ppermute | solution.py:648
  27.8 1.6 %slopes.1 = (f32[8,8,64,128]{3,2,1,0:T(8,128)S(1)}, f32[8,10,64,128]{3,2,1,0:T(8,128)S(1)}) custom-call(f32[8,4,64,128]{3,2,1,0:T(8,128)S(1)} %get-tuple-element.89.z_ref, f32[8,4,64,128]{3,2,1,0:T(8,128)S(1)} %get-tuple-element.90.zo_ref, f32[8,10,64,128]{3,2,1,0:T(8,128)S(1)} %get-tuple-element.91.z2_ref, f32[8,8,64,128]{3,2,1,0:T(8,128)S(1)} %get-tuple-element.71.m_ref, ...), custom_call_target="tpu_custom_call" | custom-call | flops 1207959552 | bytes 7864320 | tf_op jit(solution)/shard_map/slopes/pallas_call | solution.py:606
  29.4 1.0 %collective-permute-done.12.refs_2_ = f32[2,8,128]{2,1,0:T(8,128)S(1)} collective-permute-done((f32[2,8,128]{2,1,0:T(8,128)S(1)}, f32[2,8,128]{2,1,0:T(8,128)S(1)}, u32[]{:S(2)}, u32[]{:S(2)}) %collective-permute-start.12) | collective-permute-done | bytes 8224 | tf_op jit(solution)/shard_map/ppermute | solution.py:648
  30.9 2.4 %conv2_back.1 = (bf16[8,10,64,128]{3,2,1,0:T(8,128)(2,1)S(1)}, f32[8,8,64,128]{3,2,1,0:T(8,128)S(1)}, f32[8,128]{1,0:T(8,128)S(1)}, f32[8,128]{1,0:T(8,128)S(1)}) custom-call(f32[8,128]{1,0:T(8,128)S(1)} %get-tuple-element.87.refs_0_.own_ref, f32[8,128]{1,0:T(8,128)S(1)} %get-tuple-element.75.st_ref.own_ref.st1_ref, f32[8,128]{1,0:T(8,128)S(1)} %get-tuple-element.88.c1_ref, ...), custom_call_target="tpu_custom_call" | custom-call | flops 1207959552 | bytes 12628992 | tf_op jit(solution)/shard_map/conv2_back/pallas_call | solution.py:606
  33.5 1.0 %collective-permute-done.14.refs_1_ = f32[1,8,128]{2,1,0:T(8,128)S(1)} collective-permute-done((f32[1,8,128]{2,1,0:T(8,128)S(1)}, f32[1,8,128]{2,1,0:T(8,128)S(1)}, u32[]{:S(2)}, u32[]{:S(2)}) %collective-permute-start.14) | collective-permute-done | bytes 4128 | tf_op jit(solution)/shard_map/ppermute | solution.py:620
  35.1 1.8 %collective-permute-start.16 = (f32[2,8,128]{2,1,0:T(8,128)S(1)}, f32[2,8,128]{2,1,0:T(8,128)S(1)}, u32[]{:S(2)}, u32[]{:S(2)}) collective-permute-start(f32[2,8,128]{2,1,0:T(8,128)S(1)} %blocks.5.after_ref.refs_0_), channel_id=1, source_target_pairs={{0,7},{1,6},{2,5},{3,4},{4,3},{5,2},{6,1},{7,0},{8,15},{9,14},{10,... | collective-permute-start | bytes 24584 | tf_op jit(solution)/shard_map/ppermute | solution.py:648
  37.5 1.8 %conv2_weight_grad.1 = (bf16[1152,128]{1,0:T(8,128)(2,1)S(1)}, f32[8,128]{1,0:T(8,128)S(1)}) custom-call(bf16[8,12,64,128]{3,2,1,0:T(8,128)(2,1)S(1)} %get-tuple-element.99.n_ref, bf16[8,10,64,128]{3,2,1,0:T(8,128)(2,1)S(1)} %get-tuple-element.100.d_ref, f32[2,8,128]{2,1,0:T(8,128)S(1)} %blocks.5.after_ref.refs_0_), custom_call_target="tpu_custom_call" | custom-call | flops 1207959552 | bytes 2883584 | tf_op jit(solution)/shard_map/conv2_weight_grad/pallas_call | solution.py:606
  40.1 2.2 %conv1_weight_grad.1 = (bf16[8,8,64,128]{3,2,1,0:T(8,128)(2,1)S(1)}, bf16[4,304,128]{2,1,0:T(8,128)(2,1)S(1)}, bf16[4,304,128]{2,1,0:T(8,128)(2,1)S(1)}) custom-call(f32[8,128]{1,0:T(8,128)S(1)} %get-tuple-element.88.c1_ref, f32[8,128]{1,0:T(8,128)S(1)} %get-tuple-element.96.c2_ref, f32[8,8,64,128]{3,2,1,0:T(8,128)S(1)} %get-tuple-element.97.dn_ref, ...), custom_call_target="tpu_custom_call" | custom-call | flops 1207959552 | bytes 7942656 | tf_op jit(solution)/shard_map/conv1_weight_grad/pallas_call | solution.py:606
  42.6 1.3 %collective-permute-done.18.refs_1_ = bf16[4,304,128]{2,1,0:T(8,128)(2,1)S(1)} collective-permute-done((bf16[4,304,128]{2,1,0:T(8,128)(2,1)S(1)}, bf16[4,304,128]{2,1,0:T(8,128)(2,1)S(1)}, u32[]{:S(2)}, u32[]{:S(2)}) %collective-permute-start.18) | collective-permute-done | bytes 311328 | tf_op jit(solution)/shard_map/ppermute | solution.py:620
  44.0 2.5 %collective-permute-start.21 = (bf16[304,128]{1,0:T(8,128)(2,1)S(1)}, bf16[304,128]{1,0:T(8,128)(2,1)S(1)}, u32[]{:S(2)}, u32[]{:S(2)}) collective-permute-start(bf16[304,128]{1,0:T(8,128)(2,1)S(1)} %get-tuple-element.112), channel_id=1, source_target_pairs={{0,24},{1,25},{2,26},{3,27},{4,7},{5,6},{6,5},{7,4},{8,16},{9,17},... | collective-permute-start | bytes 233480 | tf_op jit(solution)/shard_map/ppermute | solution.py:632
  48.0 1.3 %collective-permute-start.20 = (bf16[8,64,128]{2,1,0:T(8,128)(2,1)S(1)}, bf16[8,64,128]{2,1,0:T(8,128)(2,1)S(1)}, u32[]{:S(2)}, u32[]{:S(2)}) collective-permute-start(bf16[8,64,128]{2,1,0:T(8,128)(2,1)S(1)} %get-tuple-element.110), channel_id=1, source_target_pairs={{0,1},{1,0},{2,3},{3,2},{4,5},{5,4},{6,7},{7,6},{8,9},{9,8},{10,11... | collective-permute-start | bytes 393224 | tf_op jit(solution)/shard_map/ppermute | solution.py:648
  49.4 1.1 %output.1 = (bf16[8,8,64,128]{3,2,1,0:T(8,128)(2,1)}, f32[8,128]{1,0:T(8,128)S(1)}) custom-call(bf16[8,8,64,128]{3,2,1,0:T(8,128)(2,1)S(1)} %bitcast.29, f32[8,10,64,128]{3,2,1,0:T(8,128)S(1)} %get-tuple-element.86.a2_ref, f32[8,8,64,128]{3,2,1,0:T(8,128)S(1)} %get-tuple-element.71.m_ref, f32[8,128]{1,0:T(8,128)S(1)} %get-tuple-element.96.c2_ref, ...), custom_call_target="tpu_custom_call" | custom-call | flops 603979776 | bytes 5771264 | tf_op jit(solution)/shard_map/output/pallas_call | solution.py:606
  51.5 2.0 %collective-permute-start.26 = (bf16[304,128]{1,0:T(8,128)(2,1)S(1)}, bf16[304,128]{1,0:T(8,128)(2,1)S(1)}, u32[]{:S(2)}, u32[]{:S(2)}) collective-permute-start(bf16[304,128]{1,0:T(8,128)(2,1)S(1)} %add_first.1.refs_0_), channel_id=1, source_target_pairs={{0,3},{1,2},{2,1},{3,0},{4,28},{5,29},{6,30},{7,31},{8,11},{9,10},... | collective-permute-start | bytes 233480 | tf_op jit(solution)/shard_map/ppermute | solution.py:632
  53.7 2.2 %collective-permute-start.24 = (bf16[304,128]{1,0:T(8,128)(2,1)S(1)}, bf16[304,128]{1,0:T(8,128)(2,1)S(1)}, u32[]{:S(2)}, u32[]{:S(2)}) collective-permute-start(bf16[304,128]{1,0:T(8,128)(2,1)S(1)} %add_first.1.refs_0_), channel_id=1, source_target_pairs={{0,1},{1,0},{2,3},{3,2},{4,12},{5,13},{6,14},{7,15},{8,9},{9,8},{1... | collective-permute-start | bytes 233480 | tf_op jit(solution)/shard_map/ppermute | solution.py:632
  55.9 1.9 %conv1_back.1 = (bf16[8,8,64,128]{3,2,1,0:T(8,128)(2,1)S(1)}, f32[8,128]{1,0:T(8,128)S(1)}) custom-call(bf16[8,64,128]{2,1,0:T(8,128)(2,1)S(1)} %collective-permute-done.19.ep_ref, bf16[8,64,128]{2,1,0:T(8,128)(2,1)S(1)} %collective-permute-done.20.ex_ref, bf16[8,8,64,128]{3,2,1,0:T(8,128)(2,1)S(1)} %get-tuple-element.108.d_ref, ...), custom_call_target="tpu_custom_call" | custom-call | flops 1207959552 | bytes 2654208 | tf_op jit(solution)/shard_map/conv1_back/pallas_call | solution.py:606
  57.9 1.5 %collective-permute-done.25.refs_2_ = bf16[304,128]{1,0:T(8,128)(2,1)S(1)} collective-permute-done((bf16[304,128]{1,0:T(8,128)(2,1)S(1)}, bf16[304,128]{1,0:T(8,128)(2,1)S(1)}, u32[]{:S(2)}, u32[]{:S(2)}) %collective-permute-start.25) | collective-permute-done | bytes 77856 | tf_op jit(solution)/shard_map/ppermute | solution.py:632
  59.5 1.6 %collective-permute-start.29 = (bf16[304,128]{1,0:T(8,128)(2,1)S(1)}, bf16[304,128]{1,0:T(8,128)(2,1)S(1)}, u32[]{:S(2)}, u32[]{:S(2)}) collective-permute-start(bf16[304,128]{1,0:T(8,128)(2,1)S(1)} %add_second.1.refs_0_), channel_id=1, source_target_pairs={{0,24},{1,25},{2,26},{3,27},{4,7},{5,6},{6,5},{7,4},{8,16},{9,17},... | collective-permute-start | bytes 233480 | tf_op jit(solution)/shard_map/ppermute | solution.py:632
  61.6 1.4 %collective-permute-start.27 = (bf16[304,128]{1,0:T(8,128)(2,1)S(1)}, bf16[304,128]{1,0:T(8,128)(2,1)S(1)}, u32[]{:S(2)}, u32[]{:S(2)}) collective-permute-start(bf16[304,128]{1,0:T(8,128)(2,1)S(1)} %add_second.1.refs_0_), channel_id=1, source_target_pairs={{0,8},{1,9},{2,10},{3,11},{4,5},{5,4},{6,7},{7,6},{8,0},{9,1},{10,... | collective-permute-start | bytes 233480 | tf_op jit(solution)/shard_map/ppermute | solution.py:632
  63.0 1.8 %collective-permute-done.29.refs_3_ = bf16[304,128]{1,0:T(8,128)(2,1)S(1)} collective-permute-done((bf16[304,128]{1,0:T(8,128)(2,1)S(1)}, bf16[304,128]{1,0:T(8,128)(2,1)S(1)}, u32[]{:S(2)}, u32[]{:S(2)}) %collective-permute-start.29) | collective-permute-done | bytes 77856 | tf_op jit(solution)/shard_map/ppermute | solution.py:632
  66.1 1.2 %leave.1 = (bf16[8,8,64,128]{3,2,1,0:T(8,128)(2,1)}, f32[1152,128]{1,0:T(8,128)}, f32[1152,128]{1,0:T(8,128)}) custom-call(bf16[8,8,64,128]{3,2,1,0:T(8,128)(2,1)S(1)} %get-tuple-element.111.grad_ref, bf16[1168,128]{1,0:T(8,128)(2,1)S(1)} %join.1.own_ref), custom_call_target="tpu_custom_call" | custom-call | bytes 1347584 | tf_op jit(solution)/shard_map/leave/pallas_call | solution.py:606
  67.7 0.9 %finish.1 = (f32[1152,128]{1,0:T(8,128)}, f32[1152,128]{1,0:T(8,128)}, f32[1,128]{1,0:T(1,128)}, f32[1,128]{1,0:T(1,128)}, f32[1,128]{1,0:T(1,128)}, /*index=5*/...) custom-call(bf16[1168,128]{1,0:T(8,128)(2,1)S(1)} %join.1.own_ref, ...), custom_call_target="tpu_custom_call", output_to_operand_aliasing={{0}: (2, {}), {1}: (3, {})} | custom-call | bytes 1777664 | tf_op jit(solution)/shard_map/finish/pallas_call | solution.py:606
  (82 shorter events, 12.1 us)
Async XLA Ops:
  1.8 8.5 %collective-permute-start = (bf16[8,1,64,128]{3,2,1,0:T(8,128)(2,1)S(1)}, bf16[8,1,64,128]{3,2,1,0:T(8,128)(2,1)S(1)}, u32[]{:S(2)}, u32[]{:S(2)}) collective-permute-start(bf16[8,1,64,128]{3,2,1,0:T(8,128)(2,1)S(1)} %get-tuple-element.69), channel_id=1, source_target_pairs={{0,4},{1,2},{2,1},{3,7},{4,0},{5,6},{6,5},{7,3},{8,12},{9,10},{10,... | collective-permute-start | bytes 393224 | tf_op jit(solution)/shard_map/ppermute | solution.py:648
  2.3 8.0 %collective-permute-start.1 = (bf16[8,1,64,128]{3,2,1,0:T(8,128)(2,1)S(1)}, bf16[8,1,64,128]{3,2,1,0:T(8,128)(2,1)S(1)}, u32[]{:S(2)}, u32[]{:S(2)}) collective-permute-start(bf16[8,1,64,128]{3,2,1,0:T(8,128)(2,1)S(1)} %get-tuple-element.70), channel_id=1, source_target_pairs={{0,1},{1,0},{2,3},{3,2},{4,5},{5,4},{6,7},{7,6},{8,9},{9,8},{10,11... | collective-permute-start | bytes 393224 | tf_op jit(solution)/shard_map/ppermute | solution.py:648
  8.6 7.3 %collective-permute-start.2 = (bf16[17,64,128]{2,1,0:T(8,128)(2,1)S(1)}, bf16[17,64,128]{2,1,0:T(8,128)(2,1)S(1)}, u32[]{:S(2)}, u32[]{:S(2)}) collective-permute-start(bf16[17,64,128]{2,1,0:T(8,128)(2,1)S(1)} %get-tuple-element.79), channel_id=1, source_target_pairs={{0,4},{1,2},{2,1},{3,7},{4,0},{5,6},{6,5},{7,3},{8,12},{9,10},{10,... | collective-permute-start | bytes 835592 | tf_op jit(solution)/shard_map/ppermute | solution.py:648
  8.7 9.2 %collective-permute-start.3 = (bf16[17,64,128]{2,1,0:T(8,128)(2,1)S(1)}, bf16[17,64,128]{2,1,0:T(8,128)(2,1)S(1)}, u32[]{:S(2)}, u32[]{:S(2)}) collective-permute-start(bf16[17,64,128]{2,1,0:T(8,128)(2,1)S(1)} %get-tuple-element.80), channel_id=1, source_target_pairs={{0,1},{1,0},{2,3},{3,2},{4,5},{5,4},{6,7},{7,6},{8,9},{9,8},{10,11... | collective-permute-start | bytes 835592 | tf_op jit(solution)/shard_map/ppermute | solution.py:648
  11.5 1.2 %collective-permute-start.4 = (f32[1,8,128]{2,1,0:T(8,128)S(1)}, f32[1,8,128]{2,1,0:T(8,128)S(1)}, u32[]{:S(2)}, u32[]{:S(2)}) collective-permute-start(f32[1,8,128]{2,1,0:T(8,128)S(1)} %bitcast.33), channel_id=1, source_target_pairs={{0,4},{4,0},{1,5},{5,1},{2,6},{6,2},{3,7},{7,3},{8,12},{12,8},{9,1... | collective-permute-start | bytes 12296 | tf_op jit(solution)/shard_map/ppermute | solution.py:620
  12.0 7.0 %copy-start.3 = (f32[128]{0:T(128)S(1)}, f32[128]{0:T(128)}, u32[]{:S(2)}) copy-start(f32[128]{0:T(128)} %param.16) | copy-start | bytes 1540
  12.7 6.3 %collective-permute-start.7 = (f32[2,8,128]{2,1,0:T(8,128)S(1)}, f32[2,8,128]{2,1,0:T(8,128)S(1)}, u32[]{:S(2)}, u32[]{:S(2)}) collective-permute-start(f32[2,8,128]{2,1,0:T(8,128)S(1)} %blocks.3.refs_0_), channel_id=1, source_target_pairs={{0,6},{1,7},{2,4},{3,5},{4,2},{5,3},{6,0},{7,1},{8,14},{9,15},{10,... | collective-permute-start | bytes 24584 | tf_op jit(solution)/shard_map/ppermute | solution.py:648
  13.8 5.2 %collective-permute-start.6 = (f32[2,8,128]{2,1,0:T(8,128)S(1)}, f32[2,8,128]{2,1,0:T(8,128)S(1)}, u32[]{:S(2)}, u32[]{:S(2)}) collective-permute-start(f32[2,8,128]{2,1,0:T(8,128)S(1)} %blocks.3.refs_0_), channel_id=1, source_target_pairs={{0,7},{1,6},{2,5},{3,4},{4,3},{5,2},{6,1},{7,0},{8,15},{9,14},{10,... | collective-permute-start | bytes 24584 | tf_op jit(solution)/shard_map/ppermute | solution.py:648
  15.9 3.1 %collective-permute-start.5 = (f32[2,8,128]{2,1,0:T(8,128)S(1)}, f32[2,8,128]{2,1,0:T(8,128)S(1)}, u32[]{:S(2)}, u32[]{:S(2)}) collective-permute-start(f32[2,8,128]{2,1,0:T(8,128)S(1)} %blocks.3.refs_0_), channel_id=1, source_target_pairs={{0,5},{1,4},{2,7},{3,6},{4,1},{5,0},{6,3},{7,2},{8,13},{9,12},{10,... | collective-permute-start | bytes 24584 | tf_op jit(solution)/shard_map/ppermute | solution.py:648
  22.3 1.4 %collective-permute-start.8 = (f32[1,8,128]{2,1,0:T(8,128)S(1)}, f32[1,8,128]{2,1,0:T(8,128)S(1)}, u32[]{:S(2)}, u32[]{:S(2)}) collective-permute-start(f32[1,8,128]{2,1,0:T(8,128)S(1)} %bitcast.35), channel_id=1, source_target_pairs={{0,4},{4,0},{1,5},{5,1},{2,6},{6,2},{3,7},{7,3},{8,12},{12,8},{9,1... | collective-permute-start | bytes 12296 | tf_op jit(solution)/shard_map/ppermute | solution.py:620
  22.5 8.4 %collective-permute-start.9 = (bf16[8,64,128]{2,1,0:T(8,128)(2,1)S(1)}, bf16[8,64,128]{2,1,0:T(8,128)(2,1)S(1)}, u32[]{:S(2)}, u32[]{:S(2)}) collective-permute-start(bf16[8,64,128]{2,1,0:T(8,128)(2,1)S(1)} %get-tuple-element.93), channel_id=1, source_target_pairs={{0,1},{1,0},{2,3},{3,2},{4,5},{5,4},{6,7},{7,6},{8,9},{9,8},{10,11... | collective-permute-start | bytes 393224 | tf_op jit(solution)/shard_map/ppermute | solution.py:648
  23.4 7.5 %collective-permute-start.10 = (bf16[8,64,128]{2,1,0:T(8,128)(2,1)S(1)}, bf16[8,64,128]{2,1,0:T(8,128)(2,1)S(1)}, u32[]{:S(2)}, u32[]{:S(2)}) collective-permute-start(bf16[8,64,128]{2,1,0:T(8,128)(2,1)S(1)} %get-tuple-element.94), channel_id=1, source_target_pairs={{0,4},{1,2},{2,1},{3,7},{4,0},{5,6},{6,5},{7,3},{8,12},{9,10},{10,... | collective-permute-start | bytes 393224 | tf_op jit(solution)/shard_map/ppermute | solution.py:648
  23.6 5.7 %collective-permute-start.13 = (f32[2,8,128]{2,1,0:T(8,128)S(1)}, f32[2,8,128]{2,1,0:T(8,128)S(1)}, u32[]{:S(2)}, u32[]{:S(2)}) collective-permute-start(f32[2,8,128]{2,1,0:T(8,128)S(1)} %blocks.4.after_ref.refs_0_), channel_id=1, source_target_pairs={{0,6},{1,7},{2,4},{3,5},{4,2},{5,3},{6,0},{7,1},{8,14},{9,15},{10,... | collective-permute-start | bytes 24584 | tf_op jit(solution)/shard_map/ppermute | solution.py:648
  25.5 4.9 %collective-permute-start.12 = (f32[2,8,128]{2,1,0:T(8,128)S(1)}, f32[2,8,128]{2,1,0:T(8,128)S(1)}, u32[]{:S(2)}, u32[]{:S(2)}) collective-permute-start(f32[2,8,128]{2,1,0:T(8,128)S(1)} %blocks.4.after_ref.refs_0_), channel_id=1, source_target_pairs={{0,7},{1,6},{2,5},{3,4},{4,3},{5,2},{6,1},{7,0},{8,15},{9,14},{10,... | collective-permute-start | bytes 24584 | tf_op jit(solution)/shard_map/ppermute | solution.py:648
  27.8 3.1 %collective-permute-start.11 = (f32[2,8,128]{2,1,0:T(8,128)S(1)}, f32[2,8,128]{2,1,0:T(8,128)S(1)}, u32[]{:S(2)}, u32[]{:S(2)}) collective-permute-start(f32[2,8,128]{2,1,0:T(8,128)S(1)} %blocks.4.after_ref.refs_0_), channel_id=1, source_target_pairs={{0,5},{1,4},{2,7},{3,6},{4,1},{5,0},{6,3},{7,2},{8,13},{9,12},{10,... | collective-permute-start | bytes 24584 | tf_op jit(solution)/shard_map/ppermute | solution.py:648
  33.3 1.2 %collective-permute-start.14 = (f32[1,8,128]{2,1,0:T(8,128)S(1)}, f32[1,8,128]{2,1,0:T(8,128)S(1)}, u32[]{:S(2)}, u32[]{:S(2)}) collective-permute-start(f32[1,8,128]{2,1,0:T(8,128)S(1)} %bitcast.37), channel_id=1, source_target_pairs={{0,4},{4,0},{1,5},{5,1},{2,6},{6,2},{3,7},{7,3},{8,12},{12,8},{9,1... | collective-permute-start | bytes 12296 | tf_op jit(solution)/shard_map/ppermute | solution.py:620
  34.5 4.8 %collective-permute-start.17 = (f32[2,8,128]{2,1,0:T(8,128)S(1)}, f32[2,8,128]{2,1,0:T(8,128)S(1)}, u32[]{:S(2)}, u32[]{:S(2)}) collective-permute-start(f32[2,8,128]{2,1,0:T(8,128)S(1)} %blocks.5.after_ref.refs_0_), channel_id=1, source_target_pairs={{0,6},{1,7},{2,4},{3,5},{4,2},{5,3},{6,0},{7,1},{8,14},{9,15},{10,... | collective-permute-start | bytes 24584 | tf_op jit(solution)/shard_map/ppermute | solution.py:648
  35.1 4.9 %collective-permute-start.16 = (f32[2,8,128]{2,1,0:T(8,128)S(1)}, f32[2,8,128]{2,1,0:T(8,128)S(1)}, u32[]{:S(2)}, u32[]{:S(2)}) collective-permute-start(f32[2,8,128]{2,1,0:T(8,128)S(1)} %blocks.5.after_ref.refs_0_), channel_id=1, source_target_pairs={{0,7},{1,6},{2,5},{3,4},{4,3},{5,2},{6,1},{7,0},{8,15},{9,14},{10,... | collective-permute-start | bytes 24584 | tf_op jit(solution)/shard_map/ppermute | solution.py:648
  36.9 3.1 %collective-permute-start.15 = (f32[2,8,128]{2,1,0:T(8,128)S(1)}, f32[2,8,128]{2,1,0:T(8,128)S(1)}, u32[]{:S(2)}, u32[]{:S(2)}) collective-permute-start(f32[2,8,128]{2,1,0:T(8,128)S(1)} %blocks.5.after_ref.refs_0_), channel_id=1, source_target_pairs={{0,5},{1,4},{2,7},{3,6},{4,1},{5,0},{6,3},{7,2},{8,13},{9,12},{10,... | collective-permute-start | bytes 24584 | tf_op jit(solution)/shard_map/ppermute | solution.py:648
  42.2 1.7 %collective-permute-start.18 = (bf16[4,304,128]{2,1,0:T(8,128)(2,1)S(1)}, bf16[4,304,128]{2,1,0:T(8,128)(2,1)S(1)}, u32[]{:S(2)}, u32[]{:S(2)}) collective-permute-start(bf16[4,304,128]{2,1,0:T(8,128)(2,1)S(1)} %get-tuple-element.105), channel_id=1, source_target_pairs={{0,4},{4,0},{1,5},{5,1},{2,6},{6,2},{3,7},{7,3},{8,12},{12,8},{9,1... | collective-permute-start | bytes 933896 | tf_op jit(solution)/shard_map/ppermute | solution.py:620
  44.0 6.5 %collective-permute-start.21 = (bf16[304,128]{1,0:T(8,128)(2,1)S(1)}, bf16[304,128]{1,0:T(8,128)(2,1)S(1)}, u32[]{:S(2)}, u32[]{:S(2)}) collective-permute-start(bf16[304,128]{1,0:T(8,128)(2,1)S(1)} %get-tuple-element.112), channel_id=1, source_target_pairs={{0,24},{1,25},{2,26},{3,27},{4,7},{5,6},{6,5},{7,4},{8,16},{9,17},... | collective-permute-start | bytes 233480 | tf_op jit(solution)/shard_map/ppermute | solution.py:632
  46.5 4.4 %collective-permute-start.22 = (bf16[304,128]{1,0:T(8,128)(2,1)S(1)}, bf16[304,128]{1,0:T(8,128)(2,1)S(1)}, u32[]{:S(2)}, u32[]{:S(2)}) collective-permute-start(bf16[304,128]{1,0:T(8,128)(2,1)S(1)} %get-tuple-element.113), channel_id=1, source_target_pairs={{0,16},{1,17},{2,18},{3,19},{4,6},{5,7},{6,4},{7,5},{8,24},{9,25},... | collective-permute-start | bytes 233480 | tf_op jit(solution)/shard_map/ppermute | solution.py:632
  47.0 4.4 %collective-permute-start.23 = (bf16[304,128]{1,0:T(8,128)(2,1)S(1)}, bf16[304,128]{1,0:T(8,128)(2,1)S(1)}, u32[]{:S(2)}, u32[]{:S(2)}) collective-permute-start(bf16[304,128]{1,0:T(8,128)(2,1)S(1)} %get-tuple-element.114), channel_id=1, source_target_pairs={{0,8},{1,9},{2,10},{3,11},{4,5},{5,4},{6,7},{7,6},{8,0},{9,1},{10,... | collective-permute-start | bytes 233480 | tf_op jit(solution)/shard_map/ppermute | solution.py:632
  47.6 8.3 %collective-permute-start.19 = (bf16[8,64,128]{2,1,0:T(8,128)(2,1)S(1)}, bf16[8,64,128]{2,1,0:T(8,128)(2,1)S(1)}, u32[]{:S(2)}, u32[]{:S(2)}) collective-permute-start(bf16[8,64,128]{2,1,0:T(8,128)(2,1)S(1)} %get-tuple-element.109), channel_id=1, source_target_pairs={{0,4},{1,2},{2,1},{3,7},{4,0},{5,6},{6,5},{7,3},{8,12},{9,10},{10,... | collective-permute-start | bytes 393224 | tf_op jit(solution)/shard_map/ppermute | solution.py:648
  48.0 7.9 %collective-permute-start.20 = (bf16[8,64,128]{2,1,0:T(8,128)(2,1)S(1)}, bf16[8,64,128]{2,1,0:T(8,128)(2,1)S(1)}, u32[]{:S(2)}, u32[]{:S(2)}) collective-permute-start(bf16[8,64,128]{2,1,0:T(8,128)(2,1)S(1)} %get-tuple-element.110), channel_id=1, source_target_pairs={{0,1},{1,0},{2,3},{3,2},{4,5},{5,4},{6,7},{7,6},{8,9},{9,8},{10,11... | collective-permute-start | bytes 393224 | tf_op jit(solution)/shard_map/ppermute | solution.py:648
  51.5 6.4 %collective-permute-start.26 = (bf16[304,128]{1,0:T(8,128)(2,1)S(1)}, bf16[304,128]{1,0:T(8,128)(2,1)S(1)}, u32[]{:S(2)}, u32[]{:S(2)}) collective-permute-start(bf16[304,128]{1,0:T(8,128)(2,1)S(1)} %add_first.1.refs_0_), channel_id=1, source_target_pairs={{0,3},{1,2},{2,1},{3,0},{4,28},{5,29},{6,30},{7,31},{8,11},{9,10},... | collective-permute-start | bytes 233480 | tf_op jit(solution)/shard_map/ppermute | solution.py:632
  53.5 5.9 %collective-permute-start.25 = (bf16[304,128]{1,0:T(8,128)(2,1)S(1)}, bf16[304,128]{1,0:T(8,128)(2,1)S(1)}, u32[]{:S(2)}, u32[]{:S(2)}) collective-permute-start(bf16[304,128]{1,0:T(8,128)(2,1)S(1)} %add_first.1.refs_0_), channel_id=1, source_target_pairs={{0,2},{1,3},{2,0},{3,1},{4,20},{5,21},{6,22},{7,23},{8,10},{9,11},... | collective-permute-start | bytes 233480 | tf_op jit(solution)/shard_map/ppermute | solution.py:632
  53.7 5.7 %collective-permute-start.24 = (bf16[304,128]{1,0:T(8,128)(2,1)S(1)}, bf16[304,128]{1,0:T(8,128)(2,1)S(1)}, u32[]{:S(2)}, u32[]{:S(2)}) collective-permute-start(bf16[304,128]{1,0:T(8,128)(2,1)S(1)} %add_first.1.refs_0_), channel_id=1, source_target_pairs={{0,1},{1,0},{2,3},{3,2},{4,12},{5,13},{6,14},{7,15},{8,9},{9,8},{1... | collective-permute-start | bytes 233480 | tf_op jit(solution)/shard_map/ppermute | solution.py:632
  59.5 5.4 %collective-permute-start.29 = (bf16[304,128]{1,0:T(8,128)(2,1)S(1)}, bf16[304,128]{1,0:T(8,128)(2,1)S(1)}, u32[]{:S(2)}, u32[]{:S(2)}) collective-permute-start(bf16[304,128]{1,0:T(8,128)(2,1)S(1)} %add_second.1.refs_0_), channel_id=1, source_target_pairs={{0,24},{1,25},{2,26},{3,27},{4,7},{5,6},{6,5},{7,4},{8,16},{9,17},... | collective-permute-start | bytes 233480 | tf_op jit(solution)/shard_map/ppermute | solution.py:632
  61.1 4.6 %collective-permute-start.28 = (bf16[304,128]{1,0:T(8,128)(2,1)S(1)}, bf16[304,128]{1,0:T(8,128)(2,1)S(1)}, u32[]{:S(2)}, u32[]{:S(2)}) collective-permute-start(bf16[304,128]{1,0:T(8,128)(2,1)S(1)} %add_second.1.refs_0_), channel_id=1, source_target_pairs={{0,16},{1,17},{2,18},{3,19},{4,6},{5,7},{6,4},{7,5},{8,24},{9,25},... | collective-permute-start | bytes 233480 | tf_op jit(solution)/shard_map/ppermute | solution.py:632
  61.6 4.4 %collective-permute-start.27 = (bf16[304,128]{1,0:T(8,128)(2,1)S(1)}, bf16[304,128]{1,0:T(8,128)(2,1)S(1)}, u32[]{:S(2)}, u32[]{:S(2)}) collective-permute-start(bf16[304,128]{1,0:T(8,128)(2,1)S(1)} %add_second.1.refs_0_), channel_id=1, source_target_pairs={{0,8},{1,9},{2,10},{3,11},{4,5},{5,4},{6,7},{7,6},{8,0},{9,1},{10,... | collective-permute-start | bytes 233480 | tf_op jit(solution)/shard_map/ppermute | solution.py:632
  66.0 1.7 %collective-permute-start.30 = (bf16[1168,128]{1,0:T(8,128)(2,1)S(1)}, bf16[1168,128]{1,0:T(8,128)(2,1)S(1)}, u32[]{:S(2)}, u32[]{:S(2)}) collective-permute-start(bf16[1168,128]{1,0:T(8,128)(2,1)S(1)} %join.1.own_ref), channel_id=1, source_target_pairs={{0,4},{4,0},{1,5},{5,1},{2,6},{6,2},{3,7},{7,3},{8,12},{12,8},{9,1... | collective-permute-start | bytes 897032 | tf_op jit(solution)/shard_map/ppermute | solution.py:620
  (12 other events, 50.9 us)

commit v9 on v8

--- a/solution.py
+++ b/solution.py
@@ -695,7 +695,7 @@
 def sum_everywhere(send, keep, edges, block_output, input_grad):
     leads, lats = lax.axis_size("lead"), lax.axis_size("lat")
     chunks = add_chunks([keep, swap(send, "dp", 1)], "add_dp", leads)
-    got = [cross(chunks[k], k, True) for k in reversed(range(1, leads))]
+    got = [cross(chunks[k], k, True) for k in [*range(2, leads), 1]]
     output = block_output(chunks[0])
     rows = edges(chunks[0])
     (mine,) = add_chunks([chunks[0]] + got, "add_first", waits=(output[1],), flops=HIDE)

time: 68.9 us -> 69.3 us (level)
  no operation moved by 1% of the time
where the time goes in v9:
time: 69.3 us; the launch traced here: 69.1 us
  starting transfers between devices  32 us (46%)
  Pallas kernels  21.5 us (31%)
  waiting for transfers between devices  13.4 us (19%)
  between operations  1.15 us (2%)
  local copies, waits for them, and re-layouts  1.06 us (2%)
    pallas_call x25, Pallas kernels, call(): pl.pallas_call(kernel, out_shape=outs, in_specs=(ins or [spaces[0]] * len...  21.5 us
    ppermute x17, starting transfers between devices, over_dp_and_lat(): return lax.ppermute(value, ('dp', 'lat'), pairs)  19.6 us
    ppermute x9, starting transfers between devices, cross(): return lax.ppermute(value, ('lead', 'dp', 'lat'), pairs)  11.6 us
    ppermute x9, waiting for transfers between devices, cross(): return lax.ppermute(value, ('lead', 'dp', 'lat'), pairs)  5.77 us
    ppermute x17, waiting for transfers between devices, over_dp_and_lat(): return lax.ppermute(value, ('dp', 'lat'), pairs)  4.25 us
    ppermute x5, waiting for transfers between devices, swap(): lax.ppermute(value, axis, [(i, i ^ k) for i in range(lax.axis_size(axis))])  3.35 us
  transfers between devices with their start and end apart: 31, of which 15 were waited for; matrix products, arithmetic and copies ran while one was open for 0% of the time, Pallas kernels for 18%

profile of v9, /device:TPU:0, one launch (start us, length us, event | category | flops | bytes accessed | tf_op | source)
XLA Modules:
  0.0 69.1 jit_solution(14055143644780083979)
XLA Ops:
  0.6 1.0 %fusion = (bf16[8,1,64,128]{3,2,1,0:T(8,128)(2,1)S(1)}, bf16[8,1,64,128]{3,2,1,0:T(8,128)(2,1)S(1)}) fusion(bf16[8,8,64,128]{3,2,1,0:T(8,128)(2,1)} %bitcast.22), kind=kLoop, calls=%fused_computation | loop fusion | bytes 524288 | tf_op jit(solution)/shard_map/slice | solution.py:778
  2.3 4.1 %collective-permute-start.1 = (bf16[8,1,64,128]{3,2,1,0:T(8,128)(2,1)S(1)}, bf16[8,1,64,128]{3,2,1,0:T(8,128)(2,1)S(1)}, u32[]{:S(2)}, u32[]{:S(2)}) collective-permute-start(bf16[8,1,64,128]{3,2,1,0:T(8,128)(2,1)S(1)} %get-tuple-element.70), channel_id=1, source_target_pairs={{0,1},{1,0},{2,3},{3,2},{4,5},{5,4},{6,7},{7,6},{8,9},{9,8},{10,11... | collective-permute-start | bytes 393224 | tf_op jit(solution)/shard_map/ppermute | solution.py:648
  7.3 1.2 %conv1_inner.1 = (f32[8,4,64,128]{3,2,1,0:T(8,128)S(1)}, f32[8,4,64,128]{3,2,1,0:T(8,128)S(1)}, bf16[3,512,256]{2,1,0:T(8,128)(2,1)S(1)}, f32[8,128]{1,0:T(8,128)S(1)}) custom-call(bf16[8,8,64,128]{3,2,1,0:T(8,128)(2,1)S(1)} %bitcast.24, f32[8,8,64,128]{3,2,1,0:T(8,128)S(1)} %get-tuple-element.71.m_ref, bf16[3,3,128,128]{3,2,1,0:T(8,128)(2,1)S(1)} %copy-done.10, ...), custom_call_target="tpu_custom_call" | custom-call | flops 4831838208 | bytes 3441152 | tf_op jit(solution)/shard_map/conv1_inner/pallas_call | solution.py:606
  8.7 1.6 %collective-permute-start.3 = (bf16[17,64,128]{2,1,0:T(8,128)(2,1)S(1)}, bf16[17,64,128]{2,1,0:T(8,128)(2,1)S(1)}, u32[]{:S(2)}, u32[]{:S(2)}) collective-permute-start(bf16[17,64,128]{2,1,0:T(8,128)(2,1)S(1)} %get-tuple-element.80), channel_id=1, source_target_pairs={{0,1},{1,0},{2,3},{3,2},{4,5},{5,4},{6,7},{7,6},{8,9},{9,8},{10,11... | collective-permute-start | bytes 835592 | tf_op jit(solution)/shard_map/ppermute | solution.py:648
  10.3 1.2 %conv1_outer.1 = (f32[8,4,64,128]{3,2,1,0:T(8,128)S(1)}, f32[8,4,64,128]{3,2,1,0:T(8,128)S(1)}, f32[8,128]{1,0:T(8,128)S(1)}) custom-call(bf16[8,1,64,128]{3,2,1,0:T(8,128)(2,1)S(1)} %collective-permute-done.gp_ref, bf16[8,1,64,128]{3,2,1,0:T(8,128)(2,1)S(1)} %collective-permute-done.1.gx_ref, bf16[8,8,64,128]{3,2,1,0:T(8,128)(2,1)S(1)} %bitcast.26, ...), custom_call_target="tpu_custom_call" | custom-call | flops 19327352832 | bytes 4203008 | tf_op jit(solution)/shard_map/conv1_outer/pallas_call | solution.py:606
  12.7 1.1 %collective-permute-start.7 = (f32[2,8,128]{2,1,0:T(8,128)S(1)}, f32[2,8,128]{2,1,0:T(8,128)S(1)}, u32[]{:S(2)}, u32[]{:S(2)}) collective-permute-start(f32[2,8,128]{2,1,0:T(8,128)S(1)} %blocks.3.refs_0_), channel_id=1, source_target_pairs={{0,6},{1,7},{2,4},{3,5},{4,2},{5,3},{6,0},{7,1},{8,14},{9,15},{10,... | collective-permute-start | bytes 24584 | tf_op jit(solution)/shard_map/ppermute | solution.py:648
  13.8 2.1 %collective-permute-start.6 = (f32[2,8,128]{2,1,0:T(8,128)S(1)}, f32[2,8,128]{2,1,0:T(8,128)S(1)}, u32[]{:S(2)}, u32[]{:S(2)}) collective-permute-start(f32[2,8,128]{2,1,0:T(8,128)S(1)} %blocks.3.refs_0_), channel_id=1, source_target_pairs={{0,7},{1,6},{2,5},{3,4},{4,3},{5,2},{6,1},{7,0},{8,15},{9,14},{10,... | collective-permute-start | bytes 24584 | tf_op jit(solution)/shard_map/ppermute | solution.py:648
  15.9 2.0 %collective-permute-done.3.hx_ref = bf16[17,64,128]{2,1,0:T(8,128)(2,1)S(1)} collective-permute-done((bf16[17,64,128]{2,1,0:T(8,128)(2,1)S(1)}, bf16[17,64,128]{2,1,0:T(8,128)(2,1)S(1)}, u32[]{:S(2)}, u32[]{:S(2)}) %collective-permute-start.3) | collective-permute-done | bytes 278560 | tf_op jit(solution)/shard_map/ppermute | solution.py:648
  17.9 1.1 %conv1_edges.1 = (f32[8,4,64,128]{3,2,1,0:T(8,128)S(1)}, f32[8,4,64,128]{3,2,1,0:T(8,128)S(1)}) custom-call(bf16[17,64,128]{2,1,0:T(8,128)(2,1)S(1)} %collective-permute-done.2.hp_ref, bf16[17,64,128]{2,1,0:T(8,128)(2,1)S(1)} %collective-permute-done.3.hx_ref, bf16[8,1,64,128]{3,2,1,0:T(8,128)(2,1)S(1)} %collective-permute-done.gp_ref, ...), custom_call_target="tpu_custom_call" | custom-call | flops 603979776 | bytes 2658816 | tf_op jit(solution)/shard_map/conv1_edges/pallas_call | solution.py:606
  19.1 3.2 %conv2.1 = (bf16[8,12,64,128]{3,2,1,0:T(8,128)(2,1)S(1)}, f32[8,10,64,128]{3,2,1,0:T(8,128)S(1)}, f32[8,10,64,128]{3,2,1,0:T(8,128)S(1)}, f32[8,128]{1,0:T(8,128)S(1)}, f32[8,128]{1,0:T(8,128)S(1)}) custom-call(f32[8,128]{1,0:T(8,128)S(1)} %get-tuple-element.75.st_ref.own_ref.st1_ref, f32[8,4,64,128]{3,2,1,0:T(8,128)S(1)} %get-tuple-element.76.a_ref, ...), custom_call_target="tpu_custom_call" | custom-call | flops 1207959552 | bytes 9217536 | tf_op jit(solution)/shard_map/conv2/pallas_call | solution.py:606
  23.6 1.9 %collective-permute-start.13 = (f32[2,8,128]{2,1,0:T(8,128)S(1)}, f32[2,8,128]{2,1,0:T(8,128)S(1)}, u32[]{:S(2)}, u32[]{:S(2)}) collective-permute-start(f32[2,8,128]{2,1,0:T(8,128)S(1)} %blocks.4.after_ref.refs_0_), channel_id=1, source_target_pairs={{0,6},{1,7},{2,4},{3,5},{4,2},{5,3},{6,0},{7,1},{8,14},{9,15},{10,... | collective-permute-start | bytes 24584 | tf_op jit(solution)/shard_map/ppermute | solution.py:648
  25.5 2.3 %collective-permute-start.12 = (f32[2,8,128]{2,1,0:T(8,128)S(1)}, f32[2,8,128]{2,1,0:T(8,128)S(1)}, u32[]{:S(2)}, u32[]{:S(2)}) collective-permute-start(f32[2,8,128]{2,1,0:T(8,128)S(1)} %blocks.4.after_ref.refs_0_), channel_id=1, source_target_pairs={{0,7},{1,6},{2,5},{3,4},{4,3},{5,2},{6,1},{7,0},{8,15},{9,14},{10,... | collective-permute-start | bytes 24584 | tf_op jit(solution)/shard_map/ppermute | solution.py:648
  27.8 1.6 %slopes.1 = (f32[8,8,64,128]{3,2,1,0:T(8,128)S(1)}, f32[8,10,64,128]{3,2,1,0:T(8,128)S(1)}) custom-call(f32[8,4,64,128]{3,2,1,0:T(8,128)S(1)} %get-tuple-element.89.z_ref, f32[8,4,64,128]{3,2,1,0:T(8,128)S(1)} %get-tuple-element.90.zo_ref, f32[8,10,64,128]{3,2,1,0:T(8,128)S(1)} %get-tuple-element.91.z2_ref, f32[8,8,64,128]{3,2,1,0:T(8,128)S(1)} %get-tuple-element.71.m_ref, ...), custom_call_target="tpu_custom_call" | custom-call | flops 1207959552 | bytes 7864320 | tf_op jit(solution)/shard_map/slopes/pallas_call | solution.py:606
  29.4 1.0 %collective-permute-done.12.refs_2_ = f32[2,8,128]{2,1,0:T(8,128)S(1)} collective-permute-done((f32[2,8,128]{2,1,0:T(8,128)S(1)}, f32[2,8,128]{2,1,0:T(8,128)S(1)}, u32[]{:S(2)}, u32[]{:S(2)}) %collective-permute-start.12) | collective-permute-done | bytes 8224 | tf_op jit(solution)/shard_map/ppermute | solution.py:648
  30.9 2.4 %conv2_back.1 = (bf16[8,10,64,128]{3,2,1,0:T(8,128)(2,1)S(1)}, f32[8,8,64,128]{3,2,1,0:T(8,128)S(1)}, f32[8,128]{1,0:T(8,128)S(1)}, f32[8,128]{1,0:T(8,128)S(1)}) custom-call(f32[8,128]{1,0:T(8,128)S(1)} %get-tuple-element.87.refs_0_.own_ref, f32[8,128]{1,0:T(8,128)S(1)} %get-tuple-element.75.st_ref.own_ref.st1_ref, f32[8,128]{1,0:T(8,128)S(1)} %get-tuple-element.88.c1_ref, ...), custom_call_target="tpu_custom_call" | custom-call | flops 1207959552 | bytes 12628992 | tf_op jit(solution)/shard_map/conv2_back/pallas_call | solution.py:606
  33.5 1.0 %collective-permute-done.14.refs_1_ = f32[1,8,128]{2,1,0:T(8,128)S(1)} collective-permute-done((f32[1,8,128]{2,1,0:T(8,128)S(1)}, f32[1,8,128]{2,1,0:T(8,128)S(1)}, u32[]{:S(2)}, u32[]{:S(2)}) %collective-permute-start.14) | collective-permute-done | bytes 4128 | tf_op jit(solution)/shard_map/ppermute | solution.py:620
  35.1 1.8 %collective-permute-start.16 = (f32[2,8,128]{2,1,0:T(8,128)S(1)}, f32[2,8,128]{2,1,0:T(8,128)S(1)}, u32[]{:S(2)}, u32[]{:S(2)}) collective-permute-start(f32[2,8,128]{2,1,0:T(8,128)S(1)} %blocks.5.after_ref.refs_0_), channel_id=1, source_target_pairs={{0,7},{1,6},{2,5},{3,4},{4,3},{5,2},{6,1},{7,0},{8,15},{9,14},{10,... | collective-permute-start | bytes 24584 | tf_op jit(solution)/shard_map/ppermute | solution.py:648
  37.5 1.8 %conv2_weight_grad.1 = (bf16[1152,128]{1,0:T(8,128)(2,1)S(1)}, f32[8,128]{1,0:T(8,128)S(1)}) custom-call(bf16[8,12,64,128]{3,2,1,0:T(8,128)(2,1)S(1)} %get-tuple-element.99.n_ref, bf16[8,10,64,128]{3,2,1,0:T(8,128)(2,1)S(1)} %get-tuple-element.100.d_ref, f32[2,8,128]{2,1,0:T(8,128)S(1)} %blocks.5.after_ref.refs_0_), custom_call_target="tpu_custom_call" | custom-call | flops 1207959552 | bytes 2883584 | tf_op jit(solution)/shard_map/conv2_weight_grad/pallas_call | solution.py:606
  40.1 2.2 %conv1_weight_grad.1 = (bf16[8,8,64,128]{3,2,1,0:T(8,128)(2,1)S(1)}, bf16[4,304,128]{2,1,0:T(8,128)(2,1)S(1)}, bf16[4,304,128]{2,1,0:T(8,128)(2,1)S(1)}) custom-call(f32[8,128]{1,0:T(8,128)S(1)} %get-tuple-element.88.c1_ref, f32[8,128]{1,0:T(8,128)S(1)} %get-tuple-element.96.c2_ref, f32[8,8,64,128]{3,2,1,0:T(8,128)S(1)} %get-tuple-element.97.dn_ref, ...), custom_call_target="tpu_custom_call" | custom-call | flops 1207959552 | bytes 7942656 | tf_op jit(solution)/shard_map/conv1_weight_grad/pallas_call | solution.py:606
  42.6 1.3 %collective-permute-done.18.refs_1_ = bf16[4,304,128]{2,1,0:T(8,128)(2,1)S(1)} collective-permute-done((bf16[4,304,128]{2,1,0:T(8,128)(2,1)S(1)}, bf16[4,304,128]{2,1,0:T(8,128)(2,1)S(1)}, u32[]{:S(2)}, u32[]{:S(2)}) %collective-permute-start.18) | collective-permute-done | bytes 311328 | tf_op jit(solution)/shard_map/ppermute | solution.py:620
  44.0 1.6 %collective-permute-start.21 = (bf16[304,128]{1,0:T(8,128)(2,1)S(1)}, bf16[304,128]{1,0:T(8,128)(2,1)S(1)}, u32[]{:S(2)}, u32[]{:S(2)}) collective-permute-start(bf16[304,128]{1,0:T(8,128)(2,1)S(1)} %get-tuple-element.112), channel_id=1, source_target_pairs={{0,16},{1,17},{2,18},{3,19},{4,6},{5,7},{6,4},{7,5},{8,24},{9,25},... | collective-permute-start | bytes 233480 | tf_op jit(solution)/shard_map/ppermute | solution.py:632
  45.6 1.4 %collective-permute-start.22 = (bf16[304,128]{1,0:T(8,128)(2,1)S(1)}, bf16[304,128]{1,0:T(8,128)(2,1)S(1)}, u32[]{:S(2)}, u32[]{:S(2)}) collective-permute-start(bf16[304,128]{1,0:T(8,128)(2,1)S(1)} %get-tuple-element.113), channel_id=1, source_target_pairs={{0,24},{1,25},{2,26},{3,27},{4,7},{5,6},{6,5},{7,4},{8,16},{9,17},... | collective-permute-start | bytes 233480 | tf_op jit(solution)/shard_map/ppermute | solution.py:632
  47.7 1.7 %collective-permute-start.20 = (bf16[8,64,128]{2,1,0:T(8,128)(2,1)S(1)}, bf16[8,64,128]{2,1,0:T(8,128)(2,1)S(1)}, u32[]{:S(2)}, u32[]{:S(2)}) collective-permute-start(bf16[8,64,128]{2,1,0:T(8,128)(2,1)S(1)} %get-tuple-element.110), channel_id=1, source_target_pairs={{0,1},{1,0},{2,3},{3,2},{4,5},{5,4},{6,7},{7,6},{8,9},{9,8},{10,11... | collective-permute-start | bytes 393224 | tf_op jit(solution)/shard_map/ppermute | solution.py:648
  49.4 1.1 %output.1 = (bf16[8,8,64,128]{3,2,1,0:T(8,128)(2,1)}, f32[8,128]{1,0:T(8,128)S(1)}) custom-call(bf16[8,8,64,128]{3,2,1,0:T(8,128)(2,1)S(1)} %bitcast.29, f32[8,10,64,128]{3,2,1,0:T(8,128)S(1)} %get-tuple-element.86.a2_ref, f32[8,8,64,128]{3,2,1,0:T(8,128)S(1)} %get-tuple-element.71.m_ref, f32[8,128]{1,0:T(8,128)S(1)} %get-tuple-element.96.c2_ref, ...), custom_call_target="tpu_custom_call" | custom-call | flops 603979776 | bytes 5771264 | tf_op jit(solution)/shard_map/output/pallas_call | solution.py:606
  51.5 2.0 %collective-permute-start.26 = (bf16[304,128]{1,0:T(8,128)(2,1)S(1)}, bf16[304,128]{1,0:T(8,128)(2,1)S(1)}, u32[]{:S(2)}, u32[]{:S(2)}) collective-permute-start(bf16[304,128]{1,0:T(8,128)(2,1)S(1)} %add_first.1.refs_0_), channel_id=1, source_target_pairs={{0,3},{1,2},{2,1},{3,0},{4,28},{5,29},{6,30},{7,31},{8,11},{9,10},... | collective-permute-start | bytes 233480 | tf_op jit(solution)/shard_map/ppermute | solution.py:632
  53.7 2.2 %collective-permute-start.24 = (bf16[304,128]{1,0:T(8,128)(2,1)S(1)}, bf16[304,128]{1,0:T(8,128)(2,1)S(1)}, u32[]{:S(2)}, u32[]{:S(2)}) collective-permute-start(bf16[304,128]{1,0:T(8,128)(2,1)S(1)} %add_first.1.refs_0_), channel_id=1, source_target_pairs={{0,1},{1,0},{2,3},{3,2},{4,12},{5,13},{6,14},{7,15},{8,9},{9,8},{1... | collective-permute-start | bytes 233480 | tf_op jit(solution)/shard_map/ppermute | solution.py:632
  55.9 1.9 %conv1_back.1 = (bf16[8,8,64,128]{3,2,1,0:T(8,128)(2,1)S(1)}, f32[8,128]{1,0:T(8,128)S(1)}) custom-call(bf16[8,64,128]{2,1,0:T(8,128)(2,1)S(1)} %collective-permute-done.19.ep_ref, bf16[8,64,128]{2,1,0:T(8,128)(2,1)S(1)} %collective-permute-done.20.ex_ref, bf16[8,8,64,128]{3,2,1,0:T(8,128)(2,1)S(1)} %get-tuple-element.108.d_ref, ...), custom_call_target="tpu_custom_call" | custom-call | flops 1207959552 | bytes 2654208 | tf_op jit(solution)/shard_map/conv1_back/pallas_call | solution.py:606
  57.9 1.5 %collective-permute-done.25.refs_2_ = bf16[304,128]{1,0:T(8,128)(2,1)S(1)} collective-permute-done((bf16[304,128]{1,0:T(8,128)(2,1)S(1)}, bf16[304,128]{1,0:T(8,128)(2,1)S(1)}, u32[]{:S(2)}, u32[]{:S(2)}) %collective-permute-start.25) | collective-permute-done | bytes 77856 | tf_op jit(solution)/shard_map/ppermute | solution.py:632
  59.4 1.9 %collective-permute-start.29 = (bf16[304,128]{1,0:T(8,128)(2,1)S(1)}, bf16[304,128]{1,0:T(8,128)(2,1)S(1)}, u32[]{:S(2)}, u32[]{:S(2)}) collective-permute-start(bf16[304,128]{1,0:T(8,128)(2,1)S(1)} %add_second.1.refs_0_), channel_id=1, source_target_pairs={{0,24},{1,25},{2,26},{3,27},{4,7},{5,6},{6,5},{7,4},{8,16},{9,17},... | collective-permute-start | bytes 233480 | tf_op jit(solution)/shard_map/ppermute | solution.py:632
  61.9 1.1 %collective-permute-start.27 = (bf16[304,128]{1,0:T(8,128)(2,1)S(1)}, bf16[304,128]{1,0:T(8,128)(2,1)S(1)}, u32[]{:S(2)}, u32[]{:S(2)}) collective-permute-start(bf16[304,128]{1,0:T(8,128)(2,1)S(1)} %add_second.1.refs_0_), channel_id=1, source_target_pairs={{0,8},{1,9},{2,10},{3,11},{4,5},{5,4},{6,7},{7,6},{8,0},{9,1},{10,... | collective-permute-start | bytes 233480 | tf_op jit(solution)/shard_map/ppermute | solution.py:632
  63.0 1.8 %collective-permute-done.29.refs_3_ = bf16[304,128]{1,0:T(8,128)(2,1)S(1)} collective-permute-done((bf16[304,128]{1,0:T(8,128)(2,1)S(1)}, bf16[304,128]{1,0:T(8,128)(2,1)S(1)}, u32[]{:S(2)}, u32[]{:S(2)}) %collective-permute-start.29) | collective-permute-done | bytes 77856 | tf_op jit(solution)/shard_map/ppermute | solution.py:632
  66.4 1.2 %leave.1 = (bf16[8,8,64,128]{3,2,1,0:T(8,128)(2,1)}, f32[1152,128]{1,0:T(8,128)}, f32[1152,128]{1,0:T(8,128)}) custom-call(bf16[8,8,64,128]{3,2,1,0:T(8,128)(2,1)S(1)} %get-tuple-element.111.grad_ref, bf16[1168,128]{1,0:T(8,128)(2,1)S(1)} %join.1.own_ref), custom_call_target="tpu_custom_call" | custom-call | bytes 1347584 | tf_op jit(solution)/shard_map/leave/pallas_call | solution.py:606
  (82 shorter events, 12.7 us)
Async XLA Ops:
  1.8 8.5 %collective-permute-start = (bf16[8,1,64,128]{3,2,1,0:T(8,128)(2,1)S(1)}, bf16[8,1,64,128]{3,2,1,0:T(8,128)(2,1)S(1)}, u32[]{:S(2)}, u32[]{:S(2)}) collective-permute-start(bf16[8,1,64,128]{3,2,1,0:T(8,128)(2,1)S(1)} %get-tuple-element.69), channel_id=1, source_target_pairs={{0,4},{1,2},{2,1},{3,7},{4,0},{5,6},{6,5},{7,3},{8,12},{9,10},{10,... | collective-permute-start | bytes 393224 | tf_op jit(solution)/shard_map/ppermute | solution.py:648
  2.3 8.0 %collective-permute-start.1 = (bf16[8,1,64,128]{3,2,1,0:T(8,128)(2,1)S(1)}, bf16[8,1,64,128]{3,2,1,0:T(8,128)(2,1)S(1)}, u32[]{:S(2)}, u32[]{:S(2)}) collective-permute-start(bf16[8,1,64,128]{3,2,1,0:T(8,128)(2,1)S(1)} %get-tuple-element.70), channel_id=1, source_target_pairs={{0,1},{1,0},{2,3},{3,2},{4,5},{5,4},{6,7},{7,6},{8,9},{9,8},{10,11... | collective-permute-start | bytes 393224 | tf_op jit(solution)/shard_map/ppermute | solution.py:648
  8.6 7.3 %collective-permute-start.2 = (bf16[17,64,128]{2,1,0:T(8,128)(2,1)S(1)}, bf16[17,64,128]{2,1,0:T(8,128)(2,1)S(1)}, u32[]{:S(2)}, u32[]{:S(2)}) collective-permute-start(bf16[17,64,128]{2,1,0:T(8,128)(2,1)S(1)} %get-tuple-element.79), channel_id=1, source_target_pairs={{0,4},{1,2},{2,1},{3,7},{4,0},{5,6},{6,5},{7,3},{8,12},{9,10},{10,... | collective-permute-start | bytes 835592 | tf_op jit(solution)/shard_map/ppermute | solution.py:648
  8.7 9.2 %collective-permute-start.3 = (bf16[17,64,128]{2,1,0:T(8,128)(2,1)S(1)}, bf16[17,64,128]{2,1,0:T(8,128)(2,1)S(1)}, u32[]{:S(2)}, u32[]{:S(2)}) collective-permute-start(bf16[17,64,128]{2,1,0:T(8,128)(2,1)S(1)} %get-tuple-element.80), channel_id=1, source_target_pairs={{0,1},{1,0},{2,3},{3,2},{4,5},{5,4},{6,7},{7,6},{8,9},{9,8},{10,11... | collective-permute-start | bytes 835592 | tf_op jit(solution)/shard_map/ppermute | solution.py:648
  11.5 1.2 %collective-permute-start.4 = (f32[1,8,128]{2,1,0:T(8,128)S(1)}, f32[1,8,128]{2,1,0:T(8,128)S(1)}, u32[]{:S(2)}, u32[]{:S(2)}) collective-permute-start(f32[1,8,128]{2,1,0:T(8,128)S(1)} %bitcast.33), channel_id=1, source_target_pairs={{0,4},{4,0},{1,5},{5,1},{2,6},{6,2},{3,7},{7,3},{8,12},{12,8},{9,1... | collective-permute-start | bytes 12296 | tf_op jit(solution)/shard_map/ppermute | solution.py:620
  12.0 7.0 %copy-start.3 = (f32[128]{0:T(128)S(1)}, f32[128]{0:T(128)}, u32[]{:S(2)}) copy-start(f32[128]{0:T(128)} %param.16) | copy-start | bytes 1540
  12.7 6.3 %collective-permute-start.7 = (f32[2,8,128]{2,1,0:T(8,128)S(1)}, f32[2,8,128]{2,1,0:T(8,128)S(1)}, u32[]{:S(2)}, u32[]{:S(2)}) collective-permute-start(f32[2,8,128]{2,1,0:T(8,128)S(1)} %blocks.3.refs_0_), channel_id=1, source_target_pairs={{0,6},{1,7},{2,4},{3,5},{4,2},{5,3},{6,0},{7,1},{8,14},{9,15},{10,... | collective-permute-start | bytes 24584 | tf_op jit(solution)/shard_map/ppermute | solution.py:648
  13.8 5.2 %collective-permute-start.6 = (f32[2,8,128]{2,1,0:T(8,128)S(1)}, f32[2,8,128]{2,1,0:T(8,128)S(1)}, u32[]{:S(2)}, u32[]{:S(2)}) collective-permute-start(f32[2,8,128]{2,1,0:T(8,128)S(1)} %blocks.3.refs_0_), channel_id=1, source_target_pairs={{0,7},{1,6},{2,5},{3,4},{4,3},{5,2},{6,1},{7,0},{8,15},{9,14},{10,... | collective-permute-start | bytes 24584 | tf_op jit(solution)/shard_map/ppermute | solution.py:648
  15.9 3.1 %collective-permute-start.5 = (f32[2,8,128]{2,1,0:T(8,128)S(1)}, f32[2,8,128]{2,1,0:T(8,128)S(1)}, u32[]{:S(2)}, u32[]{:S(2)}) collective-permute-start(f32[2,8,128]{2,1,0:T(8,128)S(1)} %blocks.3.refs_0_), channel_id=1, source_target_pairs={{0,5},{1,4},{2,7},{3,6},{4,1},{5,0},{6,3},{7,2},{8,13},{9,12},{10,... | collective-permute-start | bytes 24584 | tf_op jit(solution)/shard_map/ppermute | solution.py:648
  22.3 1.4 %collective-permute-start.8 = (f32[1,8,128]{2,1,0:T(8,128)S(1)}, f32[1,8,128]{2,1,0:T(8,128)S(1)}, u32[]{:S(2)}, u32[]{:S(2)}) collective-permute-start(f32[1,8,128]{2,1,0:T(8,128)S(1)} %bitcast.35), channel_id=1, source_target_pairs={{0,4},{4,0},{1,5},{5,1},{2,6},{6,2},{3,7},{7,3},{8,12},{12,8},{9,1... | collective-permute-start | bytes 12296 | tf_op jit(solution)/shard_map/ppermute | solution.py:620
  22.5 8.4 %collective-permute-start.9 = (bf16[8,64,128]{2,1,0:T(8,128)(2,1)S(1)}, bf16[8,64,128]{2,1,0:T(8,128)(2,1)S(1)}, u32[]{:S(2)}, u32[]{:S(2)}) collective-permute-start(bf16[8,64,128]{2,1,0:T(8,128)(2,1)S(1)} %get-tuple-element.93), channel_id=1, source_target_pairs={{0,1},{1,0},{2,3},{3,2},{4,5},{5,4},{6,7},{7,6},{8,9},{9,8},{10,11... | collective-permute-start | bytes 393224 | tf_op jit(solution)/shard_map/ppermute | solution.py:648
  23.4 7.5 %collective-permute-start.10 = (bf16[8,64,128]{2,1,0:T(8,128)(2,1)S(1)}, bf16[8,64,128]{2,1,0:T(8,128)(2,1)S(1)}, u32[]{:S(2)}, u32[]{:S(2)}) collective-permute-start(bf16[8,64,128]{2,1,0:T(8,128)(2,1)S(1)} %get-tuple-element.94), channel_id=1, source_target_pairs={{0,4},{1,2},{2,1},{3,7},{4,0},{5,6},{6,5},{7,3},{8,12},{9,10},{10,... | collective-permute-start | bytes 393224 | tf_op jit(solution)/shard_map/ppermute | solution.py:648
  23.6 5.7 %collective-permute-start.13 = (f32[2,8,128]{2,1,0:T(8,128)S(1)}, f32[2,8,128]{2,1,0:T(8,128)S(1)}, u32[]{:S(2)}, u32[]{:S(2)}) collective-permute-start(f32[2,8,128]{2,1,0:T(8,128)S(1)} %blocks.4.after_ref.refs_0_), channel_id=1, source_target_pairs={{0,6},{1,7},{2,4},{3,5},{4,2},{5,3},{6,0},{7,1},{8,14},{9,15},{10,... | collective-permute-start | bytes 24584 | tf_op jit(solution)/shard_map/ppermute | solution.py:648
  25.5 4.9 %collective-permute-start.12 = (f32[2,8,128]{2,1,0:T(8,128)S(1)}, f32[2,8,128]{2,1,0:T(8,128)S(1)}, u32[]{:S(2)}, u32[]{:S(2)}) collective-permute-start(f32[2,8,128]{2,1,0:T(8,128)S(1)} %blocks.4.after_ref.refs_0_), channel_id=1, source_target_pairs={{0,7},{1,6},{2,5},{3,4},{4,3},{5,2},{6,1},{7,0},{8,15},{9,14},{10,... | collective-permute-start | bytes 24584 | tf_op jit(solution)/shard_map/ppermute | solution.py:648
  27.8 3.1 %collective-permute-start.11 = (f32[2,8,128]{2,1,0:T(8,128)S(1)}, f32[2,8,128]{2,1,0:T(8,128)S(1)}, u32[]{:S(2)}, u32[]{:S(2)}) collective-permute-start(f32[2,8,128]{2,1,0:T(8,128)S(1)} %blocks.4.after_ref.refs_0_), channel_id=1, source_target_pairs={{0,5},{1,4},{2,7},{3,6},{4,1},{5,0},{6,3},{7,2},{8,13},{9,12},{10,... | collective-permute-start | bytes 24584 | tf_op jit(solution)/shard_map/ppermute | solution.py:648
  33.3 1.2 %collective-permute-start.14 = (f32[1,8,128]{2,1,0:T(8,128)S(1)}, f32[1,8,128]{2,1,0:T(8,128)S(1)}, u32[]{:S(2)}, u32[]{:S(2)}) collective-permute-start(f32[1,8,128]{2,1,0:T(8,128)S(1)} %bitcast.37), channel_id=1, source_target_pairs={{0,4},{4,0},{1,5},{5,1},{2,6},{6,2},{3,7},{7,3},{8,12},{12,8},{9,1... | collective-permute-start | bytes 12296 | tf_op jit(solution)/shard_map/ppermute | solution.py:620
  34.5 4.8 %collective-permute-start.17 = (f32[2,8,128]{2,1,0:T(8,128)S(1)}, f32[2,8,128]{2,1,0:T(8,128)S(1)}, u32[]{:S(2)}, u32[]{:S(2)}) collective-permute-start(f32[2,8,128]{2,1,0:T(8,128)S(1)} %blocks.5.after_ref.refs_0_), channel_id=1, source_target_pairs={{0,6},{1,7},{2,4},{3,5},{4,2},{5,3},{6,0},{7,1},{8,14},{9,15},{10,... | collective-permute-start | bytes 24584 | tf_op jit(solution)/shard_map/ppermute | solution.py:648
  35.1 4.9 %collective-permute-start.16 = (f32[2,8,128]{2,1,0:T(8,128)S(1)}, f32[2,8,128]{2,1,0:T(8,128)S(1)}, u32[]{:S(2)}, u32[]{:S(2)}) collective-permute-start(f32[2,8,128]{2,1,0:T(8,128)S(1)} %blocks.5.after_ref.refs_0_), channel_id=1, source_target_pairs={{0,7},{1,6},{2,5},{3,4},{4,3},{5,2},{6,1},{7,0},{8,15},{9,14},{10,... | collective-permute-start | bytes 24584 | tf_op jit(solution)/shard_map/ppermute | solution.py:648
  36.9 3.1 %collective-permute-start.15 = (f32[2,8,128]{2,1,0:T(8,128)S(1)}, f32[2,8,128]{2,1,0:T(8,128)S(1)}, u32[]{:S(2)}, u32[]{:S(2)}) collective-permute-start(f32[2,8,128]{2,1,0:T(8,128)S(1)} %blocks.5.after_ref.refs_0_), channel_id=1, source_target_pairs={{0,5},{1,4},{2,7},{3,6},{4,1},{5,0},{6,3},{7,2},{8,13},{9,12},{10,... | collective-permute-start | bytes 24584 | tf_op jit(solution)/shard_map/ppermute | solution.py:648
  42.2 1.7 %collective-permute-start.18 = (bf16[4,304,128]{2,1,0:T(8,128)(2,1)S(1)}, bf16[4,304,128]{2,1,0:T(8,128)(2,1)S(1)}, u32[]{:S(2)}, u32[]{:S(2)}) collective-permute-start(bf16[4,304,128]{2,1,0:T(8,128)(2,1)S(1)} %get-tuple-element.105), channel_id=1, source_target_pairs={{0,4},{4,0},{1,5},{5,1},{2,6},{6,2},{3,7},{7,3},{8,12},{12,8},{9,1... | collective-permute-start | bytes 933896 | tf_op jit(solution)/shard_map/ppermute | solution.py:620
  44.0 6.5 %collective-permute-start.21 = (bf16[304,128]{1,0:T(8,128)(2,1)S(1)}, bf16[304,128]{1,0:T(8,128)(2,1)S(1)}, u32[]{:S(2)}, u32[]{:S(2)}) collective-permute-start(bf16[304,128]{1,0:T(8,128)(2,1)S(1)} %get-tuple-element.112), channel_id=1, source_target_pairs={{0,16},{1,17},{2,18},{3,19},{4,6},{5,7},{6,4},{7,5},{8,24},{9,25},... | collective-permute-start | bytes 233480 | tf_op jit(solution)/shard_map/ppermute | solution.py:632
  45.6 5.3 %collective-permute-start.22 = (bf16[304,128]{1,0:T(8,128)(2,1)S(1)}, bf16[304,128]{1,0:T(8,128)(2,1)S(1)}, u32[]{:S(2)}, u32[]{:S(2)}) collective-permute-start(bf16[304,128]{1,0:T(8,128)(2,1)S(1)} %get-tuple-element.113), channel_id=1, source_target_pairs={{0,24},{1,25},{2,26},{3,27},{4,7},{5,6},{6,5},{7,4},{8,16},{9,17},... | collective-permute-start | bytes 233480 | tf_op jit(solution)/shard_map/ppermute | solution.py:632
  47.0 4.4 %collective-permute-start.23 = (bf16[304,128]{1,0:T(8,128)(2,1)S(1)}, bf16[304,128]{1,0:T(8,128)(2,1)S(1)}, u32[]{:S(2)}, u32[]{:S(2)}) collective-permute-start(bf16[304,128]{1,0:T(8,128)(2,1)S(1)} %get-tuple-element.114), channel_id=1, source_target_pairs={{0,8},{1,9},{2,10},{3,11},{4,5},{5,4},{6,7},{7,6},{8,0},{9,1},{10,... | collective-permute-start | bytes 233480 | tf_op jit(solution)/shard_map/ppermute | solution.py:632
  47.6 8.3 %collective-permute-start.19 = (bf16[8,64,128]{2,1,0:T(8,128)(2,1)S(1)}, bf16[8,64,128]{2,1,0:T(8,128)(2,1)S(1)}, u32[]{:S(2)}, u32[]{:S(2)}) collective-permute-start(bf16[8,64,128]{2,1,0:T(8,128)(2,1)S(1)} %get-tuple-element.109), channel_id=1, source_target_pairs={{0,4},{1,2},{2,1},{3,7},{4,0},{5,6},{6,5},{7,3},{8,12},{9,10},{10,... | collective-permute-start | bytes 393224 | tf_op jit(solution)/shard_map/ppermute | solution.py:648
  47.7 8.2 %collective-permute-start.20 = (bf16[8,64,128]{2,1,0:T(8,128)(2,1)S(1)}, bf16[8,64,128]{2,1,0:T(8,128)(2,1)S(1)}, u32[]{:S(2)}, u32[]{:S(2)}) collective-permute-start(bf16[8,64,128]{2,1,0:T(8,128)(2,1)S(1)} %get-tuple-element.110), channel_id=1, source_target_pairs={{0,1},{1,0},{2,3},{3,2},{4,5},{5,4},{6,7},{7,6},{8,9},{9,8},{10,11... | collective-permute-start | bytes 393224 | tf_op jit(solution)/shard_map/ppermute | solution.py:648
  51.5 6.4 %collective-permute-start.26 = (bf16[304,128]{1,0:T(8,128)(2,1)S(1)}, bf16[304,128]{1,0:T(8,128)(2,1)S(1)}, u32[]{:S(2)}, u32[]{:S(2)}) collective-permute-start(bf16[304,128]{1,0:T(8,128)(2,1)S(1)} %add_first.1.refs_0_), channel_id=1, source_target_pairs={{0,3},{1,2},{2,1},{3,0},{4,28},{5,29},{6,30},{7,31},{8,11},{9,10},... | collective-permute-start | bytes 233480 | tf_op jit(solution)/shard_map/ppermute | solution.py:632
  53.5 5.9 %collective-permute-start.25 = (bf16[304,128]{1,0:T(8,128)(2,1)S(1)}, bf16[304,128]{1,0:T(8,128)(2,1)S(1)}, u32[]{:S(2)}, u32[]{:S(2)}) collective-permute-start(bf16[304,128]{1,0:T(8,128)(2,1)S(1)} %add_first.1.refs_0_), channel_id=1, source_target_pairs={{0,2},{1,3},{2,0},{3,1},{4,20},{5,21},{6,22},{7,23},{8,10},{9,11},... | collective-permute-start | bytes 233480 | tf_op jit(solution)/shard_map/ppermute | solution.py:632
  53.7 5.7 %collective-permute-start.24 = (bf16[304,128]{1,0:T(8,128)(2,1)S(1)}, bf16[304,128]{1,0:T(8,128)(2,1)S(1)}, u32[]{:S(2)}, u32[]{:S(2)}) collective-permute-start(bf16[304,128]{1,0:T(8,128)(2,1)S(1)} %add_first.1.refs_0_), channel_id=1, source_target_pairs={{0,1},{1,0},{2,3},{3,2},{4,12},{5,13},{6,14},{7,15},{8,9},{9,8},{1... | collective-permute-start | bytes 233480 | tf_op jit(solution)/shard_map/ppermute | solution.py:632
  59.4 5.4 %collective-permute-start.29 = (bf16[304,128]{1,0:T(8,128)(2,1)S(1)}, bf16[304,128]{1,0:T(8,128)(2,1)S(1)}, u32[]{:S(2)}, u32[]{:S(2)}) collective-permute-start(bf16[304,128]{1,0:T(8,128)(2,1)S(1)} %add_second.1.refs_0_), channel_id=1, source_target_pairs={{0,24},{1,25},{2,26},{3,27},{4,7},{5,6},{6,5},{7,4},{8,16},{9,17},... | collective-permute-start | bytes 233480 | tf_op jit(solution)/shard_map/ppermute | solution.py:632
  61.3 4.4 %collective-permute-start.28 = (bf16[304,128]{1,0:T(8,128)(2,1)S(1)}, bf16[304,128]{1,0:T(8,128)(2,1)S(1)}, u32[]{:S(2)}, u32[]{:S(2)}) collective-permute-start(bf16[304,128]{1,0:T(8,128)(2,1)S(1)} %add_second.1.refs_0_), channel_id=1, source_target_pairs={{0,16},{1,17},{2,18},{3,19},{4,6},{5,7},{6,4},{7,5},{8,24},{9,25},... | collective-permute-start | bytes 233480 | tf_op jit(solution)/shard_map/ppermute | solution.py:632
  61.9 4.4 %collective-permute-start.27 = (bf16[304,128]{1,0:T(8,128)(2,1)S(1)}, bf16[304,128]{1,0:T(8,128)(2,1)S(1)}, u32[]{:S(2)}, u32[]{:S(2)}) collective-permute-start(bf16[304,128]{1,0:T(8,128)(2,1)S(1)} %add_second.1.refs_0_), channel_id=1, source_target_pairs={{0,8},{1,9},{2,10},{3,11},{4,5},{5,4},{6,7},{7,6},{8,0},{9,1},{10,... | collective-permute-start | bytes 233480 | tf_op jit(solution)/shard_map/ppermute | solution.py:632
  66.4 1.7 %collective-permute-start.30 = (bf16[1168,128]{1,0:T(8,128)(2,1)S(1)}, bf16[1168,128]{1,0:T(8,128)(2,1)S(1)}, u32[]{:S(2)}, u32[]{:S(2)}) collective-permute-start(bf16[1168,128]{1,0:T(8,128)(2,1)S(1)} %join.1.own_ref), channel_id=1, source_target_pairs={{0,4},{4,0},{1,5},{5,1},{2,6},{6,2},{3,7},{7,3},{8,12},{12,8},{9,1... | collective-permute-start | bytes 897032 | tf_op jit(solution)/shard_map/ppermute | solution.py:620
  (12 other events, 50.9 us)
